TPU v7x, 32 devices: a whole 2x2x4 slice. The times are simulated.
32 devices in a mesh: groups: 1, ep: 32 (over z, y, x, core), section: 1.
Axes of the slice: x: 2, y: 2, z: 4, core: 2. Of those that a mesh axis runs over, the one named last changes fastest.
Arguments:
- moe_rows: bfloat16 [2, 1024, 7168], P('section', ('groups', 'ep')), may hold values from -6 to 6
- routes: int32 [2, 1024, 2], P('section', ('groups', 'ep')), may hold values from 0 to 3, all different within a row; in each aligned block of 32 rows (0 to 31, 32 to 63, ..., all dimensions but the last counted through in order) at most 24 rows name the same one
- route_gates: float32 [2, 1024, 2], P('section', ('groups', 'ep')), may hold values from 0.1 to 1
- gate_proj: bfloat16 [7168, 4096], P(None, 'ep'), may hold values from -0.0625 to 0.0625
- up_proj: bfloat16 [7168, 4096], P(None, 'ep'), may hold values from -0.0625 to 0.0625
- down_proj: bfloat16 [4096, 7168], P('ep'), may hold values from -0.1875 to 0.1875
- queries: bfloat16 [256, 128, 576], P(('groups', 'ep')), may hold values from -400 to 400
- cache_latents: bfloat16 [256, 256, 576], P(('groups', 'ep')), may hold values from -5 to 5
- cache_lens: int32 [256], P(('groups', 'ep')), may hold values from 1 to 256, 32768 in all
- prompt_latents: bfloat16 [4096, 576], P(('groups', 'ep')), may hold values from -5 to 5
- kv_owner: int32 [4096, 1], P(('groups', 'ep')), may hold values from 0 to 31; in each aligned block of 128 rows (0 to 127, 128 to 255, ...) at most 8 rows name the same one
- kv_request: int32 [4096], P(('groups', 'ep')), may hold values from 0 to 7
Outputs:
- expert_out: bfloat16 [2, 1024, 7168], P('section', ('groups', 'ep'))
- attended: bfloat16 [256, 128, 512], P(('groups', 'ep'))
Inputs may be any that keep to these rules, and one draw needn't show every extreme that they name: `routes`: within each block of 32 rows of one section index and one ep index no expert is named by more than 24 rows, a bound that some block reaches. `kv_owner`: among the 128 rows of one ep index no owner is named by more than 8 rows, a bound that some block reaches.
All inputs are finite; a program needn't handle non-finite values. No bound on the sum of `cache_lens` on one device may be relied on, other than what follows from the above.
Results may differ from a plain program's by a relative error of at most 0.0057.
Values may be sent and summed in bfloat16 or wider, within the bound.
No kernel may reach another device: no remote copies, remote signals or barrier semaphores. Data moves between devices by JAX's collectives and lax.ppermute only.
A program may use at most 128 MiB of HBM per device.

v0:
```python
from functools import partial

import jax
import jax.numpy as jnp
from jax import lax
from jax.sharding import PartitionSpec as P

VDIM = 512
FF_WIN = 1024


score_scale = 0.07216878364870323


def slot_index(picks, expert_count, capacity):
    flat = picks.reshape(-1)
    hits = (flat[:, None] == jnp.arange(expert_count, dtype=jnp.int32)[None, :]).astype(jnp.int32)
    before = jnp.cumsum(hits, axis=0) - hits
    slot = jnp.sum(before * hits, axis=1)
    return (flat * capacity + slot).reshape(picks.shape)


def attend(query_part, cache_latents, cache_lens, handed, handed_id):
    requests = query_part.shape[0]
    cache_scores = (
        jnp.einsum("qhl,qcl->qhc", query_part, cache_latents, preferred_element_type=jnp.float32)
        * score_scale
    )
    hand_scores = (
        jnp.einsum("qhl,rl->qhr", query_part, handed, preferred_element_type=jnp.float32)
        * score_scale
    )
    cache_mask = (
        jnp.arange(cache_latents.shape[1], dtype=jnp.int32)[None, :] < cache_lens[:, None]
    )[:, None, :]
    hand_mask = (handed_id[None, :] == jnp.arange(requests, dtype=jnp.int32)[:, None])[:, None, :]
    cache_scores = jnp.where(cache_mask, cache_scores, -jnp.inf)
    hand_scores = jnp.where(hand_mask, hand_scores, -jnp.inf)
    top = jnp.maximum(jnp.max(cache_scores, axis=2), jnp.max(hand_scores, axis=2))[:, :, None]
    cache_expo = jnp.exp(cache_scores - top)
    hand_expo = jnp.exp(hand_scores - top)
    denom = (jnp.sum(cache_expo, axis=2) + jnp.sum(hand_expo, axis=2))[:, :, None]
    cache_prob = (cache_expo / denom).astype(jnp.bfloat16)
    hand_prob = (hand_expo / denom).astype(jnp.bfloat16)
    result = jnp.einsum(
        "qhc,qcv->qhv", cache_prob, cache_latents[:, :, :VDIM], preferred_element_type=jnp.float32
    )
    result = result + jnp.einsum(
        "qhr,rv->qhv", hand_prob, handed[:, :VDIM], preferred_element_type=jnp.float32
    )
    return result.astype(jnp.bfloat16)


def expert_section(rows, picks, gates, gate_proj, up_proj, down_proj):
    n_ep = lax.axis_size("ep")
    row_count, top_count = picks.shape
    width = rows.shape[1]
    hidden_dev = gate_proj.shape[1]
    split = FF_WIN // hidden_dev
    expert_count = n_ep // split
    capacity = min(row_count, 3 * row_count * top_count // (2 * expert_count))
    dest = slot_index(picks, expert_count, capacity)
    positions = jnp.arange(expert_count * capacity, dtype=jnp.int32)
    combine = jnp.sum(
        jnp.where(
            dest[:, :, None] == positions[None, None, :],
            gates[:, :, None],
            jnp.zeros_like(gates)[:, :, None],
        ),
        axis=1,
    )
    chosen = jnp.any(dest[None, :, :] == positions[:, None, None], axis=2).astype(jnp.bfloat16)
    packed = jnp.dot(chosen, rows, preferred_element_type=jnp.float32).astype(jnp.bfloat16)
    outgoing = jnp.broadcast_to(
        packed.reshape(expert_count, 1, capacity, width), (expert_count, split, capacity, width)
    ).reshape(n_ep, capacity, width)
    received = lax.all_to_all(outgoing, "ep", split_axis=0, concat_axis=0, tiled=True)
    flat = received.reshape(-1, received.shape[2])
    gate_val = jnp.dot(flat, gate_proj, preferred_element_type=jnp.float32)
    up_val = jnp.dot(flat, up_proj, preferred_element_type=jnp.float32)
    hidden = (jax.nn.silu(gate_val) * up_val).astype(jnp.bfloat16)
    partial_rows = (
        jnp.dot(hidden, down_proj, preferred_element_type=jnp.float32)
        .astype(jnp.bfloat16)
        .reshape(received.shape)
    )
    returned = lax.all_to_all(partial_rows, "ep", split_axis=0, concat_axis=0, tiled=True)
    value = jnp.sum(
        returned.reshape(expert_count, split, capacity, width), axis=1, dtype=jnp.float32
    ).reshape(expert_count * capacity, width)
    mixed = jnp.dot(
        combine, value, precision=lax.Precision.HIGHEST, preferred_element_type=jnp.float32
    )
    return mixed.astype(jnp.bfloat16)


def on_device(
    moe_rows,
    routes,
    route_gates,
    gate_proj,
    up_proj,
    down_proj,
    queries,
    cache_latents,
    cache_lens,
    prompt_latents,
    kv_owner,
    kv_request,
):
    n_ep = lax.axis_size("ep")
    outputs = []
    for section_pos in range(moe_rows.shape[0]):
        outputs.append(
            expert_section(
                moe_rows[section_pos],
                routes[section_pos],
                route_gates[section_pos],
                gate_proj,
                up_proj,
                down_proj,
            )
        )
    expert_out = jnp.stack(outputs, axis=0)
    stretch = prompt_latents.shape[0]
    sendcap = 2 * stretch // n_ep
    owners = kv_owner[:, 0]
    all_lat, all_owner, all_req = (
        lax.all_gather(prompt_latents, "ep", axis=0, tiled=True),
        lax.all_gather(owners, "ep", axis=0, tiled=True),
        lax.all_gather(kv_request, "ep", axis=0, tiled=True),
    )
    block_place = jax.vmap(partial(slot_index, expert_count=n_ep, capacity=sendcap))(
        all_owner.reshape(n_ep, stretch, 1)
    )[:, :, 0]
    targets = lax.axis_index("ep") * sendcap + jnp.arange(sendcap, dtype=jnp.int32)
    match = block_place[:, None, :] == targets[None, :, None]
    handed = jnp.einsum(
        "nsc,ncl->nsl",
        match.astype(jnp.bfloat16),
        all_lat.reshape(n_ep, stretch, -1),
        preferred_element_type=jnp.float32,
    ).astype(jnp.bfloat16)
    handed_id = (
        jnp.sum(jnp.where(match, all_req.reshape(n_ep, 1, stretch) + 1, 0), axis=2).astype(
            jnp.int32
        )
        - 1
    )
    handed = handed.reshape(n_ep * sendcap, -1)
    handed_id = handed_id.reshape(-1)
    attended = attend(queries, cache_latents, cache_lens, handed, handed_id)
    return (expert_out, attended)


def solution(mesh):
    placed = (
        P("section", ("groups", "ep"), None),
        P("section", ("groups", "ep"), None),
        P("section", ("groups", "ep"), None),
        P(None, "ep"),
        P(None, "ep"),
        P("ep", None),
        P(("groups", "ep"), None, None),
        P(("groups", "ep"), None, None),
        P(("groups", "ep")),
        P(("groups", "ep"), None),
        P(("groups", "ep"), None),
        P(("groups", "ep")),
    )
    return jax.shard_map(
        on_device,
        mesh=mesh,
        in_specs=placed,
        out_specs=(P("section", ("groups", "ep"), None), P(("groups", "ep"), None, None)),
        check_vma=False,
    )
```

profile of v0, /device:TPU:16, one launch (start us, length us, event | category | flops | bytes accessed | tf_op | source)
XLA Modules:
  0.0 1135.5 jit_solution(3934415471931144751)
XLA Ops:
  10.3 1.6 convolution_convert_fusion.2
  11.9 5.4 broadcast_in_dim.95
  17.3 6.0 all-to-all-start.2
  23.3 1.6 convolution_convert_fusion.3
  24.9 239.3 %all-to-all-done.2 = bf16[32,24,7168]{2,1,0:T(8,128)(2,1)} async-done(((bf16[32,24,7168]{2,1,0:T(8,128)(2,1)}), bf16[32,24,7168]{2,1,0:T(8,128)(2,1)}, u32[]{:S(2)}, u32[]{:S(2)}) %all-to-all-start.2) | async-done | bytes 11010080 | tf_op jit(solution)/shard_map/all_to_all | solution.py:77
  264.1 5.4 broadcast_in_dim.91
  269.5 6.8 all-to-all-start
  276.3 6.3 fusion.43
  282.6 17.3 %convolution_convert_fusion = bf16[768,7168]{1,0:T(8,128)(2,1)} fusion(bf16[128,7168]{1,0:T(8,128)(2,1)S(1)} %copy-done, bf16[768,7168]{1,0:T(8,128)(2,1)} %bitcast.17, bf16[7168,128]{1,0:T(8,128)(2,1)} %param.16, f32[768,128]{1,0:T(8,128)S(1)} %fusion.43), kind=kOutput, calls=%fused_computation.2 | convolution fusion | flops 2824667136 | bytes 26083328 | tf_op jit(solution)/shard_map/dot_general | solution.py:83
  299.9 217.3 %all-to-all-done = bf16[32,24,7168]{2,1,0:T(8,128)(2,1)} async-done(((bf16[32,24,7168]{2,1,0:T(8,128)(2,1)}), bf16[32,24,7168]{2,1,0:T(8,128)(2,1)}, u32[]{:S(2)}, u32[]{:S(2)}) %all-to-all-start) | async-done | bytes 11010080 | tf_op jit(solution)/shard_map/all_to_all | solution.py:77
  517.3 6.8 all-to-all-start.3
  524.0 6.3 fusion.42
  530.4 17.3 %convolution_convert_fusion.1 = bf16[768,7168]{1,0:T(8,128)(2,1)} fusion(bf16[128,7168]{1,0:T(8,128)(2,1)S(1)} %copy-done, bf16[768,7168]{1,0:T(8,128)(2,1)} %bitcast.6, bf16[7168,128]{1,0:T(8,128)(2,1)} %param.16, f32[768,128]{1,0:T(8,128)S(1)} %fusion.42), kind=kOutput, calls=%fused_computation.3 | convolution fusion | flops 2824667136 | bytes 26083328 | tf_op jit(solution)/shard_map/dot_general | solution.py:83
  547.7 217.6 %all-to-all-done.3 = bf16[32,24,7168]{2,1,0:T(8,128)(2,1)} async-done(((bf16[32,24,7168]{2,1,0:T(8,128)(2,1)}), bf16[32,24,7168]{2,1,0:T(8,128)(2,1)}, u32[]{:S(2)}, u32[]{:S(2)}) %all-to-all-start.3) | async-done | bytes 11010080 | tf_op jit(solution)/shard_map/all_to_all | solution.py:87
  765.2 6.9 all-to-all-start.1
  773.3 294.4 %all-gather = s32[4096,1]{0,1:T(1,128)S(1)} all-gather(s32[128,1]{0,1:T(1,128)S(1)} %copy-done.6), channel_id=2, replica_groups=mesh['groups'=1,'ep'=32,'section'=1] {'ep'}, dimensions={0}, use_global_device_ids=true | all-gather | bytes 16896 | tf_op jit(solution)/shard_map/all_gather | solution.py:130
  1067.7 3.3 fusion.8
  1071.1 29.4 %all-gather.1 = s32[32,1,128]{2,1,0:T(1,128)S(1)} all-gather(s32[1,1,128]{2,1,0:T(1,128)S(1)} %bitcast.113), channel_id=1, replica_groups=mesh['groups'=1,'ep'=32,'section'=1] {'ep'}, dimensions={0}, use_global_device_ids=true | all-gather | bytes 16896 | tf_op jit(solution)/shard_map/all_gather | solution.py:131
  1101.6 2.4 fusion.40
  1104.1 3.8 fusion.14
  1110.6 1.5 add_convert_fusion
  1112.1 6.3 convert_reduce_fusion
  1118.5 1.4 fusion.1
  1119.9 6.3 convert_reduce_fusion.1
  (63 shorter events, 10.5 us)
Async XLA Ops:
  7.2 275.5 %copy-start = (bf16[128,7168]{1,0:T(8,128)(2,1)S(1)}, bf16[128,7168]{1,0:T(8,128)(2,1)}, u32[]{:S(2)}) copy-start(bf16[128,7168]{1,0:T(8,128)(2,1)} %param.17) | copy-start | bytes 5505028
  17.3 246.8 %all-to-all-start.2 = ((bf16[32,24,7168]{2,1,0:T(8,128)(2,1)}), bf16[32,24,7168]{2,1,0:T(8,128)(2,1)}, u32[]{:S(2)}, u32[]{:S(2)}) async-start(bf16[32,24,7168]{2,1,0:T(8,128)(2,1)} %bitcast.104), calls=%async_computation.2 | async-start | bytes 22020096 | tf_op jit(solution)/shard_map/all_to_all | solution.py:77
  269.5 247.7 %all-to-all-start = ((bf16[32,24,7168]{2,1,0:T(8,128)(2,1)}), bf16[32,24,7168]{2,1,0:T(8,128)(2,1)}, u32[]{:S(2)}, u32[]{:S(2)}) async-start(bf16[32,24,7168]{2,1,0:T(8,128)(2,1)} %bitcast.103), calls=%async_computation | async-start | bytes 22020096 | tf_op jit(solution)/shard_map/all_to_all | solution.py:77
  517.3 248.0 %all-to-all-start.3 = ((bf16[32,24,7168]{2,1,0:T(8,128)(2,1)}), bf16[32,24,7168]{2,1,0:T(8,128)(2,1)}, u32[]{:S(2)}, u32[]{:S(2)}) async-start(bf16[32,24,7168]{2,1,0:T(8,128)(2,1)} %bitcast.102), calls=%async_computation.3 | async-start | bytes 22020096 | tf_op jit(solution)/shard_map/all_to_all | solution.py:87
  765.2 8.1 copy-start.6
  765.2 305.9 %copy-start.7 = (s32[128]{0:T(128)S(1)}, s32[128]{0:T(128)}, u32[]{:S(2)}) copy-start(s32[128]{0:T(128)} %param.23) | copy-start | bytes 1540
  765.2 336.2 %copy-start.5 = (f32[2,32,2]{1,2,0:T(2,128)S(1)}, f32[2,32,2]{1,2,0:T(2,128)}, u32[]{:S(2)}) copy-start(f32[2,32,2]{1,2,0:T(2,128)} %param.14) | copy-start | bytes 1540
  765.2 336.2 %copy-start.4 = (s32[2,32,2]{1,2,0:T(2,128)S(1)}, s32[2,32,2]{1,2,0:T(2,128)}, u32[]{:S(2)}) copy-start(s32[2,32,2]{1,2,0:T(2,128)} %param.13) | copy-start | bytes 1540
  765.2 336.3 %copy-start.8 = (s32[8]{0:T(128)S(1)}, s32[8]{0:T(128)}, u32[]{:S(2)}) copy-start(s32[8]{0:T(128)} %param.20) | copy-start | bytes 100
  765.2 336.4 %copy-start.3 = (bf16[8,128,576]{1,2,0:T(8,128)(2,1)S(1)}, bf16[8,128,576]{1,2,0:T(8,128)(2,1)}, u32[]{:S(2)}) copy-start(bf16[8,128,576]{1,2,0:T(8,128)(2,1)} %param.18) | copy-start | bytes 3538948
  765.2 354.6 %all-to-all-start.1 = ((bf16[32,24,7168]{2,1,0:T(8,128)(2,1)}), bf16[32,24,7168]{2,1,0:T(8,128)(2,1)}, u32[]{:S(2)}, u32[]{:S(2)}) async-start(bf16[32,24,7168]{2,1,0:T(8,128)(2,1)} %bitcast.101), calls=%async_computation.1 | async-start | bytes 22020096 | tf_op jit(solution)/shard_map/all_to_all | solution.py:87
  772.2 331.9 %all-gather.4.cloned.1.call-start = ((), (), s32[]{:S(2)}) async-start(), calls=%async_computation.4 | async-start | bytes 4866048 | tf_op jit(solution)/shard_map/all_gather | solution.py:129
  1107.9 1.7 copy-start.2
  1126.2 2.4 copy-start.1
Sparse Core Ops, SparseCore 0:
  775.9 162.1 all-gather.3
where the time goes:
time: 1140 us
  waiting for transfers between devices  675 us (59%)
  blocking collectives  324 us (28%)
  matrix products  62.7 us (6%)
  starting transfers between devices  26.5 us (2%)
  other arithmetic  20.2 us (2%)
  between operations  14.3 us (1%)
  local copies, waits for them, and re-layouts  13.1 us (1%)
    all_to_all x2, waiting for transfers between devices, expert_section(): lax.all_to_all(outgoing, 'ep', split_axis=0, concat_axis=0, tiled=True)  457 us
    all_gather x1, blocking collectives, on_device(): lax.all_gather(owners, 'ep', axis=0, tiled=True)  294 us
    all_to_all x2, waiting for transfers between devices, expert_section(): lax.all_to_all(partial_rows, 'ep', split_axis=0, concat_axis=0, tiled=True)  218 us
    dot_general x2, matrix products, expert_section(): jnp.dot(hidden, down_proj, preferred_element_type=jnp.float32)  34.6 us
    all_gather x1, blocking collectives, on_device(): lax.all_gather(kv_request, 'ep', axis=0, tiled=True)  29.4 us
  transfers between devices with their start and end apart: 5, of which 3 were waited for; matrix products, arithmetic and copies ran while one was open for 6% of the time, Pallas kernels for 0%

commit v1 on v0

v1 whole, which is shorter than its diff:
```python
from functools import partial

import jax
import jax.numpy as jnp
from jax import lax
from jax.experimental import pallas as pl
from jax.experimental.pallas import tpu as pltpu
from jax.sharding import PartitionSpec as P

VDIM = 512
FF_WIN = 1024
SLOT_ROWS = 8
CORE, XBIT, YBIT = 1, 2, 4
VMEM_BYTES = 48 * 1024 * 1024


score_scale = 0.07216878364870323


def swap(value, bit):
    count = lax.axis_size("ep")
    return lax.ppermute(value, "ep", [(i, i ^ bit) for i in range(count)])


def shift(value, step):
    count = lax.axis_size("ep")
    return lax.ppermute(value, "ep", [(i, (i + step) % count) for i in range(count)])


def hidden_kernel(*refs):
    units, blocks, (mine, theirs, acc) = refs[:8], refs[8:12], refs[12:]
    step = pl.program_id(0)

    @pl.when(step == 0)
    def _():
        acc[...] = jnp.zeros_like(acc)

    rows = jnp.concatenate([unit[...] for unit in units], axis=0)
    wide = blocks[0].shape[1]
    for at, block in enumerate(blocks):
        acc[:, at * wide : (at + 1) * wide] += jnp.dot(
            rows, block[...], preferred_element_type=jnp.float32
        )

    @pl.when(step == pl.num_programs(0) - 1)
    def _():
        half = wide // 2
        count = mine.shape[0]
        for at in range(len(blocks)):
            gate = acc[:, at * wide : at * wide + half]
            up = acc[:, at * wide + half : (at + 1) * wide]
            hidden = (gate / (1.0 + jnp.exp(-gate)) * up).astype(jnp.bfloat16)
            mine[:, at * half : (at + 1) * half] = hidden[:count]
            theirs[:, at * half : (at + 1) * half] = hidden[count:]


def hidden_units(units, blocks):
    rows, width = units[0].shape
    wide = blocks[0].shape[1]
    chunk = 1024
    count = rows * len(units) // 2
    out = jax.ShapeDtypeStruct((count, len(blocks) * wide // 2), jnp.bfloat16)
    return pl.pallas_call(
        hidden_kernel,
        grid=(width // chunk,),
        in_specs=[pl.BlockSpec((rows, chunk), lambda k: (0, k)) for _ in units]
        + [pl.BlockSpec((chunk, wide), lambda k: (k, 0)) for _ in blocks],
        out_specs=[pl.BlockSpec(out.shape, lambda k: (0, 0))] * 2,
        out_shape=[out, out],
        scratch_shapes=[pltpu.VMEM((2 * count, len(blocks) * wide), jnp.float32)],
        compiler_params=pltpu.CompilerParams(vmem_limit_bytes=VMEM_BYTES),
        cost_estimate=pl.CostEstimate(
            flops=2 * 2 * count * width * len(blocks) * wide,
            bytes_accessed=2 * (2 * count * width + len(blocks) * wide * width),
            transcendentals=0,
        ),
    )(*units, *blocks)


def down_kernel(planes, *refs):
    mine, other, weight, blocks, outs = refs[0], refs[1], refs[2], refs[3:-planes], refs[-planes:]
    hidden = jnp.concatenate([mine[...], other[...]], axis=1)
    table = jnp.concatenate([block[...] for block in blocks], axis=0)
    value = jnp.dot(hidden, table, preferred_element_type=jnp.float32) * weight[...]
    rows = outs[0].shape[0]
    for at, out in enumerate(outs):
        out[...] = value[at * rows : (at + 1) * rows].astype(out.dtype)


def down_values(mine, other, weight, blocks, planes):
    count, inner = mine.shape
    width = blocks[0].shape[1]
    rows = count // planes
    chunk = 1024 if width % 1024 == 0 else 512
    kinds = [jnp.float32] * (planes - 1) + [jnp.bfloat16]
    return pl.pallas_call(
        partial(down_kernel, planes),
        grid=(width // chunk,),
        in_specs=[
            pl.BlockSpec((count, inner), lambda k: (0, 0)),
            pl.BlockSpec((count, inner), lambda k: (0, 0)),
            pl.BlockSpec((count, 1), lambda k: (0, 0)),
        ]
        + [pl.BlockSpec((block.shape[0], chunk), lambda k: (0, k)) for block in blocks],
        out_specs=[pl.BlockSpec((rows, chunk), lambda k: (0, k)) for _ in kinds],
        out_shape=[jax.ShapeDtypeStruct((rows, width), kind) for kind in kinds],
        compiler_params=pltpu.CompilerParams(vmem_limit_bytes=VMEM_BYTES),
        cost_estimate=pl.CostEstimate(
            flops=2 * count * 2 * inner * width,
            bytes_accessed=2 * 2 * inner * width + 4 * count * width,
            transcendentals=0,
        ),
    )(mine, other, weight, *blocks)


def after(value, *others):
    return lax.optimization_barrier((value, *others))[0]


def expert_rows(rows, weight, gate_proj, up_proj, down_proj):
    n_ep = lax.axis_size("ep")
    split = FF_WIN // gate_proj.shape[1]
    planes = n_ep // split
    gate_up = jnp.concatenate([gate_proj, up_proj], axis=1)
    units = [rows]
    for _ in range(planes - 1):
        units.append(shift(units[-1], split))
    peers = [swap(unit, YBIT) for unit in units]
    block_x = swap(gate_up, XBIT)
    blocks = [gate_up, swap(gate_up, CORE), block_x, swap(block_x, CORE)]
    mine, theirs = hidden_units(units + peers, blocks)
    other = swap(theirs, YBIT)

    down = after(down_proj, block_x, peers[-1])
    half = down.shape[0] // 2
    down_x, down_y = swap(down, XBIT), swap(down, YBIT)
    corner = jnp.concatenate([swap(down_x[:half], YBIT), swap(down_y[half:], XBIT)], axis=0)
    tables = []
    for own in (down, down_x, down_y, corner):
        tables += [own, swap(own, CORE)]
    values = down_values(mine, other, weight, tables, planes)
    total = values[-1]
    for at in range(planes - 2, -1, -1):
        total = (shift(total, n_ep - split).astype(jnp.float32) + values[at]).astype(jnp.bfloat16)
    return total


def attend(query_part, cache_latents, cache_lens, handed, handed_mark):
    requests = query_part.shape[0]
    cache_scores = (
        jnp.einsum("qhl,qcl->qhc", query_part, cache_latents, preferred_element_type=jnp.float32)
        * score_scale
    )
    hand_scores = (
        jnp.einsum("qhl,rl->qhr", query_part, handed, preferred_element_type=jnp.float32)
        * score_scale
    )
    cache_mask = (
        jnp.arange(cache_latents.shape[1], dtype=jnp.int32)[None, :] < cache_lens[:, None]
    )[:, None, :]
    marks = jnp.arange(1, requests + 1, dtype=jnp.int32).astype(jnp.float32)
    hand_mask = (handed_mark[None, :] == marks[:, None])[:, None, :]
    cache_scores = jnp.where(cache_mask, cache_scores, -jnp.inf)
    hand_scores = jnp.where(hand_mask, hand_scores, -jnp.inf)
    top = jnp.maximum(jnp.max(cache_scores, axis=2), jnp.max(hand_scores, axis=2))[:, :, None]
    cache_expo = jnp.exp(cache_scores - top)
    hand_expo = jnp.exp(hand_scores - top)
    denom = (jnp.sum(cache_expo, axis=2) + jnp.sum(hand_expo, axis=2))[:, :, None]
    cache_prob = (cache_expo / denom).astype(jnp.bfloat16)
    hand_prob = (hand_expo / denom).astype(jnp.bfloat16)
    result = jnp.einsum(
        "qhc,qcv->qhv", cache_prob, cache_latents[:, :, :VDIM], preferred_element_type=jnp.float32
    )
    result = result + jnp.einsum(
        "qhr,rv->qhv", hand_prob, handed[:, :VDIM], preferred_element_type=jnp.float32
    )
    return result.astype(jnp.bfloat16)


def pieces(value):
    parts = []
    for _ in range(3):
        part = lax.reduce_precision(value, 8, 7)
        parts.append(part.astype(jnp.bfloat16))
        value = value - part
    return parts


def hand_over(prompt_latents, owners, requests, picks, gates, split):
    n_ep = lax.axis_size("ep")
    stretch, lat = prompt_latents.shape
    cap = 2 * stretch // n_ep
    places = jnp.arange(stretch, dtype=jnp.int32)
    earlier = (owners[:, None] == owners[None, :]) & (places[None, :] < places[:, None])
    target = owners * cap + jnp.sum(earlier.astype(jnp.int32), axis=1)
    slots = jnp.arange(n_ep * cap, dtype=jnp.int32)
    chosen = slots[:, None] == target[None, :]
    packed = jnp.dot(
        chosen.astype(jnp.bfloat16), prompt_latents, preferred_element_type=jnp.float32
    ).astype(jnp.bfloat16)
    mark = jnp.sum(jnp.where(chosen, requests[None, :] + 1, 0), axis=1).astype(jnp.bfloat16)
    planes = n_ep // split
    experts = jnp.arange(planes, dtype=jnp.int32)
    weights = jnp.sum(
        jnp.where(picks[None] == experts[:, None, None], gates[None], jnp.zeros_like(gates)[None]),
        axis=2,
    )
    lanes = weights.shape[1] // cap
    table = jnp.concatenate(
        [part.reshape(planes, 1, cap, lanes) for part in pieces(weights)], axis=3
    )
    table = jnp.broadcast_to(table, (planes, split, cap, 3 * lanes)).reshape(n_ep, cap, 3 * lanes)
    fill = -(lat + 1 + 3 * lanes) % 128
    outgoing = jnp.concatenate(
        [
            packed.reshape(n_ep, cap, lat),
            mark.reshape(n_ep, cap, 1),
            table,
            jnp.zeros((n_ep, cap, fill), jnp.bfloat16),
        ],
        axis=2,
    )
    incoming = lax.all_to_all(outgoing, "ep", split_axis=0, concat_axis=0, tiled=True)
    handed = incoming[:, :, :lat].reshape(n_ep * cap, lat)
    handed_mark = incoming[:, :, lat].reshape(n_ep * cap).astype(jnp.float32)
    here = lax.axis_index("ep")
    found = []
    for step in range(planes):
        source = (here - step * split + n_ep) % n_ep
        tile = lax.dynamic_index_in_dim(incoming, source, 0, keepdims=False)
        tile = tile[:, lat + 1 : lat + 1 + 3 * lanes].astype(jnp.float32)
        tile = tile.reshape(cap, 3, lanes)
        found.append((tile[:, 0] + tile[:, 1] + tile[:, 2]).reshape(cap * lanes, 1))
    return handed, handed_mark, jnp.concatenate(found, axis=0)


def on_device(
    moe_rows,
    routes,
    route_gates,
    gate_proj,
    up_proj,
    down_proj,
    queries,
    cache_latents,
    cache_lens,
    prompt_latents,
    kv_owner,
    kv_request,
):
    sections, count, width = moe_rows.shape
    top = routes.shape[2]
    split = FF_WIN // gate_proj.shape[1]
    handed, handed_mark, weight = hand_over(
        prompt_latents,
        kv_owner[:, 0],
        kv_request,
        routes.reshape(sections * count, top),
        route_gates.reshape(sections * count, top),
        split,
    )
    expert_out = expert_rows(
        moe_rows.reshape(sections * count, width), weight, gate_proj, up_proj, down_proj
    ).reshape(moe_rows.shape)
    attended = attend(queries, cache_latents, cache_lens, handed, handed_mark)
    return (expert_out, attended)


def solution(mesh):
    placed = (
        P("section", ("groups", "ep"), None),
        P("section", ("groups", "ep"), None),
        P("section", ("groups", "ep"), None),
        P(None, "ep"),
        P(None, "ep"),
        P("ep", None),
        P(("groups", "ep"), None, None),
        P(("groups", "ep"), None, None),
        P(("groups", "ep")),
        P(("groups", "ep"), None),
        P(("groups", "ep"), None),
        P(("groups", "ep")),
    )
    return jax.shard_map(
        on_device,
        mesh=mesh,
        in_specs=placed,
        out_specs=(P("section", ("groups", "ep"), None), P(("groups", "ep"), None, None)),
        check_vma=False,
    )
```

time: 1140 us -> 322 us (0.28)
  waiting for transfers between devices: 675 us -> 234 us
  blocking collectives: 324 us -> 0 us
  matrix products: 62.7 us -> 5.91 us
  Pallas kernels: 0 us -> 23.5 us
  other arithmetic: 20.2 us -> 6.56 us
  between operations: 14.3 us -> 0.92 us
    all_to_all x4 -> x1, waiting for transfers between devices: 674 us -> 16.4 us  [hand_over(): lax.all_to_all(outgoing, 'ep', split_axis=0, concat_axis=0, tiled=True)]
    all_gather x2 -> x0, blocking collectives: 324 us -> none  [the longest x1 294 us: on_device(): lax.all_gather(owners, 'ep', axis=0, tiled=True)]
    ppermute x0 -> x22, waiting for transfers between devices: none -> 218 us  [the longest x6 109 us: shift(): lax.ppermute(value, 'ep', [(i, (i + step) % count) for i in range(count)])]
    dot_general x9 -> x1, matrix products: 57 us -> 0.97 us  [hand_over(): jnp.dot(chosen.astype(jnp.bfloat16), prompt_latents, preferred_element_ty...]
    pallas_call x0 -> x2, Pallas kernels: none -> 23.5 us  [the longest x1 13.1 us: hidden_units(): pl.pallas_call(hidden_kernel, grid=(width // chunk,), in_specs=[pl.BlockS...]
    all_to_all x4 -> x1, starting transfers between devices: 26.5 us -> 3.15 us  [hand_over(): lax.all_to_all(outgoing, 'ep', split_axis=0, concat_axis=0, tiled=True)]
    ppermute x0 -> x22, starting transfers between devices: none -> 21 us  [the longest x16 15.2 us: swap(): return lax.ppermute(value, 'ep', [(i, i ^ bit) for i in range(count)])]
    reduce_sum x6 -> x3, other arithmetic: 13.8 us -> 0.3 us  [the longest x1 0.18 us: hand_over(): target = owners * cap + jnp.sum(earlier.astype(jnp.int32), axis=1)]
  transfers between devices with their start and end apart: 5 -> 23, of which waited for: 3 -> 14; matrix products, arithmetic and copies ran while one was open for 6% -> 8% of each run, Pallas kernels for 0% -> 4%
where the time goes in v1:
time: 322 us; the launch traced here: 319 us
  waiting for transfers between devices  234 us (73%)
  starting transfers between devices  24.1 us (7%)
  local copies, waits for them, and re-layouts  24 us (7%)
  Pallas kernels  23.5 us (7%)
  other arithmetic  6.56 us (2%)
  matrix products  5.91 us (2%)
    ppermute x6, waiting for transfers between devices, shift(): lax.ppermute(value, 'ep', [(i, (i + step) % count) for i in range(count)])  109 us
    ppermute x16, waiting for transfers between devices, swap(): return lax.ppermute(value, 'ep', [(i, i ^ bit) for i in range(count)])  108 us
    all_to_all x1, waiting for transfers between devices, hand_over(): lax.all_to_all(outgoing, 'ep', split_axis=0, concat_axis=0, tiled=True)  16.4 us
    ppermute x16, starting transfers between devices, swap(): return lax.ppermute(value, 'ep', [(i, i ^ bit) for i in range(count)])  15.2 us
    unnamed x58, local copies, waits for them, and re-layouts  13.4 us
    pallas_call x1, Pallas kernels, hidden_units(): pl.pallas_call(hidden_kernel, grid=(width // chunk,), in_specs=[pl.BlockS...  13.1 us
    pallas_call x1, Pallas kernels, down_values(): pl.pallas_call(partial(down_kernel, planes), grid=(width // chunk,), in_s...  10.3 us
  transfers between devices with their start and end apart: 23, of which 14 were waited for; matrix products, arithmetic and copies ran while one was open for 8% of the time, Pallas kernels for 4%

profile of v1, /device:TPU:16, one launch (start us, length us, event | category | flops | bytes accessed | tf_op | source)
XLA Modules:
  0.0 318.8 jit_solution(5631727780453598503)
XLA Ops:
  0.7 1.6 collective-permute-start
  2.3 2.9 constant_dynamic-update-slice_fusion.1
  8.2 14.8 %collective-permute-done.refs_1_ = bf16[64,7168]{1,0:T(8,128)(2,1)S(1)} collective-permute-done((bf16[64,7168]{1,0:T(8,128)(2,1)}, bf16[64,7168]{1,0:T(8,128)(2,1)S(1)}, u32[]{:S(2)}, u32[]{:S(2)}) %collective-permute-start) | collective-permute-done | bytes 917536 | tf_op jit(solution)/shard_map/ppermute | solution.py:27
  24.6 19.7 %collective-permute-done.1.refs_2_ = bf16[64,7168]{1,0:T(8,128)(2,1)S(1)} collective-permute-done((bf16[64,7168]{1,0:T(8,128)(2,1)S(1)}, bf16[64,7168]{1,0:T(8,128)(2,1)S(1)}, u32[]{:S(2)}, u32[]{:S(2)}) %collective-permute-start.1) | collective-permute-done | bytes 917536 | tf_op jit(solution)/shard_map/ppermute | solution.py:27
  45.9 18.9 %collective-permute-done.2.refs_3_ = bf16[64,7168]{1,0:T(8,128)(2,1)S(1)} collective-permute-done((bf16[64,7168]{1,0:T(8,128)(2,1)S(1)}, bf16[64,7168]{1,0:T(8,128)(2,1)S(1)}, u32[]{:S(2)}, u32[]{:S(2)}) %collective-permute-start.2) | collective-permute-done | bytes 917536 | tf_op jit(solution)/shard_map/ppermute | solution.py:27
  67.3 17.2 %collective-permute-done.6.refs_7_ = bf16[64,7168]{1,0:T(8,128)(2,1)S(1)} collective-permute-done((bf16[64,7168]{1,0:T(8,128)(2,1)S(1)}, bf16[64,7168]{1,0:T(8,128)(2,1)S(1)}, u32[]{:S(2)}, u32[]{:S(2)}) %collective-permute-start.6) | collective-permute-done | bytes 917536 | tf_op jit(solution)/shard_map/ppermute | solution.py:22
  84.5 3.2 %collective-permute-done.8.refs_10_ = bf16[7168,256]{1,0:T(8,128)(2,1)} collective-permute-done((bf16[7168,256]{1,0:T(8,128)(2,1)}, bf16[7168,256]{1,0:T(8,128)(2,1)}, u32[]{:S(2)}, u32[]{:S(2)}) %collective-permute-start.8) | collective-permute-done | bytes 3670048 | tf_op jit(solution)/shard_map/ppermute | solution.py:22
  94.5 34.2 %collective-permute-done.12.refs_5_ = bf16[128,7168]{1,0:T(8,128)(2,1)} collective-permute-done((bf16[128,7168]{1,0:T(8,128)(2,1)}, bf16[128,7168]{1,0:T(8,128)(2,1)}, u32[]{:S(2)}, u32[]{:S(2)}) %collective-permute-start.12) | collective-permute-done | bytes 1835040 | tf_op jit(solution)/shard_map/ppermute | solution.py:22
  128.7 2.2 slice.104
  132.4 2.2 slice.105
  136.9 3.2 all-to-all-start
  141.6 16.4 %all-to-all-done = bf16[32,8,640]{2,1,0:T(8,128)(2,1)S(1)} async-done(((bf16[32,8,640]{2,1,0:T(8,128)(2,1)}), bf16[32,8,640]{2,1,0:T(8,128)(2,1)S(1)}, u32[]{:S(2)}, u32[]{:S(2)}) %all-to-all-start) | async-done | bytes 327712 | tf_op jit(solution)/shard_map/all_to_all | solution.py:223
  160.1 2.2 constant_dynamic-update-slice_fusion.3
  162.3 2.2 constant_dynamic-update-slice_fusion.2.refs_9_
  164.5 13.1 %collective-permute-done.3.refs_4_ = bf16[64,7168]{1,0:T(8,128)(2,1)} collective-permute-done((bf16[64,7168]{1,0:T(8,128)(2,1)S(1)}, bf16[64,7168]{1,0:T(8,128)(2,1)}, u32[]{:S(2)}, u32[]{:S(2)}) %collective-permute-start.3) | collective-permute-done | bytes 917536 | tf_op jit(solution)/shard_map/ppermute | solution.py:22
  177.6 19.6 %collective-permute-done.4.refs_5_ = bf16[64,7168]{1,0:T(8,128)(2,1)S(1)} collective-permute-done((bf16[64,7168]{1,0:T(8,128)(2,1)S(1)}, bf16[64,7168]{1,0:T(8,128)(2,1)S(1)}, u32[]{:S(2)}, u32[]{:S(2)}) %collective-permute-start.4) | collective-permute-done | bytes 917536 | tf_op jit(solution)/shard_map/ppermute | solution.py:22
  198.1 15.4 %collective-permute-done.5.refs_6_ = bf16[64,7168]{1,0:T(8,128)(2,1)S(1)} collective-permute-done((bf16[64,7168]{1,0:T(8,128)(2,1)}, bf16[64,7168]{1,0:T(8,128)(2,1)S(1)}, u32[]{:S(2)}, u32[]{:S(2)}) %collective-permute-start.5) | collective-permute-done | bytes 917536 | tf_op jit(solution)/shard_map/ppermute | solution.py:22
  218.5 13.1 %shard_map.131 = (bf16[256,512]{1,0:T(8,128)(2,1)S(1)}, bf16[256,512]{1,0:T(8,128)(2,1)}) custom-call(bf16[64,7168]{1,0:T(8,128)(2,1)S(1)} %bitcast.41, bf16[64,7168]{1,0:T(8,128)(2,1)S(1)} %collective-permute-done.refs_1_, bf16[64,7168]{1,0:T(8,128)(2,1)S(1)} %copy-done.7, bf16[64,7168]{1,0:T(8,128)(2,1)S(1)} %copy-done.9, ...), custom_call_target="tpu_custom_call" | custom-call | flops 7516192768 | bytes 22020096 | tf_op jit(solution)/shard_map/pallas_call | solution.py:63
  234.0 5.7 %collective-permute-done.10.refs_1_ = bf16[256,512]{1,0:T(8,128)(2,1)S(1)} collective-permute-done((bf16[256,512]{1,0:T(8,128)(2,1)}, bf16[256,512]{1,0:T(8,128)(2,1)S(1)}, u32[]{:S(2)}, u32[]{:S(2)}) %collective-permute-start.10) | collective-permute-done | bytes 262176 | tf_op jit(solution)/shard_map/ppermute | solution.py:22
  241.3 10.3 %shard_map.132 = (f32[64,7168]{1,0:T(8,128)S(1)}, f32[64,7168]{1,0:T(8,128)S(1)}, f32[64,7168]{1,0:T(8,128)}, bf16[64,7168]{1,0:T(8,128)(2,1)S(1)}) custom-call(bf16[256,512]{1,0:T(8,128)(2,1)S(1)} %get-tuple-element.9.refs_0_, bf16[256,512]{1,0:T(8,128)(2,1)S(1)} %copy-done.4, f32[256,1]{1,0:T(8,128)S(1)} %copy.52.refs_2_, bf16[128,7168]{1,0:T(8,128)(2,1)} %refs_3_, ...), custom_call_target="tpu_custom_call" | custom-call | flops 3758096384 | bytes 22020096 | tf_op jit(solution)/shard_map/pallas_call | solution.py:96
  252.2 1.6 fusion.21
  253.9 18.8 %collective-permute-done.19 = bf16[64,7168]{1,0:T(8,128)(2,1)S(1)} collective-permute-done((bf16[64,7168]{1,0:T(8,128)(2,1)S(1)}, bf16[64,7168]{1,0:T(8,128)(2,1)S(1)}, u32[]{:S(2)}, u32[]{:S(2)}) %collective-permute-start.19) | collective-permute-done | bytes 917536 | tf_op jit(solution)/shard_map/ppermute | solution.py:27
  276.5 18.7 %collective-permute-done.20 = bf16[64,7168]{1,0:T(8,128)(2,1)} collective-permute-done((bf16[64,7168]{1,0:T(8,128)(2,1)}, bf16[64,7168]{1,0:T(8,128)(2,1)}, u32[]{:S(2)}, u32[]{:S(2)}) %collective-permute-start.20) | collective-permute-done | bytes 917536 | tf_op jit(solution)/shard_map/ppermute | solution.py:27
  299.7 18.0 %collective-permute-done.21 = bf16[64,7168]{1,0:T(8,128)(2,1)S(1)} collective-permute-done((bf16[64,7168]{1,0:T(8,128)(2,1)S(1)}, bf16[64,7168]{1,0:T(8,128)(2,1)S(1)}, u32[]{:S(2)}, u32[]{:S(2)}) %collective-permute-start.21) | collective-permute-done | bytes 917536 | tf_op jit(solution)/shard_map/ppermute | solution.py:27
  (137 shorter events, 42.5 us)
Async XLA Ops:
  0.6 251.6 %copy-start = (bf16[8,128,576]{1,2,0:T(8,128)(2,1)S(1)}, bf16[8,128,576]{1,2,0:T(8,128)(2,1)}, u32[]{:S(2)}) copy-start(bf16[8,128,576]{1,2,0:T(8,128)(2,1)} %param.18) | copy-start | bytes 3538948
  0.7 22.4 %collective-permute-start = (bf16[64,7168]{1,0:T(8,128)(2,1)}, bf16[64,7168]{1,0:T(8,128)(2,1)S(1)}, u32[]{:S(2)}, u32[]{:S(2)}) collective-permute-start(bf16[64,7168]{1,0:T(8,128)(2,1)} %bitcast.39), channel_id=1, source_target_pairs={{0,8},{1,9},{2,10},{3,11},{4,12},{5,13},{6,14},{7,15},{8,16},{9,17... | collective-permute-start | bytes 2752520 | tf_op jit(solution)/shard_map/ppermute | solution.py:27
  6.7 81.1 %collective-permute-start.8 = (bf16[7168,256]{1,0:T(8,128)(2,1)}, bf16[7168,256]{1,0:T(8,128)(2,1)}, u32[]{:S(2)}, u32[]{:S(2)}) collective-permute-start(bf16[7168,256]{1,0:T(8,128)(2,1)} %constant_dynamic-update-slice_fusion.refs_8_), channel_id=1, source_target_pairs={{0,2},{1,3},{2,0},{3,1},{4,6},{5,7},{6,4},{7,5},{8,10},{9,11},{10,... | collective-permute-start | bytes 11010056 | tf_op jit(solution)/shard_map/ppermute | solution.py:22
  23.0 21.3 %collective-permute-start.1 = (bf16[64,7168]{1,0:T(8,128)(2,1)S(1)}, bf16[64,7168]{1,0:T(8,128)(2,1)S(1)}, u32[]{:S(2)}, u32[]{:S(2)}) collective-permute-start(bf16[64,7168]{1,0:T(8,128)(2,1)S(1)} %collective-permute-done.refs_1_), channel_id=1, source_target_pairs={{0,8},{1,9},{2,10},{3,11},{4,12},{5,13},{6,14},{7,15},{8,16},{9,17... | collective-permute-start | bytes 2752520 | tf_op jit(solution)/shard_map/ppermute | solution.py:27
  44.3 20.5 %collective-permute-start.2 = (bf16[64,7168]{1,0:T(8,128)(2,1)S(1)}, bf16[64,7168]{1,0:T(8,128)(2,1)S(1)}, u32[]{:S(2)}, u32[]{:S(2)}) collective-permute-start(bf16[64,7168]{1,0:T(8,128)(2,1)S(1)} %collective-permute-done.1.refs_2_), channel_id=1, source_target_pairs={{0,8},{1,9},{2,10},{3,11},{4,12},{5,13},{6,14},{7,15},{8,16},{9,17... | collective-permute-start | bytes 2752520 | tf_op jit(solution)/shard_map/ppermute | solution.py:27
  64.8 19.7 %collective-permute-start.6 = (bf16[64,7168]{1,0:T(8,128)(2,1)S(1)}, bf16[64,7168]{1,0:T(8,128)(2,1)S(1)}, u32[]{:S(2)}, u32[]{:S(2)}) collective-permute-start(bf16[64,7168]{1,0:T(8,128)(2,1)S(1)} %collective-permute-done.2.refs_3_), channel_id=1, source_target_pairs={{0,4},{1,5},{2,6},{3,7},{4,0},{5,1},{6,2},{7,3},{8,12},{9,13},{10,... | collective-permute-start | bytes 2752520 | tf_op jit(solution)/shard_map/ppermute | solution.py:22
  87.8 40.9 %collective-permute-start.12 = (bf16[128,7168]{1,0:T(8,128)(2,1)}, bf16[128,7168]{1,0:T(8,128)(2,1)}, u32[]{:S(2)}, u32[]{:S(2)}) collective-permute-start(bf16[128,7168]{1,0:T(8,128)(2,1)} %refs_3_), channel_id=1, source_target_pairs={{0,2},{1,3},{2,0},{3,1},{4,6},{5,7},{6,4},{7,5},{8,10},{9,11},{10,... | collective-permute-start | bytes 5505032 | tf_op jit(solution)/shard_map/ppermute | solution.py:22
  89.3 43.1 %collective-permute-start.14 = (bf16[128,7168]{1,0:T(8,128)(2,1)}, bf16[128,7168]{1,0:T(8,128)(2,1)}, u32[]{:S(2)}, u32[]{:S(2)}) collective-permute-start(bf16[128,7168]{1,0:T(8,128)(2,1)} %refs_3_), channel_id=1, source_target_pairs={{0,4},{1,5},{2,6},{3,7},{4,0},{5,1},{6,2},{7,3},{8,12},{9,13},{10,... | collective-permute-start | bytes 5505032 | tf_op jit(solution)/shard_map/ppermute | solution.py:22
  90.8 122.7 %collective-permute-start.7 = (bf16[7168,256]{1,0:T(8,128)(2,1)}, bf16[7168,256]{1,0:T(8,128)(2,1)}, u32[]{:S(2)}, u32[]{:S(2)}) collective-permute-start(bf16[7168,256]{1,0:T(8,128)(2,1)} %constant_dynamic-update-slice_fusion.refs_8_), channel_id=1, source_target_pairs={{0,1},{1,0},{2,3},{3,2},{4,5},{5,4},{6,7},{7,6},{8,9},{9,8},{10,11... | collective-permute-start | bytes 11010056 | tf_op jit(solution)/shard_map/ppermute | solution.py:22
  92.3 122.7 %collective-permute-start.9 = (bf16[7168,256]{1,0:T(8,128)(2,1)}, bf16[7168,256]{1,0:T(8,128)(2,1)}, u32[]{:S(2)}, u32[]{:S(2)}) collective-permute-start(bf16[7168,256]{1,0:T(8,128)(2,1)} %collective-permute-done.8.refs_10_), channel_id=1, source_target_pairs={{0,1},{1,0},{2,3},{3,2},{4,5},{5,4},{6,7},{7,6},{8,9},{9,8},{10,11... | collective-permute-start | bytes 11010056 | tf_op jit(solution)/shard_map/ppermute | solution.py:22
  130.8 27.2 %collective-permute-start.16 = (bf16[64,7168]{1,0:T(8,128)(2,1)}, bf16[64,7168]{1,0:T(8,128)(2,1)}, u32[]{:S(2)}, u32[]{:S(2)}) collective-permute-start(bf16[64,7168]{1,0:T(8,128)(2,1)} %slice.104), channel_id=1, source_target_pairs={{0,4},{1,5},{2,6},{3,7},{4,0},{5,1},{6,2},{7,3},{8,12},{9,13},{10,... | collective-permute-start | bytes 2752520 | tf_op jit(solution)/shard_map/ppermute | solution.py:22
  134.6 24.9 %collective-permute-start.17 = (bf16[64,7168]{1,0:T(8,128)(2,1)}, bf16[64,7168]{1,0:T(8,128)(2,1)}, u32[]{:S(2)}, u32[]{:S(2)}) collective-permute-start(bf16[64,7168]{1,0:T(8,128)(2,1)} %slice.105), channel_id=1, source_target_pairs={{0,2},{1,3},{2,0},{3,1},{4,6},{5,7},{6,4},{7,5},{8,10},{9,11},{10,... | collective-permute-start | bytes 2752520 | tf_op jit(solution)/shard_map/ppermute | solution.py:22
  136.9 21.1 %all-to-all-start = ((bf16[32,8,640]{2,1,0:T(8,128)(2,1)}), bf16[32,8,640]{2,1,0:T(8,128)(2,1)S(1)}, u32[]{:S(2)}, u32[]{:S(2)}) async-start(bf16[32,8,640]{2,1,0:T(8,128)(2,1)} %maximum_maximum_fusion), calls=%async_computation | async-start | bytes 655360 | tf_op jit(solution)/shard_map/all_to_all | solution.py:223
  140.1 37.5 %collective-permute-start.3 = (bf16[64,7168]{1,0:T(8,128)(2,1)S(1)}, bf16[64,7168]{1,0:T(8,128)(2,1)}, u32[]{:S(2)}, u32[]{:S(2)}) collective-permute-start(bf16[64,7168]{1,0:T(8,128)(2,1)S(1)} %bitcast.40), channel_id=1, source_target_pairs={{0,4},{1,5},{2,6},{3,7},{4,0},{5,1},{6,2},{7,3},{8,12},{9,13},{10,... | collective-permute-start | bytes 2752520 | tf_op jit(solution)/shard_map/ppermute | solution.py:22
  158.0 39.2 %collective-permute-start.4 = (bf16[64,7168]{1,0:T(8,128)(2,1)S(1)}, bf16[64,7168]{1,0:T(8,128)(2,1)S(1)}, u32[]{:S(2)}, u32[]{:S(2)}) collective-permute-start(bf16[64,7168]{1,0:T(8,128)(2,1)S(1)} %collective-permute-done.refs_1_), channel_id=1, source_target_pairs={{0,4},{1,5},{2,6},{3,7},{4,0},{5,1},{6,2},{7,3},{8,12},{9,13},{10,... | collective-permute-start | bytes 2752520 | tf_op jit(solution)/shard_map/ppermute | solution.py:22
  159.4 54.1 %collective-permute-start.5 = (bf16[64,7168]{1,0:T(8,128)(2,1)}, bf16[64,7168]{1,0:T(8,128)(2,1)S(1)}, u32[]{:S(2)}, u32[]{:S(2)}) collective-permute-start(bf16[64,7168]{1,0:T(8,128)(2,1)} %copy-done.6), channel_id=1, source_target_pairs={{0,4},{1,5},{2,6},{3,7},{4,0},{5,1},{6,2},{7,3},{8,12},{9,13},{10,... | collective-permute-start | bytes 2752520 | tf_op jit(solution)/shard_map/ppermute | solution.py:22
  177.6 56.3 %collective-permute-start.11 = (bf16[128,7168]{1,0:T(8,128)(2,1)}, bf16[128,7168]{1,0:T(8,128)(2,1)}, u32[]{:S(2)}, u32[]{:S(2)}) collective-permute-start(bf16[128,7168]{1,0:T(8,128)(2,1)} %refs_3_), channel_id=1, source_target_pairs={{0,1},{1,0},{2,3},{3,2},{4,5},{5,4},{6,7},{7,6},{8,9},{9,8},{10,11... | collective-permute-start | bytes 5505032 | tf_op jit(solution)/shard_map/ppermute | solution.py:22
  198.1 35.8 %collective-permute-start.13 = (bf16[128,7168]{1,0:T(8,128)(2,1)}, bf16[128,7168]{1,0:T(8,128)(2,1)}, u32[]{:S(2)}, u32[]{:S(2)}) collective-permute-start(bf16[128,7168]{1,0:T(8,128)(2,1)} %collective-permute-done.12.refs_5_), channel_id=1, source_target_pairs={{0,1},{1,0},{2,3},{3,2},{4,5},{5,4},{6,7},{7,6},{8,9},{9,8},{10,11... | collective-permute-start | bytes 5505032 | tf_op jit(solution)/shard_map/ppermute | solution.py:22
  213.5 20.4 %collective-permute-start.15 = (bf16[128,7168]{1,0:T(8,128)(2,1)}, bf16[128,7168]{1,0:T(8,128)(2,1)}, u32[]{:S(2)}, u32[]{:S(2)}) collective-permute-start(bf16[128,7168]{1,0:T(8,128)(2,1)} %collective-permute-done.14.refs_7_), channel_id=1, source_target_pairs={{0,1},{1,0},{2,3},{3,2},{4,5},{5,4},{6,7},{7,6},{8,9},{9,8},{10,11... | collective-permute-start | bytes 5505032 | tf_op jit(solution)/shard_map/ppermute | solution.py:22
  213.5 26.8 %collective-permute-start.18 = (bf16[128,7168]{1,0:T(8,128)(2,1)}, bf16[128,7168]{1,0:T(8,128)(2,1)}, u32[]{:S(2)}, u32[]{:S(2)}) collective-permute-start(bf16[128,7168]{1,0:T(8,128)(2,1)} %constant_dynamic-update-slice_fusion.2.refs_9_), channel_id=1, source_target_pairs={{0,1},{1,0},{2,3},{3,2},{4,5},{5,4},{6,7},{7,6},{8,9},{9,8},{10,11... | collective-permute-start | bytes 5505032 | tf_op jit(solution)/shard_map/ppermute | solution.py:22
  231.6 8.0 %collective-permute-start.10 = (bf16[256,512]{1,0:T(8,128)(2,1)}, bf16[256,512]{1,0:T(8,128)(2,1)S(1)}, u32[]{:S(2)}, u32[]{:S(2)}) collective-permute-start(bf16[256,512]{1,0:T(8,128)(2,1)} %get-tuple-element.10), channel_id=1, source_target_pairs={{0,4},{1,5},{2,6},{3,7},{4,0},{5,1},{6,2},{7,3},{8,12},{9,13},{10,... | collective-permute-start | bytes 786440 | tf_op jit(solution)/shard_map/ppermute | solution.py:22
  251.7 21.0 %collective-permute-start.19 = (bf16[64,7168]{1,0:T(8,128)(2,1)S(1)}, bf16[64,7168]{1,0:T(8,128)(2,1)S(1)}, u32[]{:S(2)}, u32[]{:S(2)}) collective-permute-start(bf16[64,7168]{1,0:T(8,128)(2,1)S(1)} %get-tuple-element.12), channel_id=1, source_target_pairs={{0,24},{1,25},{2,26},{3,27},{4,28},{5,29},{6,30},{7,31},{8,0},{9,1... | collective-permute-start | bytes 2752520 | tf_op jit(solution)/shard_map/ppermute | solution.py:27
  273.7 21.5 %collective-permute-start.20 = (bf16[64,7168]{1,0:T(8,128)(2,1)}, bf16[64,7168]{1,0:T(8,128)(2,1)}, u32[]{:S(2)}, u32[]{:S(2)}) collective-permute-start(bf16[64,7168]{1,0:T(8,128)(2,1)} %add_convert_fusion.3), channel_id=1, source_target_pairs={{0,24},{1,25},{2,26},{3,27},{4,28},{5,29},{6,30},{7,31},{8,0},{9,1... | collective-permute-start | bytes 2752520 | tf_op jit(solution)/shard_map/ppermute | solution.py:27
  296.7 21.0 %collective-permute-start.21 = (bf16[64,7168]{1,0:T(8,128)(2,1)S(1)}, bf16[64,7168]{1,0:T(8,128)(2,1)S(1)}, u32[]{:S(2)}, u32[]{:S(2)}) collective-permute-start(bf16[64,7168]{1,0:T(8,128)(2,1)S(1)} %add_convert_fusion.2), channel_id=1, source_target_pairs={{0,24},{1,25},{2,26},{3,27},{4,28},{5,29},{6,30},{7,31},{8,0},{9,1... | collective-permute-start | bytes 2752520 | tf_op jit(solution)/shard_map/ppermute | solution.py:27
  (26 other events, 617.6 us)

commit v2 on v1

--- a/solution.py
+++ b/solution.py
@@ -27,26 +27,40 @@
     return lax.ppermute(value, "ep", [(i, (i + step) % count) for i in range(count)])
 
 
-def hidden_kernel(*refs):
-    units, blocks, (mine, theirs, acc) = refs[:8], refs[8:12], refs[12:]
+def together(*values):
+    return lax.optimization_barrier(values)
+
+
+def hidden_kernel(lead, *refs):
+    units, firsts, seconds, (mine, theirs, acc) = refs[:8], refs[8:12], refs[12:16], refs[16:]
     step = pl.program_id(0)
 
     @pl.when(step == 0)
     def _():
         acc[...] = jnp.zeros_like(acc)
 
-    rows = jnp.concatenate([unit[...] for unit in units], axis=0)
-    wide = blocks[0].shape[1]
-    for at, block in enumerate(blocks):
-        acc[:, at * wide : (at + 1) * wide] += jnp.dot(
-            rows, block[...], preferred_element_type=jnp.float32
-        )
+    wide = firsts[0].shape[1]
+
+    def add(blocks):
+        rows = jnp.concatenate([unit[...] for unit in units], axis=0)
+        for at, block in enumerate(blocks):
+            acc[:, at * wide : (at + 1) * wide] += jnp.dot(
+                rows, block[...], preferred_element_type=jnp.float32
+            )
+
+    @pl.when(step < lead)
+    def _():
+        add(firsts)
+
+    @pl.when(step >= lead)
+    def _():
+        add(seconds)
 
     @pl.when(step == pl.num_programs(0) - 1)
     def _():
         half = wide // 2
         count = mine.shape[0]
-        for at in range(len(blocks)):
+        for at in range(len(firsts)):
             gate = acc[:, at * wide : at * wide + half]
             up = acc[:, at * wide + half : (at + 1) * wide]
             hidden = (gate / (1.0 + jnp.exp(-gate)) * up).astype(jnp.bfloat16)
@@ -54,27 +68,28 @@
             theirs[:, at * half : (at + 1) * half] = hidden[count:]
 
 
-def hidden_units(units, blocks):
+def hidden_units(units, firsts, seconds, chunk):
     rows, width = units[0].shape
-    wide = blocks[0].shape[1]
-    chunk = 1024
+    lead, wide = firsts[0].shape[0] // chunk, firsts[0].shape[1]
     count = rows * len(units) // 2
-    out = jax.ShapeDtypeStruct((count, len(blocks) * wide // 2), jnp.bfloat16)
+    across = len(firsts) * wide
+    out = jax.ShapeDtypeStruct((count, across // 2), jnp.bfloat16)
     return pl.pallas_call(
-        hidden_kernel,
+        partial(hidden_kernel, lead),
         grid=(width // chunk,),
         in_specs=[pl.BlockSpec((rows, chunk), lambda k: (0, k)) for _ in units]
-        + [pl.BlockSpec((chunk, wide), lambda k: (k, 0)) for _ in blocks],
+        + [pl.BlockSpec((chunk, wide), lambda k: (jnp.minimum(k, lead - 1), 0)) for _ in firsts]
+        + [pl.BlockSpec((chunk, wide), lambda k: (jnp.maximum(k - lead, 0), 0)) for _ in seconds],
         out_specs=[pl.BlockSpec(out.shape, lambda k: (0, 0))] * 2,
         out_shape=[out, out],
-        scratch_shapes=[pltpu.VMEM((2 * count, len(blocks) * wide), jnp.float32)],
+        scratch_shapes=[pltpu.VMEM((2 * count, across), jnp.float32)],
         compiler_params=pltpu.CompilerParams(vmem_limit_bytes=VMEM_BYTES),
         cost_estimate=pl.CostEstimate(
-            flops=2 * 2 * count * width * len(blocks) * wide,
-            bytes_accessed=2 * (2 * count * width + len(blocks) * wide * width),
+            flops=2 * 2 * count * width * across,
+            bytes_accessed=2 * (2 * count * width + across * width),
             transcendentals=0,
         ),
-    )(*units, *blocks)
+    )(*units, *firsts, *seconds)
 
 
 def down_kernel(planes, *refs):
@@ -91,7 +106,7 @@
     count, inner = mine.shape
     width = blocks[0].shape[1]
     rows = count // planes
-    chunk = 1024 if width % 1024 == 0 else 512
+    chunk = 896 if width % 896 == 0 else 512
     kinds = [jnp.float32] * (planes - 1) + [jnp.bfloat16]
     return pl.pallas_call(
         partial(down_kernel, planes),
@@ -113,36 +128,53 @@
     )(mine, other, weight, *blocks)
 
 
-def after(value, *others):
-    return lax.optimization_barrier((value, *others))[0]
-
-
 def expert_rows(rows, weight, gate_proj, up_proj, down_proj):
     n_ep = lax.axis_size("ep")
     split = FF_WIN // gate_proj.shape[1]
     planes = n_ep // split
-    gate_up = jnp.concatenate([gate_proj, up_proj], axis=1)
-    units = [rows]
-    for _ in range(planes - 1):
-        units.append(shift(units[-1], split))
-    peers = [swap(unit, YBIT) for unit in units]
-    block_x = swap(gate_up, XBIT)
-    blocks = [gate_up, swap(gate_up, CORE), block_x, swap(block_x, CORE)]
-    mine, theirs = hidden_units(units + peers, blocks)
+    width = rows.shape[1]
+    chunk = width // 7
+    cut = 5 * chunk
+    first = jnp.concatenate([gate_proj[:cut], up_proj[:cut]], axis=1)
+    second = jnp.concatenate([gate_proj[cut:], up_proj[cut:]], axis=1)
+    first_x = swap(first, XBIT)
+    second, first_x = together(second, first_x)
+    second_x = swap(second, XBIT)
+    firsts = [first, swap(first, CORE), first_x, swap(first_x, CORE)]
+    seconds = [second, swap(second, CORE), second_x, swap(second_x, CORE)]
+
+    units, peers = [], []
+    unit = rows
+    for at in range(planes):
+        units.append(unit)
+        peer = swap(unit, YBIT)
+        if at < planes - 1:
+            unit, peer = together(shift(unit, split), peer)
+        peers.append(peer)
+    mine, theirs = hidden_units(units + peers, firsts, seconds, chunk)
     other = swap(theirs, YBIT)
 
-    down = after(down_proj, block_x, peers[-1])
-    half = down.shape[0] // 2
-    down_x, down_y = swap(down, XBIT), swap(down, YBIT)
-    corner = jnp.concatenate([swap(down_x[:half], YBIT), swap(down_y[half:], XBIT)], axis=0)
-    tables = []
-    for own in (down, down_x, down_y, corner):
-        tables += [own, swap(own, CORE)]
-    values = down_values(mine, other, weight, tables, planes)
-    total = values[-1]
-    for at in range(planes - 2, -1, -1):
-        total = (shift(total, n_ep - split).astype(jnp.float32) + values[at]).astype(jnp.bfloat16)
-    return total
+    half = down_proj.shape[0] // 2
+    span = width // 2
+    ready = (second_x, peers[-1])
+    values = []
+    for at in range(2):
+        down = together(down_proj[:, at * span : (at + 1) * span], *ready)[0]
+        down_x, down_y = together(swap(down, XBIT), swap(down, YBIT))
+        upper, lower = swap(down_x[:half], YBIT), swap(down_y[half:], XBIT)
+        ready = (upper, lower)
+        tables = []
+        for own in (down, down_x, down_y):
+            tables += [own, swap(own, CORE)]
+        tables += [upper, lower, swap(upper, CORE), swap(lower, CORE)]
+        values.append(down_values(mine, other, weight, tables, planes))
+    outs = []
+    for value in values:
+        total = value[-1]
+        for at in range(planes - 2, -1, -1):
+            total = (shift(total, n_ep - split).astype(jnp.float32) + value[at]).astype(jnp.bfloat16)
+        outs.append(total)
+    return jnp.concatenate(outs, axis=1)
 
 
 def attend(query_part, cache_latents, cache_lens, handed, handed_mark):

time: 322 us -> 261 us (0.81)
  waiting for transfers between devices: 234 us -> 150 us
  starting transfers between devices: 24.1 us -> 39.5 us
  local copies, waits for them, and re-layouts: 24 us -> 18.7 us
  matrix products: 5.91 us -> 11.2 us
  other arithmetic: 6.56 us -> 11.7 us
    ppermute x16 -> x29, waiting for transfers between devices: 108 us -> 58 us  [swap(): return lax.ppermute(value, 'ep', [(i, i ^ bit) for i in range(count)])]
    ppermute x6 -> x9, waiting for transfers between devices: 109 us -> 82.1 us  [shift(): lax.ppermute(value, 'ep', [(i, (i + step) % count) for i in range(count)])]
    unnamed x58 -> x50, local copies, waits for them, and re-layouts: 13.4 us -> 5.19 us
    ppermute x16 -> x29, starting transfers between devices: 15.2 us -> 22.5 us  [swap(): return lax.ppermute(value, 'ep', [(i, i ^ bit) for i in range(count)])]
    all_to_all x1, waiting for transfers between devices: 16.4 us -> 10.2 us  [hand_over(): lax.all_to_all(outgoing, 'ep', split_axis=0, concat_axis=0, tiled=True)]
    ppermute x6 -> x9, starting transfers between devices: 5.78 us -> 11.1 us  [shift(): lax.ppermute(value, 'ep', [(i, (i + step) % count) for i in range(count)])]
    concatenate x0 -> x3, other arithmetic: none -> 4.02 us  [the longest x1 1.76 us: expert_rows(): first = jnp.concatenate([gate_proj[:cut], up_proj[:cut]], axis=1)]
    concatenate x2 -> x0, local copies, waits for them, and re-layouts: 3.6 us -> none  [the longest x1 2.19 us: expert_rows(): jnp.concatenate([swap(down_x[:half], YBIT), swap(down_y[half:], XBIT)], a...]
  transfers between devices with their start and end apart: 23 -> 39, of which waited for: 14 -> 20; matrix products, arithmetic and copies ran while one was open for 8% -> 14% of each run, Pallas kernels for 4% -> 9%
where the time goes in v2:
time: 261 us; the launch traced here: 257 us
  waiting for transfers between devices  150 us (57%)
  starting transfers between devices  39.5 us (15%)
  Pallas kernels  24.1 us (9%)
  local copies, waits for them, and re-layouts  18.7 us (7%)
  other arithmetic  11.7 us (4%)
  matrix products  11.2 us (4%)
    ppermute x9, waiting for transfers between devices, shift(): lax.ppermute(value, 'ep', [(i, (i + step) % count) for i in range(count)])  82.1 us
    ppermute x29, waiting for transfers between devices, swap(): return lax.ppermute(value, 'ep', [(i, i ^ bit) for i in range(count)])  58 us
    ppermute x29, starting transfers between devices, swap(): return lax.ppermute(value, 'ep', [(i, i ^ bit) for i in range(count)])  22.5 us
    pallas_call x1, Pallas kernels, hidden_units(): pl.pallas_call(partial(hidden_kernel, lead), grid=(width // chunk,), in_s...  13.4 us
    ppermute x9, starting transfers between devices, shift(): lax.ppermute(value, 'ep', [(i, (i + step) % count) for i in range(count)])  11.1 us
    pallas_call x2, Pallas kernels, down_values(): pl.pallas_call(partial(down_kernel, planes), grid=(width // chunk,), in_s...  10.7 us
    all_to_all x1, waiting for transfers between devices, hand_over(): lax.all_to_all(outgoing, 'ep', split_axis=0, concat_axis=0, tiled=True)  10.2 us
    all_to_all x1, starting transfers between devices, hand_over(): lax.all_to_all(outgoing, 'ep', split_axis=0, concat_axis=0, tiled=True)  5.92 us
  transfers between devices with their start and end apart: 39, of which 20 were waited for; matrix products, arithmetic and copies ran while one was open for 14% of the time, Pallas kernels for 9%

profile of v2, /device:TPU:16, one launch (start us, length us, event | category | flops | bytes accessed | tf_op | source)
XLA Modules:
  0.0 256.6 jit_solution(2736066482591682574)
XLA Ops:
  7.1 15.9 %collective-permute-done.refs_1_ = bf16[64,7168]{1,0:T(8,128)(2,1)S(1)} collective-permute-done((bf16[64,7168]{1,0:T(8,128)(2,1)}, bf16[64,7168]{1,0:T(8,128)(2,1)S(1)}, u32[]{:S(2)}, u32[]{:S(2)}) %collective-permute-start) | collective-permute-done | bytes 917536 | tf_op jit(solution)/shard_map/ppermute | solution.py:27
  30.3 16.0 %collective-permute-done.2.refs_2_ = bf16[64,7168]{1,0:T(8,128)(2,1)S(1)} collective-permute-done((bf16[64,7168]{1,0:T(8,128)(2,1)S(1)}, bf16[64,7168]{1,0:T(8,128)(2,1)S(1)}, u32[]{:S(2)}, u32[]{:S(2)}) %collective-permute-start.2) | collective-permute-done | bytes 917536 | tf_op jit(solution)/shard_map/ppermute | solution.py:27
  46.9 2.2 collective-permute-start.4
  59.6 4.3 %collective-permute-done.8.refs_10_ = bf16[5120,256]{1,0:T(8,128)(2,1)} collective-permute-done((bf16[5120,256]{1,0:T(8,128)(2,1)}, bf16[5120,256]{1,0:T(8,128)(2,1)}, u32[]{:S(2)}, u32[]{:S(2)}) %collective-permute-start.8) | collective-permute-done | bytes 2621472 | tf_op jit(solution)/shard_map/ppermute | solution.py:22
  67.1 2.2 collective-permute-done.5.refs_6_
  71.8 17.0 %collective-permute-done.6.refs_7_ = bf16[64,7168]{1,0:T(8,128)(2,1)S(1)} collective-permute-done((bf16[64,7168]{1,0:T(8,128)(2,1)}, bf16[64,7168]{1,0:T(8,128)(2,1)S(1)}, u32[]{:S(2)}, u32[]{:S(2)}) %collective-permute-start.6) | collective-permute-done | bytes 917536 | tf_op jit(solution)/shard_map/ppermute | solution.py:22
  92.3 5.9 %all-to-all-start = ((bf16[32,8,640]{2,1,0:T(8,128)(2,1)}), bf16[32,8,640]{2,1,0:T(8,128)(2,1)S(1)}, u32[]{:S(2)}, u32[]{:S(2)}) async-start(bf16[32,8,640]{2,1,0:T(8,128)(2,1)} %maximum_maximum_fusion), calls=%async_computation | async-start | bytes 655360 | tf_op jit(solution)/shard_map/all_to_all | solution.py:255
  98.4 3.3 %fusion.22 = (f32[8,128]{1,0:T(8,128)S(1)}, f32[8,128,256]{2,1,0:T(8,128)}) fusion(bf16[8,128,576]{1,2,0:T(8,128)(2,1)S(1)} %copy-done, bf16[8,256,576]{1,2,0:T(8,128)(2,1)} %param.19, pred[8,256]{1,0:T(8,128)(4,1)S(1)} %iota_compare_fusion.3), kind=kOutput, calls=%fused_computation.76 | convolution fusion | flops 302775296 | bytes 4593664 | tf_op jit(solution)/shard_map/qhl,qcl->qhc/dot_general | solution.py:183
  101.8 10.2 %all-to-all-done = bf16[32,8,640]{2,1,0:T(8,128)(2,1)S(1)} async-done(((bf16[32,8,640]{2,1,0:T(8,128)(2,1)}), bf16[32,8,640]{2,1,0:T(8,128)(2,1)S(1)}, u32[]{:S(2)}, u32[]{:S(2)}) %all-to-all-start) | async-done | bytes 327712 | tf_op jit(solution)/shard_map/all_to_all | solution.py:255
  116.8 8.8 %collective-permute-done.19.refs_9_ = bf16[64,3584]{1,0:T(8,128)(2,1)S(1)} collective-permute-done((bf16[64,3584]{1,0:T(8,128)(2,1)S(1)}, bf16[64,3584]{1,0:T(8,128)(2,1)S(1)}, u32[]{:S(2)}, u32[]{:S(2)}) %collective-permute-start.19) | collective-permute-done | bytes 458784 | tf_op jit(solution)/shard_map/ppermute | solution.py:22
  128.6 8.6 %collective-permute-done.20.refs_10_ = bf16[64,3584]{1,0:T(8,128)(2,1)S(1)} collective-permute-done((bf16[64,3584]{1,0:T(8,128)(2,1)S(1)}, bf16[64,3584]{1,0:T(8,128)(2,1)S(1)}, u32[]{:S(2)}, u32[]{:S(2)}) %collective-permute-start.20) | collective-permute-done | bytes 458784 | tf_op jit(solution)/shard_map/ppermute | solution.py:22
  144.0 13.4 %shard_map.131 = (bf16[256,512]{1,0:T(8,128)(2,1)S(1)}, bf16[256,512]{1,0:T(8,128)(2,1)S(1)}) custom-call(bf16[64,7168]{1,0:T(8,128)(2,1)S(1)} %bitcast.41, bf16[64,7168]{1,0:T(8,128)(2,1)S(1)} %copy-done.4, bf16[64,7168]{1,0:T(8,128)(2,1)S(1)} %copy-done.8, bf16[64,7168]{1,0:T(8,128)(2,1)} %collective-permute-done.4.refs_3_, ...), custom_call_target="tpu_custom_call" | custom-call | flops 7516192768 | bytes 22020096 | tf_op jit(solution)/shard_map/pallas_call | solution.py:77
  160.8 6.6 %collective-permute-done.13.refs_1_ = bf16[256,512]{1,0:T(8,128)(2,1)S(1)} collective-permute-done((bf16[256,512]{1,0:T(8,128)(2,1)S(1)}, bf16[256,512]{1,0:T(8,128)(2,1)S(1)}, u32[]{:S(2)}, u32[]{:S(2)}) %collective-permute-start.13) | collective-permute-done | bytes 262176 | tf_op jit(solution)/shard_map/ppermute | solution.py:22
  176.2 2.8 %fusion = f32[8,128,512]{2,1,0:T(8,128)S(1)} fusion(bf16[8,256,576]{1,2,0:T(8,128)(2,1)} %param.19, f32[8,128,256]{2,1,0:T(8,128)} %get-tuple-element.62, f32[8,128]{1,0:T(8,128)S(1)} %add.226, f32[8,128]{1,0:T(8,128)S(1)} %max.7), kind=kOutput, calls=%fused_computation.2 | convolution fusion | flops 269221888 | bytes 5251072 | tf_op jit(solution)/shard_map/qhc,qcv->qhv/dot_general | solution.py:203
  179.0 7.5 %collective-permute-done.31.refs_9_ = bf16[64,3584]{1,0:T(8,128)(2,1)S(1)} collective-permute-done((bf16[64,3584]{1,0:T(8,128)(2,1)}, bf16[64,3584]{1,0:T(8,128)(2,1)S(1)}, u32[]{:S(2)}, u32[]{:S(2)}) %collective-permute-start.31) | collective-permute-done | bytes 458784 | tf_op jit(solution)/shard_map/ppermute | solution.py:22
  187.5 5.4 %shard_map.132 = (f32[64,3584]{1,0:T(8,128)S(1)}, f32[64,3584]{1,0:T(8,128)S(1)}, f32[64,3584]{1,0:T(8,128)S(1)}, bf16[64,3584]{1,0:T(8,128)(2,1)S(1)}) custom-call(bf16[256,512]{1,0:T(8,128)(2,1)S(1)} %get-tuple-element.34.refs_0_, bf16[256,512]{1,0:T(8,128)(2,1)S(1)} %collective-permute-done.13.refs_1_, f32[256,1]{1,0:T(8,128)S(1)} %copy.53.refs_2_, ...), custom_call_target="tpu_custom_call" | custom-call | flops 1879048192 | bytes 11010048 | tf_op jit(solution)/shard_map/pallas_call | solution.py:111
  194.7 5.3 %shard_map.133 = (f32[64,3584]{1,0:T(8,128)S(1)}, f32[64,3584]{1,0:T(8,128)S(1)}, f32[64,3584]{1,0:T(8,128)S(1)}, bf16[64,3584]{1,0:T(8,128)(2,1)S(1)}) custom-call(bf16[256,512]{1,0:T(8,128)(2,1)S(1)} %get-tuple-element.34.refs_0_, bf16[256,512]{1,0:T(8,128)(2,1)S(1)} %collective-permute-done.13.refs_1_, f32[256,1]{1,0:T(8,128)S(1)} %copy.53.refs_2_, ...), custom_call_target="tpu_custom_call" | custom-call | flops 1879048192 | bytes 11010048 | tf_op jit(solution)/shard_map/pallas_call | solution.py:111
  200.0 3.3 %collective-permute-start.35 = (bf16[64,3584]{1,0:T(8,128)(2,1)S(1)}, bf16[64,3584]{1,0:T(8,128)(2,1)S(1)}, u32[]{:S(2)}, u32[]{:S(2)}) collective-permute-start(bf16[64,3584]{1,0:T(8,128)(2,1)S(1)} %get-tuple-element.46), channel_id=1, source_target_pairs={{0,24},{1,25},{2,26},{3,27},{4,28},{5,29},{6,30},{7,31},{8,0},{9,1... | collective-permute-start | bytes 1376264 | tf_op jit(solution)/shard_map/ppermute | solution.py:27
  203.4 3.2 %collective-permute-done.23 = bf16[64,3584]{1,0:T(8,128)(2,1)S(1)} collective-permute-done((bf16[64,3584]{1,0:T(8,128)(2,1)S(1)}, bf16[64,3584]{1,0:T(8,128)(2,1)S(1)}, u32[]{:S(2)}, u32[]{:S(2)}) %collective-permute-start.23) | collective-permute-done | bytes 458784 | tf_op jit(solution)/shard_map/ppermute | solution.py:27
  207.4 8.9 %collective-permute-done.35 = bf16[64,3584]{1,0:T(8,128)(2,1)S(1)} collective-permute-done((bf16[64,3584]{1,0:T(8,128)(2,1)S(1)}, bf16[64,3584]{1,0:T(8,128)(2,1)S(1)}, u32[]{:S(2)}, u32[]{:S(2)}) %collective-permute-start.35) | collective-permute-done | bytes 458784 | tf_op jit(solution)/shard_map/ppermute | solution.py:27
  217.3 8.9 %collective-permute-done.24 = bf16[64,3584]{1,0:T(8,128)(2,1)S(1)} collective-permute-done((bf16[64,3584]{1,0:T(8,128)(2,1)S(1)}, bf16[64,3584]{1,0:T(8,128)(2,1)S(1)}, u32[]{:S(2)}, u32[]{:S(2)}) %collective-permute-start.24) | collective-permute-done | bytes 458784 | tf_op jit(solution)/shard_map/ppermute | solution.py:27
  227.1 8.9 %collective-permute-done.36 = bf16[64,3584]{1,0:T(8,128)(2,1)S(1)} collective-permute-done((bf16[64,3584]{1,0:T(8,128)(2,1)S(1)}, bf16[64,3584]{1,0:T(8,128)(2,1)S(1)}, u32[]{:S(2)}, u32[]{:S(2)}) %collective-permute-start.36) | collective-permute-done | bytes 458784 | tf_op jit(solution)/shard_map/ppermute | solution.py:27
  236.9 8.9 %collective-permute-done.25 = bf16[64,3584]{1,0:T(8,128)(2,1)S(1)} collective-permute-done((bf16[64,3584]{1,0:T(8,128)(2,1)S(1)}, bf16[64,3584]{1,0:T(8,128)(2,1)S(1)}, u32[]{:S(2)}, u32[]{:S(2)}) %collective-permute-start.25) | collective-permute-done | bytes 458784 | tf_op jit(solution)/shard_map/ppermute | solution.py:27
  246.0 9.6 %collective-permute-done.37 = bf16[64,3584]{1,0:T(8,128)(2,1)S(1)} collective-permute-done((bf16[64,3584]{1,0:T(8,128)(2,1)S(1)}, bf16[64,3584]{1,0:T(8,128)(2,1)S(1)}, u32[]{:S(2)}, u32[]{:S(2)}) %collective-permute-start.37) | collective-permute-done | bytes 458784 | tf_op jit(solution)/shard_map/ppermute | solution.py:27
  (176 shorter events, 68.1 us)
Async XLA Ops:
  0.7 22.4 %collective-permute-start = (bf16[64,7168]{1,0:T(8,128)(2,1)}, bf16[64,7168]{1,0:T(8,128)(2,1)S(1)}, u32[]{:S(2)}, u32[]{:S(2)}) collective-permute-start(bf16[64,7168]{1,0:T(8,128)(2,1)} %bitcast.39), channel_id=1, source_target_pairs={{0,8},{1,9},{2,10},{3,11},{4,12},{5,13},{6,14},{7,15},{8,16},{9,17... | collective-permute-start | bytes 2752520 | tf_op jit(solution)/shard_map/ppermute | solution.py:27
  2.3 22.0 %collective-permute-start.1 = (bf16[64,7168]{1,0:T(8,128)(2,1)}, bf16[64,7168]{1,0:T(8,128)(2,1)S(1)}, u32[]{:S(2)}, u32[]{:S(2)}) collective-permute-start(bf16[64,7168]{1,0:T(8,128)(2,1)} %bitcast.40), channel_id=1, source_target_pairs={{0,4},{1,5},{2,6},{3,7},{4,0},{5,1},{6,2},{7,3},{8,12},{9,13},{10,... | collective-permute-start | bytes 2752520 | tf_op jit(solution)/shard_map/ppermute | solution.py:22
  5.6 58.4 %collective-permute-start.8 = (bf16[5120,256]{1,0:T(8,128)(2,1)}, bf16[5120,256]{1,0:T(8,128)(2,1)}, u32[]{:S(2)}, u32[]{:S(2)}) collective-permute-start(bf16[5120,256]{1,0:T(8,128)(2,1)} %pad_maximum_fusion.refs_8_), channel_id=1, source_target_pairs={{0,2},{1,3},{2,0},{3,1},{4,6},{5,7},{6,4},{7,5},{8,10},{9,11},{10,... | collective-permute-start | bytes 7864328 | tf_op jit(solution)/shard_map/ppermute | solution.py:22
  25.3 21.0 %collective-permute-start.2 = (bf16[64,7168]{1,0:T(8,128)(2,1)S(1)}, bf16[64,7168]{1,0:T(8,128)(2,1)S(1)}, u32[]{:S(2)}, u32[]{:S(2)}) collective-permute-start(bf16[64,7168]{1,0:T(8,128)(2,1)S(1)} %collective-permute-done.refs_1_), channel_id=1, source_target_pairs={{0,8},{1,9},{2,10},{3,11},{4,12},{5,13},{6,14},{7,15},{8,16},{9,17... | collective-permute-start | bytes 2752520 | tf_op jit(solution)/shard_map/ppermute | solution.py:27
  25.7 21.1 %collective-permute-start.3 = (bf16[64,7168]{1,0:T(8,128)(2,1)S(1)}, bf16[64,7168]{1,0:T(8,128)(2,1)}, u32[]{:S(2)}, u32[]{:S(2)}) collective-permute-start(bf16[64,7168]{1,0:T(8,128)(2,1)S(1)} %collective-permute-done.refs_1_), channel_id=1, source_target_pairs={{0,4},{1,5},{2,6},{3,7},{4,0},{5,1},{6,2},{7,3},{8,12},{9,13},{10,... | collective-permute-start | bytes 2752520 | tf_op jit(solution)/shard_map/ppermute | solution.py:22
  27.2 110.0 %collective-permute-start.7 = (bf16[5120,256]{1,0:T(8,128)(2,1)}, bf16[5120,256]{1,0:T(8,128)(2,1)}, u32[]{:S(2)}, u32[]{:S(2)}) collective-permute-start(bf16[5120,256]{1,0:T(8,128)(2,1)} %pad_maximum_fusion.refs_8_), channel_id=1, source_target_pairs={{0,1},{1,0},{2,3},{3,2},{4,5},{5,4},{6,7},{7,6},{8,9},{9,8},{10,11... | collective-permute-start | bytes 7864328 | tf_op jit(solution)/shard_map/ppermute | solution.py:22
  46.9 20.2 %collective-permute-start.4 = (bf16[64,7168]{1,0:T(8,128)(2,1)S(1)}, bf16[64,7168]{1,0:T(8,128)(2,1)}, u32[]{:S(2)}, u32[]{:S(2)}) collective-permute-start(bf16[64,7168]{1,0:T(8,128)(2,1)S(1)} %collective-permute-done.2.refs_2_), channel_id=1, source_target_pairs={{0,8},{1,9},{2,10},{3,11},{4,12},{5,13},{6,14},{7,15},{8,16},{9,17... | collective-permute-start | bytes 2752520 | tf_op jit(solution)/shard_map/ppermute | solution.py:27
  49.0 20.3 %collective-permute-start.5 = (bf16[64,7168]{1,0:T(8,128)(2,1)S(1)}, bf16[64,7168]{1,0:T(8,128)(2,1)}, u32[]{:S(2)}, u32[]{:S(2)}) collective-permute-start(bf16[64,7168]{1,0:T(8,128)(2,1)S(1)} %collective-permute-done.2.refs_2_), channel_id=1, source_target_pairs={{0,4},{1,5},{2,6},{3,7},{4,0},{5,1},{6,2},{7,3},{8,12},{9,13},{10,... | collective-permute-start | bytes 2752520 | tf_op jit(solution)/shard_map/ppermute | solution.py:22
  64.0 24.8 %collective-permute-start.11 = (bf16[2048,256]{1,0:T(8,128)(2,1)S(1)}, bf16[2048,256]{1,0:T(8,128)(2,1)S(1)}, u32[]{:S(2)}, u32[]{:S(2)}) collective-permute-start(bf16[2048,256]{1,0:T(8,128)(2,1)S(1)} %pad_maximum_fusion.1.refs_12_), channel_id=1, source_target_pairs={{0,2},{1,3},{2,0},{3,1},{4,6},{5,7},{6,4},{7,5},{8,10},{9,11},{10,... | collective-permute-start | bytes 3145736 | tf_op jit(solution)/shard_map/ppermute | solution.py:22
  71.7 67.5 %collective-permute-start.9 = (bf16[5120,256]{1,0:T(8,128)(2,1)}, bf16[5120,256]{1,0:T(8,128)(2,1)}, u32[]{:S(2)}, u32[]{:S(2)}) collective-permute-start(bf16[5120,256]{1,0:T(8,128)(2,1)} %collective-permute-done.8.refs_10_), channel_id=1, source_target_pairs={{0,1},{1,0},{2,3},{3,2},{4,5},{5,4},{6,7},{7,6},{8,9},{9,8},{10,11... | collective-permute-start | bytes 7864328 | tf_op jit(solution)/shard_map/ppermute | solution.py:22
  88.8 23.2 %collective-permute-start.15 = (bf16[128,3584]{1,0:T(8,128)(2,1)S(1)}, bf16[128,3584]{1,0:T(8,128)(2,1)}, u32[]{:S(2)}, u32[]{:S(2)}) collective-permute-start(bf16[128,3584]{1,0:T(8,128)(2,1)S(1)} %get-tuple-element.36.refs_3_), channel_id=1, source_target_pairs={{0,2},{1,3},{2,0},{3,1},{4,6},{5,7},{6,4},{7,5},{8,10},{9,11},{10,... | collective-permute-start | bytes 2752520 | tf_op jit(solution)/shard_map/ppermute | solution.py:22
  90.2 21.8 %collective-permute-start.16 = (bf16[128,3584]{1,0:T(8,128)(2,1)S(1)}, bf16[128,3584]{1,0:T(8,128)(2,1)}, u32[]{:S(2)}, u32[]{:S(2)}) collective-permute-start(bf16[128,3584]{1,0:T(8,128)(2,1)S(1)} %get-tuple-element.36.refs_3_), channel_id=1, source_target_pairs={{0,4},{1,5},{2,6},{3,7},{4,0},{5,1},{6,2},{7,3},{8,12},{9,13},{10,... | collective-permute-start | bytes 2752520 | tf_op jit(solution)/shard_map/ppermute | solution.py:22
  92.3 19.7 %all-to-all-start = ((bf16[32,8,640]{2,1,0:T(8,128)(2,1)}), bf16[32,8,640]{2,1,0:T(8,128)(2,1)S(1)}, u32[]{:S(2)}, u32[]{:S(2)}) async-start(bf16[32,8,640]{2,1,0:T(8,128)(2,1)} %maximum_maximum_fusion), calls=%async_computation | async-start | bytes 655360 | tf_op jit(solution)/shard_map/all_to_all | solution.py:255
  114.8 22.9 %collective-permute-start.10 = (bf16[2048,256]{1,0:T(8,128)(2,1)}, bf16[2048,256]{1,0:T(8,128)(2,1)}, u32[]{:S(2)}, u32[]{:S(2)}) collective-permute-start(bf16[2048,256]{1,0:T(8,128)(2,1)} %copy-done.13), channel_id=1, source_target_pairs={{0,1},{1,0},{2,3},{3,2},{4,5},{5,4},{6,7},{7,6},{8,9},{9,8},{10,11... | collective-permute-start | bytes 3145736 | tf_op jit(solution)/shard_map/ppermute | solution.py:22
  114.9 23.0 %collective-permute-start.12 = (bf16[2048,256]{1,0:T(8,128)(2,1)}, bf16[2048,256]{1,0:T(8,128)(2,1)}, u32[]{:S(2)}, u32[]{:S(2)}) collective-permute-start(bf16[2048,256]{1,0:T(8,128)(2,1)} %copy-done.22), channel_id=1, source_target_pairs={{0,1},{1,0},{2,3},{3,2},{4,5},{5,4},{6,7},{7,6},{8,9},{9,8},{10,11... | collective-permute-start | bytes 3145736 | tf_op jit(solution)/shard_map/ppermute | solution.py:22
  137.2 20.2 %collective-permute-start.14 = (bf16[128,3584]{1,0:T(8,128)(2,1)}, bf16[128,3584]{1,0:T(8,128)(2,1)S(1)}, u32[]{:S(2)}, u32[]{:S(2)}) collective-permute-start(bf16[128,3584]{1,0:T(8,128)(2,1)} %copy-done.10), channel_id=1, source_target_pairs={{0,1},{1,0},{2,3},{3,2},{4,5},{5,4},{6,7},{7,6},{8,9},{9,8},{10,11... | collective-permute-start | bytes 2752520 | tf_op jit(solution)/shard_map/ppermute | solution.py:22
  137.2 35.6 %collective-permute-start.17 = (bf16[128,3584]{1,0:T(8,128)(2,1)}, bf16[128,3584]{1,0:T(8,128)(2,1)}, u32[]{:S(2)}, u32[]{:S(2)}) collective-permute-start(bf16[128,3584]{1,0:T(8,128)(2,1)} %collective-permute-done.15.refs_5_), channel_id=1, source_target_pairs={{0,1},{1,0},{2,3},{3,2},{4,5},{5,4},{6,7},{7,6},{8,9},{9,8},{10,11... | collective-permute-start | bytes 2752520 | tf_op jit(solution)/shard_map/ppermute | solution.py:22
  137.7 35.6 %collective-permute-start.18 = (bf16[128,3584]{1,0:T(8,128)(2,1)}, bf16[128,3584]{1,0:T(8,128)(2,1)}, u32[]{:S(2)}, u32[]{:S(2)}) collective-permute-start(bf16[128,3584]{1,0:T(8,128)(2,1)} %collective-permute-done.16.refs_7_), channel_id=1, source_target_pairs={{0,1},{1,0},{2,3},{3,2},{4,5},{5,4},{6,7},{7,6},{8,9},{9,8},{10,11... | collective-permute-start | bytes 2752520 | tf_op jit(solution)/shard_map/ppermute | solution.py:22
  137.8 29.6 %collective-permute-start.27 = (bf16[128,3584]{1,0:T(8,128)(2,1)}, bf16[128,3584]{1,0:T(8,128)(2,1)}, u32[]{:S(2)}, u32[]{:S(2)}) collective-permute-start(bf16[128,3584]{1,0:T(8,128)(2,1)} %get-tuple-element.43.refs_3_), channel_id=1, source_target_pairs={{0,2},{1,3},{2,0},{3,1},{4,6},{5,7},{6,4},{7,5},{8,10},{9,11},{10,... | collective-permute-start | bytes 2752520 | tf_op jit(solution)/shard_map/ppermute | solution.py:22
  139.2 28.8 %collective-permute-start.28 = (bf16[128,3584]{1,0:T(8,128)(2,1)}, bf16[128,3584]{1,0:T(8,128)(2,1)}, u32[]{:S(2)}, u32[]{:S(2)}) collective-permute-start(bf16[128,3584]{1,0:T(8,128)(2,1)} %get-tuple-element.43.refs_3_), channel_id=1, source_target_pairs={{0,4},{1,5},{2,6},{3,7},{4,0},{5,1},{6,2},{7,3},{8,12},{9,13},{10,... | collective-permute-start | bytes 2752520 | tf_op jit(solution)/shard_map/ppermute | solution.py:22
  168.0 24.9 %collective-permute-start.26 = (bf16[128,3584]{1,0:T(8,128)(2,1)}, bf16[128,3584]{1,0:T(8,128)(2,1)}, u32[]{:S(2)}, u32[]{:S(2)}) collective-permute-start(bf16[128,3584]{1,0:T(8,128)(2,1)} %get-tuple-element.43.refs_3_), channel_id=1, source_target_pairs={{0,1},{1,0},{2,3},{3,2},{4,5},{5,4},{6,7},{7,6},{8,9},{9,8},{10,11... | collective-permute-start | bytes 2752520 | tf_op jit(solution)/shard_map/ppermute | solution.py:22
  172.9 21.8 %collective-permute-start.29 = (bf16[128,3584]{1,0:T(8,128)(2,1)}, bf16[128,3584]{1,0:T(8,128)(2,1)}, u32[]{:S(2)}, u32[]{:S(2)}) collective-permute-start(bf16[128,3584]{1,0:T(8,128)(2,1)} %collective-permute-done.27.refs_5_), channel_id=1, source_target_pairs={{0,1},{1,0},{2,3},{3,2},{4,5},{5,4},{6,7},{7,6},{8,9},{9,8},{10,11... | collective-permute-start | bytes 2752520 | tf_op jit(solution)/shard_map/ppermute | solution.py:22
  173.4 21.3 %collective-permute-start.30 = (bf16[128,3584]{1,0:T(8,128)(2,1)}, bf16[128,3584]{1,0:T(8,128)(2,1)}, u32[]{:S(2)}, u32[]{:S(2)}) collective-permute-start(bf16[128,3584]{1,0:T(8,128)(2,1)} %collective-permute-done.28.refs_7_), channel_id=1, source_target_pairs={{0,1},{1,0},{2,3},{3,2},{4,5},{5,4},{6,7},{7,6},{8,9},{9,8},{10,11... | collective-permute-start | bytes 2752520 | tf_op jit(solution)/shard_map/ppermute | solution.py:22
  216.5 19.6 %collective-permute-start.36 = (bf16[64,3584]{1,0:T(8,128)(2,1)S(1)}, bf16[64,3584]{1,0:T(8,128)(2,1)S(1)}, u32[]{:S(2)}, u32[]{:S(2)}) collective-permute-start(bf16[64,3584]{1,0:T(8,128)(2,1)S(1)} %add_convert_fusion.3), channel_id=1, source_target_pairs={{0,24},{1,25},{2,26},{3,27},{4,28},{5,29},{6,30},{7,31},{8,0},{9,1... | collective-permute-start | bytes 1376264 | tf_op jit(solution)/shard_map/ppermute | solution.py:27
  (42 other events, 719.0 us)

commit v3 on v1

v3 whole, which is shorter than its diff:
```python
from functools import partial

import jax
import jax.numpy as jnp
from jax import lax
from jax.experimental import pallas as pl
from jax.experimental.pallas import tpu as pltpu
from jax.sharding import PartitionSpec as P

VDIM = 512
FF_WIN = 1024
SLOT_ROWS = 8
CORE, XBIT, YBIT = 1, 2, 4
VMEM_BYTES = 48 * 1024 * 1024


score_scale = 0.07216878364870323


def swap(value, bit):
    count = lax.axis_size("ep")
    return lax.ppermute(value, "ep", [(i, i ^ bit) for i in range(count)])


def shift(value, step):
    count = lax.axis_size("ep")
    return lax.ppermute(value, "ep", [(i, (i + step) % count) for i in range(count)])


def together(*values):
    return lax.optimization_barrier(values)


def pair_dot(rows, left, right):
    both = jnp.concatenate([left[...], right[...]], axis=1)
    return jnp.dot(rows, both, preferred_element_type=jnp.float32)


def gated(gate, up):
    return (gate / (1.0 + jnp.exp(-gate)) * up).astype(jnp.bfloat16)


def early_kernel(count, *refs):
    units, (gate_o, gate_c, gate_x, gate_xc, up_o, up_c) = refs[:count], refs[count : count + 6]
    near, far, acc_near, acc_up = refs[count + 6 :]
    step = pl.program_id(0)

    @pl.when(step == 0)
    def _():
        far[...] = jnp.zeros_like(far)
        acc_near[...] = jnp.zeros_like(acc_near)
        acc_up[...] = jnp.zeros_like(acc_up)

    rows = jnp.concatenate([unit[...] for unit in units], axis=0)
    far[...] += pair_dot(rows, gate_x, gate_xc)
    acc_near[...] += pair_dot(rows, gate_o, gate_c)
    acc_up[...] += pair_dot(rows, up_o, up_c)

    @pl.when(step == pl.num_programs(0) - 1)
    def _():
        near[...] = gated(acc_near[...], acc_up[...])


def early_hidden(units, weights, chunk):
    rows, width = units[0].shape
    wide = weights[0].shape[1]
    count = rows * len(units)
    return pl.pallas_call(
        partial(early_kernel, len(units)),
        grid=(width // chunk,),
        in_specs=[pl.BlockSpec((rows, chunk), lambda k: (0, k)) for _ in units]
        + [pl.BlockSpec((chunk, wide), lambda k: (k, 0)) for _ in weights],
        out_specs=[pl.BlockSpec((count, 2 * wide), lambda k: (0, 0))] * 2,
        out_shape=[
            jax.ShapeDtypeStruct((count, 2 * wide), jnp.bfloat16),
            jax.ShapeDtypeStruct((count, 2 * wide), jnp.float32),
        ],
        scratch_shapes=[pltpu.VMEM((count, 2 * wide), jnp.float32)] * 2,
        compiler_params=pltpu.CompilerParams(vmem_limit_bytes=VMEM_BYTES),
        cost_estimate=pl.CostEstimate(
            flops=2 * count * width * wide * len(weights),
            bytes_accessed=2 * width * (count + wide * len(weights)),
            transcendentals=0,
        ),
    )(*units, *weights)


def late_kernel(lead, count, *refs):
    units, last, (near, far) = refs[:count], refs[count : count + 2], refs[count + 2 : count + 4]
    gate_o, gate_c, gate_x, gate_xc, up_o, up_c = refs[count + 4 : count + 10]
    up_xa, up_xca, up_xb, up_xcb = refs[count + 10 : count + 14]
    out, acc, acc_last = refs[count + 14 :]
    step = pl.program_id(0)
    two = acc.shape[1]

    @pl.when(step == 0)
    def _():
        acc[...] = jnp.zeros_like(acc)
        acc_last[...] = jnp.zeros_like(acc_last)

    tail = jnp.concatenate([part[...] for part in last], axis=0)
    acc_last[:, :two] += pair_dot(tail, gate_o, gate_c)
    acc_last[:, two : 2 * two] += pair_dot(tail, gate_x, gate_xc)
    acc_last[:, 2 * two : 3 * two] += pair_dot(tail, up_o, up_c)

    def add(left, right):
        rows = jnp.concatenate([unit[...] for unit in units] + [tail], axis=0)
        acc[...] += pair_dot(rows, left, right)

    @pl.when(step < lead)
    def _():
        add(up_xa, up_xca)

    @pl.when(step >= lead)
    def _():
        add(up_xb, up_xcb)

    @pl.when(step == pl.num_programs(0) - 1)
    def _():
        early = far.shape[0]
        out[:early, :two] = near[...]
        out[:early, two:] = gated(far[...], acc[:early, :])
        out[early:, :two] = gated(acc_last[:, :two], acc_last[:, 2 * two : 3 * two])
        out[early:, two:] = gated(acc_last[:, two : 2 * two], acc[early:, :])


def late_hidden(units, last, near, far, weights, leads, rests, chunk):
    rows, width = units[0].shape
    wide = weights[0].shape[1]
    lead = leads[0].shape[0] // chunk
    early = rows * len(units)
    total = early + rows
    out = jax.ShapeDtypeStruct((total, 4 * wide), jnp.bfloat16)
    return pl.pallas_call(
        partial(late_kernel, lead, len(units)),
        grid=(width // chunk,),
        in_specs=[pl.BlockSpec((rows, chunk), lambda k: (0, k)) for _ in units]
        + [pl.BlockSpec((part.shape[0], chunk), lambda k: (0, k)) for part in last]
        + [pl.BlockSpec((early, 2 * wide), lambda k: (0, 0))] * 2
        + [pl.BlockSpec((chunk, wide), lambda k: (k, 0)) for _ in weights]
        + [pl.BlockSpec((chunk, wide), lambda k: (jnp.minimum(k, lead - 1), 0)) for _ in leads]
        + [pl.BlockSpec((chunk, wide), lambda k: (jnp.maximum(k - lead, 0), 0)) for _ in rests],
        out_specs=pl.BlockSpec(out.shape, lambda k: (0, 0)),
        out_shape=out,
        scratch_shapes=[
            pltpu.VMEM((total, 2 * wide), jnp.float32),
            pltpu.VMEM((rows, 6 * wide), jnp.float32),
        ],
        compiler_params=pltpu.CompilerParams(vmem_limit_bytes=VMEM_BYTES),
        cost_estimate=pl.CostEstimate(
            flops=2 * width * wide * (2 * total + 6 * rows),
            bytes_accessed=2 * width * (total + 8 * wide),
            transcendentals=0,
        ),
    )(*units, *last, near, far, *weights, *leads, *rests)


def down_kernel(planes, mine, other, weight, *refs):
    blocks, outs = refs[:-planes], refs[-planes:]
    table = jnp.concatenate([block[...] for block in blocks], axis=0)
    count = mine.shape[0] // 2
    rows = count // planes
    for part in range(2):
        here = slice(part * count, (part + 1) * count)
        there = slice((1 - part) * count, (2 - part) * count)
        joined = jnp.concatenate([mine[here, :], other[there, :]], axis=1)
        value = jnp.dot(joined, table, preferred_element_type=jnp.float32) * weight[here, :]
        for at, out in enumerate(outs):
            out[part * rows : (part + 1) * rows, :] = value[at * rows : (at + 1) * rows].astype(
                out.dtype
            )


def down_values(mine, other, weight, own, blocks, planes, chunk, offset):
    count, inner = mine.shape
    depth, width = blocks[0].shape
    rows = count // planes
    kinds = [jnp.float32] * (planes - 1) + [jnp.bfloat16]
    return pl.pallas_call(
        partial(down_kernel, planes),
        grid=(width // chunk,),
        in_specs=[pl.BlockSpec((count, inner), lambda k: (0, 0))] * 2
        + [pl.BlockSpec((count, 1), lambda k: (0, 0))]
        + [pl.BlockSpec((depth, chunk), lambda k: (0, k + offset)) for _ in own]
        + [pl.BlockSpec((depth, chunk), lambda k: (0, k)) for _ in blocks],
        out_specs=[pl.BlockSpec((rows, chunk), lambda k: (0, k)) for _ in kinds],
        out_shape=[jax.ShapeDtypeStruct((rows, width), kind) for kind in kinds],
        compiler_params=pltpu.CompilerParams(vmem_limit_bytes=VMEM_BYTES),
        cost_estimate=pl.CostEstimate(
            flops=2 * count * 2 * inner * width,
            bytes_accessed=2 * 2 * inner * width + 4 * count * width,
            transcendentals=0,
        ),
    )(mine, other, weight, *own, *blocks)


def expert_rows(rows, outgoing, gate_proj, up_proj, down_proj):
    n_ep = lax.axis_size("ep")
    split = FF_WIN // gate_proj.shape[1]
    planes = n_ep // split
    count, width = rows.shape
    chunk = width // 7
    cut = 5 * chunk

    upper = lax.axis_index("ep") // YBIT % 2
    span = width // 4
    keep = lax.dynamic_slice_in_dim(down_proj, 2 * upper * span, 2 * span, 1)
    send = lax.dynamic_slice_in_dim(down_proj, (2 - 2 * upper) * span, 2 * span, 1)
    keep_0, keep_1, send_0, send_1 = keep[:, :span], keep[:, span:], send[:, :span], send[:, span:]
    up_a, up_b = up_proj[:cut], up_proj[cut:]

    gate_x, gate_c = swap(gate_proj, XBIT), swap(gate_proj, CORE)
    unit_1, peer_0 = shift(rows, split), swap(rows, YBIT)
    unit_1, peer_0, gate_c = together(unit_1, peer_0, gate_c)
    up_c = swap(up_proj, CORE)
    unit_2, peer_1 = shift(unit_1, split), swap(unit_1, YBIT)
    unit_2, peer_1, gate_x, up_c, up_a, keep, outgoing = together(
        unit_2, peer_1, gate_x, up_c, up_a, keep, outgoing
    )
    up_xa, gate_xc, keep_c = swap(up_a, XBIT), swap(gate_x, CORE), swap(keep, CORE)
    incoming = lax.all_to_all(outgoing, "ep", split_axis=0, concat_axis=0, tiled=True)
    unit_3, peer_2 = shift(unit_2, split), swap(unit_2, YBIT)
    unit_3, peer_2, up_xa, gate_xc, keep_c, up_b, incoming = together(
        unit_3, peer_2, up_xa, gate_xc, keep_c, up_b, incoming
    )
    up_xb, up_xca = swap(up_b, XBIT), swap(up_xa, CORE)
    half = count // 2
    last = (shift(peer_2[:half], split), swap(unit_3[half:], YBIT))
    early = (rows, unit_1, unit_2, unit_3, peer_0, peer_1, peer_2)
    weights = (gate_proj, gate_c, gate_x, gate_xc, up_proj, up_c)
    near, far = early_hidden(early, weights, chunk)
    up_xb, up_xca, near, keep_0, send_0, *last = together(
        up_xb, up_xca, near, keep_0, send_0, *last
    )
    up_xcb = swap(up_xb, CORE)
    down_x, down_y = swap(keep_0, XBIT), swap(send_0, YBIT)
    hidden = late_hidden(
        early, last, near, far, weights, (up_xa, up_xca), (up_xb, up_xcb), chunk
    )
    other = swap(hidden, YBIT)
    down_x, down_y, hidden, incoming = together(down_x, down_y, hidden, incoming)
    weight = row_weights(incoming, count, planes, split)
    down_yx = swap(down_y, XBIT)
    first = (down_x, swap(down_x, CORE), down_y, swap(down_y, CORE), down_yx, swap(down_yx, CORE))
    keep_1, send_1, down_yx, other = together(keep_1, send_1, down_yx, other)
    down_x, down_y = swap(keep_1, XBIT), swap(send_1, YBIT)
    down_yx = swap(down_y, XBIT)
    second = (down_x, swap(down_x, CORE), down_y, swap(down_y, CORE), down_yx, swap(down_yx, CORE))

    outs, others = [], []
    for at, parts in enumerate((first, second)):
        values = down_values(
            hidden, other, weight, (keep, keep_c), parts, planes, span // 2, 2 * at
        )
        total = values[-1]
        for step in range(planes - 2, -1, -1):
            total = shift(total, n_ep - split).astype(jnp.float32) + values[step]
            total = total.astype(jnp.bfloat16)
        outs.append(total[:count])
        others.append(swap(total[count:], YBIT))
    low = jnp.concatenate(outs + others, axis=1)
    high = jnp.concatenate(others + outs, axis=1)
    return jnp.where(upper == 0, low, high), incoming


def attend(query_part, cache_latents, cache_lens, handed, handed_mark):
    requests = query_part.shape[0]
    cache_scores = (
        jnp.einsum("qhl,qcl->qhc", query_part, cache_latents, preferred_element_type=jnp.float32)
        * score_scale
    )
    hand_scores = (
        jnp.einsum("qhl,rl->qhr", query_part, handed, preferred_element_type=jnp.float32)
        * score_scale
    )
    cache_mask = (
        jnp.arange(cache_latents.shape[1], dtype=jnp.int32)[None, :] < cache_lens[:, None]
    )[:, None, :]
    marks = jnp.arange(1, requests + 1, dtype=jnp.int32).astype(jnp.float32)
    hand_mask = (handed_mark[None, :] == marks[:, None])[:, None, :]
    cache_scores = jnp.where(cache_mask, cache_scores, -jnp.inf)
    hand_scores = jnp.where(hand_mask, hand_scores, -jnp.inf)
    top = jnp.maximum(jnp.max(cache_scores, axis=2), jnp.max(hand_scores, axis=2))[:, :, None]
    cache_expo = jnp.exp(cache_scores - top)
    hand_expo = jnp.exp(hand_scores - top)
    denom = (jnp.sum(cache_expo, axis=2) + jnp.sum(hand_expo, axis=2))[:, :, None]
    cache_prob = (cache_expo / denom).astype(jnp.bfloat16)
    hand_prob = (hand_expo / denom).astype(jnp.bfloat16)
    result = jnp.einsum(
        "qhc,qcv->qhv", cache_prob, cache_latents[:, :, :VDIM], preferred_element_type=jnp.float32
    )
    result = result + jnp.einsum(
        "qhr,rv->qhv", hand_prob, handed[:, :VDIM], preferred_element_type=jnp.float32
    )
    return result.astype(jnp.bfloat16)


def pieces(value):
    parts = []
    for _ in range(3):
        part = lax.reduce_precision(value, 8, 7)
        parts.append(part.astype(jnp.bfloat16))
        value = value - part
    return parts


def hand_over(prompt_latents, owners, requests, picks, gates, split):
    n_ep = lax.axis_size("ep")
    stretch, lat = prompt_latents.shape
    cap = 2 * stretch // n_ep
    places = jnp.arange(stretch, dtype=jnp.int32)
    earlier = (owners[:, None] == owners[None, :]) & (places[None, :] < places[:, None])
    target = owners * cap + jnp.sum(earlier.astype(jnp.int32), axis=1)
    slots = jnp.arange(n_ep * cap, dtype=jnp.int32)
    chosen = slots[:, None] == target[None, :]
    packed = jnp.dot(
        chosen.astype(jnp.bfloat16), prompt_latents, preferred_element_type=jnp.float32
    ).astype(jnp.bfloat16)
    mark = jnp.sum(jnp.where(chosen, requests[None, :] + 1, 0), axis=1).astype(jnp.bfloat16)
    planes = n_ep // split
    experts = jnp.arange(planes, dtype=jnp.int32)
    weights = jnp.sum(
        jnp.where(picks[None] == experts[:, None, None], gates[None], jnp.zeros_like(gates)[None]),
        axis=2,
    )
    lanes = weights.shape[1] // cap
    table = jnp.concatenate(
        [part.reshape(planes, 1, cap, lanes) for part in pieces(weights)], axis=3
    )
    table = jnp.broadcast_to(table, (planes, split, cap, 3 * lanes)).reshape(n_ep, cap, 3 * lanes)
    fill = -(lat + 1 + 3 * lanes) % 128
    outgoing = jnp.concatenate(
        [
            packed.reshape(n_ep, cap, lat),
            mark.reshape(n_ep, cap, 1),
            jnp.zeros((n_ep, cap, fill), jnp.bfloat16),
            table,
        ],
        axis=2,
    )
    return outgoing


def row_weights(incoming, count, planes, split):
    n_ep, cap, width = incoming.shape
    lanes = count // cap
    start = width - 3 * lanes
    here = lax.axis_index("ep")
    found = []
    for place in (here, here ^ YBIT):
        for step in range(planes):
            source = (place - step * split + n_ep) % n_ep
            tile = lax.dynamic_slice(incoming, (source, 0, start), (1, cap, 3 * lanes))
            tile = tile.astype(jnp.float32).reshape(cap, 3, lanes)
            found.append((tile[:, 0] + tile[:, 1] + tile[:, 2]).reshape(count, 1))
    return jnp.concatenate(found, axis=0)


def on_device(
    moe_rows,
    routes,
    route_gates,
    gate_proj,
    up_proj,
    down_proj,
    queries,
    cache_latents,
    cache_lens,
    prompt_latents,
    kv_owner,
    kv_request,
):
    sections, count, width = moe_rows.shape
    top = routes.shape[2]
    split = FF_WIN // gate_proj.shape[1]
    outgoing = hand_over(
        prompt_latents,
        kv_owner[:, 0],
        kv_request,
        routes.reshape(sections * count, top),
        route_gates.reshape(sections * count, top),
        split,
    )
    expert_out, incoming = expert_rows(
        moe_rows.reshape(sections * count, width), outgoing, gate_proj, up_proj, down_proj
    )
    expert_out = expert_out.reshape(moe_rows.shape)
    lat = prompt_latents.shape[1]
    handed = incoming[:, :, :lat].reshape(-1, lat)
    handed_mark = incoming[:, :, lat].reshape(-1).astype(jnp.float32)
    attended = attend(queries, cache_latents, cache_lens, handed, handed_mark)
    return (expert_out, attended)


def solution(mesh):
    placed = (
        P("section", ("groups", "ep"), None),
        P("section", ("groups", "ep"), None),
        P("section", ("groups", "ep"), None),
        P(None, "ep"),
        P(None, "ep"),
        P("ep", None),
        P(("groups", "ep"), None, None),
        P(("groups", "ep"), None, None),
        P(("groups", "ep")),
        P(("groups", "ep"), None),
        P(("groups", "ep"), None),
        P(("groups", "ep")),
    )
    return jax.shard_map(
        on_device,
        mesh=mesh,
        in_specs=placed,
        out_specs=(P("section", ("groups", "ep"), None), P(("groups", "ep"), None, None)),
        check_vma=False,
    )
```

time: 322 us -> 230 us (0.71)
  waiting for transfers between devices: 234 us -> 125 us
  starting transfers between devices: 24.1 us -> 35.8 us
  Pallas kernels: 23.5 us -> 31.7 us
    ppermute x16 -> x28, waiting for transfers between devices: 108 us -> 39.7 us  [swap(): return lax.ppermute(value, 'ep', [(i, i ^ bit) for i in range(count)])]
    ppermute x6 -> x10, waiting for transfers between devices: 109 us -> 61.4 us  [shift(): lax.ppermute(value, 'ep', [(i, (i + step) % count) for i in range(count)])]
    pallas_call x1 -> x2, Pallas kernels: 13.1 us -> 21.7 us  [the longest x1 11.7 us: late_hidden(): pl.pallas_call(partial(late_kernel, lead, len(units)), grid=(width // chu...]
    all_to_all x1, waiting for transfers between devices: 16.4 us -> 24.1 us  [expert_rows(): lax.all_to_all(outgoing, 'ep', split_axis=0, concat_axis=0, tiled=True)]
    unnamed x58 -> x64, local copies, waits for them, and re-layouts: 13.4 us -> 7.45 us
    ppermute x16 -> x28, starting transfers between devices: 15.2 us -> 20.5 us  [swap(): return lax.ppermute(value, 'ep', [(i, i ^ bit) for i in range(count)])]
    ppermute x6 -> x10, starting transfers between devices: 5.78 us -> 10.5 us  [shift(): lax.ppermute(value, 'ep', [(i, (i + step) % count) for i in range(count)])]
    slice x2 -> x7, local copies, waits for them, and re-layouts: 4.38 us -> 8.39 us  [the longest x2 4.31 us: expert_rows(): up_a, up_b = (up_proj[:cut], up_proj[cut:])]
  transfers between devices with their start and end apart: 23 -> 39, of which waited for: 14 -> 17; matrix products, arithmetic and copies ran while one was open for 8% -> 11% of each run, Pallas kernels for 4% -> 14%
where the time goes in v3:
time: 230 us; the launch traced here: 227 us
  waiting for transfers between devices  125 us (54%)
  starting transfers between devices  35.8 us (16%)
  Pallas kernels  31.7 us (14%)
  local copies, waits for them, and re-layouts  21.4 us (9%)
  matrix products  5.9 us (3%)
  other arithmetic  5.75 us (2%)
    ppermute x10, waiting for transfers between devices, shift(): lax.ppermute(value, 'ep', [(i, (i + step) % count) for i in range(count)])  61.4 us
    ppermute x28, waiting for transfers between devices, swap(): return lax.ppermute(value, 'ep', [(i, i ^ bit) for i in range(count)])  39.7 us
    all_to_all x1, waiting for transfers between devices, expert_rows(): lax.all_to_all(outgoing, 'ep', split_axis=0, concat_axis=0, tiled=True)  24.1 us
    ppermute x28, starting transfers between devices, swap(): return lax.ppermute(value, 'ep', [(i, i ^ bit) for i in range(count)])  20.5 us
    pallas_call x1, Pallas kernels, late_hidden(): pl.pallas_call(partial(late_kernel, lead, len(units)), grid=(width // chu...  11.7 us
    ppermute x10, starting transfers between devices, shift(): lax.ppermute(value, 'ep', [(i, (i + step) % count) for i in range(count)])  10.5 us
    pallas_call x2, Pallas kernels, down_values(): pl.pallas_call(partial(down_kernel, planes), grid=(width // chunk,), in_s...  9.99 us
    pallas_call x1, Pallas kernels, early_hidden(): pl.pallas_call(partial(early_kernel, len(units)), grid=(width // chunk,),...  9.97 us
  transfers between devices with their start and end apart: 39, of which 17 were waited for; matrix products, arithmetic and copies ran while one was open for 11% of the time, Pallas kernels for 14%

profile of v3, /device:TPU:16, one launch (start us, length us, event | category | flops | bytes accessed | tf_op | source)
XLA Modules:
  0.0 226.8 jit_solution(1486275187993519138)
XLA Ops:
  5.4 2.4 %slice.120 = bf16[5120,128]{1,0:T(8,128)(2,1)} slice(bf16[7168,128]{1,0:T(8,128)(2,1)} %refs_15_.1), slice={[0:5120], [0:128]} | slice | bytes 2621440 | tf_op jit(solution)/shard_map/slice | solution.py:210
  9.3 14.4 %collective-permute-done.refs_1_ = bf16[64,7168]{1,0:T(8,128)(2,1)S(1)} collective-permute-done((bf16[64,7168]{1,0:T(8,128)(2,1)}, bf16[64,7168]{1,0:T(8,128)(2,1)S(1)}, u32[]{:S(2)}, u32[]{:S(2)}) %collective-permute-start) | collective-permute-done | bytes 917536 | tf_op jit(solution)/shard_map/ppermute | solution.py:27
  29.5 2.2 constant_dynamic-slice_fusion.12.refs_0_
  31.6 14.4 %collective-permute-done.5.refs_9_.refs_13_ = bf16[7168,128]{1,0:T(8,128)(2,1)} collective-permute-done((bf16[7168,128]{1,0:T(8,128)(2,1)}, bf16[7168,128]{1,0:T(8,128)(2,1)}, u32[]{:S(2)}, u32[]{:S(2)}) %collective-permute-start.5) | collective-permute-done | bytes 1835040 | tf_op jit(solution)/shard_map/ppermute | solution.py:22
  48.7 2.0 collective-permute-start.7
  52.3 4.8 %all-to-all-start = ((bf16[32,8,640]{2,1,0:T(8,128)(2,1)}), bf16[32,8,640]{2,1,0:T(8,128)(2,1)S(1)}, u32[]{:S(2)}, u32[]{:S(2)}) async-start(bf16[32,8,640]{2,1,0:T(8,128)(2,1)} %pad_maximum_fusion), calls=%async_computation | async-start | bytes 655360 | tf_op jit(solution)/shard_map/all_to_all | solution.py:221
  57.1 1.9 slice.121
  59.0 24.1 %all-to-all-done = bf16[32,8,640]{2,1,0:T(8,128)(2,1)S(1)} async-done(((bf16[32,8,640]{2,1,0:T(8,128)(2,1)}), bf16[32,8,640]{2,1,0:T(8,128)(2,1)S(1)}, u32[]{:S(2)}, u32[]{:S(2)}) %all-to-all-start) | async-done | bytes 327712 | tf_op jit(solution)/shard_map/all_to_all | solution.py:221
  84.5 2.8 %constant_dynamic-slice_fusion.10 = (bf16[128,1792]{1,0:T(8,128)(2,1)}, bf16[128,1792]{1,0:T(8,128)(2,1)}, bf16[128,1792]{1,0:T(8,128)(2,1)}, bf16[128,1792]{1,0:T(8,128)(2,1)}) fusion(bf16[128,7168]{1,0:T(8,128)(2,1)} %param.17, s32[]{:T(128)S(6)} %add.423, s32[]{:T(128)S(6)} %add.422, s32[]{:T(128)S(6)} %select_n.103, s32[]{:T(128)S(6)} %select_n.100), kind=kLoop, calls=%fused_computation.83 | loop fusion | bytes 3670032 | tf_op jit(solution)/shard_map/slice | solution.py:209
  88.5 2.1 collective-permute-start.14
  91.4 10.0 %shard_map.131 = (bf16[448,256]{1,0:T(8,128)(2,1)S(1)}, f32[448,256]{1,0:T(8,128)S(1)}) custom-call(bf16[64,7168]{1,0:T(8,128)(2,1)S(1)} %bitcast.36, bf16[64,7168]{1,0:T(8,128)(2,1)S(1)} %copy-done.4, bf16[64,7168]{1,0:T(8,128)(2,1)} %collective-permute-done.3.refs_2_, bf16[64,7168]{1,0:T(8,128)(2,1)S(1)} %collective-permute-done.7.refs_3_, ...), custom_call_target="tpu_custom_call" | custom-call | flops 4932501504 | bytes 17432576 | tf_op jit(solution)/shard_map/pallas_call | solution.py:68
  112.4 11.7 %shard_map.132.mine = bf16[512,512]{1,0:T(8,128)(2,1)} custom-call(bf16[64,7168]{1,0:T(8,128)(2,1)S(1)} %bitcast.37, bf16[64,7168]{1,0:T(8,128)(2,1)S(1)} %copy-done.5, bf16[64,7168]{1,0:T(8,128)(2,1)} %collective-permute-done.3.refs_2_, bf16[64,7168]{1,0:T(8,128)(2,1)} %copy-done.1, bf16[64,7168]{1,0:T(8,128)(2,1)} %copy-done.6, ...), custom_call_target="tpu_custom_call" | custom-call | flops 2583691264 | bytes 22020096 | tf_op jit(solution)/shard_map/pallas_call | solution.py:134
  128.0 8.9 %collective-permute-done.19.refs_6_ = bf16[128,1792]{1,0:T(8,128)(2,1)S(1)} collective-permute-done((bf16[128,1792]{1,0:T(8,128)(2,1)}, bf16[128,1792]{1,0:T(8,128)(2,1)S(1)}, u32[]{:S(2)}, u32[]{:S(2)}) %collective-permute-start.19) | collective-permute-done | bytes 458784 | tf_op jit(solution)/shard_map/ppermute | solution.py:22
  142.0 5.1 %shard_map.133 = (f32[128,1792]{1,0:T(8,128)S(1)}, f32[128,1792]{1,0:T(8,128)}, f32[128,1792]{1,0:T(8,128)}, bf16[128,1792]{1,0:T(8,128)(2,1)S(1)}) custom-call(bf16[512,512]{1,0:T(8,128)(2,1)} %shard_map.132.mine, bf16[512,512]{1,0:T(8,128)(2,1)S(1)} %collective-permute-done.20.other, f32[512,1]{1,0:T(8,128)S(1)} %copy.61.weight, ...), custom_call_target="tpu_custom_call" | custom-call | flops 1879048192 | bytes 7340032 | tf_op jit(solution)/shard_map/pallas_call | solution.py:179
  149.1 4.4 %collective-permute-done.29.refs_4_ = bf16[128,1792]{1,0:T(8,128)(2,1)S(1)} collective-permute-done((bf16[128,1792]{1,0:T(8,128)(2,1)}, bf16[128,1792]{1,0:T(8,128)(2,1)S(1)}, u32[]{:S(2)}, u32[]{:S(2)}) %collective-permute-start.29) | collective-permute-done | bytes 458784 | tf_op jit(solution)/shard_map/ppermute | solution.py:22
  154.4 5.5 %collective-permute-done.24 = bf16[128,1792]{1,0:T(8,128)(2,1)S(1)} collective-permute-done((bf16[128,1792]{1,0:T(8,128)(2,1)S(1)}, bf16[128,1792]{1,0:T(8,128)(2,1)S(1)}, u32[]{:S(2)}, u32[]{:S(2)}) %collective-permute-start.24) | collective-permute-done | bytes 458784 | tf_op jit(solution)/shard_map/ppermute | solution.py:27
  160.2 6.2 %collective-permute-done.31.refs_6_ = bf16[128,1792]{1,0:T(8,128)(2,1)S(1)} collective-permute-done((bf16[128,1792]{1,0:T(8,128)(2,1)S(1)}, bf16[128,1792]{1,0:T(8,128)(2,1)S(1)}, u32[]{:S(2)}, u32[]{:S(2)}) %collective-permute-start.31) | collective-permute-done | bytes 458784 | tf_op jit(solution)/shard_map/ppermute | solution.py:22
  168.2 4.9 %shard_map.134 = (f32[128,1792]{1,0:T(8,128)S(1)}, f32[128,1792]{1,0:T(8,128)}, f32[128,1792]{1,0:T(8,128)}, bf16[128,1792]{1,0:T(8,128)(2,1)S(1)}) custom-call(bf16[512,512]{1,0:T(8,128)(2,1)} %shard_map.132.mine, bf16[512,512]{1,0:T(8,128)(2,1)S(1)} %collective-permute-done.20.other, f32[512,1]{1,0:T(8,128)S(1)} %copy.61.weight, ...), custom_call_target="tpu_custom_call" | custom-call | flops 1879048192 | bytes 7340032 | tf_op jit(solution)/shard_map/pallas_call | solution.py:179
  173.6 2.9 %collective-permute-start.26 = (bf16[128,1792]{1,0:T(8,128)(2,1)S(1)}, bf16[128,1792]{1,0:T(8,128)(2,1)S(1)}, u32[]{:S(2)}, u32[]{:S(2)}) collective-permute-start(bf16[128,1792]{1,0:T(8,128)(2,1)S(1)} %add_convert_fusion.5), channel_id=1, source_target_pairs={{0,24},{1,25},{2,26},{3,27},{4,28},{5,29},{6,30},{7,31},{8,0},{9,1... | collective-permute-start | bytes 1376264 | tf_op jit(solution)/shard_map/ppermute | solution.py:27
  176.4 10.0 %collective-permute-done.33 = bf16[128,1792]{1,0:T(8,128)(2,1)S(1)} collective-permute-done((bf16[128,1792]{1,0:T(8,128)(2,1)S(1)}, bf16[128,1792]{1,0:T(8,128)(2,1)S(1)}, u32[]{:S(2)}, u32[]{:S(2)}) %collective-permute-start.33) | collective-permute-done | bytes 458784 | tf_op jit(solution)/shard_map/ppermute | solution.py:27
  187.3 9.0 %collective-permute-done.26 = bf16[128,1792]{1,0:T(8,128)(2,1)S(1)} collective-permute-done((bf16[128,1792]{1,0:T(8,128)(2,1)S(1)}, bf16[128,1792]{1,0:T(8,128)(2,1)S(1)}, u32[]{:S(2)}, u32[]{:S(2)}) %collective-permute-start.26) | collective-permute-done | bytes 458784 | tf_op jit(solution)/shard_map/ppermute | solution.py:27
  196.4 9.3 %collective-permute-done.34 = bf16[128,1792]{1,0:T(8,128)(2,1)S(1)} collective-permute-done((bf16[128,1792]{1,0:T(8,128)(2,1)S(1)}, bf16[128,1792]{1,0:T(8,128)(2,1)S(1)}, u32[]{:S(2)}, u32[]{:S(2)}) %collective-permute-start.34) | collective-permute-done | bytes 458784 | tf_op jit(solution)/shard_map/ppermute | solution.py:27
  207.2 12.1 %collective-permute-done.35 = bf16[128,1792]{1,0:T(8,128)(2,1)S(1)} collective-permute-done((bf16[128,1792]{1,0:T(8,128)(2,1)S(1)}, bf16[128,1792]{1,0:T(8,128)(2,1)S(1)}, u32[]{:S(2)}, u32[]{:S(2)}) %collective-permute-start.35) | collective-permute-done | bytes 458784 | tf_op jit(solution)/shard_map/ppermute | solution.py:27
  222.4 3.3 %collective-permute-done.37 = bf16[64,1792]{1,0:T(8,128)(2,1)S(1)} collective-permute-done((bf16[64,1792]{1,0:T(8,128)(2,1)S(1)}, bf16[64,1792]{1,0:T(8,128)(2,1)S(1)}, u32[]{:S(2)}, u32[]{:S(2)}) %collective-permute-start.37) | collective-permute-done | bytes 229408 | tf_op jit(solution)/shard_map/ppermute | solution.py:22
  (194 shorter events, 51.4 us)
Async XLA Ops:
  0.7 24.3 %collective-permute-start.2 = (bf16[7168,128]{1,0:T(8,128)(2,1)}, bf16[7168,128]{1,0:T(8,128)(2,1)}, u32[]{:S(2)}, u32[]{:S(2)}) collective-permute-start(bf16[7168,128]{1,0:T(8,128)(2,1)} %refs_11_.3), channel_id=1, source_target_pairs={{0,1},{1,0},{2,3},{3,2},{4,5},{5,4},{6,7},{7,6},{8,9},{9,8},{10,11... | collective-permute-start | bytes 5505032 | tf_op jit(solution)/shard_map/ppermute | solution.py:22
  0.8 23.0 %collective-permute-start = (bf16[64,7168]{1,0:T(8,128)(2,1)}, bf16[64,7168]{1,0:T(8,128)(2,1)S(1)}, u32[]{:S(2)}, u32[]{:S(2)}) collective-permute-start(bf16[64,7168]{1,0:T(8,128)(2,1)} %bitcast.34), channel_id=1, source_target_pairs={{0,8},{1,9},{2,10},{3,11},{4,12},{5,13},{6,14},{7,15},{8,16},{9,17... | collective-permute-start | bytes 2752520 | tf_op jit(solution)/shard_map/ppermute | solution.py:27
  2.4 22.6 %collective-permute-start.1 = (bf16[64,7168]{1,0:T(8,128)(2,1)}, bf16[64,7168]{1,0:T(8,128)(2,1)S(1)}, u32[]{:S(2)}, u32[]{:S(2)}) collective-permute-start(bf16[64,7168]{1,0:T(8,128)(2,1)} %bitcast.35), channel_id=1, source_target_pairs={{0,4},{1,5},{2,6},{3,7},{4,0},{5,1},{6,2},{7,3},{8,12},{9,13},{10,... | collective-permute-start | bytes 2752520 | tf_op jit(solution)/shard_map/ppermute | solution.py:22
  3.9 42.1 %collective-permute-start.5 = (bf16[7168,128]{1,0:T(8,128)(2,1)}, bf16[7168,128]{1,0:T(8,128)(2,1)}, u32[]{:S(2)}, u32[]{:S(2)}) collective-permute-start(bf16[7168,128]{1,0:T(8,128)(2,1)} %refs_11_.3), channel_id=1, source_target_pairs={{0,2},{1,3},{2,0},{3,1},{4,6},{5,7},{6,4},{7,5},{8,10},{9,11},{10,... | collective-permute-start | bytes 5505032 | tf_op jit(solution)/shard_map/ppermute | solution.py:22
  5.4 40.6 %collective-permute-start.6 = (bf16[7168,128]{1,0:T(8,128)(2,1)}, bf16[7168,128]{1,0:T(8,128)(2,1)}, u32[]{:S(2)}, u32[]{:S(2)}) collective-permute-start(bf16[7168,128]{1,0:T(8,128)(2,1)} %refs_15_.1), channel_id=1, source_target_pairs={{0,1},{1,0},{2,3},{3,2},{4,5},{5,4},{6,7},{7,6},{8,9},{9,8},{10,11... | collective-permute-start | bytes 5505032 | tf_op jit(solution)/shard_map/ppermute | solution.py:22
  25.0 21.8 %collective-permute-start.3 = (bf16[64,7168]{1,0:T(8,128)(2,1)S(1)}, bf16[64,7168]{1,0:T(8,128)(2,1)}, u32[]{:S(2)}, u32[]{:S(2)}) collective-permute-start(bf16[64,7168]{1,0:T(8,128)(2,1)S(1)} %collective-permute-done.refs_1_), channel_id=1, source_target_pairs={{0,8},{1,9},{2,10},{3,11},{4,12},{5,13},{6,14},{7,15},{8,16},{9,17... | collective-permute-start | bytes 2752520 | tf_op jit(solution)/shard_map/ppermute | solution.py:27
  25.4 21.8 %collective-permute-start.4 = (bf16[64,7168]{1,0:T(8,128)(2,1)S(1)}, bf16[64,7168]{1,0:T(8,128)(2,1)}, u32[]{:S(2)}, u32[]{:S(2)}) collective-permute-start(bf16[64,7168]{1,0:T(8,128)(2,1)S(1)} %collective-permute-done.refs_1_), channel_id=1, source_target_pairs={{0,4},{1,5},{2,6},{3,7},{4,0},{5,1},{6,2},{7,3},{8,12},{9,13},{10,... | collective-permute-start | bytes 2752520 | tf_op jit(solution)/shard_map/ppermute | solution.py:22
  47.2 35.9 %collective-permute-start.10 = (bf16[7168,128]{1,0:T(8,128)(2,1)}, bf16[7168,128]{1,0:T(8,128)(2,1)}, u32[]{:S(2)}, u32[]{:S(2)}) collective-permute-start(bf16[7168,128]{1,0:T(8,128)(2,1)} %collective-permute-done.5.refs_9_.refs_13_), channel_id=1, source_target_pairs={{0,1},{1,0},{2,3},{3,2},{4,5},{5,4},{6,7},{7,6},{8,9},{9,8},{10,11... | collective-permute-start | bytes 5505032 | tf_op jit(solution)/shard_map/ppermute | solution.py:22
  47.2 35.9 %collective-permute-start.9 = (bf16[5120,128]{1,0:T(8,128)(2,1)}, bf16[5120,128]{1,0:T(8,128)(2,1)}, u32[]{:S(2)}, u32[]{:S(2)}) collective-permute-start(bf16[5120,128]{1,0:T(8,128)(2,1)} %slice.120), channel_id=1, source_target_pairs={{0,2},{1,3},{2,0},{3,1},{4,6},{5,7},{6,4},{7,5},{8,10},{9,11},{10,... | collective-permute-start | bytes 3932168 | tf_op jit(solution)/shard_map/ppermute | solution.py:22
  48.7 34.4 %collective-permute-start.7 = (bf16[64,7168]{1,0:T(8,128)(2,1)}, bf16[64,7168]{1,0:T(8,128)(2,1)S(1)}, u32[]{:S(2)}, u32[]{:S(2)}) collective-permute-start(bf16[64,7168]{1,0:T(8,128)(2,1)} %collective-permute-done.3.refs_2_), channel_id=1, source_target_pairs={{0,8},{1,9},{2,10},{3,11},{4,12},{5,13},{6,14},{7,15},{8,16},{9,17... | collective-permute-start | bytes 2752520 | tf_op jit(solution)/shard_map/ppermute | solution.py:27
  50.8 32.3 %collective-permute-start.8 = (bf16[64,7168]{1,0:T(8,128)(2,1)}, bf16[64,7168]{1,0:T(8,128)(2,1)}, u32[]{:S(2)}, u32[]{:S(2)}) collective-permute-start(bf16[64,7168]{1,0:T(8,128)(2,1)} %collective-permute-done.3.refs_2_), channel_id=1, source_target_pairs={{0,4},{1,5},{2,6},{3,7},{4,0},{5,1},{6,2},{7,3},{8,12},{9,13},{10,... | collective-permute-start | bytes 2752520 | tf_op jit(solution)/shard_map/ppermute | solution.py:22
  52.3 30.8 %collective-permute-start.11 = (bf16[128,3584]{1,0:T(8,128)(2,1)}, bf16[128,3584]{1,0:T(8,128)(2,1)}, u32[]{:S(2)}, u32[]{:S(2)}) collective-permute-start(bf16[128,3584]{1,0:T(8,128)(2,1)} %constant_dynamic-slice_fusion.12.refs_0_), channel_id=1, source_target_pairs={{0,1},{1,0},{2,3},{3,2},{4,5},{5,4},{6,7},{7,6},{8,9},{9,8},{10,11... | collective-permute-start | bytes 2752520 | tf_op jit(solution)/shard_map/ppermute | solution.py:22
  52.3 30.8 %all-to-all-start = ((bf16[32,8,640]{2,1,0:T(8,128)(2,1)}), bf16[32,8,640]{2,1,0:T(8,128)(2,1)S(1)}, u32[]{:S(2)}, u32[]{:S(2)}) async-start(bf16[32,8,640]{2,1,0:T(8,128)(2,1)} %pad_maximum_fusion), calls=%async_computation | async-start | bytes 655360 | tf_op jit(solution)/shard_map/all_to_all | solution.py:221
  83.1 21.3 %collective-permute-start.13 = (bf16[5120,128]{1,0:T(8,128)(2,1)}, bf16[5120,128]{1,0:T(8,128)(2,1)}, u32[]{:S(2)}, u32[]{:S(2)}) collective-permute-start(bf16[5120,128]{1,0:T(8,128)(2,1)} %collective-permute-done.9.refs_17_), channel_id=1, source_target_pairs={{0,1},{1,0},{2,3},{3,2},{4,5},{5,4},{6,7},{7,6},{8,9},{9,8},{10,11... | collective-permute-start | bytes 3932168 | tf_op jit(solution)/shard_map/ppermute | solution.py:22
  83.2 21.2 %collective-permute-start.12 = (bf16[2048,128]{1,0:T(8,128)(2,1)}, bf16[2048,128]{1,0:T(8,128)(2,1)S(1)}, u32[]{:S(2)}, u32[]{:S(2)}) collective-permute-start(bf16[2048,128]{1,0:T(8,128)(2,1)} %slice.121), channel_id=1, source_target_pairs={{0,2},{1,3},{2,0},{3,1},{4,6},{5,7},{6,4},{7,5},{8,10},{9,11},{10,... | collective-permute-start | bytes 1572872 | tf_op jit(solution)/shard_map/ppermute | solution.py:22
  104.5 20.1 %collective-permute-start.16 = (bf16[128,1792]{1,0:T(8,128)(2,1)}, bf16[128,1792]{1,0:T(8,128)(2,1)}, u32[]{:S(2)}, u32[]{:S(2)}) collective-permute-start(bf16[128,1792]{1,0:T(8,128)(2,1)} %get-tuple-element.59), channel_id=1, source_target_pairs={{0,2},{1,3},{2,0},{3,1},{4,6},{5,7},{6,4},{7,5},{8,10},{9,11},{10,... | collective-permute-start | bytes 1376264 | tf_op jit(solution)/shard_map/ppermute | solution.py:22
  105.2 19.4 %collective-permute-start.17 = (bf16[128,1792]{1,0:T(8,128)(2,1)}, bf16[128,1792]{1,0:T(8,128)(2,1)}, u32[]{:S(2)}, u32[]{:S(2)}) collective-permute-start(bf16[128,1792]{1,0:T(8,128)(2,1)} %get-tuple-element.60), channel_id=1, source_target_pairs={{0,4},{1,5},{2,6},{3,7},{4,0},{5,1},{6,2},{7,3},{8,12},{9,13},{10,... | collective-permute-start | bytes 1376264 | tf_op jit(solution)/shard_map/ppermute | solution.py:22
  124.0 15.2 %collective-permute-start.20 = (bf16[512,512]{1,0:T(8,128)(2,1)}, bf16[512,512]{1,0:T(8,128)(2,1)S(1)}, u32[]{:S(2)}, u32[]{:S(2)}) collective-permute-start(bf16[512,512]{1,0:T(8,128)(2,1)} %shard_map.132.mine), channel_id=1, source_target_pairs={{0,4},{1,5},{2,6},{3,7},{4,0},{5,1},{6,2},{7,3},{8,12},{9,13},{10,... | collective-permute-start | bytes 1572872 | tf_op jit(solution)/shard_map/ppermute | solution.py:22
  126.0 15.9 %collective-permute-start.22 = (bf16[128,1792]{1,0:T(8,128)(2,1)}, bf16[128,1792]{1,0:T(8,128)(2,1)S(1)}, u32[]{:S(2)}, u32[]{:S(2)}) collective-permute-start(bf16[128,1792]{1,0:T(8,128)(2,1)} %collective-permute-done.17.refs_4_), channel_id=1, source_target_pairs={{0,1},{1,0},{2,3},{3,2},{4,5},{5,4},{6,7},{7,6},{8,9},{9,8},{10,11... | collective-permute-start | bytes 1376264 | tf_op jit(solution)/shard_map/ppermute | solution.py:22
  127.4 14.5 %collective-permute-start.21 = (bf16[128,1792]{1,0:T(8,128)(2,1)}, bf16[128,1792]{1,0:T(8,128)(2,1)S(1)}, u32[]{:S(2)}, u32[]{:S(2)}) collective-permute-start(bf16[128,1792]{1,0:T(8,128)(2,1)} %collective-permute-done.16.refs_2_), channel_id=1, source_target_pairs={{0,1},{1,0},{2,3},{3,2},{4,5},{5,4},{6,7},{7,6},{8,9},{9,8},{10,11... | collective-permute-start | bytes 1376264 | tf_op jit(solution)/shard_map/ppermute | solution.py:22
  139.2 14.9 %collective-permute-start.27 = (bf16[128,1792]{1,0:T(8,128)(2,1)}, bf16[128,1792]{1,0:T(8,128)(2,1)S(1)}, u32[]{:S(2)}, u32[]{:S(2)}) collective-permute-start(bf16[128,1792]{1,0:T(8,128)(2,1)} %get-tuple-element.78), channel_id=1, source_target_pairs={{0,2},{1,3},{2,0},{3,1},{4,6},{5,7},{6,4},{7,5},{8,10},{9,11},{10,... | collective-permute-start | bytes 1376264 | tf_op jit(solution)/shard_map/ppermute | solution.py:22
  173.6 22.7 %collective-permute-start.26 = (bf16[128,1792]{1,0:T(8,128)(2,1)S(1)}, bf16[128,1792]{1,0:T(8,128)(2,1)S(1)}, u32[]{:S(2)}, u32[]{:S(2)}) collective-permute-start(bf16[128,1792]{1,0:T(8,128)(2,1)S(1)} %add_convert_fusion.5), channel_id=1, source_target_pairs={{0,24},{1,25},{2,26},{3,27},{4,28},{5,29},{6,30},{7,31},{8,0},{9,1... | collective-permute-start | bytes 1376264 | tf_op jit(solution)/shard_map/ppermute | solution.py:27
  186.5 19.1 %collective-permute-start.34 = (bf16[128,1792]{1,0:T(8,128)(2,1)S(1)}, bf16[128,1792]{1,0:T(8,128)(2,1)S(1)}, u32[]{:S(2)}, u32[]{:S(2)}) collective-permute-start(bf16[128,1792]{1,0:T(8,128)(2,1)S(1)} %add_convert_fusion.3), channel_id=1, source_target_pairs={{0,24},{1,25},{2,26},{3,27},{4,28},{5,29},{6,30},{7,31},{8,0},{9,1... | collective-permute-start | bytes 1376264 | tf_op jit(solution)/shard_map/ppermute | solution.py:27
  206.2 16.2 %collective-permute-start.36 = (bf16[64,1792]{1,0:T(8,128)(2,1)S(1)}, bf16[64,1792]{1,0:T(8,128)(2,1)S(1)}, u32[]{:S(2)}, u32[]{:S(2)}) collective-permute-start(bf16[64,1792]{1,0:T(8,128)(2,1)S(1)} %get-tuple-element.91), channel_id=1, source_target_pairs={{0,4},{1,5},{2,6},{3,7},{4,0},{5,1},{6,2},{7,3},{8,12},{9,13},{10,... | collective-permute-start | bytes 688136 | tf_op jit(solution)/shard_map/ppermute | solution.py:22
  (46 other events, 501.3 us)

commit v4 on v3

--- a/solution.py
+++ b/solution.py
@@ -11,7 +11,7 @@
 FF_WIN = 1024
 SLOT_ROWS = 8
 CORE, XBIT, YBIT = 1, 2, 4
-VMEM_BYTES = 48 * 1024 * 1024
+VMEM_BYTES = 14 * 1024 * 1024
 
 
 score_scale = 0.07216878364870323
@@ -211,17 +211,17 @@
 
     gate_x, gate_c = swap(gate_proj, XBIT), swap(gate_proj, CORE)
     unit_1, peer_0 = shift(rows, split), swap(rows, YBIT)
-    unit_1, peer_0, gate_c = together(unit_1, peer_0, gate_c)
+    unit_1, peer_0, gate_c, outgoing = together(unit_1, peer_0, gate_c, outgoing)
     up_c = swap(up_proj, CORE)
     unit_2, peer_1 = shift(unit_1, split), swap(unit_1, YBIT)
-    unit_2, peer_1, gate_x, up_c, up_a, keep, outgoing = together(
-        unit_2, peer_1, gate_x, up_c, up_a, keep, outgoing
+    unit_2, peer_1, gate_x, up_c, up_a, keep = together(
+        unit_2, peer_1, gate_x, up_c, up_a, keep
     )
     up_xa, gate_xc, keep_c = swap(up_a, XBIT), swap(gate_x, CORE), swap(keep, CORE)
     incoming = lax.all_to_all(outgoing, "ep", split_axis=0, concat_axis=0, tiled=True)
     unit_3, peer_2 = shift(unit_2, split), swap(unit_2, YBIT)
-    unit_3, peer_2, up_xa, gate_xc, keep_c, up_b, incoming = together(
-        unit_3, peer_2, up_xa, gate_xc, keep_c, up_b, incoming
+    unit_3, peer_2, up_xa, gate_xc, keep_c, up_b, keep_0, send_0 = together(
+        unit_3, peer_2, up_xa, gate_xc, keep_c, up_b, keep_0, send_0
     )
     up_xb, up_xca = swap(up_b, XBIT), swap(up_xa, CORE)
     half = count // 2
@@ -229,8 +229,8 @@
     early = (rows, unit_1, unit_2, unit_3, peer_0, peer_1, peer_2)
     weights = (gate_proj, gate_c, gate_x, gate_xc, up_proj, up_c)
     near, far = early_hidden(early, weights, chunk)
-    up_xb, up_xca, near, keep_0, send_0, *last = together(
-        up_xb, up_xca, near, keep_0, send_0, *last
+    up_xb, up_xca, near, keep_0, send_0, incoming, *last = together(
+        up_xb, up_xca, near, keep_0, send_0, incoming, *last
     )
     up_xcb = swap(up_xb, CORE)
     down_x, down_y = swap(keep_0, XBIT), swap(send_0, YBIT)
@@ -242,7 +242,8 @@
     weight = row_weights(incoming, count, planes, split)
     down_yx = swap(down_y, XBIT)
     first = (down_x, swap(down_x, CORE), down_y, swap(down_y, CORE), down_yx, swap(down_yx, CORE))
-    keep_1, send_1, down_yx, other = together(keep_1, send_1, down_yx, other)
+    keep_1, down_yx = together(keep_1, down_yx)
+    send_1, other = together(send_1, other)
     down_x, down_y = swap(keep_1, XBIT), swap(send_1, YBIT)
     down_yx = swap(down_y, XBIT)
     second = (down_x, swap(down_x, CORE), down_y, swap(down_y, CORE), down_yx, swap(down_yx, CORE))
@@ -385,6 +386,7 @@
         moe_rows.reshape(sections * count, width), outgoing, gate_proj, up_proj, down_proj
     )
     expert_out = expert_out.reshape(moe_rows.shape)
+    queries, incoming = together(queries, incoming)
     lat = prompt_latents.shape[1]
     handed = incoming[:, :, :lat].reshape(-1, lat)
     handed_mark = incoming[:, :, lat].reshape(-1).astype(jnp.float32)

time: 230 us -> 229 us (level)
  waiting for transfers between devices: 125 us -> 118 us
  matrix products: 5.9 us -> 8.54 us
  local copies, waits for them, and re-layouts: 21.4 us -> 23.9 us
    all_to_all x1, waiting for transfers between devices: 24.1 us -> 0.01 us  [expert_rows(): lax.all_to_all(outgoing, 'ep', split_axis=0, concat_axis=0, tiled=True)]
    ppermute x10, waiting for transfers between devices: 61.4 us -> 71.7 us  [shift(): lax.ppermute(value, 'ep', [(i, (i + step) % count) for i in range(count)])]
    ppermute x28, waiting for transfers between devices: 39.7 us -> 45.9 us  [swap(): return lax.ppermute(value, 'ep', [(i, i ^ bit) for i in range(count)])]
    slice x2, local copies, waits for them, and re-layouts: 1.21 us -> 3.61 us  [expert_rows(): last = (shift(peer_2[:half], split), swap(unit_3[half:], YBIT))]
    slice x2, local copies, waits for them, and re-layouts: 4.31 us -> 2.01 us  [expert_rows(): up_a, up_b = (up_proj[:cut], up_proj[cut:])]
    unnamed x64 -> x30, local copies, waits for them, and re-layouts: 7.45 us -> 9.01 us
  transfers between devices with their start and end apart: 39 -> 39, of which waited for: 17 -> 19; matrix products, arithmetic and copies ran while one was open for 11% -> 14% of each run, Pallas kernels for 14% -> 13%
where the time goes in v4:
time: 229 us; the launch traced here: 226 us
  waiting for transfers between devices  118 us (52%)
  starting transfers between devices  37.9 us (17%)
  Pallas kernels  29.5 us (13%)
  local copies, waits for them, and re-layouts  23.9 us (10%)
  matrix products  8.54 us (4%)
  other arithmetic  7.26 us (3%)
    ppermute x10, waiting for transfers between devices, shift(): lax.ppermute(value, 'ep', [(i, (i + step) % count) for i in range(count)])  71.7 us
    ppermute x28, waiting for transfers between devices, swap(): return lax.ppermute(value, 'ep', [(i, i ^ bit) for i in range(count)])  45.9 us
    ppermute x28, starting transfers between devices, swap(): return lax.ppermute(value, 'ep', [(i, i ^ bit) for i in range(count)])  20.8 us
    pallas_call x1, Pallas kernels, late_hidden(): pl.pallas_call(partial(late_kernel, lead, len(units)), grid=(width // chu...  11.3 us
    ppermute x10, starting transfers between devices, shift(): lax.ppermute(value, 'ep', [(i, (i + step) % count) for i in range(count)])  10.5 us
    pallas_call x1, Pallas kernels, early_hidden(): pl.pallas_call(partial(early_kernel, len(units)), grid=(width // chunk,),...  9.8 us
    unnamed x30, local copies, waits for them, and re-layouts  9.01 us
    pallas_call x2, Pallas kernels, down_values(): pl.pallas_call(partial(down_kernel, planes), grid=(width // chunk,), in_s...  8.44 us
  transfers between devices with their start and end apart: 39, of which 19 were waited for; matrix products, arithmetic and copies ran while one was open for 14% of the time, Pallas kernels for 13%

profile of v4, /device:TPU:16, one launch (start us, length us, event | category | flops | bytes accessed | tf_op | source)
XLA Modules:
  0.0 225.9 jit_solution(965010686281107878)
XLA Ops:
  9.0 1.9 convolution_convert_fusion
  13.0 10.8 %collective-permute-done.refs_1_ = bf16[64,7168]{1,0:T(8,128)(2,1)} collective-permute-done((bf16[64,7168]{1,0:T(8,128)(2,1)}, bf16[64,7168]{1,0:T(8,128)(2,1)}, u32[]{:S(2)}, u32[]{:S(2)}) %collective-permute-start) | collective-permute-done | bytes 917536 | tf_op jit(solution)/shard_map/ppermute | solution.py:27
  28.1 2.2 constant_dynamic-slice_fusion.11.refs_0_
  30.3 15.7 %collective-permute-done.5.refs_9_.refs_13_ = bf16[7168,128]{1,0:T(8,128)(2,1)} collective-permute-done((bf16[7168,128]{1,0:T(8,128)(2,1)}, bf16[7168,128]{1,0:T(8,128)(2,1)}, u32[]{:S(2)}, u32[]{:S(2)}) %collective-permute-start.5) | collective-permute-done | bytes 1835040 | tf_op jit(solution)/shard_map/ppermute | solution.py:22
  49.1 2.2 collective-permute-start.7
  53.6 2.7 %constant_dynamic-slice_fusion.12 = (bf16[128,1792]{1,0:T(8,128)(2,1)}, bf16[128,1792]{1,0:T(8,128)(2,1)}, bf16[128,1792]{1,0:T(8,128)(2,1)}, bf16[128,1792]{1,0:T(8,128)(2,1)}) fusion(bf16[128,7168]{1,0:T(8,128)(2,1)} %param.17, s32[]{:T(128)S(6)} %add.423, s32[]{:T(128)S(6)} %select_n.103, s32[]{:T(128)S(6)} %select_n.102, s32[]{:T(128)S(6)} %add.422), kind=kLoop, calls=%fused_computation.84 | loop fusion | bytes 3670032 | tf_op jit(solution)/shard_map/slice | solution.py:209
  56.3 15.6 %collective-permute-done.7.refs_3_ = bf16[64,7168]{1,0:T(8,128)(2,1)} collective-permute-done((bf16[64,7168]{1,0:T(8,128)(2,1)}, bf16[64,7168]{1,0:T(8,128)(2,1)}, u32[]{:S(2)}, u32[]{:S(2)}) %collective-permute-start.7) | collective-permute-done | bytes 917536 | tf_op jit(solution)/shard_map/ppermute | solution.py:27
  71.9 1.9 collective-permute-done.8.refs_6_
  73.8 5.1 %collective-permute-done.9.refs_17_ = bf16[5120,128]{1,0:T(8,128)(2,1)} collective-permute-done((bf16[5120,128]{1,0:T(8,128)(2,1)}, bf16[5120,128]{1,0:T(8,128)(2,1)}, u32[]{:S(2)}, u32[]{:S(2)}) %collective-permute-start.9) | collective-permute-done | bytes 1310752 | tf_op jit(solution)/shard_map/ppermute | solution.py:22
  78.8 6.7 %all-to-all-start = ((bf16[32,8,640]{2,1,0:T(8,128)(2,1)}), bf16[32,8,640]{2,1,0:T(8,128)(2,1)}, u32[]{:S(2)}, u32[]{:S(2)}) async-start(bf16[32,8,640]{2,1,0:T(8,128)(2,1)} %pad_maximum_fusion), calls=%async_computation | async-start | bytes 655360 | tf_op jit(solution)/shard_map/all_to_all | solution.py:221
  95.2 9.8 %shard_map.131 = (bf16[448,256]{1,0:T(8,128)(2,1)S(1)}, f32[448,256]{1,0:T(8,128)S(1)}) custom-call(bf16[64,7168]{1,0:T(8,128)(2,1)S(1)} %bitcast.32, bf16[64,7168]{1,0:T(8,128)(2,1)} %collective-permute-done.refs_1_, bf16[64,7168]{1,0:T(8,128)(2,1)} %collective-permute-done.3.refs_2_, bf16[64,7168]{1,0:T(8,128)(2,1)} %collective-permute-done.7.refs_3_, ...), custom_call_target="tpu_custom_call" | custom-call | flops 4932501504 | bytes 17432576 | tf_op jit(solution)/shard_map/pallas_call | solution.py:68
  113.3 11.3 %shard_map.132.mine = bf16[512,512]{1,0:T(8,128)(2,1)} custom-call(bf16[64,7168]{1,0:T(8,128)(2,1)S(1)} %bitcast.33, bf16[64,7168]{1,0:T(8,128)(2,1)} %collective-permute-done.refs_1_, bf16[64,7168]{1,0:T(8,128)(2,1)} %collective-permute-done.3.refs_2_, bf16[64,7168]{1,0:T(8,128)(2,1)} %collective-permute-done.7.refs_3_, ...), custom_call_target="tpu_custom_call" | custom-call | flops 2583691264 | bytes 22020096 | tf_op jit(solution)/shard_map/pallas_call | solution.py:134
  131.2 6.4 %collective-permute-done.22.refs_6_ = bf16[128,1792]{1,0:T(8,128)(2,1)S(1)} collective-permute-done((bf16[128,1792]{1,0:T(8,128)(2,1)}, bf16[128,1792]{1,0:T(8,128)(2,1)S(1)}, u32[]{:S(2)}, u32[]{:S(2)}) %collective-permute-start.22) | collective-permute-done | bytes 458784 | tf_op jit(solution)/shard_map/ppermute | solution.py:22
  137.8 2.5 %fusion.34 = (f32[8,128]{1,0:T(8,128)S(1)}, f32[8,128,256]{2,1,0:T(8,128)S(1)}) fusion(bf16[8,128,576]{1,2,0:T(8,128)(2,1)S(1)} %copy-done, bf16[8,256,576]{1,2,0:T(8,128)(2,1)} %param.19, pred[8,256]{1,0:T(8,128)(4,1)S(1)} %iota_compare_fusion.3), kind=kOutput, calls=%fused_computation.98 | convolution fusion | flops 302775296 | bytes 4593664 | tf_op jit(solution)/shard_map/qhl,qcl->qhc/dot_general | solution.py:270
  142.4 4.3 %shard_map.133 = (f32[128,1792]{1,0:T(8,128)S(1)}, f32[128,1792]{1,0:T(8,128)S(1)}, f32[128,1792]{1,0:T(8,128)S(1)}, bf16[128,1792]{1,0:T(8,128)(2,1)S(1)}) custom-call(bf16[512,512]{1,0:T(8,128)(2,1)} %shard_map.132.mine, bf16[512,512]{1,0:T(8,128)(2,1)S(1)} %collective-permute-done.19.other, f32[512,1]{1,0:T(8,128)S(1)} %copy.58.weight, ...), custom_call_target="tpu_custom_call" | custom-call | flops 1879048192 | bytes 7340032 | tf_op jit(solution)/shard_map/pallas_call | solution.py:179
  149.8 3.5 %collective-permute-done.27.refs_2_ = bf16[128,1792]{1,0:T(8,128)(2,1)S(1)} collective-permute-done((bf16[128,1792]{1,0:T(8,128)(2,1)S(1)}, bf16[128,1792]{1,0:T(8,128)(2,1)S(1)}, u32[]{:S(2)}, u32[]{:S(2)}) %collective-permute-start.27) | collective-permute-done | bytes 458784 | tf_op jit(solution)/shard_map/ppermute | solution.py:22
  155.0 4.1 %collective-permute-done.24 = bf16[128,1792]{1,0:T(8,128)(2,1)S(1)} collective-permute-done((bf16[128,1792]{1,0:T(8,128)(2,1)S(1)}, bf16[128,1792]{1,0:T(8,128)(2,1)S(1)}, u32[]{:S(2)}, u32[]{:S(2)}) %collective-permute-start.24) | collective-permute-done | bytes 458784 | tf_op jit(solution)/shard_map/ppermute | solution.py:27
  160.0 6.2 %collective-permute-done.31.refs_6_ = bf16[128,1792]{1,0:T(8,128)(2,1)S(1)} collective-permute-done((bf16[128,1792]{1,0:T(8,128)(2,1)S(1)}, bf16[128,1792]{1,0:T(8,128)(2,1)S(1)}, u32[]{:S(2)}, u32[]{:S(2)}) %collective-permute-start.31) | collective-permute-done | bytes 458784 | tf_op jit(solution)/shard_map/ppermute | solution.py:22
  168.2 4.1 %shard_map.134 = (f32[128,1792]{1,0:T(8,128)S(1)}, f32[128,1792]{1,0:T(8,128)S(1)}, f32[128,1792]{1,0:T(8,128)S(1)}, bf16[128,1792]{1,0:T(8,128)(2,1)S(1)}) custom-call(bf16[512,512]{1,0:T(8,128)(2,1)} %shard_map.132.mine, bf16[512,512]{1,0:T(8,128)(2,1)S(1)} %collective-permute-done.19.other, f32[512,1]{1,0:T(8,128)S(1)} %copy.58.weight, ...), custom_call_target="tpu_custom_call" | custom-call | flops 1879048192 | bytes 7340032 | tf_op jit(solution)/shard_map/pallas_call | solution.py:179
  174.6 11.2 %collective-permute-done.33 = bf16[128,1792]{1,0:T(8,128)(2,1)S(1)} collective-permute-done((bf16[128,1792]{1,0:T(8,128)(2,1)S(1)}, bf16[128,1792]{1,0:T(8,128)(2,1)S(1)}, u32[]{:S(2)}, u32[]{:S(2)}) %collective-permute-start.33) | collective-permute-done | bytes 458784 | tf_op jit(solution)/shard_map/ppermute | solution.py:27
  186.6 9.0 %collective-permute-done.26 = bf16[128,1792]{1,0:T(8,128)(2,1)S(1)} collective-permute-done((bf16[128,1792]{1,0:T(8,128)(2,1)S(1)}, bf16[128,1792]{1,0:T(8,128)(2,1)S(1)}, u32[]{:S(2)}, u32[]{:S(2)}) %collective-permute-start.26) | collective-permute-done | bytes 458784 | tf_op jit(solution)/shard_map/ppermute | solution.py:27
  195.7 9.4 %collective-permute-done.34 = bf16[128,1792]{1,0:T(8,128)(2,1)S(1)} collective-permute-done((bf16[128,1792]{1,0:T(8,128)(2,1)S(1)}, bf16[128,1792]{1,0:T(8,128)(2,1)S(1)}, u32[]{:S(2)}, u32[]{:S(2)}) %collective-permute-start.34) | collective-permute-done | bytes 458784 | tf_op jit(solution)/shard_map/ppermute | solution.py:27
  207.3 10.6 %collective-permute-done.35 = bf16[128,1792]{1,0:T(8,128)(2,1)S(1)} collective-permute-done((bf16[128,1792]{1,0:T(8,128)(2,1)S(1)}, bf16[128,1792]{1,0:T(8,128)(2,1)S(1)}, u32[]{:S(2)}, u32[]{:S(2)}) %collective-permute-start.35) | collective-permute-done | bytes 458784 | tf_op jit(solution)/shard_map/ppermute | solution.py:27
  221.0 3.7 %collective-permute-done.37 = bf16[64,1792]{1,0:T(8,128)(2,1)S(1)} collective-permute-done((bf16[64,1792]{1,0:T(8,128)(2,1)S(1)}, bf16[64,1792]{1,0:T(8,128)(2,1)S(1)}, u32[]{:S(2)}, u32[]{:S(2)}) %collective-permute-start.37) | collective-permute-done | bytes 229408 | tf_op jit(solution)/shard_map/ppermute | solution.py:22
  (160 shorter events, 64.0 us)
Async XLA Ops:
  0.7 24.4 %collective-permute-start.2 = (bf16[7168,128]{1,0:T(8,128)(2,1)}, bf16[7168,128]{1,0:T(8,128)(2,1)}, u32[]{:S(2)}, u32[]{:S(2)}) collective-permute-start(bf16[7168,128]{1,0:T(8,128)(2,1)} %refs_11_.3), channel_id=1, source_target_pairs={{0,1},{1,0},{2,3},{3,2},{4,5},{5,4},{6,7},{7,6},{8,9},{9,8},{10,11... | collective-permute-start | bytes 5505032 | tf_op jit(solution)/shard_map/ppermute | solution.py:22
  0.7 23.1 %collective-permute-start = (bf16[64,7168]{1,0:T(8,128)(2,1)}, bf16[64,7168]{1,0:T(8,128)(2,1)}, u32[]{:S(2)}, u32[]{:S(2)}) collective-permute-start(bf16[64,7168]{1,0:T(8,128)(2,1)} %bitcast.30), channel_id=1, source_target_pairs={{0,8},{1,9},{2,10},{3,11},{4,12},{5,13},{6,14},{7,15},{8,16},{9,17... | collective-permute-start | bytes 2752520 | tf_op jit(solution)/shard_map/ppermute | solution.py:27
  2.4 22.7 %collective-permute-start.1 = (bf16[64,7168]{1,0:T(8,128)(2,1)}, bf16[64,7168]{1,0:T(8,128)(2,1)}, u32[]{:S(2)}, u32[]{:S(2)}) collective-permute-start(bf16[64,7168]{1,0:T(8,128)(2,1)} %bitcast.31), channel_id=1, source_target_pairs={{0,4},{1,5},{2,6},{3,7},{4,0},{5,1},{6,2},{7,3},{8,12},{9,13},{10,... | collective-permute-start | bytes 2752520 | tf_op jit(solution)/shard_map/ppermute | solution.py:22
  3.9 42.1 %collective-permute-start.5 = (bf16[7168,128]{1,0:T(8,128)(2,1)}, bf16[7168,128]{1,0:T(8,128)(2,1)}, u32[]{:S(2)}, u32[]{:S(2)}) collective-permute-start(bf16[7168,128]{1,0:T(8,128)(2,1)} %refs_11_.3), channel_id=1, source_target_pairs={{0,2},{1,3},{2,0},{3,1},{4,6},{5,7},{6,4},{7,5},{8,10},{9,11},{10,... | collective-permute-start | bytes 5505032 | tf_op jit(solution)/shard_map/ppermute | solution.py:22
  5.4 40.6 %collective-permute-start.6 = (bf16[7168,128]{1,0:T(8,128)(2,1)}, bf16[7168,128]{1,0:T(8,128)(2,1)}, u32[]{:S(2)}, u32[]{:S(2)}) collective-permute-start(bf16[7168,128]{1,0:T(8,128)(2,1)} %refs_15_.1), channel_id=1, source_target_pairs={{0,1},{1,0},{2,3},{3,2},{4,5},{5,4},{6,7},{7,6},{8,9},{9,8},{10,11... | collective-permute-start | bytes 5505032 | tf_op jit(solution)/shard_map/ppermute | solution.py:22
  25.1 21.9 %collective-permute-start.3 = (bf16[64,7168]{1,0:T(8,128)(2,1)}, bf16[64,7168]{1,0:T(8,128)(2,1)}, u32[]{:S(2)}, u32[]{:S(2)}) collective-permute-start(bf16[64,7168]{1,0:T(8,128)(2,1)} %collective-permute-done.refs_1_), channel_id=1, source_target_pairs={{0,8},{1,9},{2,10},{3,11},{4,12},{5,13},{6,14},{7,15},{8,16},{9,17... | collective-permute-start | bytes 2752520 | tf_op jit(solution)/shard_map/ppermute | solution.py:27
  25.4 21.9 %collective-permute-start.4 = (bf16[64,7168]{1,0:T(8,128)(2,1)}, bf16[64,7168]{1,0:T(8,128)(2,1)}, u32[]{:S(2)}, u32[]{:S(2)}) collective-permute-start(bf16[64,7168]{1,0:T(8,128)(2,1)} %collective-permute-done.refs_1_), channel_id=1, source_target_pairs={{0,4},{1,5},{2,6},{3,7},{4,0},{5,1},{6,2},{7,3},{8,12},{9,13},{10,... | collective-permute-start | bytes 2752520 | tf_op jit(solution)/shard_map/ppermute | solution.py:22
  47.3 31.5 %collective-permute-start.10 = (bf16[7168,128]{1,0:T(8,128)(2,1)}, bf16[7168,128]{1,0:T(8,128)(2,1)}, u32[]{:S(2)}, u32[]{:S(2)}) collective-permute-start(bf16[7168,128]{1,0:T(8,128)(2,1)} %collective-permute-done.5.refs_9_.refs_13_), channel_id=1, source_target_pairs={{0,1},{1,0},{2,3},{3,2},{4,5},{5,4},{6,7},{7,6},{8,9},{9,8},{10,11... | collective-permute-start | bytes 5505032 | tf_op jit(solution)/shard_map/ppermute | solution.py:22
  47.3 31.5 %collective-permute-start.9 = (bf16[5120,128]{1,0:T(8,128)(2,1)}, bf16[5120,128]{1,0:T(8,128)(2,1)}, u32[]{:S(2)}, u32[]{:S(2)}) collective-permute-start(bf16[5120,128]{1,0:T(8,128)(2,1)} %slice.120), channel_id=1, source_target_pairs={{0,2},{1,3},{2,0},{3,1},{4,6},{5,7},{6,4},{7,5},{8,10},{9,11},{10,... | collective-permute-start | bytes 3932168 | tf_op jit(solution)/shard_map/ppermute | solution.py:22
  49.1 22.9 %collective-permute-start.7 = (bf16[64,7168]{1,0:T(8,128)(2,1)}, bf16[64,7168]{1,0:T(8,128)(2,1)}, u32[]{:S(2)}, u32[]{:S(2)}) collective-permute-start(bf16[64,7168]{1,0:T(8,128)(2,1)} %collective-permute-done.3.refs_2_), channel_id=1, source_target_pairs={{0,8},{1,9},{2,10},{3,11},{4,12},{5,13},{6,14},{7,15},{8,16},{9,17... | collective-permute-start | bytes 2752520 | tf_op jit(solution)/shard_map/ppermute | solution.py:27
  51.2 22.6 %collective-permute-start.8 = (bf16[64,7168]{1,0:T(8,128)(2,1)}, bf16[64,7168]{1,0:T(8,128)(2,1)}, u32[]{:S(2)}, u32[]{:S(2)}) collective-permute-start(bf16[64,7168]{1,0:T(8,128)(2,1)} %collective-permute-done.3.refs_2_), channel_id=1, source_target_pairs={{0,4},{1,5},{2,6},{3,7},{4,0},{5,1},{6,2},{7,3},{8,12},{9,13},{10,... | collective-permute-start | bytes 2752520 | tf_op jit(solution)/shard_map/ppermute | solution.py:22
  78.8 27.7 %collective-permute-start.13 = (bf16[5120,128]{1,0:T(8,128)(2,1)}, bf16[5120,128]{1,0:T(8,128)(2,1)}, u32[]{:S(2)}, u32[]{:S(2)}) collective-permute-start(bf16[5120,128]{1,0:T(8,128)(2,1)} %collective-permute-done.9.refs_17_), channel_id=1, source_target_pairs={{0,1},{1,0},{2,3},{3,2},{4,5},{5,4},{6,7},{7,6},{8,9},{9,8},{10,11... | collective-permute-start | bytes 3932168 | tf_op jit(solution)/shard_map/ppermute | solution.py:22
  78.8 27.7 %all-to-all-start = ((bf16[32,8,640]{2,1,0:T(8,128)(2,1)}), bf16[32,8,640]{2,1,0:T(8,128)(2,1)}, u32[]{:S(2)}, u32[]{:S(2)}) async-start(bf16[32,8,640]{2,1,0:T(8,128)(2,1)} %pad_maximum_fusion), calls=%async_computation | async-start | bytes 655360 | tf_op jit(solution)/shard_map/all_to_all | solution.py:221
  85.5 21.0 %collective-permute-start.12 = (bf16[2048,128]{1,0:T(8,128)(2,1)}, bf16[2048,128]{1,0:T(8,128)(2,1)S(1)}, u32[]{:S(2)}, u32[]{:S(2)}) collective-permute-start(bf16[2048,128]{1,0:T(8,128)(2,1)} %slice.121), channel_id=1, source_target_pairs={{0,2},{1,3},{2,0},{3,1},{4,6},{5,7},{6,4},{7,5},{8,10},{9,11},{10,... | collective-permute-start | bytes 1572872 | tf_op jit(solution)/shard_map/ppermute | solution.py:22
  88.9 17.6 %collective-permute-start.14 = (bf16[32,7168]{1,0:T(8,128)(2,1)}, bf16[32,7168]{1,0:T(8,128)(2,1)}, u32[]{:S(2)}, u32[]{:S(2)}) collective-permute-start(bf16[32,7168]{1,0:T(8,128)(2,1)} %slice.124), channel_id=1, source_target_pairs={{0,8},{1,9},{2,10},{3,11},{4,12},{5,13},{6,14},{7,15},{8,16},{9,17... | collective-permute-start | bytes 1376264 | tf_op jit(solution)/shard_map/ppermute | solution.py:27
  92.2 14.3 %collective-permute-start.15 = (bf16[32,7168]{1,0:T(8,128)(2,1)}, bf16[32,7168]{1,0:T(8,128)(2,1)}, u32[]{:S(2)}, u32[]{:S(2)}) collective-permute-start(bf16[32,7168]{1,0:T(8,128)(2,1)} %slice.125), channel_id=1, source_target_pairs={{0,4},{1,5},{2,6},{3,7},{4,0},{5,1},{6,2},{7,3},{8,12},{9,13},{10,... | collective-permute-start | bytes 1376264 | tf_op jit(solution)/shard_map/ppermute | solution.py:22
  106.8 18.7 %collective-permute-start.16 = (bf16[128,1792]{1,0:T(8,128)(2,1)}, bf16[128,1792]{1,0:T(8,128)(2,1)}, u32[]{:S(2)}, u32[]{:S(2)}) collective-permute-start(bf16[128,1792]{1,0:T(8,128)(2,1)} %get-tuple-element.65), channel_id=1, source_target_pairs={{0,2},{1,3},{2,0},{3,1},{4,6},{5,7},{6,4},{7,5},{8,10},{9,11},{10,... | collective-permute-start | bytes 1376264 | tf_op jit(solution)/shard_map/ppermute | solution.py:22
  107.4 18.1 %collective-permute-start.17 = (bf16[128,1792]{1,0:T(8,128)(2,1)}, bf16[128,1792]{1,0:T(8,128)(2,1)}, u32[]{:S(2)}, u32[]{:S(2)}) collective-permute-start(bf16[128,1792]{1,0:T(8,128)(2,1)} %get-tuple-element.66), channel_id=1, source_target_pairs={{0,4},{1,5},{2,6},{3,7},{4,0},{5,1},{6,2},{7,3},{8,12},{9,13},{10,... | collective-permute-start | bytes 1376264 | tf_op jit(solution)/shard_map/ppermute | solution.py:22
  124.6 17.1 %collective-permute-start.19 = (bf16[512,512]{1,0:T(8,128)(2,1)}, bf16[512,512]{1,0:T(8,128)(2,1)S(1)}, u32[]{:S(2)}, u32[]{:S(2)}) collective-permute-start(bf16[512,512]{1,0:T(8,128)(2,1)} %shard_map.132.mine), channel_id=1, source_target_pairs={{0,4},{1,5},{2,6},{3,7},{4,0},{5,1},{6,2},{7,3},{8,12},{9,13},{10,... | collective-permute-start | bytes 1572872 | tf_op jit(solution)/shard_map/ppermute | solution.py:22
  127.0 15.4 %collective-permute-start.21 = (bf16[128,1792]{1,0:T(8,128)(2,1)}, bf16[128,1792]{1,0:T(8,128)(2,1)S(1)}, u32[]{:S(2)}, u32[]{:S(2)}) collective-permute-start(bf16[128,1792]{1,0:T(8,128)(2,1)} %collective-permute-done.17.refs_4_), channel_id=1, source_target_pairs={{0,1},{1,0},{2,3},{3,2},{4,5},{5,4},{6,7},{7,6},{8,9},{9,8},{10,11... | collective-permute-start | bytes 1376264 | tf_op jit(solution)/shard_map/ppermute | solution.py:22
  153.2 15.0 %collective-permute-start.28 = (bf16[128,1792]{1,0:T(8,128)(2,1)S(1)}, bf16[128,1792]{1,0:T(8,128)(2,1)S(1)}, u32[]{:S(2)}, u32[]{:S(2)}) collective-permute-start(bf16[128,1792]{1,0:T(8,128)(2,1)S(1)} %collective-permute-done.27.refs_2_), channel_id=1, source_target_pairs={{0,1},{1,0},{2,3},{3,2},{4,5},{5,4},{6,7},{7,6},{8,9},{9,8},{10,11... | collective-permute-start | bytes 1376264 | tf_op jit(solution)/shard_map/ppermute | solution.py:22
  173.2 22.4 %collective-permute-start.26 = (bf16[128,1792]{1,0:T(8,128)(2,1)S(1)}, bf16[128,1792]{1,0:T(8,128)(2,1)S(1)}, u32[]{:S(2)}, u32[]{:S(2)}) collective-permute-start(bf16[128,1792]{1,0:T(8,128)(2,1)S(1)} %add_convert_fusion.5), channel_id=1, source_target_pairs={{0,24},{1,25},{2,26},{3,27},{4,28},{5,29},{6,30},{7,31},{8,0},{9,1... | collective-permute-start | bytes 1376264 | tf_op jit(solution)/shard_map/ppermute | solution.py:27
  185.8 19.2 %collective-permute-start.34 = (bf16[128,1792]{1,0:T(8,128)(2,1)S(1)}, bf16[128,1792]{1,0:T(8,128)(2,1)S(1)}, u32[]{:S(2)}, u32[]{:S(2)}) collective-permute-start(bf16[128,1792]{1,0:T(8,128)(2,1)S(1)} %add_convert_fusion.3), channel_id=1, source_target_pairs={{0,24},{1,25},{2,26},{3,27},{4,28},{5,29},{6,30},{7,31},{8,0},{9,1... | collective-permute-start | bytes 1376264 | tf_op jit(solution)/shard_map/ppermute | solution.py:27
  205.9 15.2 %collective-permute-start.36 = (bf16[64,1792]{1,0:T(8,128)(2,1)S(1)}, bf16[64,1792]{1,0:T(8,128)(2,1)S(1)}, u32[]{:S(2)}, u32[]{:S(2)}) collective-permute-start(bf16[64,1792]{1,0:T(8,128)(2,1)S(1)} %get-tuple-element.99), channel_id=1, source_target_pairs={{0,4},{1,5},{2,6},{3,7},{4,0},{5,1},{6,2},{7,3},{8,12},{9,13},{10,... | collective-permute-start | bytes 688136 | tf_op jit(solution)/shard_map/ppermute | solution.py:22
  (29 other events, 365.7 us)

commit v5 on v1

v5 whole, which is shorter than its diff:
```python
from functools import partial

import jax
import jax.numpy as jnp
from jax import lax
from jax.experimental import pallas as pl
from jax.experimental.pallas import tpu as pltpu
from jax.sharding import PartitionSpec as P

VDIM = 512
FF_WIN = 1024
CORE, XBIT, YBIT = 1, 2, 4
VMEM_BYTES = 16 * 1024 * 1024


score_scale = 0.07216878364870323


def swap(value, bit):
    count = lax.axis_size("ep")
    return lax.ppermute(value, "ep", [(i, i ^ bit) for i in range(count)])


def shift(value, step):
    count = lax.axis_size("ep")
    return lax.ppermute(value, "ep", [(i, (i + step) % count) for i in range(count)])


def together(*values):
    return lax.optimization_barrier(values)


def pair_dot(rows, left, right):
    both = jnp.concatenate([left[...], right[...]], axis=1)
    return jnp.dot(rows, both, preferred_element_type=jnp.float32)


def gated(gate, up):
    return (gate / (1.0 + jnp.exp(-gate)) * up).astype(jnp.bfloat16)


def pack_kernel(chosen, rows, *outs):
    picked = jnp.dot(chosen[...], rows[...], preferred_element_type=jnp.float32)
    picked = picked.astype(jnp.bfloat16)
    slots = outs[0].shape[0]
    for at, out in enumerate(outs):
        out[...] = picked[at * slots : (at + 1) * slots]


def packs(chosen, rows, planes, chunk):
    count, width = rows.shape
    slots = chosen.shape[0] // planes
    return pl.pallas_call(
        pack_kernel,
        grid=(width // chunk,),
        in_specs=[
            pl.BlockSpec(chosen.shape, lambda k: (0, 0)),
            pl.BlockSpec((count, chunk), lambda k: (0, k)),
        ],
        out_specs=[pl.BlockSpec((slots, chunk), lambda k: (0, k))] * planes,
        out_shape=[jax.ShapeDtypeStruct((slots, width), jnp.bfloat16)] * planes,
        compiler_params=pltpu.CompilerParams(vmem_limit_bytes=VMEM_BYTES),
        cost_estimate=pl.CostEstimate(
            flops=2 * chosen.size * width,
            bytes_accessed=2 * width * (count + planes * slots),
            transcendentals=0,
        ),
    )(chosen, rows)


def hidden_kernel(count, lead, *refs):
    units, weights = refs[:count], refs[count : count + 10]
    gate_o, gate_c, gate_x, gate_xc, up_o, up_c, up_xa, up_xca, up_xb, up_xcb = weights
    out, near_gate, far_gate, near_up, far_up = refs[count + 10 :]
    step = pl.program_id(0)

    @pl.when(step == 0)
    def _():
        for total in (near_gate, far_gate, near_up, far_up):
            total[...] = jnp.zeros_like(total)

    rows = jnp.concatenate([unit[...] for unit in units], axis=0)
    near_gate[...] += pair_dot(rows, gate_o, gate_c)
    far_gate[...] += pair_dot(rows, gate_x, gate_xc)
    near_up[...] += pair_dot(rows, up_o, up_c)

    @pl.when(step < lead)
    def _():
        far_up[...] += pair_dot(rows, up_xa, up_xca)

    @pl.when(step >= lead)
    def _():
        far_up[...] += pair_dot(rows, up_xb, up_xcb)

    @pl.when(step == pl.num_programs(0) - 1)
    def _():
        two = near_up.shape[1]
        out[:, :two] = gated(near_gate[...], near_up[...])
        out[:, two:] = gated(far_gate[...], far_up[...])


def hidden_units(units, weights, leads, rests, chunk):
    width = units[0].shape[1]
    wide = weights[0].shape[1]
    lead = leads[0].shape[0] // chunk
    count = sum(unit.shape[0] for unit in units)
    return pl.pallas_call(
        partial(hidden_kernel, len(units), lead),
        grid=(width // chunk,),
        in_specs=[pl.BlockSpec((unit.shape[0], chunk), lambda k: (0, k)) for unit in units]
        + [pl.BlockSpec((chunk, wide), lambda k: (k, 0)) for _ in weights]
        + [pl.BlockSpec((chunk, wide), lambda k: (jnp.minimum(k, lead - 1), 0)) for _ in leads]
        + [pl.BlockSpec((chunk, wide), lambda k: (jnp.maximum(k - lead, 0), 0)) for _ in rests],
        out_specs=pl.BlockSpec((count, 4 * wide), lambda k: (0, 0)),
        out_shape=jax.ShapeDtypeStruct((count, 4 * wide), jnp.bfloat16),
        scratch_shapes=[pltpu.VMEM((count, 2 * wide), jnp.float32)] * 4,
        compiler_params=pltpu.CompilerParams(vmem_limit_bytes=VMEM_BYTES),
        cost_estimate=pl.CostEstimate(
            flops=2 * count * width * wide * 8,
            bytes_accessed=2 * width * (count + wide * 8),
            transcendentals=0,
        ),
    )(*units, *weights, *leads, *rests)


def down_kernel(mine, other, *refs):
    (own, own_c, side, side_c, peer, peer_c), outs = refs[:6], refs[6:]
    deep = own.shape[0]
    table = jnp.concatenate(
        [own[...], own_c[...], side[:deep, :], side_c[:deep, :]]
        + [peer[...], peer_c[...], side[deep:, :], side_c[deep:, :]],
        axis=0,
    )
    count = mine.shape[0] // 2
    rows = count // len(outs)
    for part in range(2):
        here = slice(part * count, (part + 1) * count)
        there = slice((1 - part) * count, (2 - part) * count)
        joined = jnp.concatenate([mine[here, :], other[there, :]], axis=1)
        value = jnp.dot(joined, table, preferred_element_type=jnp.float32).astype(jnp.bfloat16)
        for at, out in enumerate(outs):
            out[part * rows : (part + 1) * rows, :] = value[at * rows : (at + 1) * rows]


def down_values(mine, other, own, side, peer, planes, chunk, offset):
    count, inner = mine.shape
    width = side[0].shape[1]
    rows = count // planes
    return pl.pallas_call(
        down_kernel,
        grid=(width // chunk,),
        in_specs=[pl.BlockSpec((count, inner), lambda k: (0, 0))] * 2
        + [pl.BlockSpec((block.shape[0], chunk), lambda k: (0, k + offset)) for block in own]
        + [pl.BlockSpec((block.shape[0], chunk), lambda k: (0, k)) for block in side]
        + [pl.BlockSpec((block.shape[0], chunk), lambda k: (0, k + offset)) for block in peer],
        out_specs=[pl.BlockSpec((rows, chunk), lambda k: (0, k))] * planes,
        out_shape=[jax.ShapeDtypeStruct((rows, width), jnp.bfloat16)] * planes,
        compiler_params=pltpu.CompilerParams(vmem_limit_bytes=VMEM_BYTES),
        cost_estimate=pl.CostEstimate(
            flops=2 * count * 2 * inner * width,
            bytes_accessed=2 * 2 * inner * width + 2 * count * width,
            transcendentals=0,
        ),
    )(mine, other, *own, *side, *peer)


def combine_kernel(high, low, *refs):
    parts, (mine, theirs) = refs[:-2], refs[-2:]
    values = jnp.concatenate([part[...] for part in parts], axis=0)
    total = jnp.dot(high[...], values, preferred_element_type=jnp.float32)
    total = total + jnp.dot(low[...], values, preferred_element_type=jnp.float32)
    rows = mine.shape[0]
    mine[...] = total[:rows].astype(jnp.bfloat16)
    theirs[...] = total[rows:].astype(jnp.bfloat16)


def combine(high, low, parts, chunk):
    rows, width = parts[0].shape
    count = high.shape[0] // 2
    out = jax.ShapeDtypeStruct((count, width), jnp.bfloat16)
    return pl.pallas_call(
        combine_kernel,
        grid=(width // chunk,),
        in_specs=[pl.BlockSpec(high.shape, lambda k: (0, 0))] * 2
        + [pl.BlockSpec((rows, chunk), lambda k: (0, k)) for _ in parts],
        out_specs=[pl.BlockSpec((count, chunk), lambda k: (0, k))] * 2,
        out_shape=[out, out],
        compiler_params=pltpu.CompilerParams(vmem_limit_bytes=VMEM_BYTES),
        cost_estimate=pl.CostEstimate(
            flops=4 * high.size * width,
            bytes_accessed=2 * width * (len(parts) * rows + 2 * count),
            transcendentals=0,
        ),
    )(high, low, *parts)


def places(picks, planes, split):
    count = picks.shape[0]
    plane = lax.axis_index("ep") // split
    experts = (plane + jnp.arange(planes, dtype=jnp.int32)) % planes
    named = jnp.any(picks[None] == experts[:, None, None], axis=2)
    order = jnp.arange(count, dtype=jnp.int32)
    before = order[:, None] < order[None, :]
    rank = jnp.sum((named[:, :, None] & before[None]).astype(jnp.int32), axis=1)
    return experts, named, rank


def gate_table(picks, gates, planes, split, slots):
    experts, named, rank = places(picks, planes, split)
    weight = jnp.sum(
        jnp.where(picks[None] == experts[:, None, None], gates[None], jnp.zeros_like(gates)[None]),
        axis=2,
    )
    at = jnp.arange(slots, dtype=jnp.int32)
    found = (rank.T[:, :, None] == at[None, None, :]) & named.T[:, :, None]
    return jnp.where(found, weight.T[:, :, None], 0.0)


def expert_rows(rows, picks, gates, latents, owners, requests, gate_proj, up_proj, down_proj):
    n_ep = lax.axis_size("ep")
    split = FF_WIN // gate_proj.shape[1]
    planes = n_ep // split
    count, width = rows.shape
    slots = -(-3 * count * picks.shape[1] // (2 * planes * 16)) * 16
    chunk = width // 4
    cut = 3 * chunk
    upper = lax.axis_index("ep") // YBIT % 2
    span = width // 4

    gate_x = swap(gate_proj, XBIT)
    _, named, rank = places(picks, planes, split)
    at = jnp.arange(slots, dtype=jnp.int32)
    chosen = (rank[:, None, :] == at[None, :, None]) & named[:, None, :]
    chosen = chosen.astype(jnp.bfloat16)

    own_0, out_1, out_2, out_3 = packs(chosen.reshape(planes * slots, count), rows, planes, span)
    own_0, out_1, out_3, latents, owners, requests, down_proj = together(
        own_0, out_1, out_3, latents, owners, requests, down_proj
    )
    own_1, own_3, peer_0 = shift(out_1, split), shift(out_3, 3 * split), swap(own_0, YBIT)
    keep = lax.dynamic_slice_in_dim(down_proj, 2 * upper * span, 2 * span, 1)
    send = lax.dynamic_slice_in_dim(down_proj, (2 - 2 * upper) * span, 2 * span, 1)
    down_y = swap(send, YBIT)
    outgoing = hand_over(latents, owners, requests)
    up_a, up_b = up_proj[:cut], up_proj[cut:]

    own_1, own_3, peer_0, down_y, gate_x, up_a, out_2, gate_proj, up_proj = together(
        own_1, own_3, peer_0, down_y, gate_x, up_a, out_2, gate_proj, up_proj
    )
    outgoing, keep, picks, gates, own_1 = together(outgoing, keep, picks, gates, own_1)
    own_2, peer_1, peer_3 = shift(out_2, 2 * split), swap(own_1, YBIT), swap(own_3, YBIT)
    up_xa, gate_xc = swap(up_a, XBIT), swap(gate_x, CORE)
    gate_c, up_c = swap(gate_proj, CORE), swap(up_proj, CORE)

    own_2, peer_1, peer_3, up_xa, gate_xc, gate_c, up_c, up_b = together(
        own_2, peer_1, peer_3, up_xa, gate_xc, gate_c, up_c, up_b
    )
    keep, down_y, picks, gates, outgoing, own_2 = together(
        keep, down_y, picks, gates, outgoing, own_2
    )
    peer_2, up_xb, up_xca = swap(own_2, YBIT), swap(up_b, XBIT), swap(up_xa, CORE)
    keep_c, down_yc = swap(keep, CORE), swap(down_y, CORE)
    incoming = lax.all_to_all(outgoing, "ep", split_axis=0, concat_axis=0, tiled=True)
    info = swap(jnp.concatenate([picks.astype(jnp.float32), gates], axis=1), YBIT)
    sides = [
        jnp.concatenate([part[:, at * span : (at + 1) * span] for part in (keep, down_y)], axis=0)
        for at in range(2)
    ]
    up_xb, sides[0] = together(up_xb, sides[0])
    up_xcb, side_0 = swap(up_xb, CORE), swap(sides[0], XBIT)

    units = (own_0, own_1, own_2, own_3, peer_0, peer_1, peer_2, peer_3)
    weights = (gate_proj, gate_c, gate_x, gate_xc, up_proj, up_c)
    hidden = hidden_units(units, weights, (up_xa, up_xca), (up_xb, up_xcb), chunk)
    other = swap(hidden, YBIT)
    side_0, sides[1] = together(side_0, sides[1])
    side_1 = swap(sides[1], XBIT)
    side = ((side_0, swap(side_0, CORE)), (side_1, swap(side_1, CORE)))

    top = picks.shape[1]
    tables = [
        gate_table(picks, gates, planes, split, slots),
        gate_table(info[:, :top].astype(jnp.int32), info[:, top:], planes, split, slots),
    ]
    tables = [
        jnp.pad(tables[0], ((0, 0), (0, 0), (0, slots))),
        jnp.pad(tables[1], ((0, 0), (0, 0), (slots, 0))),
    ]
    table = jnp.concatenate(tables, axis=0).reshape(2 * count, planes * 2 * slots)
    high = lax.reduce_precision(table, 8, 7)
    high, low = high.astype(jnp.bfloat16), (table - high).astype(jnp.bfloat16)

    outs, others = [], []
    for at in range(2):
        values = down_values(
            hidden, other, (keep, keep_c), side[at], (down_y, down_yc), planes, span // 2, 2 * at
        )
        back = [values[0]] + [shift(values[k], n_ep - k * split) for k in range(1, planes)]
        mine, theirs = combine(high, low, back, span // 2)
        outs.append(mine)
        others.append(swap(theirs, YBIT))
    low_first = jnp.concatenate(outs + others, axis=1)
    high_first = jnp.concatenate(others + outs, axis=1)
    return jnp.where(upper == 0, low_first, high_first), incoming, other


def attend(query_part, cache_latents, cache_lens, handed, handed_mark):
    requests = query_part.shape[0]
    cache_scores = (
        jnp.einsum("qhl,qcl->qhc", query_part, cache_latents, preferred_element_type=jnp.float32)
        * score_scale
    )
    hand_scores = (
        jnp.einsum("qhl,rl->qhr", query_part, handed, preferred_element_type=jnp.float32)
        * score_scale
    )
    cache_mask = (
        jnp.arange(cache_latents.shape[1], dtype=jnp.int32)[None, :] < cache_lens[:, None]
    )[:, None, :]
    marks = jnp.arange(1, requests + 1, dtype=jnp.int32).astype(jnp.float32)
    hand_mask = (handed_mark[None, :] == marks[:, None])[:, None, :]
    cache_scores = jnp.where(cache_mask, cache_scores, -jnp.inf)
    hand_scores = jnp.where(hand_mask, hand_scores, -jnp.inf)
    top = jnp.maximum(jnp.max(cache_scores, axis=2), jnp.max(hand_scores, axis=2))[:, :, None]
    cache_expo = jnp.exp(cache_scores - top)
    hand_expo = jnp.exp(hand_scores - top)
    denom = (jnp.sum(cache_expo, axis=2) + jnp.sum(hand_expo, axis=2))[:, :, None]
    cache_prob = (cache_expo / denom).astype(jnp.bfloat16)
    hand_prob = (hand_expo / denom).astype(jnp.bfloat16)
    result = jnp.einsum(
        "qhc,qcv->qhv", cache_prob, cache_latents[:, :, :VDIM], preferred_element_type=jnp.float32
    )
    result = result + jnp.einsum(
        "qhr,rv->qhv", hand_prob, handed[:, :VDIM], preferred_element_type=jnp.float32
    )
    return result.astype(jnp.bfloat16)


def hand_over(prompt_latents, owners, requests):
    n_ep = lax.axis_size("ep")
    stretch, lat = prompt_latents.shape
    cap = 2 * stretch // n_ep
    places_at = jnp.arange(stretch, dtype=jnp.int32)
    earlier = (owners[:, None] == owners[None, :]) & (places_at[None, :] < places_at[:, None])
    target = owners * cap + jnp.sum(earlier.astype(jnp.int32), axis=1)
    slots = jnp.arange(n_ep * cap, dtype=jnp.int32)
    chosen = slots[:, None] == target[None, :]
    packed = jnp.dot(
        chosen.astype(jnp.bfloat16), prompt_latents, preferred_element_type=jnp.float32
    ).astype(jnp.bfloat16)
    mark = jnp.sum(jnp.where(chosen, requests[None, :] + 1, 0), axis=1).astype(jnp.bfloat16)
    fill = -(lat + 1) % 128
    outgoing = jnp.concatenate(
        [packed, mark[:, None], jnp.zeros((n_ep * cap, fill), jnp.bfloat16)], axis=1
    )
    return outgoing.reshape(n_ep, cap, lat + 1 + fill)


def on_device(
    moe_rows,
    routes,
    route_gates,
    gate_proj,
    up_proj,
    down_proj,
    queries,
    cache_latents,
    cache_lens,
    prompt_latents,
    kv_owner,
    kv_request,
):
    sections, count, width = moe_rows.shape
    top = routes.shape[2]
    expert_out, incoming, other = expert_rows(
        moe_rows.reshape(sections * count, width),
        routes.reshape(sections * count, top),
        route_gates.reshape(sections * count, top),
        prompt_latents,
        kv_owner[:, 0],
        kv_request,
        gate_proj,
        up_proj,
        down_proj,
    )
    expert_out = expert_out.reshape(moe_rows.shape)
    queries, incoming, _ = together(queries, incoming, other)
    lat = prompt_latents.shape[1]
    handed = incoming[:, :, :lat].reshape(-1, lat)
    handed_mark = incoming[:, :, lat].reshape(-1).astype(jnp.float32)
    attended = attend(queries, cache_latents, cache_lens, handed, handed_mark)
    return (expert_out, attended)


def solution(mesh):
    placed = (
        P("section", ("groups", "ep"), None),
        P("section", ("groups", "ep"), None),
        P("section", ("groups", "ep"), None),
        P(None, "ep"),
        P(None, "ep"),
        P("ep", None),
        P(("groups", "ep"), None, None),
        P(("groups", "ep"), None, None),
        P(("groups", "ep")),
        P(("groups", "ep"), None),
        P(("groups", "ep"), None),
        P(("groups", "ep")),
    )
    return jax.shard_map(
        on_device,
        mesh=mesh,
        in_specs=placed,
        out_specs=(P("section", ("groups", "ep"), None), P(("groups", "ep"), None, None)),
        check_vma=False,
    )
```

time: 322 us -> 253 us (0.79)
  waiting for transfers between devices: 234 us -> 154 us
  starting transfers between devices: 24.1 us -> 39.1 us
  other arithmetic: 6.56 us -> 10.8 us
  local copies, waits for them, and re-layouts: 24 us -> 20 us
    ppermute x16 -> x23, waiting for transfers between devices: 108 us -> 67.2 us  [swap(): return lax.ppermute(value, 'ep', [(i, i ^ bit) for i in range(count)])]
    ppermute x6 -> x9, waiting for transfers between devices: 109 us -> 86.5 us  [shift(): lax.ppermute(value, 'ep', [(i, (i + step) % count) for i in range(count)])]
    all_to_all x1, waiting for transfers between devices: 16.4 us -> 0.01 us  [expert_rows(): lax.all_to_all(outgoing, 'ep', split_axis=0, concat_axis=0, tiled=True)]
    ppermute x6 -> x9, starting transfers between devices: 5.78 us -> 15.5 us  [shift(): lax.ppermute(value, 'ep', [(i, (i + step) % count) for i in range(count)])]
    all_to_all x1, starting transfers between devices: 3.15 us -> 9.19 us  [expert_rows(): lax.all_to_all(outgoing, 'ep', split_axis=0, concat_axis=0, tiled=True)]
    unnamed x58 -> x40, local copies, waits for them, and re-layouts: 13.4 us -> 7.61 us
    concatenate x2 -> x5, other arithmetic: 0.93 us -> 5.12 us  [the longest x2 3.51 us: expert_rows(): jnp.concatenate([part[:, at * span:(at + 1) * span] for part in (keep, do...]
    concatenate x4 -> x1, local copies, waits for them, and re-layouts: 3.81 us -> 0.08 us  [hand_over(): jnp.concatenate([packed, mark[:, None], jnp.zeros((n_ep * cap, fill), jnp...]
  transfers between devices with their start and end apart: 23 -> 33, of which waited for: 14 -> 14; matrix products, arithmetic and copies ran while one was open for 8% -> 11% of each run, Pallas kernels for 4% -> 9%
where the time goes in v5:
time: 253 us
  waiting for transfers between devices  154 us (61%)
  starting transfers between devices  39.1 us (15%)
  Pallas kernels  22.1 us (9%)
  local copies, waits for them, and re-layouts  20 us (8%)
  other arithmetic  10.8 us (4%)
  matrix products  5.94 us (2%)
    ppermute x9, waiting for transfers between devices, shift(): lax.ppermute(value, 'ep', [(i, (i + step) % count) for i in range(count)])  86.5 us
    ppermute x23, waiting for transfers between devices, swap(): return lax.ppermute(value, 'ep', [(i, i ^ bit) for i in range(count)])  67.2 us
    ppermute x9, starting transfers between devices, shift(): lax.ppermute(value, 'ep', [(i, (i + step) % count) for i in range(count)])  15.5 us
    ppermute x23, starting transfers between devices, swap(): return lax.ppermute(value, 'ep', [(i, i ^ bit) for i in range(count)])  14.4 us
    pallas_call x1, Pallas kernels, hidden_units(): pl.pallas_call(partial(hidden_kernel, len(units), lead), grid=(width // c...  10.2 us
    all_to_all x1, starting transfers between devices, expert_rows(): lax.all_to_all(outgoing, 'ep', split_axis=0, concat_axis=0, tiled=True)  9.19 us
    unnamed x40, local copies, waits for them, and re-layouts  7.61 us
    pallas_call x2, Pallas kernels, down_values(): pl.pallas_call(down_kernel, grid=(width // chunk,), in_specs=[pl.BlockSpe...  7.21 us
  transfers between devices with their start and end apart: 33, of which 14 were waited for; matrix products, arithmetic and copies ran while one was open for 11% of the time, Pallas kernels for 9%

profile of v5, /device:TPU:16, one launch (start us, length us, event | category | flops | bytes accessed | tf_op | source)
XLA Modules:
  0.0 252.5 jit_solution(3342114744016482320)
XLA Ops:
  4.6 2.5 %shard_map.131 = (bf16[48,7168]{1,0:T(8,128)(2,1)S(1)}, bf16[48,7168]{1,0:T(8,128)(2,1)}, bf16[48,7168]{1,0:T(8,128)(2,1)S(1)}, bf16[48,7168]{1,0:T(8,128)(2,1)}) custom-call(bf16[192,64]{1,0:T(8,128)(2,1)S(1)} %fusion.18.chosen, bf16[64,7168]{1,0:T(8,128)(2,1)S(1)} %bitcast.41), custom_call_target="tpu_custom_call" | custom-call | flops 176160768 | bytes 3670016 | tf_op jit(solution)/shard_map/pallas_call | solution.py:53
  8.0 2.8 %constant_dynamic-slice_fusion = (bf16[128,3584]{1,0:T(8,128)(2,1)}, bf16[128,3584]{1,0:T(8,128)(2,1)S(1)}) fusion(bf16[128,7168]{1,0:T(8,128)(2,1)} %param.17, s32[]{:T(128)S(6)} %select_n.77, s32[]{:T(128)S(6)} %select_n.76), kind=kLoop, calls=%fused_computation.69 | loop fusion | bytes 3670024 | tf_op jit(solution)/shard_map/dynamic_slice | solution.py:242
  19.7 24.3 %collective-permute-done.refs_1_ = bf16[48,7168]{1,0:T(8,128)(2,1)} collective-permute-done((bf16[48,7168]{1,0:T(8,128)(2,1)}, bf16[48,7168]{1,0:T(8,128)(2,1)}, u32[]{:S(2)}, u32[]{:S(2)}) %collective-permute-start) | collective-permute-done | bytes 688160 | tf_op jit(solution)/shard_map/ppermute | solution.py:26
  44.0 3.7 %collective-permute-done.2.refs_4_ = bf16[48,7168]{1,0:T(8,128)(2,1)} collective-permute-done((bf16[48,7168]{1,0:T(8,128)(2,1)}, bf16[48,7168]{1,0:T(8,128)(2,1)}, u32[]{:S(2)}, u32[]{:S(2)}) %collective-permute-start.2) | collective-permute-done | bytes 688160 | tf_op jit(solution)/shard_map/ppermute | solution.py:21
  50.0 13.8 %collective-permute-done.6.refs_5_ = bf16[48,7168]{1,0:T(8,128)(2,1)S(1)} collective-permute-done((bf16[48,7168]{1,0:T(8,128)(2,1)}, bf16[48,7168]{1,0:T(8,128)(2,1)S(1)}, u32[]{:S(2)}, u32[]{:S(2)}) %collective-permute-start.6) | collective-permute-done | bytes 688160 | tf_op jit(solution)/shard_map/ppermute | solution.py:21
  65.3 15.2 %collective-permute-done.5.refs_2_ = bf16[48,7168]{1,0:T(8,128)(2,1)} collective-permute-done((bf16[48,7168]{1,0:T(8,128)(2,1)}, bf16[48,7168]{1,0:T(8,128)(2,1)}, u32[]{:S(2)}, u32[]{:S(2)}) %collective-permute-start.5) | collective-permute-done | bytes 688160 | tf_op jit(solution)/shard_map/ppermute | solution.py:26
  82.8 15.0 %collective-permute-done.7.refs_7_ = bf16[48,7168]{1,0:T(8,128)(2,1)} collective-permute-done((bf16[48,7168]{1,0:T(8,128)(2,1)}, bf16[48,7168]{1,0:T(8,128)(2,1)}, u32[]{:S(2)}, u32[]{:S(2)}) %collective-permute-start.7) | collective-permute-done | bytes 688160 | tf_op jit(solution)/shard_map/ppermute | solution.py:21
  101.2 9.2 %all-to-all-start = ((bf16[32,8,640]{2,1,0:T(8,128)(2,1)}), bf16[32,8,640]{2,1,0:T(8,128)(2,1)}, u32[]{:S(2)}, u32[]{:S(2)}) async-start(bf16[32,8,640]{2,1,0:T(8,128)(2,1)} %maximum_maximum_fusion), calls=%async_computation | async-start | bytes 655360 | tf_op jit(solution)/shard_map/all_to_all | solution.py:263
  113.3 2.1 pad_maximum_fusion.1
  115.5 6.6 %collective-permute-done.12 = f32[64,4]{0,1:T(4,128)S(1)} collective-permute-done((f32[64,4]{0,1:T(4,128)S(1)}, f32[64,4]{0,1:T(4,128)S(1)}, u32[]{:S(2)}, u32[]{:S(2)}) %collective-permute-start.12) | collective-permute-done | bytes 1056 | tf_op jit(solution)/shard_map/ppermute | solution.py:21
  128.3 10.2 %shard_map.132.mine = bf16[384,512]{1,0:T(8,128)(2,1)S(1)} custom-call(bf16[48,7168]{1,0:T(8,128)(2,1)S(1)} %copy-done.7, bf16[48,7168]{1,0:T(8,128)(2,1)} %collective-permute-done.refs_1_, bf16[48,7168]{1,0:T(8,128)(2,1)} %collective-permute-done.5.refs_2_, bf16[48,7168]{1,0:T(8,128)(2,1)} %collective-permute-done.1.refs_3_, ...), custom_call_target="tpu_custom_call" | custom-call | flops 5637144576 | bytes 20185088 | tf_op jit(solution)/shard_map/pallas_call | solution.py:107
  139.0 7.0 %collective-permute-done.19.refs_2_ = bf16[256,1792]{1,0:T(8,128)(2,1)} collective-permute-done((bf16[256,1792]{1,0:T(8,128)(2,1)S(1)}, bf16[256,1792]{1,0:T(8,128)(2,1)}, u32[]{:S(2)}, u32[]{:S(2)}) %collective-permute-start.19) | collective-permute-done | bytes 917536 | tf_op jit(solution)/shard_map/ppermute | solution.py:21
  152.8 15.5 %collective-permute-done.25.refs_2_ = bf16[256,1792]{1,0:T(8,128)(2,1)} collective-permute-done((bf16[256,1792]{1,0:T(8,128)(2,1)}, bf16[256,1792]{1,0:T(8,128)(2,1)}, u32[]{:S(2)}, u32[]{:S(2)}) %collective-permute-start.25) | collective-permute-done | bytes 917536 | tf_op jit(solution)/shard_map/ppermute | solution.py:21
  171.6 3.7 %shard_map.133 = (bf16[96,1792]{1,0:T(8,128)(2,1)S(1)}, bf16[96,1792]{1,0:T(8,128)(2,1)S(1)}, bf16[96,1792]{1,0:T(8,128)(2,1)S(1)}, bf16[96,1792]{1,0:T(8,128)(2,1)S(1)}) custom-call(bf16[384,512]{1,0:T(8,128)(2,1)S(1)} %shard_map.132.mine, bf16[384,512]{1,0:T(8,128)(2,1)} %collective-permute-done.17.other, bf16[128,3584]{1,0:T(8,128)(2,1)S(1)} %get-tuple-element.95.refs_0_, ...), custom_call_target="tpu_custom_call" | custom-call | flops 1409286144 | bytes 5046272 | tf_op jit(solution)/shard_map/pallas_call | solution.py:149
  175.2 3.0 %collective-permute-start.22 = (bf16[96,1792]{1,0:T(8,128)(2,1)S(1)}, bf16[96,1792]{1,0:T(8,128)(2,1)S(1)}, u32[]{:S(2)}, u32[]{:S(2)}) collective-permute-start(bf16[96,1792]{1,0:T(8,128)(2,1)S(1)} %get-tuple-element.101), channel_id=1, source_target_pairs={{0,24},{1,25},{2,26},{3,27},{4,28},{5,29},{6,30},{7,31},{8,0},{9,1... | collective-permute-start | bytes 1032200 | tf_op jit(solution)/shard_map/ppermute | solution.py:26
  179.2 4.3 %collective-permute-start.23 = (bf16[96,1792]{1,0:T(8,128)(2,1)S(1)}, bf16[96,1792]{1,0:T(8,128)(2,1)S(1)}, u32[]{:S(2)}, u32[]{:S(2)}) collective-permute-start(bf16[96,1792]{1,0:T(8,128)(2,1)S(1)} %get-tuple-element.102), channel_id=1, source_target_pairs={{0,16},{1,17},{2,18},{3,19},{4,20},{5,21},{6,22},{7,23},{8,24},{9,... | collective-permute-start | bytes 1032200 | tf_op jit(solution)/shard_map/ppermute | solution.py:26
  183.6 3.5 %shard_map.135 = (bf16[96,1792]{1,0:T(8,128)(2,1)S(1)}, bf16[96,1792]{1,0:T(8,128)(2,1)S(1)}, bf16[96,1792]{1,0:T(8,128)(2,1)S(1)}, bf16[96,1792]{1,0:T(8,128)(2,1)S(1)}) custom-call(bf16[384,512]{1,0:T(8,128)(2,1)S(1)} %shard_map.132.mine, bf16[384,512]{1,0:T(8,128)(2,1)} %collective-permute-done.17.other, bf16[128,3584]{1,0:T(8,128)(2,1)S(1)} %get-tuple-element.95.refs_0_, ...), custom_call_target="tpu_custom_call" | custom-call | flops 1409286144 | bytes 5046272 | tf_op jit(solution)/shard_map/pallas_call | solution.py:149
  187.1 2.1 collective-permute-start.27
  191.1 1.9 collective-permute-start.29
  193.9 14.8 %collective-permute-done.23.refs_2_ = bf16[96,1792]{1,0:T(8,128)(2,1)S(1)} collective-permute-done((bf16[96,1792]{1,0:T(8,128)(2,1)S(1)}, bf16[96,1792]{1,0:T(8,128)(2,1)S(1)}, u32[]{:S(2)}, u32[]{:S(2)}) %collective-permute-start.23) | collective-permute-done | bytes 344096 | tf_op jit(solution)/shard_map/ppermute | solution.py:26
  208.7 19.2 %collective-permute-done.24.refs_3_ = bf16[96,1792]{1,0:T(8,128)(2,1)S(1)} collective-permute-done((bf16[96,1792]{1,0:T(8,128)(2,1)S(1)}, bf16[96,1792]{1,0:T(8,128)(2,1)S(1)}, u32[]{:S(2)}, u32[]{:S(2)}) %collective-permute-start.24) | collective-permute-done | bytes 344096 | tf_op jit(solution)/shard_map/ppermute | solution.py:26
  230.8 7.0 %collective-permute-done.28.refs_2_ = bf16[96,1792]{1,0:T(8,128)(2,1)S(1)} collective-permute-done((bf16[96,1792]{1,0:T(8,128)(2,1)S(1)}, bf16[96,1792]{1,0:T(8,128)(2,1)S(1)}, u32[]{:S(2)}, u32[]{:S(2)}) %collective-permute-start.28) | collective-permute-done | bytes 344096 | tf_op jit(solution)/shard_map/ppermute | solution.py:26
  237.8 4.8 %collective-permute-done.29.refs_3_ = bf16[96,1792]{1,0:T(8,128)(2,1)S(1)} collective-permute-done((bf16[96,1792]{1,0:T(8,128)(2,1)S(1)}, bf16[96,1792]{1,0:T(8,128)(2,1)S(1)}, u32[]{:S(2)}, u32[]{:S(2)}) %collective-permute-start.29) | collective-permute-done | bytes 344096 | tf_op jit(solution)/shard_map/ppermute | solution.py:26
  245.8 5.6 %collective-permute-done.31 = bf16[64,1792]{1,0:T(8,128)(2,1)S(1)} collective-permute-done((bf16[64,1792]{1,0:T(8,128)(2,1)S(1)}, bf16[64,1792]{1,0:T(8,128)(2,1)S(1)}, u32[]{:S(2)}, u32[]{:S(2)}) %collective-permute-start.31) | collective-permute-done | bytes 229408 | tf_op jit(solution)/shard_map/ppermute | solution.py:21
  (139 shorter events, 53.9 us)
Async XLA Ops:
  0.6 47.0 %collective-permute-start.4 = (bf16[7168,128]{1,0:T(8,128)(2,1)}, bf16[7168,128]{1,0:T(8,128)(2,1)}, u32[]{:S(2)}, u32[]{:S(2)}) collective-permute-start(bf16[7168,128]{1,0:T(8,128)(2,1)} %refs_8_), channel_id=1, source_target_pairs={{0,2},{1,3},{2,0},{3,1},{4,6},{5,7},{6,4},{7,5},{8,10},{9,11},{10,... | collective-permute-start | bytes 5505032 | tf_op jit(solution)/shard_map/ppermute | solution.py:21
  10.8 36.9 %collective-permute-start.3 = (bf16[128,3584]{1,0:T(8,128)(2,1)}, bf16[128,3584]{1,0:T(8,128)(2,1)S(1)}, u32[]{:S(2)}, u32[]{:S(2)}) collective-permute-start(bf16[128,3584]{1,0:T(8,128)(2,1)} %get-tuple-element.124), channel_id=1, source_target_pairs={{0,4},{1,5},{2,6},{3,7},{4,0},{5,1},{6,2},{7,3},{8,12},{9,13},{10,... | collective-permute-start | bytes 2752520 | tf_op jit(solution)/shard_map/ppermute | solution.py:21
  12.3 31.7 %collective-permute-start = (bf16[48,7168]{1,0:T(8,128)(2,1)}, bf16[48,7168]{1,0:T(8,128)(2,1)}, u32[]{:S(2)}, u32[]{:S(2)}) collective-permute-start(bf16[48,7168]{1,0:T(8,128)(2,1)} %get-tuple-element.66), channel_id=1, source_target_pairs={{0,8},{1,9},{2,10},{3,11},{4,12},{5,13},{6,14},{7,15},{8,16},{9,17... | collective-permute-start | bytes 2064392 | tf_op jit(solution)/shard_map/ppermute | solution.py:26
  13.9 30.1 %collective-permute-start.1 = (bf16[48,7168]{1,0:T(8,128)(2,1)}, bf16[48,7168]{1,0:T(8,128)(2,1)}, u32[]{:S(2)}, u32[]{:S(2)}) collective-permute-start(bf16[48,7168]{1,0:T(8,128)(2,1)} %get-tuple-element.67), channel_id=1, source_target_pairs={{0,24},{1,25},{2,26},{3,27},{4,28},{5,29},{6,30},{7,31},{8,0},{9,1... | collective-permute-start | bytes 2064392 | tf_op jit(solution)/shard_map/ppermute | solution.py:26
  14.3 33.3 %collective-permute-start.2 = (bf16[48,7168]{1,0:T(8,128)(2,1)}, bf16[48,7168]{1,0:T(8,128)(2,1)}, u32[]{:S(2)}, u32[]{:S(2)}) collective-permute-start(bf16[48,7168]{1,0:T(8,128)(2,1)} %copy-done.6), channel_id=1, source_target_pairs={{0,4},{1,5},{2,6},{3,7},{4,0},{5,1},{6,2},{7,3},{8,12},{9,13},{10,... | collective-permute-start | bytes 2064392 | tf_op jit(solution)/shard_map/ppermute | solution.py:21
  49.2 48.7 %collective-permute-start.10 = (bf16[7168,128]{1,0:T(8,128)(2,1)}, bf16[7168,128]{1,0:T(8,128)(2,1)}, u32[]{:S(2)}, u32[]{:S(2)}) collective-permute-start(bf16[7168,128]{1,0:T(8,128)(2,1)} %refs_8_), channel_id=1, source_target_pairs={{0,1},{1,0},{2,3},{3,2},{4,5},{5,4},{6,7},{7,6},{8,9},{9,8},{10,11... | collective-permute-start | bytes 5505032 | tf_op jit(solution)/shard_map/ppermute | solution.py:21
  49.2 48.7 %collective-permute-start.11 = (bf16[7168,128]{1,0:T(8,128)(2,1)}, bf16[7168,128]{1,0:T(8,128)(2,1)}, u32[]{:S(2)}, u32[]{:S(2)}) collective-permute-start(bf16[7168,128]{1,0:T(8,128)(2,1)} %refs_12_), channel_id=1, source_target_pairs={{0,1},{1,0},{2,3},{3,2},{4,5},{5,4},{6,7},{7,6},{8,9},{9,8},{10,11... | collective-permute-start | bytes 5505032 | tf_op jit(solution)/shard_map/ppermute | solution.py:21
  49.7 48.2 %collective-permute-start.9 = (bf16[7168,128]{1,0:T(8,128)(2,1)}, bf16[7168,128]{1,0:T(8,128)(2,1)}, u32[]{:S(2)}, u32[]{:S(2)}) collective-permute-start(bf16[7168,128]{1,0:T(8,128)(2,1)} %collective-permute-done.4.refs_10_), channel_id=1, source_target_pairs={{0,1},{1,0},{2,3},{3,2},{4,5},{5,4},{6,7},{7,6},{8,9},{9,8},{10,11... | collective-permute-start | bytes 5505032 | tf_op jit(solution)/shard_map/ppermute | solution.py:21
  49.7 30.8 %collective-permute-start.5 = (bf16[48,7168]{1,0:T(8,128)(2,1)}, bf16[48,7168]{1,0:T(8,128)(2,1)}, u32[]{:S(2)}, u32[]{:S(2)}) collective-permute-start(bf16[48,7168]{1,0:T(8,128)(2,1)} %copy-done.10), channel_id=1, source_target_pairs={{0,16},{1,17},{2,18},{3,19},{4,20},{5,21},{6,22},{7,23},{8,24},{9,... | collective-permute-start | bytes 2064392 | tf_op jit(solution)/shard_map/ppermute | solution.py:26
  64.7 33.2 %collective-permute-start.8 = (bf16[5376,128]{1,0:T(8,128)(2,1)}, bf16[5376,128]{1,0:T(8,128)(2,1)}, u32[]{:S(2)}, u32[]{:S(2)}) collective-permute-start(bf16[5376,128]{1,0:T(8,128)(2,1)} %slice.36), channel_id=1, source_target_pairs={{0,2},{1,3},{2,0},{3,1},{4,6},{5,7},{6,4},{7,5},{8,10},{9,11},{10,... | collective-permute-start | bytes 4128776 | tf_op jit(solution)/shard_map/ppermute | solution.py:21
  98.9 72.7 %collective-permute-start.18 = (bf16[128,3584]{1,0:T(8,128)(2,1)S(1)}, bf16[128,3584]{1,0:T(8,128)(2,1)}, u32[]{:S(2)}, u32[]{:S(2)}) collective-permute-start(bf16[128,3584]{1,0:T(8,128)(2,1)S(1)} %get-tuple-element.95.refs_0_), channel_id=1, source_target_pairs={{0,1},{1,0},{2,3},{3,2},{4,5},{5,4},{6,7},{7,6},{8,9},{9,8},{10,11... | collective-permute-start | bytes 2752520 | tf_op jit(solution)/shard_map/ppermute | solution.py:21
  99.9 22.3 %collective-permute-start.15 = (bf16[1792,128]{1,0:T(8,128)(2,1)}, bf16[1792,128]{1,0:T(8,128)(2,1)S(1)}, u32[]{:S(2)}, u32[]{:S(2)}) collective-permute-start(bf16[1792,128]{1,0:T(8,128)(2,1)} %slice.37), channel_id=1, source_target_pairs={{0,2},{1,3},{2,0},{3,1},{4,6},{5,7},{6,4},{7,5},{8,10},{9,11},{10,... | collective-permute-start | bytes 1376264 | tf_op jit(solution)/shard_map/ppermute | solution.py:21
  100.4 24.7 %collective-permute-start.14 = (bf16[5376,128]{1,0:T(8,128)(2,1)}, bf16[5376,128]{1,0:T(8,128)(2,1)}, u32[]{:S(2)}, u32[]{:S(2)}) collective-permute-start(bf16[5376,128]{1,0:T(8,128)(2,1)} %collective-permute-done.8.refs_14_), channel_id=1, source_target_pairs={{0,1},{1,0},{2,3},{3,2},{4,5},{5,4},{6,7},{7,6},{8,9},{9,8},{10,11... | collective-permute-start | bytes 4128776 | tf_op jit(solution)/shard_map/ppermute | solution.py:21
  100.6 24.2 %collective-permute-start.13 = (bf16[48,7168]{1,0:T(8,128)(2,1)}, bf16[48,7168]{1,0:T(8,128)(2,1)}, u32[]{:S(2)}, u32[]{:S(2)}) collective-permute-start(bf16[48,7168]{1,0:T(8,128)(2,1)} %collective-permute-done.5.refs_2_), channel_id=1, source_target_pairs={{0,4},{1,5},{2,6},{3,7},{4,0},{5,1},{6,2},{7,3},{8,12},{9,13},{10,... | collective-permute-start | bytes 2064392 | tf_op jit(solution)/shard_map/ppermute | solution.py:21
  101.2 50.4 %all-to-all-start = ((bf16[32,8,640]{2,1,0:T(8,128)(2,1)}), bf16[32,8,640]{2,1,0:T(8,128)(2,1)}, u32[]{:S(2)}, u32[]{:S(2)}) async-start(bf16[32,8,640]{2,1,0:T(8,128)(2,1)} %maximum_maximum_fusion), calls=%async_computation | async-start | bytes 655360 | tf_op jit(solution)/shard_map/all_to_all | solution.py:263
  123.1 22.9 %collective-permute-start.19 = (bf16[256,1792]{1,0:T(8,128)(2,1)S(1)}, bf16[256,1792]{1,0:T(8,128)(2,1)}, u32[]{:S(2)}, u32[]{:S(2)}) collective-permute-start(bf16[256,1792]{1,0:T(8,128)(2,1)S(1)} %pad_maximum_fusion), channel_id=1, source_target_pairs={{0,2},{1,3},{2,0},{3,1},{4,6},{5,7},{6,4},{7,5},{8,10},{9,11},{10,... | collective-permute-start | bytes 2752520 | tf_op jit(solution)/shard_map/ppermute | solution.py:21
  124.8 46.7 %collective-permute-start.21 = (bf16[128,3584]{1,0:T(8,128)(2,1)S(1)}, bf16[128,3584]{1,0:T(8,128)(2,1)}, u32[]{:S(2)}, u32[]{:S(2)}) collective-permute-start(bf16[128,3584]{1,0:T(8,128)(2,1)S(1)} %collective-permute-done.3.refs_4_), channel_id=1, source_target_pairs={{0,1},{1,0},{2,3},{3,2},{4,5},{5,4},{6,7},{7,6},{8,9},{9,8},{10,11... | collective-permute-start | bytes 2752520 | tf_op jit(solution)/shard_map/ppermute | solution.py:21
  145.9 22.3 %collective-permute-start.25 = (bf16[256,1792]{1,0:T(8,128)(2,1)}, bf16[256,1792]{1,0:T(8,128)(2,1)}, u32[]{:S(2)}, u32[]{:S(2)}) collective-permute-start(bf16[256,1792]{1,0:T(8,128)(2,1)} %pad_maximum_fusion.1), channel_id=1, source_target_pairs={{0,2},{1,3},{2,0},{3,1},{4,6},{5,7},{6,4},{7,5},{8,10},{9,11},{10,... | collective-permute-start | bytes 2752520 | tf_op jit(solution)/shard_map/ppermute | solution.py:21
  151.5 20.0 %collective-permute-start.20 = (bf16[256,1792]{1,0:T(8,128)(2,1)}, bf16[256,1792]{1,0:T(8,128)(2,1)}, u32[]{:S(2)}, u32[]{:S(2)}) collective-permute-start(bf16[256,1792]{1,0:T(8,128)(2,1)} %collective-permute-done.19.refs_2_), channel_id=1, source_target_pairs={{0,1},{1,0},{2,3},{3,2},{4,5},{5,4},{6,7},{7,6},{8,9},{9,8},{10,11... | collective-permute-start | bytes 2752520 | tf_op jit(solution)/shard_map/ppermute | solution.py:21
  179.2 29.5 %collective-permute-start.23 = (bf16[96,1792]{1,0:T(8,128)(2,1)S(1)}, bf16[96,1792]{1,0:T(8,128)(2,1)S(1)}, u32[]{:S(2)}, u32[]{:S(2)}) collective-permute-start(bf16[96,1792]{1,0:T(8,128)(2,1)S(1)} %get-tuple-element.102), channel_id=1, source_target_pairs={{0,16},{1,17},{2,18},{3,19},{4,20},{5,21},{6,22},{7,23},{8,24},{9,... | collective-permute-start | bytes 1032200 | tf_op jit(solution)/shard_map/ppermute | solution.py:26
  183.6 44.4 %collective-permute-start.24 = (bf16[96,1792]{1,0:T(8,128)(2,1)S(1)}, bf16[96,1792]{1,0:T(8,128)(2,1)S(1)}, u32[]{:S(2)}, u32[]{:S(2)}) collective-permute-start(bf16[96,1792]{1,0:T(8,128)(2,1)S(1)} %get-tuple-element.103), channel_id=1, source_target_pairs={{0,8},{1,9},{2,10},{3,11},{4,12},{5,13},{6,14},{7,15},{8,16},{9,17... | collective-permute-start | bytes 1032200 | tf_op jit(solution)/shard_map/ppermute | solution.py:26
  187.1 43.7 %collective-permute-start.27 = (bf16[96,1792]{1,0:T(8,128)(2,1)S(1)}, bf16[96,1792]{1,0:T(8,128)(2,1)S(1)}, u32[]{:S(2)}, u32[]{:S(2)}) collective-permute-start(bf16[96,1792]{1,0:T(8,128)(2,1)S(1)} %get-tuple-element.107), channel_id=1, source_target_pairs={{0,24},{1,25},{2,26},{3,27},{4,28},{5,29},{6,30},{7,31},{8,0},{9,1... | collective-permute-start | bytes 1032200 | tf_op jit(solution)/shard_map/ppermute | solution.py:26
  189.2 48.6 %collective-permute-start.28 = (bf16[96,1792]{1,0:T(8,128)(2,1)S(1)}, bf16[96,1792]{1,0:T(8,128)(2,1)S(1)}, u32[]{:S(2)}, u32[]{:S(2)}) collective-permute-start(bf16[96,1792]{1,0:T(8,128)(2,1)S(1)} %get-tuple-element.108), channel_id=1, source_target_pairs={{0,16},{1,17},{2,18},{3,19},{4,20},{5,21},{6,22},{7,23},{8,24},{9,... | collective-permute-start | bytes 1032200 | tf_op jit(solution)/shard_map/ppermute | solution.py:26
  191.1 51.6 %collective-permute-start.29 = (bf16[96,1792]{1,0:T(8,128)(2,1)S(1)}, bf16[96,1792]{1,0:T(8,128)(2,1)S(1)}, u32[]{:S(2)}, u32[]{:S(2)}) collective-permute-start(bf16[96,1792]{1,0:T(8,128)(2,1)S(1)} %get-tuple-element.109), channel_id=1, source_target_pairs={{0,8},{1,9},{2,10},{3,11},{4,12},{5,13},{6,14},{7,15},{8,16},{9,17... | collective-permute-start | bytes 1032200 | tf_op jit(solution)/shard_map/ppermute | solution.py:26
  (28 other events, 471.2 us)

commit v6 on v5

--- a/solution.py
+++ b/solution.py
@@ -70,7 +70,7 @@
 
 def hidden_kernel(count, lead, *refs):
     units, weights = refs[:count], refs[count : count + 10]
-    gate_o, gate_c, gate_x, gate_xc, up_o, up_c, up_xa, up_xca, up_xb, up_xcb = weights
+    gate_o, up_o, gate_x, gate_c, up_c, gate_xc, up_xa, up_xca, up_xb, up_xcb = weights
     out, near_gate, far_gate, near_up, far_up = refs[count + 10 :]
     step = pl.program_id(0)
 
@@ -216,7 +216,9 @@
     return jnp.where(found, weight.T[:, :, None], 0.0)
 
 
-def expert_rows(rows, picks, gates, latents, owners, requests, gate_proj, up_proj, down_proj):
+def expert_rows(
+    rows, picks, gates, latents, owners, requests, queries, gate_proj, up_proj, down_proj
+):
     n_ep = lax.axis_size("ep")
     split = FF_WIN // gate_proj.shape[1]
     planes = n_ep // split
@@ -238,44 +240,60 @@
         own_0, out_1, out_3, latents, owners, requests, down_proj
     )
     own_1, own_3, peer_0 = shift(out_1, split), shift(out_3, 3 * split), swap(own_0, YBIT)
-    keep = lax.dynamic_slice_in_dim(down_proj, 2 * upper * span, 2 * span, 1)
     send = lax.dynamic_slice_in_dim(down_proj, (2 - 2 * upper) * span, 2 * span, 1)
     down_y = swap(send, YBIT)
     outgoing = hand_over(latents, owners, requests)
     up_a, up_b = up_proj[:cut], up_proj[cut:]
 
-    own_1, own_3, peer_0, down_y, gate_x, up_a, out_2, gate_proj, up_proj = together(
-        own_1, own_3, peer_0, down_y, gate_x, up_a, out_2, gate_proj, up_proj
-    )
-    outgoing, keep, picks, gates, own_1 = together(outgoing, keep, picks, gates, own_1)
+    own_1, own_3, peer_0, down_y, gate_x, up_a, out_2, outgoing, down_proj, gate_proj = together(
+        own_1, own_3, peer_0, down_y, gate_x, up_a, out_2, outgoing, down_proj, gate_proj
+    )
     own_2, peer_1, peer_3 = shift(out_2, 2 * split), swap(own_1, YBIT), swap(own_3, YBIT)
-    up_xa, gate_xc = swap(up_a, XBIT), swap(gate_x, CORE)
-    gate_c, up_c = swap(gate_proj, CORE), swap(up_proj, CORE)
-
-    own_2, peer_1, peer_3, up_xa, gate_xc, gate_c, up_c, up_b = together(
-        own_2, peer_1, peer_3, up_xa, gate_xc, gate_c, up_c, up_b
-    )
-    keep, down_y, picks, gates, outgoing, own_2 = together(
-        keep, down_y, picks, gates, outgoing, own_2
-    )
-    peer_2, up_xb, up_xca = swap(own_2, YBIT), swap(up_b, XBIT), swap(up_xa, CORE)
-    keep_c, down_yc = swap(keep, CORE), swap(down_y, CORE)
+    up_xa = swap(up_a, XBIT)
+    gate_c = swap(gate_proj, CORE)
     incoming = lax.all_to_all(outgoing, "ep", split_axis=0, concat_axis=0, tiled=True)
-    info = swap(jnp.concatenate([picks.astype(jnp.float32), gates], axis=1), YBIT)
+    keep = lax.dynamic_slice_in_dim(down_proj, 2 * upper * span, 2 * span, 1)
     sides = [
         jnp.concatenate([part[:, at * span : (at + 1) * span] for part in (keep, down_y)], axis=0)
         for at in range(2)
     ]
-    up_xb, sides[0] = together(up_xb, sides[0])
-    up_xcb, side_0 = swap(up_xb, CORE), swap(sides[0], XBIT)
-
-    units = (own_0, own_1, own_2, own_3, peer_0, peer_1, peer_2, peer_3)
-    weights = (gate_proj, gate_c, gate_x, gate_xc, up_proj, up_c)
-    hidden = hidden_units(units, weights, (up_xa, up_xca), (up_xb, up_xcb), chunk)
-    other = swap(hidden, YBIT)
-    side_0, sides[1] = together(side_0, sides[1])
+    head = -(-slots // 32) * 16
+
+    own_2, peer_1, peer_3, up_xa, gate_c, up_b, sides[0], up_proj = together(
+        own_2, peer_1, peer_3, up_xa, gate_c, up_b, sides[0], up_proj
+    )
+    peer_2a, up_xb = swap(own_2[:head], YBIT), swap(up_b, XBIT)
+    up_c, gate_xc, up_xca = swap(up_proj, CORE), swap(gate_x, CORE), swap(up_xa, CORE)
+    away = own_2[head:]
+    peer_2a, up_xb, up_c, gate_xc, up_xca, away, sides[0] = together(
+        peer_2a, up_xb, up_c, gate_xc, up_xca, away, sides[0]
+    )
+    peer_2b, up_xcb, side_0 = swap(away, YBIT), swap(up_xb, CORE), swap(sides[0], XBIT)
+
+    units = (own_0, own_1, own_2, own_3, peer_0, peer_1, peer_2a, peer_2b, peer_3)
+    hidden = hidden_units(
+        units,
+        (gate_proj, up_proj, gate_x, gate_c, up_c, gate_xc),
+        (up_xa, up_xca),
+        (up_xb, up_xcb),
+        chunk,
+    )
+    hidden, side_0, keep, down_y, picks, gates = together(
+        hidden, side_0, keep, down_y, picks, gates
+    )
+    other, keep_c, down_yc = swap(hidden, YBIT), swap(keep, CORE), swap(down_y, CORE)
+    info = swap(jnp.concatenate([picks.astype(jnp.float32), gates], axis=1), YBIT)
+
+    own, peer = (keep, keep_c), (down_y, down_yc)
+    values = down_values(
+        hidden, other, own, (side_0, swap(side_0, CORE)), peer, planes, span // 2, 0
+    )
+    sides[1], *values = together(sides[1], *values)
     side_1 = swap(sides[1], XBIT)
-    side = ((side_0, swap(side_0, CORE)), (side_1, swap(side_1, CORE)))
+    side_1, info, picks, gates = together(side_1, info, picks, gates)
+    values_1 = down_values(
+        hidden, other, own, (side_1, swap(side_1, CORE)), peer, planes, span // 2, 2
+    )
 
     top = picks.shape[1]
     tables = [
@@ -290,18 +308,21 @@
     high = lax.reduce_precision(table, 8, 7)
     high, low = high.astype(jnp.bfloat16), (table - high).astype(jnp.bfloat16)
 
+    def returned(part):
+        return [part[0]] + [shift(part[k], n_ep - k * split) for k in range(1, planes)]
+
+    backs = [returned(values), returned(values_1)]
+    backs[1][0], incoming, queries, *backs[0] = together(
+        backs[1][0], incoming, queries, *backs[0]
+    )
     outs, others = [], []
-    for at in range(2):
-        values = down_values(
-            hidden, other, (keep, keep_c), side[at], (down_y, down_yc), planes, span // 2, 2 * at
-        )
-        back = [values[0]] + [shift(values[k], n_ep - k * split) for k in range(1, planes)]
+    for back in backs:
         mine, theirs = combine(high, low, back, span // 2)
         outs.append(mine)
         others.append(swap(theirs, YBIT))
     low_first = jnp.concatenate(outs + others, axis=1)
     high_first = jnp.concatenate(others + outs, axis=1)
-    return jnp.where(upper == 0, low_first, high_first), incoming, other
+    return jnp.where(upper == 0, low_first, high_first), incoming, queries
 
 
 def attend(query_part, cache_latents, cache_lens, handed, handed_mark):
@@ -372,19 +393,19 @@
 ):
     sections, count, width = moe_rows.shape
     top = routes.shape[2]
-    expert_out, incoming, other = expert_rows(
+    expert_out, incoming, queries = expert_rows(
         moe_rows.reshape(sections * count, width),
         routes.reshape(sections * count, top),
         route_gates.reshape(sections * count, top),
         prompt_latents,
         kv_owner[:, 0],
         kv_request,
+        queries,
         gate_proj,
         up_proj,
         down_proj,
     )
     expert_out = expert_out.reshape(moe_rows.shape)
-    queries, incoming, _ = together(queries, incoming, other)
     lat = prompt_latents.shape[1]
     handed = incoming[:, :, :lat].reshape(-1, lat)
     handed_mark = incoming[:, :, lat].reshape(-1).astype(jnp.float32)

time: 253 us -> 235 us (0.929)
  waiting for transfers between devices: 154 us -> 114 us
  local copies, waits for them, and re-layouts: 20 us -> 39.3 us
    ppermute x9, waiting for transfers between devices: 86.5 us -> 63.2 us  [shift(): lax.ppermute(value, 'ep', [(i, (i + step) % count) for i in range(count)])]
    ppermute x23 -> x24, waiting for transfers between devices: 67.2 us -> 50.7 us  [swap(): return lax.ppermute(value, 'ep', [(i, i ^ bit) for i in range(count)])]
    unnamed x40 -> x88, local copies, waits for them, and re-layouts: 7.61 us -> 21.1 us
    ppermute x23 -> x24, starting transfers between devices: 14.4 us -> 19.3 us  [swap(): return lax.ppermute(value, 'ep', [(i, i ^ bit) for i in range(count)])]
    all_to_all x1, starting transfers between devices: 9.19 us -> 4.95 us  [expert_rows(): lax.all_to_all(outgoing, 'ep', split_axis=0, concat_axis=0, tiled=True)]
    ppermute x9, starting transfers between devices: 15.5 us -> 12.7 us  [shift(): lax.ppermute(value, 'ep', [(i, (i + step) % count) for i in range(count)])]
  transfers between devices with their start and end apart: 33 -> 34, of which waited for: 14 -> 15; matrix products, arithmetic and copies ran while one was open for 11% -> 14% of each run, Pallas kernels for 9% -> 9%
where the time goes in v6:
time: 235 us; the launch traced here: 232 us
  waiting for transfers between devices  114 us (49%)
  local copies, waits for them, and re-layouts  39.3 us (17%)
  starting transfers between devices  36.9 us (16%)
  Pallas kernels  22.5 us (10%)
  other arithmetic  11.9 us (5%)
  matrix products  7.01 us (3%)
    ppermute x9, waiting for transfers between devices, shift(): lax.ppermute(value, 'ep', [(i, (i + step) % count) for i in range(count)])  63.2 us
    ppermute x24, waiting for transfers between devices, swap(): return lax.ppermute(value, 'ep', [(i, i ^ bit) for i in range(count)])  50.7 us
    unnamed x88, local copies, waits for them, and re-layouts  21.1 us
    ppermute x24, starting transfers between devices, swap(): return lax.ppermute(value, 'ep', [(i, i ^ bit) for i in range(count)])  19.3 us
    ppermute x9, starting transfers between devices, shift(): lax.ppermute(value, 'ep', [(i, (i + step) % count) for i in range(count)])  12.7 us
    pallas_call x1, Pallas kernels, hidden_units(): pl.pallas_call(partial(hidden_kernel, len(units), lead), grid=(width // c...  10.3 us
    pallas_call x2, Pallas kernels, down_values(): pl.pallas_call(down_kernel, grid=(width // chunk,), in_specs=[pl.BlockSpe...  5.9 us
    all_to_all x1, starting transfers between devices, expert_rows(): lax.all_to_all(outgoing, 'ep', split_axis=0, concat_axis=0, tiled=True)  4.95 us
  transfers between devices with their start and end apart: 34, of which 15 were waited for; matrix products, arithmetic and copies ran while one was open for 14% of the time, Pallas kernels for 9%

profile of v6, /device:TPU:16, one launch (start us, length us, event | category | flops | bytes accessed | tf_op | source)
XLA Modules:
  0.0 232.5 jit_solution(6751389352959082096)
XLA Ops:
  4.6 2.5 %shard_map.131 = (bf16[48,7168]{1,0:T(8,128)(2,1)S(1)}, bf16[48,7168]{1,0:T(8,128)(2,1)}, bf16[48,7168]{1,0:T(8,128)(2,1)S(1)}, bf16[48,7168]{1,0:T(8,128)(2,1)}) custom-call(bf16[192,64]{1,0:T(8,128)(2,1)S(1)} %fusion.18.chosen, bf16[64,7168]{1,0:T(8,128)(2,1)S(1)} %bitcast.41), custom_call_target="tpu_custom_call" | custom-call | flops 176160768 | bytes 3670016 | tf_op jit(solution)/shard_map/pallas_call | solution.py:53
  11.5 2.2 constant_dynamic-slice_fusion.3
  14.4 2.5 %slice.42 = bf16[5376,128]{1,0:T(8,128)(2,1)} slice(bf16[7168,128]{1,0:T(8,128)(2,1)} %refs_10_), slice={[0:5376], [0:128]} | slice | bytes 2752512 | tf_op jit(solution)/shard_map/slice | solution.py:246
  24.1 15.7 %collective-permute-done.refs_1_ = bf16[48,7168]{1,0:T(8,128)(2,1)S(1)} collective-permute-done((bf16[48,7168]{1,0:T(8,128)(2,1)}, bf16[48,7168]{1,0:T(8,128)(2,1)S(1)}, u32[]{:S(2)}, u32[]{:S(2)}) %collective-permute-start) | collective-permute-done | bytes 688160 | tf_op jit(solution)/shard_map/ppermute | solution.py:26
  39.8 6.2 %collective-permute-done.3.refs_4_ = bf16[128,3584]{1,0:T(8,128)(2,1)S(1)} collective-permute-done((bf16[128,3584]{1,0:T(8,128)(2,1)}, bf16[128,3584]{1,0:T(8,128)(2,1)S(1)}, u32[]{:S(2)}, u32[]{:S(2)}) %collective-permute-start.3) | collective-permute-done | bytes 917536 | tf_op jit(solution)/shard_map/ppermute | solution.py:21
  48.4 2.2 collective-permute-start.5
  56.4 23.4 %collective-permute-done.5.refs_2_ = bf16[48,7168]{1,0:T(8,128)(2,1)S(1)} collective-permute-done((bf16[48,7168]{1,0:T(8,128)(2,1)}, bf16[48,7168]{1,0:T(8,128)(2,1)S(1)}, u32[]{:S(2)}, u32[]{:S(2)}) %collective-permute-start.5) | collective-permute-done | bytes 688160 | tf_op jit(solution)/shard_map/ppermute | solution.py:26
  87.9 9.6 %collective-permute-done.10.refs_6_ = bf16[32,7168]{1,0:T(8,128)(2,1)S(1)} collective-permute-done((bf16[32,7168]{1,0:T(8,128)(2,1)}, bf16[32,7168]{1,0:T(8,128)(2,1)S(1)}, u32[]{:S(2)}, u32[]{:S(2)}) %collective-permute-start.10) | collective-permute-done | bytes 458784 | tf_op jit(solution)/shard_map/ppermute | solution.py:21
  102.6 2.6 %collective-permute-done.15.refs_7_ = bf16[16,7168]{1,0:T(8,128)(2,1)S(1)} collective-permute-done((bf16[16,7168]{1,0:T(8,128)(2,1)S(1)}, bf16[16,7168]{1,0:T(8,128)(2,1)S(1)}, u32[]{:S(2)}, u32[]{:S(2)}) %collective-permute-start.15) | collective-permute-done | bytes 229408 | tf_op jit(solution)/shard_map/ppermute | solution.py:21
  110.0 10.3 %shard_map.132.mine = bf16[384,512]{1,0:T(8,128)(2,1)S(1)} custom-call(bf16[48,7168]{1,0:T(8,128)(2,1)S(1)} %copy-done.18, bf16[48,7168]{1,0:T(8,128)(2,1)S(1)} %copy-done.20, bf16[48,7168]{1,0:T(8,128)(2,1)S(1)} %copy-done.11, bf16[48,7168]{1,0:T(8,128)(2,1)} %collective-permute-done.1.refs_3_, bf16[48,7168]{1,0:T(8,128)(2,1)} %collective-permute-done.2.refs_4_, ...), custom_call_target="tpu_custom_call" | custom-call | flops 5637144576 | bytes 20185088 | tf_op jit(solution)/shard_map/pallas_call | solution.py:107
  120.3 2.5 %collective-permute-done.17.refs_2_ = bf16[256,1792]{1,0:T(8,128)(2,1)S(1)} collective-permute-done((bf16[256,1792]{1,0:T(8,128)(2,1)}, bf16[256,1792]{1,0:T(8,128)(2,1)S(1)}, u32[]{:S(2)}, u32[]{:S(2)}) %collective-permute-start.17) | collective-permute-done | bytes 917536 | tf_op jit(solution)/shard_map/ppermute | solution.py:21
  125.3 9.5 %collective-permute-done.18.other = bf16[384,512]{1,0:T(8,128)(2,1)S(1)} collective-permute-done((bf16[384,512]{1,0:T(8,128)(2,1)S(1)}, bf16[384,512]{1,0:T(8,128)(2,1)S(1)}, u32[]{:S(2)}, u32[]{:S(2)}) %collective-permute-start.18) | collective-permute-done | bytes 393248 | tf_op jit(solution)/shard_map/ppermute | solution.py:21
  134.9 2.6 %shard_map.133 = (bf16[96,1792]{1,0:T(8,128)(2,1)S(1)}, bf16[96,1792]{1,0:T(8,128)(2,1)S(1)}, bf16[96,1792]{1,0:T(8,128)(2,1)S(1)}, bf16[96,1792]{1,0:T(8,128)(2,1)S(1)}) custom-call(bf16[384,512]{1,0:T(8,128)(2,1)S(1)} %shard_map.132.mine, bf16[384,512]{1,0:T(8,128)(2,1)S(1)} %collective-permute-done.18.other, ...), custom_call_target="tpu_custom_call" | custom-call | flops 1409286144 | bytes 5046272 | tf_op jit(solution)/shard_map/pallas_call | solution.py:149
  143.1 4.9 %all-to-all-start = ((bf16[32,8,640]{2,1,0:T(8,128)(2,1)}), bf16[32,8,640]{2,1,0:T(8,128)(2,1)}, u32[]{:S(2)}, u32[]{:S(2)}) async-start(bf16[32,8,640]{2,1,0:T(8,128)(2,1)} %maximum_maximum_fusion), calls=%async_computation | async-start | bytes 655360 | tf_op jit(solution)/shard_map/all_to_all | solution.py:254
  148.6 3.3 %collective-permute-start.26 = (bf16[96,1792]{1,0:T(8,128)(2,1)}, bf16[96,1792]{1,0:T(8,128)(2,1)}, u32[]{:S(2)}, u32[]{:S(2)}) collective-permute-start(bf16[96,1792]{1,0:T(8,128)(2,1)} %copy-done.29), channel_id=1, source_target_pairs={{0,16},{1,17},{2,18},{3,19},{4,20},{5,21},{6,22},{7,23},{8,24},{9,... | collective-permute-start | bytes 1032200 | tf_op jit(solution)/shard_map/ppermute | solution.py:26
  151.9 13.4 %collective-permute-done.22.refs_2_ = bf16[256,1792]{1,0:T(8,128)(2,1)} collective-permute-done((bf16[256,1792]{1,0:T(8,128)(2,1)}, bf16[256,1792]{1,0:T(8,128)(2,1)}, u32[]{:S(2)}, u32[]{:S(2)}) %collective-permute-start.22) | collective-permute-done | bytes 917536 | tf_op jit(solution)/shard_map/ppermute | solution.py:21
  173.2 3.4 %shard_map.134 = (bf16[96,1792]{1,0:T(8,128)(2,1)S(1)}, bf16[96,1792]{1,0:T(8,128)(2,1)S(1)}, bf16[96,1792]{1,0:T(8,128)(2,1)S(1)}, bf16[96,1792]{1,0:T(8,128)(2,1)S(1)}) custom-call(bf16[384,512]{1,0:T(8,128)(2,1)S(1)} %shard_map.132.mine, bf16[384,512]{1,0:T(8,128)(2,1)S(1)} %copy-done.6, bf16[128,3584]{1,0:T(8,128)(2,1)S(1)} %constant_dynamic-slice_fusion.1.refs_0_, ...), custom_call_target="tpu_custom_call" | custom-call | flops 1409286144 | bytes 5046272 | tf_op jit(solution)/shard_map/pallas_call | solution.py:149
  179.5 5.7 %collective-permute-done.26.refs_2_ = bf16[96,1792]{1,0:T(8,128)(2,1)} collective-permute-done((bf16[96,1792]{1,0:T(8,128)(2,1)}, bf16[96,1792]{1,0:T(8,128)(2,1)}, u32[]{:S(2)}, u32[]{:S(2)}) %collective-permute-start.26) | collective-permute-done | bytes 344096 | tf_op jit(solution)/shard_map/ppermute | solution.py:26
  188.9 2.5 %collective-permute-start.29 = (bf16[96,1792]{1,0:T(8,128)(2,1)}, bf16[96,1792]{1,0:T(8,128)(2,1)S(1)}, u32[]{:S(2)}, u32[]{:S(2)}) collective-permute-start(bf16[96,1792]{1,0:T(8,128)(2,1)} %copy-done.32), channel_id=1, source_target_pairs={{0,16},{1,17},{2,18},{3,19},{4,20},{5,21},{6,22},{7,23},{8,24},{9,... | collective-permute-start | bytes 1032200 | tf_op jit(solution)/shard_map/ppermute | solution.py:26
  195.3 2.7 %shard_map.135 = (bf16[64,1792]{1,0:T(8,128)(2,1)S(1)}, bf16[64,1792]{1,0:T(8,128)(2,1)}) custom-call(bf16[128,384]{1,0:T(8,128)(2,1)S(1)} %copy-done.8, bf16[128,384]{1,0:T(8,128)(2,1)S(1)} %get-tuple-element.154.low, bf16[96,1792]{1,0:T(8,128)(2,1)S(1)} %copy-done.13, bf16[96,1792]{1,0:T(8,128)(2,1)} %collective-permute-done.25.refs_1_, ...), custom_call_target="tpu_custom_call" | custom-call | flops 352321536 | bytes 1835008 | tf_op jit(solution)/shard_map/pallas_call | solution.py:181
  204.1 14.9 %collective-permute-done.29.refs_2_ = bf16[96,1792]{1,0:T(8,128)(2,1)S(1)} collective-permute-done((bf16[96,1792]{1,0:T(8,128)(2,1)}, bf16[96,1792]{1,0:T(8,128)(2,1)S(1)}, u32[]{:S(2)}, u32[]{:S(2)}) %collective-permute-start.29) | collective-permute-done | bytes 344096 | tf_op jit(solution)/shard_map/ppermute | solution.py:26
  219.0 2.6 %collective-permute-done.30.refs_3_ = bf16[96,1792]{1,0:T(8,128)(2,1)S(1)} collective-permute-done((bf16[96,1792]{1,0:T(8,128)(2,1)}, bf16[96,1792]{1,0:T(8,128)(2,1)S(1)}, u32[]{:S(2)}, u32[]{:S(2)}) %collective-permute-start.30) | collective-permute-done | bytes 344096 | tf_op jit(solution)/shard_map/ppermute | solution.py:26
  225.7 4.5 %collective-permute-done.32 = bf16[64,1792]{1,0:T(8,128)(2,1)S(1)} collective-permute-done((bf16[64,1792]{1,0:T(8,128)(2,1)S(1)}, bf16[64,1792]{1,0:T(8,128)(2,1)S(1)}, u32[]{:S(2)}, u32[]{:S(2)}) %collective-permute-start.32) | collective-permute-done | bytes 229408 | tf_op jit(solution)/shard_map/ppermute | solution.py:21
  230.3 2.2 maximum_select_fusion
  (192 shorter events, 79.6 us)
Async XLA Ops:
  0.7 45.3 %collective-permute-start.4 = (bf16[7168,128]{1,0:T(8,128)(2,1)}, bf16[7168,128]{1,0:T(8,128)(2,1)}, u32[]{:S(2)}, u32[]{:S(2)}) collective-permute-start(bf16[7168,128]{1,0:T(8,128)(2,1)} %refs_9_), channel_id=1, source_target_pairs={{0,2},{1,3},{2,0},{3,1},{4,6},{5,7},{6,4},{7,5},{8,10},{9,11},{10,... | collective-permute-start | bytes 5505032 | tf_op jit(solution)/shard_map/ppermute | solution.py:21
  8.0 31.8 %collective-permute-start = (bf16[48,7168]{1,0:T(8,128)(2,1)}, bf16[48,7168]{1,0:T(8,128)(2,1)S(1)}, u32[]{:S(2)}, u32[]{:S(2)}) collective-permute-start(bf16[48,7168]{1,0:T(8,128)(2,1)} %get-tuple-element.75), channel_id=1, source_target_pairs={{0,8},{1,9},{2,10},{3,11},{4,12},{5,13},{6,14},{7,15},{8,16},{9,17... | collective-permute-start | bytes 2064392 | tf_op jit(solution)/shard_map/ppermute | solution.py:26
  9.6 30.3 %collective-permute-start.1 = (bf16[48,7168]{1,0:T(8,128)(2,1)}, bf16[48,7168]{1,0:T(8,128)(2,1)}, u32[]{:S(2)}, u32[]{:S(2)}) collective-permute-start(bf16[48,7168]{1,0:T(8,128)(2,1)} %get-tuple-element.76), channel_id=1, source_target_pairs={{0,24},{1,25},{2,26},{3,27},{4,28},{5,29},{6,30},{7,31},{8,0},{9,1... | collective-permute-start | bytes 2064392 | tf_op jit(solution)/shard_map/ppermute | solution.py:26
  10.0 29.8 %collective-permute-start.2 = (bf16[48,7168]{1,0:T(8,128)(2,1)S(1)}, bf16[48,7168]{1,0:T(8,128)(2,1)}, u32[]{:S(2)}, u32[]{:S(2)}) collective-permute-start(bf16[48,7168]{1,0:T(8,128)(2,1)S(1)} %get-tuple-element.77.refs_0_), channel_id=1, source_target_pairs={{0,4},{1,5},{2,6},{3,7},{4,0},{5,1},{6,2},{7,3},{8,12},{9,13},{10,... | collective-permute-start | bytes 2064392 | tf_op jit(solution)/shard_map/ppermute | solution.py:21
  13.7 32.3 %collective-permute-start.3 = (bf16[128,3584]{1,0:T(8,128)(2,1)}, bf16[128,3584]{1,0:T(8,128)(2,1)S(1)}, u32[]{:S(2)}, u32[]{:S(2)}) collective-permute-start(bf16[128,3584]{1,0:T(8,128)(2,1)} %constant_dynamic-slice_fusion.3), channel_id=1, source_target_pairs={{0,4},{1,5},{2,6},{3,7},{4,0},{5,1},{6,2},{7,3},{8,12},{9,13},{10,... | collective-permute-start | bytes 2752520 | tf_op jit(solution)/shard_map/ppermute | solution.py:21
  46.0 37.5 %collective-permute-start.9 = (bf16[7168,128]{1,0:T(8,128)(2,1)}, bf16[7168,128]{1,0:T(8,128)(2,1)}, u32[]{:S(2)}, u32[]{:S(2)}) collective-permute-start(bf16[7168,128]{1,0:T(8,128)(2,1)} %refs_9_), channel_id=1, source_target_pairs={{0,1},{1,0},{2,3},{3,2},{4,5},{5,4},{6,7},{7,6},{8,9},{9,8},{10,11... | collective-permute-start | bytes 5505032 | tf_op jit(solution)/shard_map/ppermute | solution.py:21
  46.0 37.5 %collective-permute-start.8 = (bf16[5376,128]{1,0:T(8,128)(2,1)}, bf16[5376,128]{1,0:T(8,128)(2,1)}, u32[]{:S(2)}, u32[]{:S(2)}) collective-permute-start(bf16[5376,128]{1,0:T(8,128)(2,1)} %slice.42), channel_id=1, source_target_pairs={{0,2},{1,3},{2,0},{3,1},{4,6},{5,7},{6,4},{7,5},{8,10},{9,11},{10,... | collective-permute-start | bytes 4128776 | tf_op jit(solution)/shard_map/ppermute | solution.py:21
  48.4 31.5 %collective-permute-start.5 = (bf16[48,7168]{1,0:T(8,128)(2,1)}, bf16[48,7168]{1,0:T(8,128)(2,1)S(1)}, u32[]{:S(2)}, u32[]{:S(2)}) collective-permute-start(bf16[48,7168]{1,0:T(8,128)(2,1)} %copy-done.21), channel_id=1, source_target_pairs={{0,16},{1,17},{2,18},{3,19},{4,20},{5,21},{6,22},{7,23},{8,24},{9,... | collective-permute-start | bytes 2064392 | tf_op jit(solution)/shard_map/ppermute | solution.py:26
  50.6 29.4 %collective-permute-start.6 = (bf16[48,7168]{1,0:T(8,128)(2,1)S(1)}, bf16[48,7168]{1,0:T(8,128)(2,1)S(1)}, u32[]{:S(2)}, u32[]{:S(2)}) collective-permute-start(bf16[48,7168]{1,0:T(8,128)(2,1)S(1)} %collective-permute-done.refs_1_), channel_id=1, source_target_pairs={{0,4},{1,5},{2,6},{3,7},{4,0},{5,1},{6,2},{7,3},{8,12},{9,13},{10,... | collective-permute-start | bytes 2064392 | tf_op jit(solution)/shard_map/ppermute | solution.py:21
  52.1 30.5 %collective-permute-start.7 = (bf16[48,7168]{1,0:T(8,128)(2,1)}, bf16[48,7168]{1,0:T(8,128)(2,1)S(1)}, u32[]{:S(2)}, u32[]{:S(2)}) collective-permute-start(bf16[48,7168]{1,0:T(8,128)(2,1)} %collective-permute-done.1.refs_3_), channel_id=1, source_target_pairs={{0,4},{1,5},{2,6},{3,7},{4,0},{5,1},{6,2},{7,3},{8,12},{9,13},{10,... | collective-permute-start | bytes 2064392 | tf_op jit(solution)/shard_map/ppermute | solution.py:21
  83.5 15.4 %collective-permute-start.12 = (bf16[7168,128]{1,0:T(8,128)(2,1)}, bf16[7168,128]{1,0:T(8,128)(2,1)}, u32[]{:S(2)}, u32[]{:S(2)}) collective-permute-start(bf16[7168,128]{1,0:T(8,128)(2,1)} %refs_10_), channel_id=1, source_target_pairs={{0,1},{1,0},{2,3},{3,2},{4,5},{5,4},{6,7},{7,6},{8,9},{9,8},{10,11... | collective-permute-start | bytes 5505032 | tf_op jit(solution)/shard_map/ppermute | solution.py:21
  83.5 15.3 %collective-permute-start.14 = (bf16[5376,128]{1,0:T(8,128)(2,1)}, bf16[5376,128]{1,0:T(8,128)(2,1)}, u32[]{:S(2)}, u32[]{:S(2)}) collective-permute-start(bf16[5376,128]{1,0:T(8,128)(2,1)} %collective-permute-done.8.refs_15_), channel_id=1, source_target_pairs={{0,1},{1,0},{2,3},{3,2},{4,5},{5,4},{6,7},{7,6},{8,9},{9,8},{10,11... | collective-permute-start | bytes 4128776 | tf_op jit(solution)/shard_map/ppermute | solution.py:21
  84.8 12.7 %collective-permute-start.10 = (bf16[32,7168]{1,0:T(8,128)(2,1)}, bf16[32,7168]{1,0:T(8,128)(2,1)S(1)}, u32[]{:S(2)}, u32[]{:S(2)}) collective-permute-start(bf16[32,7168]{1,0:T(8,128)(2,1)} %slice.48), channel_id=1, source_target_pairs={{0,4},{1,5},{2,6},{3,7},{4,0},{5,1},{6,2},{7,3},{8,12},{9,13},{10,... | collective-permute-start | bytes 1376264 | tf_op jit(solution)/shard_map/ppermute | solution.py:21
  86.3 12.5 %collective-permute-start.11 = (bf16[1792,128]{1,0:T(8,128)(2,1)}, bf16[1792,128]{1,0:T(8,128)(2,1)}, u32[]{:S(2)}, u32[]{:S(2)}) collective-permute-start(bf16[1792,128]{1,0:T(8,128)(2,1)} %slice.45), channel_id=1, source_target_pairs={{0,2},{1,3},{2,0},{3,1},{4,6},{5,7},{6,4},{7,5},{8,10},{9,11},{10,... | collective-permute-start | bytes 1376264 | tf_op jit(solution)/shard_map/ppermute | solution.py:21
  99.8 23.0 %collective-permute-start.17 = (bf16[256,1792]{1,0:T(8,128)(2,1)}, bf16[256,1792]{1,0:T(8,128)(2,1)S(1)}, u32[]{:S(2)}, u32[]{:S(2)}) collective-permute-start(bf16[256,1792]{1,0:T(8,128)(2,1)} %pad_maximum_fusion.1), channel_id=1, source_target_pairs={{0,2},{1,3},{2,0},{3,1},{4,6},{5,7},{6,4},{7,5},{8,10},{9,11},{10,... | collective-permute-start | bytes 2752520 | tf_op jit(solution)/shard_map/ppermute | solution.py:21
  140.4 24.9 %collective-permute-start.22 = (bf16[256,1792]{1,0:T(8,128)(2,1)}, bf16[256,1792]{1,0:T(8,128)(2,1)}, u32[]{:S(2)}, u32[]{:S(2)}) collective-permute-start(bf16[256,1792]{1,0:T(8,128)(2,1)} %pad_maximum_fusion), channel_id=1, source_target_pairs={{0,2},{1,3},{2,0},{3,1},{4,6},{5,7},{6,4},{7,5},{8,10},{9,11},{10,... | collective-permute-start | bytes 2752520 | tf_op jit(solution)/shard_map/ppermute | solution.py:21
  143.1 36.4 %all-to-all-start = ((bf16[32,8,640]{2,1,0:T(8,128)(2,1)}), bf16[32,8,640]{2,1,0:T(8,128)(2,1)}, u32[]{:S(2)}, u32[]{:S(2)}) async-start(bf16[32,8,640]{2,1,0:T(8,128)(2,1)} %maximum_maximum_fusion), calls=%async_computation | async-start | bytes 655360 | tf_op jit(solution)/shard_map/all_to_all | solution.py:254
  148.0 31.5 %collective-permute-start.25 = (bf16[96,1792]{1,0:T(8,128)(2,1)}, bf16[96,1792]{1,0:T(8,128)(2,1)}, u32[]{:S(2)}, u32[]{:S(2)}) collective-permute-start(bf16[96,1792]{1,0:T(8,128)(2,1)} %copy-done.30), channel_id=1, source_target_pairs={{0,24},{1,25},{2,26},{3,27},{4,28},{5,29},{6,30},{7,31},{8,0},{9,1... | collective-permute-start | bytes 1032200 | tf_op jit(solution)/shard_map/ppermute | solution.py:26
  148.6 36.6 %collective-permute-start.26 = (bf16[96,1792]{1,0:T(8,128)(2,1)}, bf16[96,1792]{1,0:T(8,128)(2,1)}, u32[]{:S(2)}, u32[]{:S(2)}) collective-permute-start(bf16[96,1792]{1,0:T(8,128)(2,1)} %copy-done.29), channel_id=1, source_target_pairs={{0,16},{1,17},{2,18},{3,19},{4,20},{5,21},{6,22},{7,23},{8,24},{9,... | collective-permute-start | bytes 1032200 | tf_op jit(solution)/shard_map/ppermute | solution.py:26
  151.9 34.2 %collective-permute-start.27 = (bf16[96,1792]{1,0:T(8,128)(2,1)}, bf16[96,1792]{1,0:T(8,128)(2,1)}, u32[]{:S(2)}, u32[]{:S(2)}) collective-permute-start(bf16[96,1792]{1,0:T(8,128)(2,1)} %copy-done.28), channel_id=1, source_target_pairs={{0,8},{1,9},{2,10},{3,11},{4,12},{5,13},{6,14},{7,15},{8,16},{9,17... | collective-permute-start | bytes 1032200 | tf_op jit(solution)/shard_map/ppermute | solution.py:26
  188.9 15.2 %collective-permute-start.28 = (bf16[96,1792]{1,0:T(8,128)(2,1)}, bf16[96,1792]{1,0:T(8,128)(2,1)S(1)}, u32[]{:S(2)}, u32[]{:S(2)}) collective-permute-start(bf16[96,1792]{1,0:T(8,128)(2,1)} %copy-done.33), channel_id=1, source_target_pairs={{0,24},{1,25},{2,26},{3,27},{4,28},{5,29},{6,30},{7,31},{8,0},{9,1... | collective-permute-start | bytes 1032200 | tf_op jit(solution)/shard_map/ppermute | solution.py:26
  188.9 30.1 %collective-permute-start.29 = (bf16[96,1792]{1,0:T(8,128)(2,1)}, bf16[96,1792]{1,0:T(8,128)(2,1)S(1)}, u32[]{:S(2)}, u32[]{:S(2)}) collective-permute-start(bf16[96,1792]{1,0:T(8,128)(2,1)} %copy-done.32), channel_id=1, source_target_pairs={{0,16},{1,17},{2,18},{3,19},{4,20},{5,21},{6,22},{7,23},{8,24},{9,... | collective-permute-start | bytes 1032200 | tf_op jit(solution)/shard_map/ppermute | solution.py:26
  191.4 30.2 %collective-permute-start.30 = (bf16[96,1792]{1,0:T(8,128)(2,1)}, bf16[96,1792]{1,0:T(8,128)(2,1)S(1)}, u32[]{:S(2)}, u32[]{:S(2)}) collective-permute-start(bf16[96,1792]{1,0:T(8,128)(2,1)} %copy-done.31), channel_id=1, source_target_pairs={{0,8},{1,9},{2,10},{3,11},{4,12},{5,13},{6,14},{7,15},{8,16},{9,17... | collective-permute-start | bytes 1032200 | tf_op jit(solution)/shard_map/ppermute | solution.py:26
  197.9 27.8 %collective-permute-start.31 = (bf16[64,1792]{1,0:T(8,128)(2,1)}, bf16[64,1792]{1,0:T(8,128)(2,1)}, u32[]{:S(2)}, u32[]{:S(2)}) collective-permute-start(bf16[64,1792]{1,0:T(8,128)(2,1)} %get-tuple-element.138), channel_id=1, source_target_pairs={{0,4},{1,5},{2,6},{3,7},{4,0},{5,1},{6,2},{7,3},{8,12},{9,13},{10,... | collective-permute-start | bytes 688136 | tf_op jit(solution)/shard_map/ppermute | solution.py:21
  (53 other events, 567.3 us)

commit v7 on v5

v7 whole, which is shorter than its diff:
```python
from functools import partial

import jax
import jax.numpy as jnp
from jax import lax
from jax.experimental import pallas as pl
from jax.experimental.pallas import tpu as pltpu
from jax.sharding import PartitionSpec as P

VDIM = 512
FF_WIN = 1024
SLOT_ROWS = 8
CORE, XBIT, YBIT = 1, 2, 4
VMEM_BYTES = 14 * 1024 * 1024


score_scale = 0.07216878364870323


def swap(value, bit):
    count = lax.axis_size("ep")
    return lax.ppermute(value, "ep", [(i, i ^ bit) for i in range(count)])


def shift(value, step):
    count = lax.axis_size("ep")
    return lax.ppermute(value, "ep", [(i, (i + step) % count) for i in range(count)])


def together(*values):
    return lax.optimization_barrier(values)


def pair_dot(rows, left, right):
    both = jnp.concatenate([left[...], right[...]], axis=1)
    return jnp.dot(rows, both, preferred_element_type=jnp.float32)


def gated(gate, up):
    return (gate / (1.0 + jnp.exp(-gate)) * up).astype(jnp.bfloat16)


def tag_kernel(experts, rows, picks, gates, out):
    width = rows.shape[1]
    count = rows.shape[0]
    lane = lax.broadcasted_iota(jnp.int32, (count, 128), 1)
    weight = jnp.zeros((count, 128), jnp.float32)
    for at in range(picks.shape[1]):
        hit = picks[:, at : at + 1] == lane % experts
        weight = weight + jnp.where(hit, gates[:, at : at + 1], 0.0)
    high = weight.astype(jnp.bfloat16).astype(jnp.float32)
    middle = (weight - high).astype(jnp.bfloat16).astype(jnp.float32)
    low = weight - high - middle
    part = lane // experts
    tag = jnp.where(part == 0, high, jnp.where(part == 1, middle, low))
    tag = jnp.where(part < 3, tag, 0.0)
    out[:, :width] = rows[...]
    out[:, width:] = tag.astype(jnp.bfloat16)


def tagged(rows, picks, gates, experts):
    count, width = rows.shape
    return pl.pallas_call(
        partial(tag_kernel, experts),
        out_shape=jax.ShapeDtypeStruct((count, width + 128), jnp.bfloat16),
        compiler_params=pltpu.CompilerParams(vmem_limit_bytes=VMEM_BYTES),
        cost_estimate=pl.CostEstimate(
            flops=0, bytes_accessed=4 * count * width, transcendentals=0
        ),
    )(rows, picks, gates)


def hidden_kernel(count, lead, *refs):
    units, weights = refs[:count], refs[count : count + 10]
    gate_o, gate_c, gate_x, gate_xc, up_o, up_c, up_xa, up_xca, up_xb, up_xcb = weights
    out, near_gate, far_gate, near_up, far_up = refs[count + 10 :]
    step = pl.program_id(0)

    @pl.when(step == 0)
    def _():
        for total in (near_gate, far_gate, near_up, far_up):
            total[...] = jnp.zeros_like(total)

    rows = jnp.concatenate([unit[...] for unit in units], axis=0)
    near_gate[...] += pair_dot(rows, gate_o, gate_c)
    near_up[...] += pair_dot(rows, up_o, up_c)
    far_gate[...] += pair_dot(rows, gate_x, gate_xc)

    @pl.when(step < lead)
    def _():
        far_up[...] += pair_dot(rows, up_xa, up_xca)

    @pl.when(step >= lead)
    def _():
        far_up[...] += pair_dot(rows, up_xb, up_xcb)

    @pl.when(step == pl.num_programs(0) - 1)
    def _():
        two = near_up.shape[1]
        out[:, :two] = gated(near_gate[...], near_up[...])
        out[:, two:] = gated(far_gate[...], far_up[...])


def hidden_units(units, weights, leads, rests, chunk):
    width, wide = weights[0].shape
    lead = leads[0].shape[0] // chunk
    count = sum(unit.shape[0] for unit in units)
    return pl.pallas_call(
        partial(hidden_kernel, len(units), lead),
        grid=(width // chunk,),
        in_specs=[pl.BlockSpec((unit.shape[0], chunk), lambda k: (0, k)) for unit in units]
        + [pl.BlockSpec((chunk, wide), lambda k: (k, 0)) for _ in weights]
        + [pl.BlockSpec((chunk, wide), lambda k: (jnp.minimum(k, lead - 1), 0)) for _ in leads]
        + [pl.BlockSpec((chunk, wide), lambda k: (jnp.maximum(k - lead, 0), 0)) for _ in rests],
        out_specs=pl.BlockSpec((count, 4 * wide), lambda k: (0, 0)),
        out_shape=jax.ShapeDtypeStruct((count, 4 * wide), jnp.bfloat16),
        scratch_shapes=[pltpu.VMEM((count, 2 * wide), jnp.float32)] * 4,
        compiler_params=pltpu.CompilerParams(vmem_limit_bytes=VMEM_BYTES),
        cost_estimate=pl.CostEstimate(
            flops=2 * count * width * wide * 8,
            bytes_accessed=2 * width * (count + wide * 8),
            transcendentals=0,
        ),
    )(*units, *weights, *leads, *rests)


def down_kernel(pairs, tags, *refs):
    chosen, metas, (own, own_c, side, side_c), outs = (
        refs[0],
        refs[1 : 1 + tags],
        refs[1 + tags + 2 * pairs : 5 + tags + 2 * pairs],
        refs[5 + tags + 2 * pairs :],
    )
    hiddens = refs[1 + tags : 1 + tags + 2 * pairs]
    deep = own.shape[0] // 2
    parts = (own, own_c, side, side_c)
    table = jnp.concatenate(
        [part[:deep, :] for part in parts] + [part[deep:, :] for part in parts], axis=0
    )
    meta = jnp.concatenate([part[...] for part in metas], axis=0).astype(jnp.float32)
    weight = jnp.sum(meta * chosen[...], axis=1, keepdims=True)
    rows = outs[0].shape[0] // 2
    first = 0
    for pair in range(pairs):
        mine, other = hiddens[2 * pair], hiddens[2 * pair + 1]
        half = mine.shape[0] // 2
        joined = jnp.concatenate(
            [
                jnp.concatenate([mine[:half, :], other[half:, :]], axis=1),
                jnp.concatenate([mine[half:, :], other[:half, :]], axis=1),
            ],
            axis=0,
        )
        value = jnp.dot(joined, table, preferred_element_type=jnp.float32)
        base = 2 * first * rows
        value = value * weight[base : base + 2 * half]
        units = half // rows
        for at in range(units):
            out = outs[first + at]
            out[:rows, :] = value[at * rows : (at + 1) * rows].astype(out.dtype)
            out[rows:, :] = value[half + at * rows : half + (at + 1) * rows].astype(out.dtype)
        first += units


def down_values(chosen, metas, hiddens, tables, kinds, chunk):
    rows = max(meta.shape[0] for meta in metas)
    width = tables[0].shape[1]
    at_tag = metas[0].shape[1] // 128 - 1
    count = rows * 2 * len(kinds)
    return pl.pallas_call(
        partial(down_kernel, len(hiddens) // 2, len(metas)),
        grid=(width // chunk,),
        in_specs=[pl.BlockSpec(chosen.shape, lambda k: (0, 0))]
        + [pl.BlockSpec((meta.shape[0], 128), lambda k: (0, at_tag)) for meta in metas]
        + [pl.BlockSpec(hidden.shape, lambda k: (0, 0)) for hidden in hiddens]
        + [pl.BlockSpec((table.shape[0], chunk), lambda k: (0, k)) for table in tables],
        out_specs=[pl.BlockSpec((2 * rows, chunk), lambda k: (0, k)) for _ in kinds],
        out_shape=[jax.ShapeDtypeStruct((2 * rows, width), kind) for kind in kinds],
        compiler_params=pltpu.CompilerParams(vmem_limit_bytes=VMEM_BYTES),
        cost_estimate=pl.CostEstimate(
            flops=2 * count * 4 * tables[0].shape[0] * width,
            bytes_accessed=8 * tables[0].shape[0] * width + 4 * count * width,
            transcendentals=0,
        ),
    )(chosen, *metas, *hiddens, *tables)


def expert_rows(
    rows, picks, gates, latents, owners, requests, queries, gate_proj, up_proj, down_proj
):
    n_ep = lax.axis_size("ep")
    split = FF_WIN // gate_proj.shape[1]
    planes = n_ep // split
    count, width = rows.shape
    here = lax.axis_index("ep")
    upper = here // YBIT % 2
    span = width // 4
    half = count // 2

    chunk = width // 7
    cut = 2 * chunk
    gate_x, up_xa = swap(gate_proj, XBIT), swap(up_proj[:cut], XBIT)
    rows = tagged(rows, picks, gates, planes)
    keep = lax.dynamic_slice_in_dim(down_proj, 2 * upper * span, 2 * span, 1)
    send = lax.dynamic_slice_in_dim(down_proj, (2 - 2 * upper) * span, 2 * span, 1)
    unit_1, peer_0 = shift(rows, split), swap(rows, YBIT)
    down_y0 = swap(send[:, :span], YBIT)
    outgoing = hand_over(latents, owners, requests)
    unit_1, peer_0, down_y0, gate_proj, outgoing = together(
        unit_1, peer_0, down_y0, gate_proj, outgoing
    )
    unit_2, peer_1 = shift(unit_1, split), swap(unit_1, YBIT)
    gate_c = swap(gate_proj, CORE)
    own_0 = jnp.concatenate([keep[:, :span], down_y0], axis=0)
    up_b = up_proj[cut:]
    unit_2, peer_1, gate_c, gate_x, up_xa, up_proj, up_b, own_0, send = together(
        unit_2, peer_1, gate_c, gate_x, up_xa, up_proj, up_b, own_0, send
    )
    unit_3, peer_2 = shift(unit_2, split), swap(unit_2, YBIT)
    up_xb, up_c, gate_xc = swap(up_b, XBIT), swap(up_proj, CORE), swap(gate_x, CORE)
    incoming = lax.all_to_all(outgoing, "ep", split_axis=0, concat_axis=0, tiled=True)
    unit_3, peer_2, up_xb, up_c, gate_xc, up_xa, own_0 = together(
        unit_3, peer_2, up_xb, up_c, gate_xc, up_xa, own_0
    )
    up_xca, up_xcb, side_0 = swap(up_xa, CORE), swap(up_xb, CORE), swap(own_0, XBIT)
    last = (shift(peer_2[:half], split), swap(unit_3[half:], YBIT))
    up_xca, up_xcb, *last = together(up_xca, up_xcb, *last)

    weights = (gate_proj, gate_c, gate_x, gate_xc, up_proj, up_c)
    parts = ((up_xa, up_xca), (up_xb, up_xcb))
    hidden_1 = hidden_units((unit_1, peer_1), weights, *parts, chunk)
    hidden_1, send = together(hidden_1, send)
    other_1, down_y1, side_0 = together(
        swap(hidden_1, YBIT), swap(send[:, span:], YBIT), side_0
    )
    own_0c = swap(own_0, CORE)
    hidden_2 = hidden_units(
        (unit_2, unit_3, rows, peer_2, *last, peer_0), weights, *parts, chunk
    )
    other_2 = swap(hidden_2, YBIT)
    own_1 = jnp.concatenate([keep[:, span:], down_y1], axis=0)

    lane = jnp.arange(128, dtype=jnp.int32)
    chosen = ((lane % planes == here // split) & (lane < 3 * planes)).astype(jnp.float32)[None, :]
    metas_1 = (unit_1, peer_1)
    metas_2 = (unit_2, unit_3, rows, peer_2, *last, peer_0)
    wide, thin = jnp.float32, jnp.bfloat16
    tables = (own_0, own_0c, side_0, swap(side_0, CORE))
    value_1 = down_values(chosen, metas_1, (hidden_1, other_1), tables, (thin,), span // 2)
    values_2 = down_values(
        chosen, metas_2, (hidden_2, other_2), tables, (wide,) * 3, span // 2
    )
    side_0, own_1 = together(side_0, own_1)
    side_1, own_1c = swap(own_1, XBIT), swap(own_1, CORE)
    tables = (own_1, own_1c, side_1, swap(side_1, CORE))
    values = down_values(
        chosen,
        metas_1 + metas_2,
        (hidden_1, other_1, hidden_2, other_2),
        tables,
        (thin, wide, wide, wide),
        span // 2,
    )
    outs, others = [], []
    for at, parts in enumerate(((*value_1, *values_2), values)):
        total = parts[0]
        for step in range(1, planes):
            total = (shift(total, split).astype(jnp.float32) + parts[step]).astype(jnp.bfloat16)
            if at == 0 and step == 1:
                total, incoming, queries = together(total, incoming, queries)
        outs.append(total[:count])
        others.append(swap(total[count:], YBIT))
    low_first = jnp.concatenate(outs + others, axis=1)
    high_first = jnp.concatenate(others + outs, axis=1)
    return jnp.where(upper == 0, low_first, high_first), incoming, queries


def attend(query_part, cache_latents, cache_lens, handed, handed_mark):
    requests = query_part.shape[0]
    cache_scores = (
        jnp.einsum("qhl,qcl->qhc", query_part, cache_latents, preferred_element_type=jnp.float32)
        * score_scale
    )
    hand_scores = (
        jnp.einsum("qhl,rl->qhr", query_part, handed, preferred_element_type=jnp.float32)
        * score_scale
    )
    cache_mask = (
        jnp.arange(cache_latents.shape[1], dtype=jnp.int32)[None, :] < cache_lens[:, None]
    )[:, None, :]
    marks = jnp.arange(1, requests + 1, dtype=jnp.int32).astype(jnp.float32)
    hand_mask = (handed_mark[None, :] == marks[:, None])[:, None, :]
    cache_scores = jnp.where(cache_mask, cache_scores, -jnp.inf)
    hand_scores = jnp.where(hand_mask, hand_scores, -jnp.inf)
    top = jnp.maximum(jnp.max(cache_scores, axis=2), jnp.max(hand_scores, axis=2))[:, :, None]
    cache_expo = jnp.exp(cache_scores - top)
    hand_expo = jnp.exp(hand_scores - top)
    denom = (jnp.sum(cache_expo, axis=2) + jnp.sum(hand_expo, axis=2))[:, :, None]
    cache_prob = (cache_expo / denom).astype(jnp.bfloat16)
    hand_prob = (hand_expo / denom).astype(jnp.bfloat16)
    result = jnp.einsum(
        "qhc,qcv->qhv", cache_prob, cache_latents[:, :, :VDIM], preferred_element_type=jnp.float32
    )
    result = result + jnp.einsum(
        "qhr,rv->qhv", hand_prob, handed[:, :VDIM], preferred_element_type=jnp.float32
    )
    return result.astype(jnp.bfloat16)


def hand_over(prompt_latents, owners, requests):
    n_ep = lax.axis_size("ep")
    stretch, lat = prompt_latents.shape
    cap = 2 * stretch // n_ep
    places_at = jnp.arange(stretch, dtype=jnp.int32)
    earlier = (owners[:, None] == owners[None, :]) & (places_at[None, :] < places_at[:, None])
    target = owners * cap + jnp.sum(earlier.astype(jnp.int32), axis=1)
    slots = jnp.arange(n_ep * cap, dtype=jnp.int32)
    chosen = slots[:, None] == target[None, :]
    packed = jnp.dot(
        chosen.astype(jnp.bfloat16), prompt_latents, preferred_element_type=jnp.float32
    ).astype(jnp.bfloat16)
    mark = jnp.sum(jnp.where(chosen, requests[None, :] + 1, 0), axis=1).astype(jnp.bfloat16)
    fill = -(lat + 1) % 128
    outgoing = jnp.concatenate(
        [packed, mark[:, None], jnp.zeros((n_ep * cap, fill), jnp.bfloat16)], axis=1
    )
    return outgoing.reshape(n_ep, cap, lat + 1 + fill)


def on_device(
    moe_rows,
    routes,
    route_gates,
    gate_proj,
    up_proj,
    down_proj,
    queries,
    cache_latents,
    cache_lens,
    prompt_latents,
    kv_owner,
    kv_request,
):
    sections, count, width = moe_rows.shape
    top = routes.shape[2]
    expert_out, incoming, queries = expert_rows(
        moe_rows.reshape(sections * count, width),
        routes.reshape(sections * count, top),
        route_gates.reshape(sections * count, top),
        prompt_latents,
        kv_owner[:, 0],
        kv_request,
        queries,
        gate_proj,
        up_proj,
        down_proj,
    )
    expert_out = expert_out.reshape(moe_rows.shape)
    lat = prompt_latents.shape[1]
    handed = incoming[:, :, :lat].reshape(-1, lat)
    handed_mark = incoming[:, :, lat].reshape(-1).astype(jnp.float32)
    attended = attend(queries, cache_latents, cache_lens, handed, handed_mark)
    return (expert_out, attended)


def solution(mesh):
    placed = (
        P("section", ("groups", "ep"), None),
        P("section", ("groups", "ep"), None),
        P("section", ("groups", "ep"), None),
        P(None, "ep"),
        P(None, "ep"),
        P("ep", None),
        P(("groups", "ep"), None, None),
        P(("groups", "ep"), None, None),
        P(("groups", "ep")),
        P(("groups", "ep"), None),
        P(("groups", "ep"), None),
        P(("groups", "ep")),
    )
    return jax.shard_map(
        on_device,
        mesh=mesh,
        in_specs=placed,
        out_specs=(P("section", ("groups", "ep"), None), P(("groups", "ep"), None, None)),
        check_vma=False,
    )
```

time: 253 us -> 265 us (1.047)
  the two profiles are of different devices: /device:TPU:16 before, /device:TPU:0 now
where the time goes in v7:
time: 265 us; the launch traced here: 264 us
  waiting for transfers between devices  133 us (50%)
  local copies, waits for them, and re-layouts  41.2 us (16%)
  starting transfers between devices  34.8 us (13%)
  Pallas kernels  32.1 us (12%)
  other arithmetic  13 us (5%)
  matrix products  8.67 us (3%)
    ppermute x10, waiting for transfers between devices, shift(): lax.ppermute(value, 'ep', [(i, (i + step) % count) for i in range(count)])  73.7 us
    ppermute x24, waiting for transfers between devices, swap(): return lax.ppermute(value, 'ep', [(i, i ^ bit) for i in range(count)])  56.8 us
    unnamed x104, local copies, waits for them, and re-layouts  30.5 us
    ppermute x24, starting transfers between devices, swap(): return lax.ppermute(value, 'ep', [(i, i ^ bit) for i in range(count)])  21.9 us
    pallas_call x2, Pallas kernels, hidden_units(): pl.pallas_call(partial(hidden_kernel, len(units), lead), grid=(width // c...  20.3 us
    pallas_call x3, Pallas kernels, down_values(): pl.pallas_call(partial(down_kernel, len(hiddens) // 2, len(metas)), grid=...  11.7 us
    ppermute x10, starting transfers between devices, shift(): lax.ppermute(value, 'ep', [(i, (i + step) % count) for i in range(count)])  9.64 us
  transfers between devices with their start and end apart: 35, of which 16 were waited for; matrix products, arithmetic and copies ran while one was open for 11% of the time, Pallas kernels for 12%

profile of v7, /device:TPU:0, one launch (start us, length us, event | category | flops | bytes accessed | tf_op | source)
XLA Modules:
  0.0 264.0 jit_solution(5854880585923194613)
XLA Ops:
  3.6 3.1 %collective-permute-start = (bf16[64,7296]{1,0:T(8,128)(2,1)S(1)}, bf16[64,7296]{1,0:T(8,128)(2,1)S(1)}, u32[]{:S(2)}, u32[]{:S(2)}) collective-permute-start(bf16[64,7296]{1,0:T(8,128)(2,1)S(1)} %shard_map.131.refs_2_.refs_3_.refs_5_), channel_id=1, source_target_pairs={{0,8},{1,9},{2,10},{3,11},{4,12},{5,13},{6,14},{7,15},{8,16},{9,17... | collective-permute-start | bytes 2801672 | tf_op jit(solution)/shard_map/ppermute | solution.py:27
  8.2 2.3 constant_dynamic-slice_fusion.1
  13.7 1.9 convolution_convert_fusion
  19.3 19.4 %collective-permute-done.2 = bf16[128,1792]{1,0:T(8,128)(2,1)} collective-permute-done((bf16[128,1792]{1,0:T(8,128)(2,1)}, bf16[128,1792]{1,0:T(8,128)(2,1)}, u32[]{:S(2)}, u32[]{:S(2)}) %collective-permute-start.2) | collective-permute-done | bytes 458784 | tf_op jit(solution)/shard_map/ppermute | solution.py:22
  46.1 2.1 pad_maximum_fusion.refs_5_.refs_10_
  48.2 15.1 %collective-permute-done.7.refs_8_.refs_13_ = bf16[2048,128]{1,0:T(8,128)(2,1)S(1)} collective-permute-done((bf16[2048,128]{1,0:T(8,128)(2,1)S(1)}, bf16[2048,128]{1,0:T(8,128)(2,1)S(1)}, u32[]{:S(2)}, u32[]{:S(2)}) %collective-permute-start.7) | collective-permute-done | bytes 524320 | tf_op jit(solution)/shard_map/ppermute | solution.py:22
  69.5 20.5 %collective-permute-done.8.refs_1_.refs_2_.refs_4_ = bf16[64,7296]{1,0:T(8,128)(2,1)S(1)} collective-permute-done((bf16[64,7296]{1,0:T(8,128)(2,1)S(1)}, bf16[64,7296]{1,0:T(8,128)(2,1)S(1)}, u32[]{:S(2)}, u32[]{:S(2)}) %collective-permute-start.8) | collective-permute-done | bytes 933920 | tf_op jit(solution)/shard_map/ppermute | solution.py:27
  90.0 5.1 %collective-permute-done.10.refs_10_.refs_15_ = bf16[5120,128]{1,0:T(8,128)(2,1)S(1)} collective-permute-done((bf16[5120,128]{1,0:T(8,128)(2,1)S(1)}, bf16[5120,128]{1,0:T(8,128)(2,1)S(1)}, u32[]{:S(2)}, u32[]{:S(2)}) %collective-permute-start.10) | collective-permute-done | bytes 1310752 | tf_op jit(solution)/shard_map/ppermute | solution.py:22
  100.9 9.2 %collective-permute-done.15.refs_4_.refs_5_.refs_7_ = bf16[32,7296]{1,0:T(8,128)(2,1)S(1)} collective-permute-done((bf16[32,7296]{1,0:T(8,128)(2,1)S(1)}, bf16[32,7296]{1,0:T(8,128)(2,1)S(1)}, u32[]{:S(2)}, u32[]{:S(2)}) %collective-permute-start.15) | collective-permute-done | bytes 466976 | tf_op jit(solution)/shard_map/ppermute | solution.py:27
  111.1 7.7 %shard_map.132.refs_3_.refs_10_ = bf16[128,512]{1,0:T(8,128)(2,1)S(1)} custom-call(bf16[64,7296]{1,0:T(8,128)(2,1)S(1)} %collective-permute-done.refs_0_.refs_1_, bf16[64,7296]{1,0:T(8,128)(2,1)S(1)} %collective-permute-done.4.refs_1_.refs_2_, bf16[7168,128]{1,0:T(8,128)(2,1)} %refs_7_, bf16[7168,128]{1,0:T(8,128)(2,1)S(1)} %collective-permute-done.5.refs_3_.refs_8_, ...), custom_call_target="tpu_custom_call" | custom-call | flops 1879048192 | bytes 16515072 | tf_op jit(solution)/shard_map/pallas_call | solution.py:108
  126.6 12.2 %collective-permute-done.17.refs_4_.refs_11_ = bf16[128,512]{1,0:T(8,128)(2,1)S(1)} collective-permute-done((bf16[128,512]{1,0:T(8,128)(2,1)S(1)}, bf16[128,512]{1,0:T(8,128)(2,1)S(1)}, u32[]{:S(2)}, u32[]{:S(2)}) %collective-permute-start.17) | collective-permute-done | bytes 131104 | tf_op jit(solution)/shard_map/ppermute | solution.py:22
  139.5 2.3 pad_maximum_fusion.1.refs_14_
  157.1 12.6 %shard_map.134.refs_8_.refs_12_ = bf16[384,512]{1,0:T(8,128)(2,1)} custom-call(bf16[64,7296]{1,0:T(8,128)(2,1)S(1)} %copy-done.15, bf16[64,7296]{1,0:T(8,128)(2,1)S(1)} %copy-done.7, bf16[64,7296]{1,0:T(8,128)(2,1)S(1)} %shard_map.131.refs_2_.refs_3_.refs_5_, bf16[64,7296]{1,0:T(8,128)(2,1)S(1)} %copy-done.11, ...), custom_call_target="tpu_custom_call" | custom-call | flops 5637144576 | bytes 20185088 | tf_op jit(solution)/shard_map/pallas_call | solution.py:108
  171.2 3.2 %shard_map.133 = bf16[128,1792]{1,0:T(8,128)(2,1)} custom-call(f32[1,128]{1,0:T(1,128)S(1)} %and_convert_fusion.refs_0_, bf16[64,7296]{1,0:T(8,128)(2,1)S(1)} %collective-permute-done.refs_0_.refs_1_, bf16[64,7296]{1,0:T(8,128)(2,1)S(1)} %copy-done.2, bf16[128,512]{1,0:T(8,128)(2,1)S(1)} %copy-done.33, bf16[128,512]{1,0:T(8,128)(2,1)S(1)} %copy-done.41, ...), custom_call_target="tpu_custom_call" | custom-call | flops 469762048 | bytes 4587520 | tf_op jit(solution)/shard_map/pallas_call | solution.py:170
  176.0 3.3 %all-to-all-start = ((bf16[32,8,640]{2,1,0:T(8,128)(2,1)}), bf16[32,8,640]{2,1,0:T(8,128)(2,1)}, u32[]{:S(2)}, u32[]{:S(2)}) async-start(bf16[32,8,640]{2,1,0:T(8,128)(2,1)} %maximum_maximum_fusion), calls=%async_computation | async-start | bytes 655360 | tf_op jit(solution)/shard_map/all_to_all | solution.py:221
  185.8 3.9 %shard_map.135 = (f32[128,1792]{1,0:T(8,128)S(1)}, f32[128,1792]{1,0:T(8,128)S(1)}, f32[128,1792]{1,0:T(8,128)S(1)}) custom-call(f32[1,128]{1,0:T(1,128)S(1)} %and_convert_fusion.refs_0_, bf16[64,7296]{1,0:T(8,128)(2,1)S(1)} %copy-done.16, bf16[64,7296]{1,0:T(8,128)(2,1)S(1)} %copy-done.8, bf16[64,7296]{1,0:T(8,128)(2,1)S(1)} %shard_map.131.refs_2_.refs_3_.refs_5_, ...), custom_call_target="tpu_custom_call" | custom-call | flops 1409286144 | bytes 6422528 | tf_op jit(solution)/shard_map/pallas_call | solution.py:170
  193.5 2.4 all-to-all-done
  197.4 2.4 fusion.16
  204.9 4.6 %shard_map.136 = (bf16[128,1792]{1,0:T(8,128)(2,1)S(1)}, f32[128,1792]{1,0:T(8,128)S(1)}, f32[128,1792]{1,0:T(8,128)S(1)}, f32[128,1792]{1,0:T(8,128)S(1)}) custom-call(f32[1,128]{1,0:T(1,128)S(1)} %and_convert_fusion.refs_0_, bf16[64,7296]{1,0:T(8,128)(2,1)S(1)} %collective-permute-done.refs_0_.refs_1_, bf16[64,7296]{1,0:T(8,128)(2,1)S(1)} %copy-done.3, ...), custom_call_target="tpu_custom_call" | custom-call | flops 1879048192 | bytes 7340032 | tf_op jit(solution)/shard_map/pallas_call | solution.py:170
  212.1 12.7 %collective-permute-done.29 = bf16[128,1792]{1,0:T(8,128)(2,1)S(1)} collective-permute-done((bf16[128,1792]{1,0:T(8,128)(2,1)S(1)}, bf16[128,1792]{1,0:T(8,128)(2,1)S(1)}, u32[]{:S(2)}, u32[]{:S(2)}) %collective-permute-start.29) | collective-permute-done | bytes 458784 | tf_op jit(solution)/shard_map/ppermute | solution.py:27
  224.9 9.7 %collective-permute-done.25 = bf16[128,1792]{1,0:T(8,128)(2,1)S(1)} collective-permute-done((bf16[128,1792]{1,0:T(8,128)(2,1)S(1)}, bf16[128,1792]{1,0:T(8,128)(2,1)S(1)}, u32[]{:S(2)}, u32[]{:S(2)}) %collective-permute-start.25) | collective-permute-done | bytes 458784 | tf_op jit(solution)/shard_map/ppermute | solution.py:27
  234.7 8.6 %collective-permute-done.30 = bf16[128,1792]{1,0:T(8,128)(2,1)S(1)} collective-permute-done((bf16[128,1792]{1,0:T(8,128)(2,1)S(1)}, bf16[128,1792]{1,0:T(8,128)(2,1)S(1)}, u32[]{:S(2)}, u32[]{:S(2)}) %collective-permute-start.30) | collective-permute-done | bytes 458784 | tf_op jit(solution)/shard_map/ppermute | solution.py:27
  244.8 11.8 %collective-permute-done.31 = bf16[128,1792]{1,0:T(8,128)(2,1)S(1)} collective-permute-done((bf16[128,1792]{1,0:T(8,128)(2,1)S(1)}, bf16[128,1792]{1,0:T(8,128)(2,1)S(1)}, u32[]{:S(2)}, u32[]{:S(2)}) %collective-permute-start.31) | collective-permute-done | bytes 458784 | tf_op jit(solution)/shard_map/ppermute | solution.py:27
  259.5 3.4 %collective-permute-done.33 = bf16[64,1792]{1,0:T(8,128)(2,1)S(1)} collective-permute-done((bf16[64,1792]{1,0:T(8,128)(2,1)S(1)}, bf16[64,1792]{1,0:T(8,128)(2,1)S(1)}, u32[]{:S(2)}, u32[]{:S(2)}) %collective-permute-start.33) | collective-permute-done | bytes 229408 | tf_op jit(solution)/shard_map/ppermute | solution.py:22
  (200 shorter events, 83.2 us)
Async XLA Ops:
  3.6 35.2 %collective-permute-start = (bf16[64,7296]{1,0:T(8,128)(2,1)S(1)}, bf16[64,7296]{1,0:T(8,128)(2,1)S(1)}, u32[]{:S(2)}, u32[]{:S(2)}) collective-permute-start(bf16[64,7296]{1,0:T(8,128)(2,1)S(1)} %shard_map.131.refs_2_.refs_3_.refs_5_), channel_id=1, source_target_pairs={{0,8},{1,9},{2,10},{3,11},{4,12},{5,13},{6,14},{7,15},{8,16},{9,17... | collective-permute-start | bytes 2801672 | tf_op jit(solution)/shard_map/ppermute | solution.py:27
  6.7 32.1 %collective-permute-start.1 = (bf16[64,7296]{1,0:T(8,128)(2,1)S(1)}, bf16[64,7296]{1,0:T(8,128)(2,1)}, u32[]{:S(2)}, u32[]{:S(2)}) collective-permute-start(bf16[64,7296]{1,0:T(8,128)(2,1)S(1)} %shard_map.131.refs_2_.refs_3_.refs_5_), channel_id=1, source_target_pairs={{0,4},{1,5},{2,6},{3,7},{4,0},{5,1},{6,2},{7,3},{8,12},{9,13},{10,... | collective-permute-start | bytes 2801672 | tf_op jit(solution)/shard_map/ppermute | solution.py:22
  10.5 28.3 %collective-permute-start.2 = (bf16[128,1792]{1,0:T(8,128)(2,1)}, bf16[128,1792]{1,0:T(8,128)(2,1)}, u32[]{:S(2)}, u32[]{:S(2)}) collective-permute-start(bf16[128,1792]{1,0:T(8,128)(2,1)} %get-tuple-element.88), channel_id=1, source_target_pairs={{0,4},{1,5},{2,6},{3,7},{4,0},{5,1},{6,2},{7,3},{8,12},{9,13},{10,... | collective-permute-start | bytes 1376264 | tf_op jit(solution)/shard_map/ppermute | solution.py:22
  11.0 52.4 %collective-permute-start.6 = (bf16[7168,128]{1,0:T(8,128)(2,1)}, bf16[7168,128]{1,0:T(8,128)(2,1)}, u32[]{:S(2)}, u32[]{:S(2)}) collective-permute-start(bf16[7168,128]{1,0:T(8,128)(2,1)} %refs_7_), channel_id=1, source_target_pairs={{0,2},{1,3},{2,0},{3,1},{4,6},{5,7},{6,4},{7,5},{8,10},{9,11},{10,... | collective-permute-start | bytes 5505032 | tf_op jit(solution)/shard_map/ppermute | solution.py:22
  38.8 24.9 %collective-permute-start.5 = (bf16[7168,128]{1,0:T(8,128)(2,1)}, bf16[7168,128]{1,0:T(8,128)(2,1)S(1)}, u32[]{:S(2)}, u32[]{:S(2)}) collective-permute-start(bf16[7168,128]{1,0:T(8,128)(2,1)} %refs_7_), channel_id=1, source_target_pairs={{0,1},{1,0},{2,3},{3,2},{4,5},{5,4},{6,7},{7,6},{8,9},{9,8},{10,11... | collective-permute-start | bytes 5505032 | tf_op jit(solution)/shard_map/ppermute | solution.py:22
  38.8 24.9 %collective-permute-start.3 = (bf16[64,7296]{1,0:T(8,128)(2,1)S(1)}, bf16[64,7296]{1,0:T(8,128)(2,1)S(1)}, u32[]{:S(2)}, u32[]{:S(2)}) collective-permute-start(bf16[64,7296]{1,0:T(8,128)(2,1)S(1)} %collective-permute-done.refs_0_.refs_1_), channel_id=1, source_target_pairs={{0,8},{1,9},{2,10},{3,11},{4,12},{5,13},{6,14},{7,15},{8,16},{9,17... | collective-permute-start | bytes 2801672 | tf_op jit(solution)/shard_map/ppermute | solution.py:27
  40.4 23.3 %collective-permute-start.4 = (bf16[64,7296]{1,0:T(8,128)(2,1)S(1)}, bf16[64,7296]{1,0:T(8,128)(2,1)S(1)}, u32[]{:S(2)}, u32[]{:S(2)}) collective-permute-start(bf16[64,7296]{1,0:T(8,128)(2,1)S(1)} %collective-permute-done.refs_0_.refs_1_), channel_id=1, source_target_pairs={{0,4},{1,5},{2,6},{3,7},{4,0},{5,1},{6,2},{7,3},{8,12},{9,13},{10,... | collective-permute-start | bytes 2801672 | tf_op jit(solution)/shard_map/ppermute | solution.py:22
  43.0 20.3 %collective-permute-start.7 = (bf16[2048,128]{1,0:T(8,128)(2,1)S(1)}, bf16[2048,128]{1,0:T(8,128)(2,1)S(1)}, u32[]{:S(2)}, u32[]{:S(2)}) collective-permute-start(bf16[2048,128]{1,0:T(8,128)(2,1)S(1)} %slice.49), channel_id=1, source_target_pairs={{0,2},{1,3},{2,0},{3,1},{4,6},{5,7},{6,4},{7,5},{8,10},{9,11},{10,... | collective-permute-start | bytes 1572872 | tf_op jit(solution)/shard_map/ppermute | solution.py:22
  63.7 31.3 %collective-permute-start.11 = (bf16[7168,128]{1,0:T(8,128)(2,1)S(1)}, bf16[7168,128]{1,0:T(8,128)(2,1)S(1)}, u32[]{:S(2)}, u32[]{:S(2)}) collective-permute-start(bf16[7168,128]{1,0:T(8,128)(2,1)S(1)} %copy-done.4), channel_id=1, source_target_pairs={{0,1},{1,0},{2,3},{3,2},{4,5},{5,4},{6,7},{7,6},{8,9},{9,8},{10,11... | collective-permute-start | bytes 5505032 | tf_op jit(solution)/shard_map/ppermute | solution.py:22
  63.8 31.3 %collective-permute-start.12 = (bf16[7168,128]{1,0:T(8,128)(2,1)}, bf16[7168,128]{1,0:T(8,128)(2,1)S(1)}, u32[]{:S(2)}, u32[]{:S(2)}) collective-permute-start(bf16[7168,128]{1,0:T(8,128)(2,1)} %collective-permute-done.6.refs_4_.refs_9_), channel_id=1, source_target_pairs={{0,1},{1,0},{2,3},{3,2},{4,5},{5,4},{6,7},{7,6},{8,9},{9,8},{10,11... | collective-permute-start | bytes 5505032 | tf_op jit(solution)/shard_map/ppermute | solution.py:22
  64.3 30.8 %collective-permute-start.10 = (bf16[5120,128]{1,0:T(8,128)(2,1)S(1)}, bf16[5120,128]{1,0:T(8,128)(2,1)S(1)}, u32[]{:S(2)}, u32[]{:S(2)}) collective-permute-start(bf16[5120,128]{1,0:T(8,128)(2,1)S(1)} %slice.50), channel_id=1, source_target_pairs={{0,2},{1,3},{2,0},{3,1},{4,6},{5,7},{6,4},{7,5},{8,10},{9,11},{10,... | collective-permute-start | bytes 3932168 | tf_op jit(solution)/shard_map/ppermute | solution.py:22
  65.8 24.2 %collective-permute-start.8 = (bf16[64,7296]{1,0:T(8,128)(2,1)S(1)}, bf16[64,7296]{1,0:T(8,128)(2,1)S(1)}, u32[]{:S(2)}, u32[]{:S(2)}) collective-permute-start(bf16[64,7296]{1,0:T(8,128)(2,1)S(1)} %collective-permute-done.3.refs_0_.refs_1_.refs_3_), channel_id=1, source_target_pairs={{0,8},{1,9},{2,10},{3,11},{4,12},{5,13},{6,14},{7,15},{8,16},{9,17... | collective-permute-start | bytes 2801672 | tf_op jit(solution)/shard_map/ppermute | solution.py:27
  67.1 22.9 %collective-permute-start.9 = (bf16[64,7296]{1,0:T(8,128)(2,1)S(1)}, bf16[64,7296]{1,0:T(8,128)(2,1)S(1)}, u32[]{:S(2)}, u32[]{:S(2)}) collective-permute-start(bf16[64,7296]{1,0:T(8,128)(2,1)S(1)} %collective-permute-done.3.refs_0_.refs_1_.refs_3_), channel_id=1, source_target_pairs={{0,4},{1,5},{2,6},{3,7},{4,0},{5,1},{6,2},{7,3},{8,12},{9,13},{10,... | collective-permute-start | bytes 2801672 | tf_op jit(solution)/shard_map/ppermute | solution.py:22
  95.1 16.0 %collective-permute-start.14 = (bf16[5120,128]{1,0:T(8,128)(2,1)S(1)}, bf16[5120,128]{1,0:T(8,128)(2,1)S(1)}, u32[]{:S(2)}, u32[]{:S(2)}) collective-permute-start(bf16[5120,128]{1,0:T(8,128)(2,1)S(1)} %collective-permute-done.10.refs_10_.refs_15_), channel_id=1, source_target_pairs={{0,1},{1,0},{2,3},{3,2},{4,5},{5,4},{6,7},{7,6},{8,9},{9,8},{10,11... | collective-permute-start | bytes 3932168 | tf_op jit(solution)/shard_map/ppermute | solution.py:22
  99.4 27.2 %collective-permute-start.19 = (bf16[256,1792]{1,0:T(8,128)(2,1)}, bf16[256,1792]{1,0:T(8,128)(2,1)}, u32[]{:S(2)}, u32[]{:S(2)}) collective-permute-start(bf16[256,1792]{1,0:T(8,128)(2,1)} %pad_maximum_fusion.refs_5_.refs_10_), channel_id=1, source_target_pairs={{0,2},{1,3},{2,0},{3,1},{4,6},{5,7},{6,4},{7,5},{8,10},{9,11},{10,... | collective-permute-start | bytes 2752520 | tf_op jit(solution)/shard_map/ppermute | solution.py:22
  126.6 44.6 %collective-permute-start.20 = (bf16[256,1792]{1,0:T(8,128)(2,1)}, bf16[256,1792]{1,0:T(8,128)(2,1)}, u32[]{:S(2)}, u32[]{:S(2)}) collective-permute-start(bf16[256,1792]{1,0:T(8,128)(2,1)} %pad_maximum_fusion.refs_5_.refs_10_), channel_id=1, source_target_pairs={{0,1},{1,0},{2,3},{3,2},{4,5},{5,4},{6,7},{7,6},{8,9},{9,8},{10,11... | collective-permute-start | bytes 2752520 | tf_op jit(solution)/shard_map/ppermute | solution.py:22
  139.5 31.7 %collective-permute-start.21 = (bf16[256,1792]{1,0:T(8,128)(2,1)}, bf16[256,1792]{1,0:T(8,128)(2,1)}, u32[]{:S(2)}, u32[]{:S(2)}) collective-permute-start(bf16[256,1792]{1,0:T(8,128)(2,1)} %collective-permute-done.19.refs_7_.refs_12_), channel_id=1, source_target_pairs={{0,1},{1,0},{2,3},{3,2},{4,5},{5,4},{6,7},{7,6},{8,9},{9,8},{10,11... | collective-permute-start | bytes 2752520 | tf_op jit(solution)/shard_map/ppermute | solution.py:22
  141.8 37.6 %collective-permute-start.27 = (bf16[256,1792]{1,0:T(8,128)(2,1)}, bf16[256,1792]{1,0:T(8,128)(2,1)}, u32[]{:S(2)}, u32[]{:S(2)}) collective-permute-start(bf16[256,1792]{1,0:T(8,128)(2,1)} %pad_maximum_fusion.1.refs_14_), channel_id=1, source_target_pairs={{0,2},{1,3},{2,0},{3,1},{4,6},{5,7},{6,4},{7,5},{8,10},{9,11},{10,... | collective-permute-start | bytes 2752520 | tf_op jit(solution)/shard_map/ppermute | solution.py:22
  174.4 17.2 %collective-permute-start.22 = (bf16[128,1792]{1,0:T(8,128)(2,1)}, bf16[128,1792]{1,0:T(8,128)(2,1)}, u32[]{:S(2)}, u32[]{:S(2)}) collective-permute-start(bf16[128,1792]{1,0:T(8,128)(2,1)} %shard_map.133), channel_id=1, source_target_pairs={{0,8},{1,9},{2,10},{3,11},{4,12},{5,13},{6,14},{7,15},{8,16},{9,17... | collective-permute-start | bytes 1376264 | tf_op jit(solution)/shard_map/ppermute | solution.py:27
  176.0 19.9 %all-to-all-start = ((bf16[32,8,640]{2,1,0:T(8,128)(2,1)}), bf16[32,8,640]{2,1,0:T(8,128)(2,1)}, u32[]{:S(2)}, u32[]{:S(2)}) async-start(bf16[32,8,640]{2,1,0:T(8,128)(2,1)} %maximum_maximum_fusion), calls=%async_computation | async-start | bytes 655360 | tf_op jit(solution)/shard_map/all_to_all | solution.py:221
  179.3 25.5 %collective-permute-start.26 = (bf16[256,1792]{1,0:T(8,128)(2,1)}, bf16[256,1792]{1,0:T(8,128)(2,1)}, u32[]{:S(2)}, u32[]{:S(2)}) collective-permute-start(bf16[256,1792]{1,0:T(8,128)(2,1)} %pad_maximum_fusion.1.refs_14_), channel_id=1, source_target_pairs={{0,1},{1,0},{2,3},{3,2},{4,5},{5,4},{6,7},{7,6},{8,9},{9,8},{10,11... | collective-permute-start | bytes 2752520 | tf_op jit(solution)/shard_map/ppermute | solution.py:22
  179.4 25.4 %collective-permute-start.28 = (bf16[256,1792]{1,0:T(8,128)(2,1)}, bf16[256,1792]{1,0:T(8,128)(2,1)}, u32[]{:S(2)}, u32[]{:S(2)}) collective-permute-start(bf16[256,1792]{1,0:T(8,128)(2,1)} %collective-permute-done.27.refs_16_), channel_id=1, source_target_pairs={{0,1},{1,0},{2,3},{3,2},{4,5},{5,4},{6,7},{7,6},{8,9},{9,8},{10,11... | collective-permute-start | bytes 2752520 | tf_op jit(solution)/shard_map/ppermute | solution.py:22
  211.7 22.9 %collective-permute-start.25 = (bf16[128,1792]{1,0:T(8,128)(2,1)S(1)}, bf16[128,1792]{1,0:T(8,128)(2,1)S(1)}, u32[]{:S(2)}, u32[]{:S(2)}) collective-permute-start(bf16[128,1792]{1,0:T(8,128)(2,1)S(1)} %add_convert_fusion.5), channel_id=1, source_target_pairs={{0,8},{1,9},{2,10},{3,11},{4,12},{5,13},{6,14},{7,15},{8,16},{9,17... | collective-permute-start | bytes 1376264 | tf_op jit(solution)/shard_map/ppermute | solution.py:27
  224.9 18.4 %collective-permute-start.30 = (bf16[128,1792]{1,0:T(8,128)(2,1)S(1)}, bf16[128,1792]{1,0:T(8,128)(2,1)S(1)}, u32[]{:S(2)}, u32[]{:S(2)}) collective-permute-start(bf16[128,1792]{1,0:T(8,128)(2,1)S(1)} %add_convert_fusion.3), channel_id=1, source_target_pairs={{0,8},{1,9},{2,10},{3,11},{4,12},{5,13},{6,14},{7,15},{8,16},{9,17... | collective-permute-start | bytes 1376264 | tf_op jit(solution)/shard_map/ppermute | solution.py:27
  (63 other events, 631.4 us)

commit v8 on v5

--- a/solution.py
+++ b/solution.py
@@ -10,7 +10,7 @@
 VDIM = 512
 FF_WIN = 1024
 CORE, XBIT, YBIT = 1, 2, 4
-VMEM_BYTES = 16 * 1024 * 1024
+VMEM_BYTES = 60 * 1024 * 1024
 
 
 score_scale = 0.07216878364870323
@@ -68,10 +68,10 @@
     )(chosen, rows)
 
 
-def hidden_kernel(count, lead, *refs):
-    units, weights = refs[:count], refs[count : count + 10]
-    gate_o, gate_c, gate_x, gate_xc, up_o, up_c, up_xa, up_xca, up_xb, up_xcb = weights
-    out, near_gate, far_gate, near_up, far_up = refs[count + 10 :]
+def hidden_kernel(count, *refs):
+    units, weights = refs[:count], refs[count : count + 8]
+    gate_o, gate_c, gate_x, gate_xc, up_o, up_c, up_x, up_xc = weights
+    out, near_gate, far_gate, near_up, far_up = refs[count + 8 :]
     step = pl.program_id(0)
 
     @pl.when(step == 0)
@@ -81,16 +81,9 @@
 
     rows = jnp.concatenate([unit[...] for unit in units], axis=0)
     near_gate[...] += pair_dot(rows, gate_o, gate_c)
+    near_up[...] += pair_dot(rows, up_o, up_c)
     far_gate[...] += pair_dot(rows, gate_x, gate_xc)
-    near_up[...] += pair_dot(rows, up_o, up_c)
-
-    @pl.when(step < lead)
-    def _():
-        far_up[...] += pair_dot(rows, up_xa, up_xca)
-
-    @pl.when(step >= lead)
-    def _():
-        far_up[...] += pair_dot(rows, up_xb, up_xcb)
+    far_up[...] += pair_dot(rows, up_x, up_xc)
 
     @pl.when(step == pl.num_programs(0) - 1)
     def _():
@@ -99,18 +92,14 @@
         out[:, two:] = gated(far_gate[...], far_up[...])
 
 
-def hidden_units(units, weights, leads, rests, chunk):
-    width = units[0].shape[1]
-    wide = weights[0].shape[1]
-    lead = leads[0].shape[0] // chunk
+def hidden_units(units, weights, chunk):
+    width, wide = weights[0].shape
     count = sum(unit.shape[0] for unit in units)
     return pl.pallas_call(
-        partial(hidden_kernel, len(units), lead),
+        partial(hidden_kernel, len(units)),
         grid=(width // chunk,),
         in_specs=[pl.BlockSpec((unit.shape[0], chunk), lambda k: (0, k)) for unit in units]
-        + [pl.BlockSpec((chunk, wide), lambda k: (k, 0)) for _ in weights]
-        + [pl.BlockSpec((chunk, wide), lambda k: (jnp.minimum(k, lead - 1), 0)) for _ in leads]
-        + [pl.BlockSpec((chunk, wide), lambda k: (jnp.maximum(k - lead, 0), 0)) for _ in rests],
+        + [pl.BlockSpec((chunk, wide), lambda k: (k, 0)) for _ in weights],
         out_specs=pl.BlockSpec((count, 4 * wide), lambda k: (0, 0)),
         out_shape=jax.ShapeDtypeStruct((count, 4 * wide), jnp.bfloat16),
         scratch_shapes=[pltpu.VMEM((count, 2 * wide), jnp.float32)] * 4,
@@ -120,48 +109,63 @@
             bytes_accessed=2 * width * (count + wide * 8),
             transcendentals=0,
         ),
-    )(*units, *weights, *leads, *rests)
-
-
-def down_kernel(mine, other, *refs):
-    (own, own_c, side, side_c, peer, peer_c), outs = refs[:6], refs[6:]
-    deep = own.shape[0]
+    )(*units, *weights)
+
+
+def down_kernel(planes, mine, other, own, own_c, side, side_c, *outs):
+    deep = own.shape[0] // 2
+    parts = (own, own_c, side, side_c)
     table = jnp.concatenate(
-        [own[...], own_c[...], side[:deep, :], side_c[:deep, :]]
-        + [peer[...], peer_c[...], side[deep:, :], side_c[deep:, :]],
+        [part[:deep, :] for part in parts] + [part[deep:, :] for part in parts], axis=0
+    )
+    count = mine.shape[0] // 2
+    rows = count // planes
+    joined = jnp.concatenate(
+        [
+            jnp.concatenate([mine[:count, :], other[count:, :]], axis=1),
+            jnp.concatenate([mine[count:, :], other[:count, :]], axis=1),
+        ],
         axis=0,
     )
-    count = mine.shape[0] // 2
-    rows = count // len(outs)
-    for part in range(2):
-        here = slice(part * count, (part + 1) * count)
-        there = slice((1 - part) * count, (2 - part) * count)
-        joined = jnp.concatenate([mine[here, :], other[there, :]], axis=1)
-        value = jnp.dot(joined, table, preferred_element_type=jnp.float32).astype(jnp.bfloat16)
-        for at, out in enumerate(outs):
-            out[part * rows : (part + 1) * rows, :] = value[at * rows : (at + 1) * rows]
-
-
-def down_values(mine, other, own, side, peer, planes, chunk, offset):
+    value = jnp.dot(joined, table, preferred_element_type=jnp.float32).astype(jnp.bfloat16)
+
+    def put(targets):
+        for at, out in enumerate(targets):
+            out[:rows, :] = value[at * rows : (at + 1) * rows]
+            out[rows:, :] = value[count + at * rows : count + (at + 1) * rows]
+
+    first = pl.program_id(0) < pl.num_programs(0) // 2
+
+    @pl.when(first)
+    def _():
+        put(outs[:planes])
+
+    @pl.when(jnp.logical_not(first))
+    def _():
+        put(outs[planes:])
+
+
+def down_values(mine, other, tables, planes, chunk):
     count, inner = mine.shape
-    width = side[0].shape[1]
+    deep, width = tables[0].shape
     rows = count // planes
+    steps = width // chunk
+    half = steps // 2
     return pl.pallas_call(
-        down_kernel,
-        grid=(width // chunk,),
+        partial(down_kernel, planes),
+        grid=(steps,),
         in_specs=[pl.BlockSpec((count, inner), lambda k: (0, 0))] * 2
-        + [pl.BlockSpec((block.shape[0], chunk), lambda k: (0, k + offset)) for block in own]
-        + [pl.BlockSpec((block.shape[0], chunk), lambda k: (0, k)) for block in side]
-        + [pl.BlockSpec((block.shape[0], chunk), lambda k: (0, k + offset)) for block in peer],
-        out_specs=[pl.BlockSpec((rows, chunk), lambda k: (0, k))] * planes,
-        out_shape=[jax.ShapeDtypeStruct((rows, width), jnp.bfloat16)] * planes,
+        + [pl.BlockSpec((deep, chunk), lambda k: (0, k)) for _ in tables],
+        out_specs=[pl.BlockSpec((rows, chunk), lambda k: (0, jnp.minimum(k, half - 1)))] * planes
+        + [pl.BlockSpec((rows, chunk), lambda k: (0, jnp.maximum(k - half, 0)))] * planes,
+        out_shape=[jax.ShapeDtypeStruct((rows, width // 2), jnp.bfloat16)] * (2 * planes),
         compiler_params=pltpu.CompilerParams(vmem_limit_bytes=VMEM_BYTES),
         cost_estimate=pl.CostEstimate(
             flops=2 * count * 2 * inner * width,
-            bytes_accessed=2 * 2 * inner * width + 2 * count * width,
+            bytes_accessed=8 * deep * width + 2 * count * width,
             transcendentals=0,
         ),
-    )(mine, other, *own, *side, *peer)
+    )(mine, other, *tables)
 
 
 def combine_kernel(high, low, *refs):
@@ -216,14 +220,15 @@
     return jnp.where(found, weight.T[:, :, None], 0.0)
 
 
-def expert_rows(rows, picks, gates, latents, owners, requests, gate_proj, up_proj, down_proj):
+def expert_rows(
+    rows, picks, gates, latents, owners, requests, queries, gate_proj, up_proj, down_proj
+):
     n_ep = lax.axis_size("ep")
     split = FF_WIN // gate_proj.shape[1]
     planes = n_ep // split
     count, width = rows.shape
     slots = -(-3 * count * picks.shape[1] // (2 * planes * 16)) * 16
     chunk = width // 4
-    cut = 3 * chunk
     upper = lax.axis_index("ep") // YBIT % 2
     span = width // 4
 
@@ -238,44 +243,45 @@
         own_0, out_1, out_3, latents, owners, requests, down_proj
     )
     own_1, own_3, peer_0 = shift(out_1, split), shift(out_3, 3 * split), swap(own_0, YBIT)
-    keep = lax.dynamic_slice_in_dim(down_proj, 2 * upper * span, 2 * span, 1)
     send = lax.dynamic_slice_in_dim(down_proj, (2 - 2 * upper) * span, 2 * span, 1)
     down_y = swap(send, YBIT)
     outgoing = hand_over(latents, owners, requests)
-    up_a, up_b = up_proj[:cut], up_proj[cut:]
-
-    own_1, own_3, peer_0, down_y, gate_x, up_a, out_2, gate_proj, up_proj = together(
-        own_1, own_3, peer_0, down_y, gate_x, up_a, out_2, gate_proj, up_proj
-    )
-    outgoing, keep, picks, gates, own_1 = together(outgoing, keep, picks, gates, own_1)
+
+    own_1, own_3, peer_0, down_y, gate_x, out_2, outgoing, down_proj, gate_proj = together(
+        own_1, own_3, peer_0, down_y, gate_x, out_2, outgoing, down_proj, gate_proj
+    )
     own_2, peer_1, peer_3 = shift(out_2, 2 * split), swap(own_1, YBIT), swap(own_3, YBIT)
-    up_xa, gate_xc = swap(up_a, XBIT), swap(gate_x, CORE)
-    gate_c, up_c = swap(gate_proj, CORE), swap(up_proj, CORE)
-
-    own_2, peer_1, peer_3, up_xa, gate_xc, gate_c, up_c, up_b = together(
-        own_2, peer_1, peer_3, up_xa, gate_xc, gate_c, up_c, up_b
-    )
-    keep, down_y, picks, gates, outgoing, own_2 = together(
-        keep, down_y, picks, gates, outgoing, own_2
-    )
-    peer_2, up_xb, up_xca = swap(own_2, YBIT), swap(up_b, XBIT), swap(up_xa, CORE)
-    keep_c, down_yc = swap(keep, CORE), swap(down_y, CORE)
+    up_x, gate_c = swap(up_proj, XBIT), swap(gate_proj, CORE)
     incoming = lax.all_to_all(outgoing, "ep", split_axis=0, concat_axis=0, tiled=True)
+    keep = lax.dynamic_slice_in_dim(down_proj, 2 * upper * span, 2 * span, 1)
+    own = jnp.concatenate([keep, down_y], axis=0)
+
+    own_2, peer_1, peer_3, up_x, gate_x, gate_c, up_proj, own, incoming = together(
+        own_2, peer_1, peer_3, up_x, gate_x, gate_c, up_proj, own, incoming
+    )
+    peer_2, side = swap(own_2, YBIT), swap(own, XBIT)
+    up_c, gate_xc, up_xc = swap(up_proj, CORE), swap(gate_x, CORE), swap(up_x, CORE)
+
+    peer_2, up_c, gate_xc, up_xc = together(peer_2, up_c, gate_xc, up_xc)
+    units = (own_0, own_1, own_2, own_3, peer_0, peer_1, peer_2, peer_3)
+    weights = (gate_proj, gate_c, gate_x, gate_xc, up_proj, up_c, up_x, up_xc)
+    hidden = hidden_units(units, weights, chunk)
+    hidden, own, picks, gates = together(hidden, own, picks, gates)
+    other, own_c = swap(hidden, YBIT), swap(own, CORE)
+    other, own_c, side = together(other, own_c, side)
+    side_c = swap(side, CORE)
     info = swap(jnp.concatenate([picks.astype(jnp.float32), gates], axis=1), YBIT)
-    sides = [
-        jnp.concatenate([part[:, at * span : (at + 1) * span] for part in (keep, down_y)], axis=0)
-        for at in range(2)
-    ]
-    up_xb, sides[0] = together(up_xb, sides[0])
-    up_xcb, side_0 = swap(up_xb, CORE), swap(sides[0], XBIT)
-
-    units = (own_0, own_1, own_2, own_3, peer_0, peer_1, peer_2, peer_3)
-    weights = (gate_proj, gate_c, gate_x, gate_xc, up_proj, up_c)
-    hidden = hidden_units(units, weights, (up_xa, up_xca), (up_xb, up_xcb), chunk)
-    other = swap(hidden, YBIT)
-    side_0, sides[1] = together(side_0, sides[1])
-    side_1 = swap(sides[1], XBIT)
-    side = ((side_0, swap(side_0, CORE)), (side_1, swap(side_1, CORE)))
+    values = down_values(hidden, other, (own, own_c, side, side_c), planes, span // 2)
+
+    def returned(part):
+        return [part[0]] + [shift(part[k], n_ep - k * split) for k in range(1, planes)]
+
+    first = returned(values[:planes])
+    first[1], info, picks, gates, *values = together(
+        first[1], info, picks, gates, *values[planes:]
+    )
+    second = returned(values)
+    backs = (together(*first), together(*second))
 
     top = picks.shape[1]
     tables = [
@@ -291,17 +297,15 @@
     high, low = high.astype(jnp.bfloat16), (table - high).astype(jnp.bfloat16)
 
     outs, others = [], []
-    for at in range(2):
-        values = down_values(
-            hidden, other, (keep, keep_c), side[at], (down_y, down_yc), planes, span // 2, 2 * at
-        )
-        back = [values[0]] + [shift(values[k], n_ep - k * split) for k in range(1, planes)]
+    for back in backs:
         mine, theirs = combine(high, low, back, span // 2)
+        if not outs:
+            mine, theirs, incoming, queries = together(mine, theirs, incoming, queries)
         outs.append(mine)
         others.append(swap(theirs, YBIT))
     low_first = jnp.concatenate(outs + others, axis=1)
     high_first = jnp.concatenate(others + outs, axis=1)
-    return jnp.where(upper == 0, low_first, high_first), incoming, other
+    return jnp.where(upper == 0, low_first, high_first), incoming, queries
 
 
 def attend(query_part, cache_latents, cache_lens, handed, handed_mark):
@@ -372,19 +376,19 @@
 ):
     sections, count, width = moe_rows.shape
     top = routes.shape[2]
-    expert_out, incoming, other = expert_rows(
+    expert_out, incoming, queries = expert_rows(
         moe_rows.reshape(sections * count, width),
         routes.reshape(sections * count, top),
         route_gates.reshape(sections * count, top),
         prompt_latents,
         kv_owner[:, 0],
         kv_request,
+        queries,
         gate_proj,
         up_proj,
         down_proj,
     )
     expert_out = expert_out.reshape(moe_rows.shape)
-    queries, incoming, _ = together(queries, incoming, other)
     lat = prompt_latents.shape[1]
     handed = incoming[:, :, :lat].reshape(-1, lat)
     handed_mark = incoming[:, :, lat].reshape(-1).astype(jnp.float32)

time: 253 us -> 237 us (0.937); the launches traced: 253 us -> 233 us
  starting transfers between devices: 39.1 us -> 26.2 us
  local copies, waits for them, and re-layouts: 20 us -> 9.44 us
  Pallas kernels: 22.1 us -> 29 us
  waiting for transfers between devices: 154 us -> 151 us
    ppermute x9, waiting for transfers between devices: 86.5 us -> 76.3 us  [shift(): lax.ppermute(value, 'ep', [(i, (i + step) % count) for i in range(count)])]
    ppermute x9, starting transfers between devices: 15.5 us -> 8.62 us  [shift(): lax.ppermute(value, 'ep', [(i, (i + step) % count) for i in range(count)])]
    slice x4 -> x0, local copies, waits for them, and re-layouts: 4.99 us -> none  [the longest x2 2.98 us: expert_rows(): up_a, up_b = (up_proj[:cut], up_proj[cut:])]
    ppermute x23 -> x18, waiting for transfers between devices: 67.2 us -> 71.7 us  [swap(): return lax.ppermute(value, 'ep', [(i, i ^ bit) for i in range(count)])]
    all_to_all x1, starting transfers between devices: 9.19 us -> 5.41 us  [expert_rows(): lax.all_to_all(outgoing, 'ep', split_axis=0, concat_axis=0, tiled=True)]
    pallas_call x2, Pallas kernels: 2.2 us -> 5.91 us  [combine(): pl.pallas_call(combine_kernel, grid=(width // chunk,), in_specs=[pl.Block...]
    all_to_all x1, waiting for transfers between devices: 0.01 us -> 2.78 us  [expert_rows(): lax.all_to_all(outgoing, 'ep', split_axis=0, concat_axis=0, tiled=True)]
    unnamed x40 -> x46, local copies, waits for them, and re-layouts: 7.61 us -> 5.04 us
  transfers between devices with their start and end apart: 33 -> 28, of which waited for: 14 -> 15; matrix products, arithmetic and copies ran while one was open for 11% -> 6% of each run, Pallas kernels for 9% -> 8%
where the time goes in v8:
time: 237 us; the launch traced here: 233 us
  waiting for transfers between devices  151 us (64%)
  Pallas kernels  29 us (12%)
  starting transfers between devices  26.2 us (11%)
  other arithmetic  9.58 us (4%)
  local copies, waits for them, and re-layouts  9.44 us (4%)
  matrix products  7.02 us (3%)
    ppermute x9, waiting for transfers between devices, shift(): lax.ppermute(value, 'ep', [(i, (i + step) % count) for i in range(count)])  76.3 us
    ppermute x18, waiting for transfers between devices, swap(): return lax.ppermute(value, 'ep', [(i, i ^ bit) for i in range(count)])  71.7 us
    ppermute x18, starting transfers between devices, swap(): return lax.ppermute(value, 'ep', [(i, i ^ bit) for i in range(count)])  12.1 us
    pallas_call x1, Pallas kernels, hidden_units(): pl.pallas_call(partial(hidden_kernel, len(units)), grid=(width // chunk,)...  11.1 us
    ppermute x9, starting transfers between devices, shift(): lax.ppermute(value, 'ep', [(i, (i + step) % count) for i in range(count)])  8.62 us
    pallas_call x1, Pallas kernels, down_values(): pl.pallas_call(partial(down_kernel, planes), grid=(steps,), in_specs=[pl....  7.91 us
    pallas_call x2, Pallas kernels, combine(): pl.pallas_call(combine_kernel, grid=(width // chunk,), in_specs=[pl.Block...  5.91 us
    all_to_all x1, starting transfers between devices, expert_rows(): lax.all_to_all(outgoing, 'ep', split_axis=0, concat_axis=0, tiled=True)  5.41 us
  transfers between devices with their start and end apart: 28, of which 15 were waited for; matrix products, arithmetic and copies ran while one was open for 6% of the time, Pallas kernels for 8%

profile of v8, /device:TPU:16, one launch (start us, length us, event | category | flops | bytes accessed | tf_op | source)
XLA Modules:
  0.0 233.0 jit_solution(5425781709854286273)
XLA Ops:
  4.0 4.1 %shard_map.131 = (bf16[48,7168]{1,0:T(8,128)(2,1)}, bf16[48,7168]{1,0:T(8,128)(2,1)}, bf16[48,7168]{1,0:T(8,128)(2,1)}, bf16[48,7168]{1,0:T(8,128)(2,1)}) custom-call(bf16[192,64]{1,0:T(8,128)(2,1)} %fusion.18.chosen, bf16[64,7168]{1,0:T(8,128)(2,1)} %bitcast.42), custom_call_target="tpu_custom_call" | custom-call | flops 176160768 | bytes 3670016 | tf_op jit(solution)/shard_map/pallas_call | solution.py:53
  15.2 27.2 %collective-permute-done.refs_1_ = bf16[48,7168]{1,0:T(8,128)(2,1)} collective-permute-done((bf16[48,7168]{1,0:T(8,128)(2,1)}, bf16[48,7168]{1,0:T(8,128)(2,1)}, u32[]{:S(2)}, u32[]{:S(2)}) %collective-permute-start) | collective-permute-done | bytes 688160 | tf_op jit(solution)/shard_map/ppermute | solution.py:26
  43.1 2.9 %collective-permute-done.2.refs_4_ = bf16[48,7168]{1,0:T(8,128)(2,1)} collective-permute-done((bf16[48,7168]{1,0:T(8,128)(2,1)}, bf16[48,7168]{1,0:T(8,128)(2,1)}, u32[]{:S(2)}, u32[]{:S(2)}) %collective-permute-start.2) | collective-permute-done | bytes 688160 | tf_op jit(solution)/shard_map/ppermute | solution.py:21
  48.6 5.4 %all-to-all-start = ((bf16[32,8,640]{2,1,0:T(8,128)(2,1)}), bf16[32,8,640]{2,1,0:T(8,128)(2,1)S(1)}, u32[]{:S(2)}, u32[]{:S(2)}) async-start(bf16[32,8,640]{2,1,0:T(8,128)(2,1)} %maximum_maximum_fusion), calls=%async_computation | async-start | bytes 655360 | tf_op jit(solution)/shard_map/all_to_all | solution.py:255
  56.5 28.2 %collective-permute-done.8.refs_14_ = bf16[7168,128]{1,0:T(8,128)(2,1)} collective-permute-done((bf16[7168,128]{1,0:T(8,128)(2,1)}, bf16[7168,128]{1,0:T(8,128)(2,1)}, u32[]{:S(2)}, u32[]{:S(2)}) %collective-permute-start.8) | collective-permute-done | bytes 1835040 | tf_op jit(solution)/shard_map/ppermute | solution.py:21
  84.8 2.8 %all-to-all-done = bf16[32,8,640]{2,1,0:T(8,128)(2,1)S(1)} async-done(((bf16[32,8,640]{2,1,0:T(8,128)(2,1)}), bf16[32,8,640]{2,1,0:T(8,128)(2,1)S(1)}, u32[]{:S(2)}, u32[]{:S(2)}) %all-to-all-start) | async-done | bytes 327712 | tf_op jit(solution)/shard_map/all_to_all | solution.py:255
  89.8 16.5 %collective-permute-done.10.refs_6_ = bf16[48,7168]{1,0:T(8,128)(2,1)} collective-permute-done((bf16[48,7168]{1,0:T(8,128)(2,1)}, bf16[48,7168]{1,0:T(8,128)(2,1)}, u32[]{:S(2)}, u32[]{:S(2)}) %collective-permute-start.10) | collective-permute-done | bytes 688160 | tf_op jit(solution)/shard_map/ppermute | solution.py:21
  106.3 11.1 %shard_map.132.mine = bf16[384,512]{1,0:T(8,128)(2,1)} custom-call(bf16[48,7168]{1,0:T(8,128)(2,1)} %get-tuple-element.77.refs_0_, bf16[48,7168]{1,0:T(8,128)(2,1)} %collective-permute-done.refs_1_, bf16[48,7168]{1,0:T(8,128)(2,1)} %collective-permute-done.5.refs_2_, bf16[48,7168]{1,0:T(8,128)(2,1)} %collective-permute-done.1.refs_3_, ...), custom_call_target="tpu_custom_call" | custom-call | flops 5637144576 | bytes 20185088 | tf_op jit(solution)/shard_map/pallas_call | solution.py:98
  118.2 13.1 %collective-permute-done.16.side = bf16[256,3584]{1,0:T(8,128)(2,1)} collective-permute-done((bf16[256,3584]{1,0:T(8,128)(2,1)}, bf16[256,3584]{1,0:T(8,128)(2,1)}, u32[]{:S(2)}, u32[]{:S(2)}) %collective-permute-start.16) | collective-permute-done | bytes 1835040 | tf_op jit(solution)/shard_map/ppermute | solution.py:21
  132.7 4.0 %collective-permute-done.17.side_c = bf16[256,3584]{1,0:T(8,128)(2,1)S(1)} collective-permute-done((bf16[256,3584]{1,0:T(8,128)(2,1)}, bf16[256,3584]{1,0:T(8,128)(2,1)S(1)}, u32[]{:S(2)}, u32[]{:S(2)}) %collective-permute-start.17) | collective-permute-done | bytes 1835040 | tf_op jit(solution)/shard_map/ppermute | solution.py:21
  137.9 7.9 %shard_map.133 = (bf16[96,1792]{1,0:T(8,128)(2,1)}, bf16[96,1792]{1,0:T(8,128)(2,1)}, bf16[96,1792]{1,0:T(8,128)(2,1)}, bf16[96,1792]{1,0:T(8,128)(2,1)}, bf16[9...) custom-call(bf16[384,512]{1,0:T(8,128)(2,1)} %shard_map.132.mine, ...), custom_call_target="tpu_custom_call" | custom-call | flops 2818572288 | bytes 10092544 | tf_op jit(solution)/shard_map/pallas_call | solution.py:154
  145.9 4.0 %collective-permute-start.20 = (bf16[96,1792]{1,0:T(8,128)(2,1)}, bf16[96,1792]{1,0:T(8,128)(2,1)S(1)}, u32[]{:S(2)}, u32[]{:S(2)}) collective-permute-start(bf16[96,1792]{1,0:T(8,128)(2,1)} %get-tuple-element.123), channel_id=1, source_target_pairs={{0,16},{1,17},{2,18},{3,19},{4,20},{5,21},{6,22},{7,23},{8,24},{9,... | collective-permute-start | bytes 1032200 | tf_op jit(solution)/shard_map/ppermute | solution.py:26
  150.6 3.0 %collective-permute-done.19 = f32[64,4]{0,1:T(4,128)S(1)} collective-permute-done((f32[64,4]{0,1:T(4,128)S(1)}, f32[64,4]{0,1:T(4,128)S(1)}, u32[]{:S(2)}, u32[]{:S(2)}) %collective-permute-start.19) | collective-permute-done | bytes 1056 | tf_op jit(solution)/shard_map/ppermute | solution.py:21
  153.7 3.4 %collective-permute-done.18.refs_1_ = bf16[96,1792]{1,0:T(8,128)(2,1)S(1)} collective-permute-done((bf16[96,1792]{1,0:T(8,128)(2,1)}, bf16[96,1792]{1,0:T(8,128)(2,1)S(1)}, u32[]{:S(2)}, u32[]{:S(2)}) %collective-permute-start.18) | collective-permute-done | bytes 344096 | tf_op jit(solution)/shard_map/ppermute | solution.py:26
  157.0 19.2 %collective-permute-done.20.refs_2_ = bf16[96,1792]{1,0:T(8,128)(2,1)S(1)} collective-permute-done((bf16[96,1792]{1,0:T(8,128)(2,1)}, bf16[96,1792]{1,0:T(8,128)(2,1)S(1)}, u32[]{:S(2)}, u32[]{:S(2)}) %collective-permute-start.20) | collective-permute-done | bytes 344096 | tf_op jit(solution)/shard_map/ppermute | solution.py:26
  176.3 3.3 %collective-permute-done.21.refs_3_ = bf16[96,1792]{1,0:T(8,128)(2,1)S(1)} collective-permute-done((bf16[96,1792]{1,0:T(8,128)(2,1)}, bf16[96,1792]{1,0:T(8,128)(2,1)S(1)}, u32[]{:S(2)}, u32[]{:S(2)}) %collective-permute-start.21) | collective-permute-done | bytes 344096 | tf_op jit(solution)/shard_map/ppermute | solution.py:26
  184.5 3.0 %shard_map.134 = (bf16[64,1792]{1,0:T(8,128)(2,1)}, bf16[64,1792]{1,0:T(8,128)(2,1)}) custom-call(bf16[128,384]{1,0:T(8,128)(2,1)} %get-tuple-element.155.high, bf16[128,384]{1,0:T(8,128)(2,1)} %get-tuple-element.154.low, bf16[96,1792]{1,0:T(8,128)(2,1)} %get-tuple-element.125.refs_0_, bf16[96,1792]{1,0:T(8,128)(2,1)} %copy-done.8, ...), custom_call_target="tpu_custom_call" | custom-call | flops 352321536 | bytes 1835008 | tf_op jit(solution)/shard_map/pallas_call | solution.py:185
  194.7 2.2 fusion
  196.9 4.3 %collective-permute-done.22.refs_1_ = bf16[96,1792]{1,0:T(8,128)(2,1)} collective-permute-done((bf16[96,1792]{1,0:T(8,128)(2,1)}, bf16[96,1792]{1,0:T(8,128)(2,1)}, u32[]{:S(2)}, u32[]{:S(2)}) %collective-permute-start.22) | collective-permute-done | bytes 344096 | tf_op jit(solution)/shard_map/ppermute | solution.py:26
  201.2 18.6 %collective-permute-done.23.refs_2_ = bf16[96,1792]{1,0:T(8,128)(2,1)} collective-permute-done((bf16[96,1792]{1,0:T(8,128)(2,1)}, bf16[96,1792]{1,0:T(8,128)(2,1)}, u32[]{:S(2)}, u32[]{:S(2)}) %collective-permute-start.23) | collective-permute-done | bytes 344096 | tf_op jit(solution)/shard_map/ppermute | solution.py:26
  220.1 2.9 %shard_map.135 = (bf16[64,1792]{1,0:T(8,128)(2,1)}, bf16[64,1792]{1,0:T(8,128)(2,1)}) custom-call(bf16[128,384]{1,0:T(8,128)(2,1)} %get-tuple-element.155.high, bf16[128,384]{1,0:T(8,128)(2,1)} %get-tuple-element.154.low, bf16[96,1792]{1,0:T(8,128)(2,1)} %get-tuple-element.137.refs_0_, bf16[96,1792]{1,0:T(8,128)(2,1)} %collective-permute-done.22.refs_1_, ...), custom_call_target="tpu_custom_call" | custom-call | flops 352321536 | bytes 1835008 | tf_op jit(solution)/shard_map/pallas_call | solution.py:185
  223.8 3.1 %add_convert_fusion = bf16[8,128,512]{2,1,0:T(8,128)(2,1)} fusion(f32[8,128,512]{2,1,0:T(8,128)} %fusion, f32[8,128,256]{2,1,0:T(8,128)S(1)} %copy-done.5, f32[8,128]{1,0:T(8,128)S(1)} %add.81, f32[8,128]{1,0:T(8,128)S(1)} %max.7, bf16[256,576]{1,0:T(8,128)(2,1)S(1)} %copy-done.11), kind=kOutput, calls=%fused_computation | convolution fusion | flops 270270464 | bytes 4464640 | tf_op jit(solution)/shard_map/qhr,rv->qhv/dot_general | solution.py:337
  226.9 3.9 %collective-permute-done.26 = bf16[64,1792]{1,0:T(8,128)(2,1)S(1)} collective-permute-done((bf16[64,1792]{1,0:T(8,128)(2,1)}, bf16[64,1792]{1,0:T(8,128)(2,1)S(1)}, u32[]{:S(2)}, u32[]{:S(2)}) %collective-permute-start.26) | collective-permute-done | bytes 229408 | tf_op jit(solution)/shard_map/ppermute | solution.py:21
  230.8 2.2 maximum_select_fusion
  (130 shorter events, 35.6 us)
Async XLA Ops:
  0.7 45.4 %collective-permute-start.4 = (bf16[7168,128]{1,0:T(8,128)(2,1)}, bf16[7168,128]{1,0:T(8,128)(2,1)}, u32[]{:S(2)}, u32[]{:S(2)}) collective-permute-start(bf16[7168,128]{1,0:T(8,128)(2,1)} %refs_8_), channel_id=1, source_target_pairs={{0,2},{1,3},{2,0},{3,1},{4,6},{5,7},{6,4},{7,5},{8,10},{9,11},{10,... | collective-permute-start | bytes 5505032 | tf_op jit(solution)/shard_map/ppermute | solution.py:21
  9.2 36.9 %collective-permute-start.3 = (bf16[128,3584]{1,0:T(8,128)(2,1)}, bf16[128,3584]{1,0:T(8,128)(2,1)S(1)}, u32[]{:S(2)}, u32[]{:S(2)}) collective-permute-start(bf16[128,3584]{1,0:T(8,128)(2,1)} %constant_dynamic-slice_fusion.1), channel_id=1, source_target_pairs={{0,4},{1,5},{2,6},{3,7},{4,0},{5,1},{6,2},{7,3},{8,12},{9,13},{10,... | collective-permute-start | bytes 2752520 | tf_op jit(solution)/shard_map/ppermute | solution.py:21
  10.7 31.7 %collective-permute-start = (bf16[48,7168]{1,0:T(8,128)(2,1)}, bf16[48,7168]{1,0:T(8,128)(2,1)}, u32[]{:S(2)}, u32[]{:S(2)}) collective-permute-start(bf16[48,7168]{1,0:T(8,128)(2,1)} %get-tuple-element.78), channel_id=1, source_target_pairs={{0,8},{1,9},{2,10},{3,11},{4,12},{5,13},{6,14},{7,15},{8,16},{9,17... | collective-permute-start | bytes 2064392 | tf_op jit(solution)/shard_map/ppermute | solution.py:26
  12.3 30.8 %collective-permute-start.1 = (bf16[48,7168]{1,0:T(8,128)(2,1)}, bf16[48,7168]{1,0:T(8,128)(2,1)}, u32[]{:S(2)}, u32[]{:S(2)}) collective-permute-start(bf16[48,7168]{1,0:T(8,128)(2,1)} %get-tuple-element.79), channel_id=1, source_target_pairs={{0,24},{1,25},{2,26},{3,27},{4,28},{5,29},{6,30},{7,31},{8,0},{9,1... | collective-permute-start | bytes 2064392 | tf_op jit(solution)/shard_map/ppermute | solution.py:26
  12.7 33.3 %collective-permute-start.2 = (bf16[48,7168]{1,0:T(8,128)(2,1)}, bf16[48,7168]{1,0:T(8,128)(2,1)}, u32[]{:S(2)}, u32[]{:S(2)}) collective-permute-start(bf16[48,7168]{1,0:T(8,128)(2,1)} %get-tuple-element.77.refs_0_), channel_id=1, source_target_pairs={{0,4},{1,5},{2,6},{3,7},{4,0},{5,1},{6,2},{7,3},{8,12},{9,13},{10,... | collective-permute-start | bytes 2064392 | tf_op jit(solution)/shard_map/ppermute | solution.py:21
  42.4 42.4 %collective-permute-start.8 = (bf16[7168,128]{1,0:T(8,128)(2,1)}, bf16[7168,128]{1,0:T(8,128)(2,1)}, u32[]{:S(2)}, u32[]{:S(2)}) collective-permute-start(bf16[7168,128]{1,0:T(8,128)(2,1)} %refs_12_), channel_id=1, source_target_pairs={{0,2},{1,3},{2,0},{3,1},{4,6},{5,7},{6,4},{7,5},{8,10},{9,11},{10,... | collective-permute-start | bytes 5505032 | tf_op jit(solution)/shard_map/ppermute | solution.py:21
  46.0 41.5 %collective-permute-start.9 = (bf16[7168,128]{1,0:T(8,128)(2,1)}, bf16[7168,128]{1,0:T(8,128)(2,1)}, u32[]{:S(2)}, u32[]{:S(2)}) collective-permute-start(bf16[7168,128]{1,0:T(8,128)(2,1)} %refs_8_), channel_id=1, source_target_pairs={{0,1},{1,0},{2,3},{3,2},{4,5},{5,4},{6,7},{7,6},{8,9},{9,8},{10,11... | collective-permute-start | bytes 5505032 | tf_op jit(solution)/shard_map/ppermute | solution.py:21
  46.1 41.4 %collective-permute-start.5 = (bf16[48,7168]{1,0:T(8,128)(2,1)}, bf16[48,7168]{1,0:T(8,128)(2,1)}, u32[]{:S(2)}, u32[]{:S(2)}) collective-permute-start(bf16[48,7168]{1,0:T(8,128)(2,1)} %get-tuple-element.86), channel_id=1, source_target_pairs={{0,16},{1,17},{2,18},{3,19},{4,20},{5,21},{6,22},{7,23},{8,24},{9,... | collective-permute-start | bytes 2064392 | tf_op jit(solution)/shard_map/ppermute | solution.py:26
  46.5 41.0 %collective-permute-start.6 = (bf16[48,7168]{1,0:T(8,128)(2,1)}, bf16[48,7168]{1,0:T(8,128)(2,1)}, u32[]{:S(2)}, u32[]{:S(2)}) collective-permute-start(bf16[48,7168]{1,0:T(8,128)(2,1)} %collective-permute-done.refs_1_), channel_id=1, source_target_pairs={{0,4},{1,5},{2,6},{3,7},{4,0},{5,1},{6,2},{7,3},{8,12},{9,13},{10,... | collective-permute-start | bytes 2064392 | tf_op jit(solution)/shard_map/ppermute | solution.py:21
  48.1 39.5 %collective-permute-start.7 = (bf16[48,7168]{1,0:T(8,128)(2,1)}, bf16[48,7168]{1,0:T(8,128)(2,1)}, u32[]{:S(2)}, u32[]{:S(2)}) collective-permute-start(bf16[48,7168]{1,0:T(8,128)(2,1)} %collective-permute-done.1.refs_3_), channel_id=1, source_target_pairs={{0,4},{1,5},{2,6},{3,7},{4,0},{5,1},{6,2},{7,3},{8,12},{9,13},{10,... | collective-permute-start | bytes 2064392 | tf_op jit(solution)/shard_map/ppermute | solution.py:21
  48.6 39.0 %all-to-all-start = ((bf16[32,8,640]{2,1,0:T(8,128)(2,1)}), bf16[32,8,640]{2,1,0:T(8,128)(2,1)S(1)}, u32[]{:S(2)}, u32[]{:S(2)}) async-start(bf16[32,8,640]{2,1,0:T(8,128)(2,1)} %maximum_maximum_fusion), calls=%async_computation | async-start | bytes 655360 | tf_op jit(solution)/shard_map/all_to_all | solution.py:255
  87.6 18.8 %collective-permute-start.11 = (bf16[7168,128]{1,0:T(8,128)(2,1)}, bf16[7168,128]{1,0:T(8,128)(2,1)}, u32[]{:S(2)}, u32[]{:S(2)}) collective-permute-start(bf16[7168,128]{1,0:T(8,128)(2,1)} %refs_12_), channel_id=1, source_target_pairs={{0,1},{1,0},{2,3},{3,2},{4,5},{5,4},{6,7},{7,6},{8,9},{9,8},{10,11... | collective-permute-start | bytes 5505032 | tf_op jit(solution)/shard_map/ppermute | solution.py:21
  87.7 18.6 %collective-permute-start.12 = (bf16[7168,128]{1,0:T(8,128)(2,1)}, bf16[7168,128]{1,0:T(8,128)(2,1)}, u32[]{:S(2)}, u32[]{:S(2)}) collective-permute-start(bf16[7168,128]{1,0:T(8,128)(2,1)} %collective-permute-done.4.refs_10_), channel_id=1, source_target_pairs={{0,1},{1,0},{2,3},{3,2},{4,5},{5,4},{6,7},{7,6},{8,9},{9,8},{10,11... | collective-permute-start | bytes 5505032 | tf_op jit(solution)/shard_map/ppermute | solution.py:21
  88.1 18.2 %collective-permute-start.13 = (bf16[7168,128]{1,0:T(8,128)(2,1)}, bf16[7168,128]{1,0:T(8,128)(2,1)}, u32[]{:S(2)}, u32[]{:S(2)}) collective-permute-start(bf16[7168,128]{1,0:T(8,128)(2,1)} %collective-permute-done.8.refs_14_), channel_id=1, source_target_pairs={{0,1},{1,0},{2,3},{3,2},{4,5},{5,4},{6,7},{7,6},{8,9},{9,8},{10,11... | collective-permute-start | bytes 5505032 | tf_op jit(solution)/shard_map/ppermute | solution.py:21
  88.2 18.1 %collective-permute-start.10 = (bf16[48,7168]{1,0:T(8,128)(2,1)}, bf16[48,7168]{1,0:T(8,128)(2,1)}, u32[]{:S(2)}, u32[]{:S(2)}) collective-permute-start(bf16[48,7168]{1,0:T(8,128)(2,1)} %collective-permute-done.5.refs_2_), channel_id=1, source_target_pairs={{0,4},{1,5},{2,6},{3,7},{4,0},{5,1},{6,2},{7,3},{8,12},{9,13},{10,... | collective-permute-start | bytes 2064392 | tf_op jit(solution)/shard_map/ppermute | solution.py:21
  89.0 42.4 %collective-permute-start.16 = (bf16[256,3584]{1,0:T(8,128)(2,1)}, bf16[256,3584]{1,0:T(8,128)(2,1)}, u32[]{:S(2)}, u32[]{:S(2)}) collective-permute-start(bf16[256,3584]{1,0:T(8,128)(2,1)} %pad_maximum_fusion.own), channel_id=1, source_target_pairs={{0,2},{1,3},{2,0},{3,1},{4,6},{5,7},{6,4},{7,5},{8,10},{9,11},{10,... | collective-permute-start | bytes 5505032 | tf_op jit(solution)/shard_map/ppermute | solution.py:21
  117.4 14.0 %collective-permute-start.15 = (bf16[256,3584]{1,0:T(8,128)(2,1)S(1)}, bf16[256,3584]{1,0:T(8,128)(2,1)S(1)}, u32[]{:S(2)}, u32[]{:S(2)}) collective-permute-start(bf16[256,3584]{1,0:T(8,128)(2,1)S(1)} %copy-done.2), channel_id=1, source_target_pairs={{0,1},{1,0},{2,3},{3,2},{4,5},{5,4},{6,7},{7,6},{8,9},{9,8},{10,11... | collective-permute-start | bytes 5505032 | tf_op jit(solution)/shard_map/ppermute | solution.py:21
  117.5 13.9 %collective-permute-start.14 = (bf16[384,512]{1,0:T(8,128)(2,1)}, bf16[384,512]{1,0:T(8,128)(2,1)S(1)}, u32[]{:S(2)}, u32[]{:S(2)}) collective-permute-start(bf16[384,512]{1,0:T(8,128)(2,1)} %shard_map.132.mine), channel_id=1, source_target_pairs={{0,4},{1,5},{2,6},{3,7},{4,0},{5,1},{6,2},{7,3},{8,12},{9,13},{10,... | collective-permute-start | bytes 1179656 | tf_op jit(solution)/shard_map/ppermute | solution.py:21
  145.9 30.3 %collective-permute-start.20 = (bf16[96,1792]{1,0:T(8,128)(2,1)}, bf16[96,1792]{1,0:T(8,128)(2,1)S(1)}, u32[]{:S(2)}, u32[]{:S(2)}) collective-permute-start(bf16[96,1792]{1,0:T(8,128)(2,1)} %get-tuple-element.123), channel_id=1, source_target_pairs={{0,16},{1,17},{2,18},{3,19},{4,20},{5,21},{6,22},{7,23},{8,24},{9,... | collective-permute-start | bytes 1032200 | tf_op jit(solution)/shard_map/ppermute | solution.py:26
  149.9 29.7 %collective-permute-start.21 = (bf16[96,1792]{1,0:T(8,128)(2,1)}, bf16[96,1792]{1,0:T(8,128)(2,1)S(1)}, u32[]{:S(2)}, u32[]{:S(2)}) collective-permute-start(bf16[96,1792]{1,0:T(8,128)(2,1)} %get-tuple-element.124), channel_id=1, source_target_pairs={{0,8},{1,9},{2,10},{3,11},{4,12},{5,13},{6,14},{7,15},{8,16},{9,17... | collective-permute-start | bytes 1032200 | tf_op jit(solution)/shard_map/ppermute | solution.py:26
  188.5 38.3 %collective-permute-start.25 = (bf16[64,1792]{1,0:T(8,128)(2,1)}, bf16[64,1792]{1,0:T(8,128)(2,1)}, u32[]{:S(2)}, u32[]{:S(2)}) collective-permute-start(bf16[64,1792]{1,0:T(8,128)(2,1)} %get-tuple-element.142), channel_id=1, source_target_pairs={{0,4},{1,5},{2,6},{3,7},{4,0},{5,1},{6,2},{7,3},{8,12},{9,13},{10,... | collective-permute-start | bytes 688136 | tf_op jit(solution)/shard_map/ppermute | solution.py:21
  189.9 11.3 %collective-permute-start.22 = (bf16[96,1792]{1,0:T(8,128)(2,1)}, bf16[96,1792]{1,0:T(8,128)(2,1)}, u32[]{:S(2)}, u32[]{:S(2)}) collective-permute-start(bf16[96,1792]{1,0:T(8,128)(2,1)} %get-tuple-element.134), channel_id=1, source_target_pairs={{0,24},{1,25},{2,26},{3,27},{4,28},{5,29},{6,30},{7,31},{8,0},{9,1... | collective-permute-start | bytes 1032200 | tf_op jit(solution)/shard_map/ppermute | solution.py:26
  189.9 29.9 %collective-permute-start.23 = (bf16[96,1792]{1,0:T(8,128)(2,1)}, bf16[96,1792]{1,0:T(8,128)(2,1)}, u32[]{:S(2)}, u32[]{:S(2)}) collective-permute-start(bf16[96,1792]{1,0:T(8,128)(2,1)} %get-tuple-element.135), channel_id=1, source_target_pairs={{0,16},{1,17},{2,18},{3,19},{4,20},{5,21},{6,22},{7,23},{8,24},{9,... | collective-permute-start | bytes 1032200 | tf_op jit(solution)/shard_map/ppermute | solution.py:26
  190.0 30.0 %collective-permute-start.24 = (bf16[96,1792]{1,0:T(8,128)(2,1)}, bf16[96,1792]{1,0:T(8,128)(2,1)}, u32[]{:S(2)}, u32[]{:S(2)}) collective-permute-start(bf16[96,1792]{1,0:T(8,128)(2,1)} %get-tuple-element.136), channel_id=1, source_target_pairs={{0,8},{1,9},{2,10},{3,11},{4,12},{5,13},{6,14},{7,15},{8,16},{9,17... | collective-permute-start | bytes 1032200 | tf_op jit(solution)/shard_map/ppermute | solution.py:26
  (26 other events, 292.7 us)

commit v9 on v1

v9 whole, which is shorter than its diff:
```python
from functools import partial

import jax
import jax.numpy as jnp
from jax import lax
from jax.experimental import pallas as pl
from jax.experimental.pallas import tpu as pltpu
from jax.sharding import PartitionSpec as P

VDIM = 512
FF_WIN = 1024
SLOT_ROWS = 8
CORE, XBIT, YBIT = 1, 2, 4
VMEM_BYTES = 60 * 1024 * 1024


score_scale = 0.07216878364870323


def swap(value, bit):
    count = lax.axis_size("ep")
    return lax.ppermute(value, "ep", [(i, i ^ bit) for i in range(count)])


def shift(value, step):
    count = lax.axis_size("ep")
    return lax.ppermute(value, "ep", [(i, (i + step) % count) for i in range(count)])


def together(*values):
    return lax.optimization_barrier(values)


def pair_dot(rows, left, right):
    both = jnp.concatenate([left[...], right[...]], axis=1)
    return jnp.dot(rows, both, preferred_element_type=jnp.float32)


def gated(gate, up):
    return (gate / (1.0 + jnp.exp(-gate)) * up).astype(jnp.bfloat16)


def hidden_kernel(count, lead, *refs):
    units, weights = refs[:count], refs[count : count + 10]
    gate_o, gate_c, gate_x, gate_xc, up_o, up_c, up_xa, up_xca, up_xb, up_xcb = weights
    out, near_gate, far_gate, near_up, far_up = refs[count + 10 :]
    step = pl.program_id(0)

    @pl.when(step == 0)
    def _():
        for total in (near_gate, far_gate, near_up, far_up):
            total[...] = jnp.zeros_like(total)

    rows = jnp.concatenate([unit[...] for unit in units], axis=0)
    near_gate[...] += pair_dot(rows, gate_o, gate_c)
    near_up[...] += pair_dot(rows, up_o, up_c)
    far_gate[...] += pair_dot(rows, gate_x, gate_xc)

    @pl.when(step < lead)
    def _():
        far_up[...] += pair_dot(rows, up_xa, up_xca)

    @pl.when(step >= lead)
    def _():
        far_up[...] += pair_dot(rows, up_xb, up_xcb)

    @pl.when(step == pl.num_programs(0) - 1)
    def _():
        two = near_up.shape[1]
        out[:, :two] = gated(near_gate[...], near_up[...])
        out[:, two:] = gated(far_gate[...], far_up[...])


def hidden_units(units, weights, leads, rests, chunk):
    width, wide = weights[0].shape
    lead = leads[0].shape[0] // chunk
    count = sum(unit.shape[0] for unit in units)
    return pl.pallas_call(
        partial(hidden_kernel, len(units), lead),
        grid=(width // chunk,),
        in_specs=[pl.BlockSpec((unit.shape[0], chunk), lambda k: (0, k)) for unit in units]
        + [pl.BlockSpec((chunk, wide), lambda k: (k, 0)) for _ in weights]
        + [pl.BlockSpec((chunk, wide), lambda k: (jnp.minimum(k, lead - 1), 0)) for _ in leads]
        + [pl.BlockSpec((chunk, wide), lambda k: (jnp.maximum(k - lead, 0), 0)) for _ in rests],
        out_specs=pl.BlockSpec((count, 4 * wide), lambda k: (0, 0)),
        out_shape=jax.ShapeDtypeStruct((count, 4 * wide), jnp.bfloat16),
        scratch_shapes=[pltpu.VMEM((count, 2 * wide), jnp.float32)] * 4,
        compiler_params=pltpu.CompilerParams(vmem_limit_bytes=VMEM_BYTES),
        cost_estimate=pl.CostEstimate(
            flops=2 * count * width * wide * 8,
            bytes_accessed=2 * width * (count + wide * 8),
            transcendentals=0,
        ),
    )(*units, *weights, *leads, *rests)


def down_kernel(planes, mine, other, weight, *refs):
    blocks, outs = refs[:-planes], refs[-planes:]
    table = jnp.concatenate([block[...] for block in blocks], axis=0)
    count = mine.shape[0] // 2
    rows = count // planes
    joined = jnp.concatenate(
        [
            jnp.concatenate([mine[:count, :], other[count:, :]], axis=1),
            jnp.concatenate([mine[count:, :], other[:count, :]], axis=1),
        ],
        axis=0,
    )
    value = jnp.dot(joined, table, preferred_element_type=jnp.float32) * weight[...]
    for at, out in enumerate(outs):
        out[:rows, :] = value[at * rows : (at + 1) * rows].astype(out.dtype)
        out[rows:, :] = value[count + at * rows : count + (at + 1) * rows].astype(out.dtype)


def down_values(mine, other, weight, blocks, planes, chunk, offset):
    count, inner = mine.shape
    width = min(block.shape[1] for block in blocks)
    depth = blocks[0].shape[0]
    rows = count // planes
    kinds = [jnp.float32] * (planes - 1) + [jnp.bfloat16]
    return pl.pallas_call(
        partial(down_kernel, planes),
        grid=(width // chunk,),
        in_specs=[pl.BlockSpec((count, inner), lambda k: (0, 0))] * 2
        + [pl.BlockSpec((count, 1), lambda k: (0, 0))]
        + [
            pl.BlockSpec((depth, chunk), lambda k: (0, k))
            if block.shape[1] == width
            else pl.BlockSpec((depth, chunk), lambda k: (0, k + offset))
            for block in blocks
        ],
        out_specs=[pl.BlockSpec((rows, chunk), lambda k: (0, k)) for _ in kinds],
        out_shape=[jax.ShapeDtypeStruct((rows, width), kind) for kind in kinds],
        compiler_params=pltpu.CompilerParams(vmem_limit_bytes=VMEM_BYTES),
        cost_estimate=pl.CostEstimate(
            flops=2 * count * 2 * inner * width,
            bytes_accessed=2 * 2 * inner * width + 4 * count * width,
            transcendentals=0,
        ),
    )(mine, other, weight, *blocks)


def expert_rows(rows, outgoing, queries, gate_proj, up_proj, down_proj):
    n_ep = lax.axis_size("ep")
    split = FF_WIN // gate_proj.shape[1]
    planes = n_ep // split
    count, width = rows.shape
    chunk = width // 7

    cut = 2 * chunk
    upper = lax.axis_index("ep") // YBIT % 2
    span = width // 4
    half = count // 2

    gate_x, up_xa = swap(gate_proj, XBIT), swap(up_proj[:cut], XBIT)
    unit_1, peer_0, gate_c = shift(rows, split), swap(rows, YBIT), swap(gate_proj, CORE)
    unit_1, peer_0, gate_c, outgoing, up_proj, down_proj = together(
        unit_1, peer_0, gate_c, outgoing, up_proj, down_proj
    )
    up_b = up_proj[cut:]
    unit_2, peer_1, up_c = shift(unit_1, split), swap(unit_1, YBIT), swap(up_proj, CORE)
    keep = lax.dynamic_slice_in_dim(down_proj, 2 * upper * span, 2 * span, 1)
    unit_2, peer_1, gate_x, up_xa, up_c, up_b, keep, down_proj = together(
        unit_2, peer_1, gate_x, up_xa, up_c, up_b, keep, down_proj
    )
    unit_3, peer_2 = shift(unit_2, split), swap(unit_2, YBIT)
    up_xb, gate_xc = swap(up_b, XBIT), swap(gate_x, CORE)
    send = lax.dynamic_slice_in_dim(down_proj, (2 - 2 * upper) * span, 2 * span, 1)
    send_0, send_1 = send[:, :span], send[:, span:]
    unit_3, peer_2, up_xb, gate_xc, up_xa, keep, send_0, send_1 = together(
        unit_3, peer_2, up_xb, gate_xc, up_xa, keep, send_0, send_1
    )
    up_xca, up_xcb, keep_x = swap(up_xa, CORE), swap(up_xb, CORE), swap(keep, XBIT)
    last = (shift(peer_2[:half], split), swap(unit_3[half:], YBIT))
    up_xca, up_xcb, send_0, send_1, keep, *last = together(
        up_xca, up_xcb, send_0, send_1, keep, *last
    )
    down_y0, down_y1, keep_c = swap(send_0, YBIT), swap(send_1, YBIT), swap(keep, CORE)
    incoming = lax.all_to_all(outgoing, "ep", split_axis=0, concat_axis=0, tiled=True)

    units = (rows, unit_1, unit_2, unit_3, peer_0, peer_1, peer_2, *last)
    weights = (gate_proj, gate_c, gate_x, gate_xc, up_proj, up_c)
    hidden = hidden_units(units, weights, (up_xa, up_xca), (up_xb, up_xcb), chunk)
    hidden, keep_x, keep_c, down_y0, down_y1, incoming = together(
        hidden, keep_x, keep_c, down_y0, down_y1, incoming
    )
    other, down_yx0 = swap(hidden, YBIT), swap(down_y0, XBIT)
    keep_xc, down_yc0 = swap(keep_x, CORE), swap(down_y0, CORE)
    weight = row_weights(incoming, count, planes, split)
    down_yx0, down_y1 = together(down_yx0, down_y1)
    down_yx1, down_yc1 = swap(down_y1, XBIT), swap(down_y1, CORE)
    whole = (keep, keep_c, keep_x, keep_xc)
    parts = (
        (down_y0, down_yc0, down_yx0, swap(down_yx0, CORE)),
        (down_y1, down_yc1, down_yx1, swap(down_yx1, CORE)),
    )

    outs, others = [], []
    for at, part in enumerate(parts):
        values = down_values(hidden, other, weight, whole + part, planes, span // 2, 2 * at)
        total = values[-1]
        for step in range(planes - 2, -1, -1):
            total = shift(total, n_ep - split).astype(jnp.float32) + values[step]
            total = total.astype(jnp.bfloat16)
            if at == 0 and step == planes - 2:
                total, incoming, queries = together(total, incoming, queries)
        outs.append(total[:count])
        others.append(swap(total[count:], YBIT))
    low = jnp.concatenate(outs + others, axis=1)
    high = jnp.concatenate(others + outs, axis=1)
    return jnp.where(upper == 0, low, high), incoming, queries


def attend(query_part, cache_latents, cache_lens, handed, handed_mark):
    requests = query_part.shape[0]
    cache_scores = (
        jnp.einsum("qhl,qcl->qhc", query_part, cache_latents, preferred_element_type=jnp.float32)
        * score_scale
    )
    hand_scores = (
        jnp.einsum("qhl,rl->qhr", query_part, handed, preferred_element_type=jnp.float32)
        * score_scale
    )
    cache_mask = (
        jnp.arange(cache_latents.shape[1], dtype=jnp.int32)[None, :] < cache_lens[:, None]
    )[:, None, :]
    marks = jnp.arange(1, requests + 1, dtype=jnp.int32).astype(jnp.float32)
    hand_mask = (handed_mark[None, :] == marks[:, None])[:, None, :]
    cache_scores = jnp.where(cache_mask, cache_scores, -jnp.inf)
    hand_scores = jnp.where(hand_mask, hand_scores, -jnp.inf)
    top = jnp.maximum(jnp.max(cache_scores, axis=2), jnp.max(hand_scores, axis=2))[:, :, None]
    cache_expo = jnp.exp(cache_scores - top)
    hand_expo = jnp.exp(hand_scores - top)
    denom = (jnp.sum(cache_expo, axis=2) + jnp.sum(hand_expo, axis=2))[:, :, None]
    cache_prob = (cache_expo / denom).astype(jnp.bfloat16)
    hand_prob = (hand_expo / denom).astype(jnp.bfloat16)
    result = jnp.einsum(
        "qhc,qcv->qhv", cache_prob, cache_latents[:, :, :VDIM], preferred_element_type=jnp.float32
    )
    result = result + jnp.einsum(
        "qhr,rv->qhv", hand_prob, handed[:, :VDIM], preferred_element_type=jnp.float32
    )
    return result.astype(jnp.bfloat16)


def pieces(value):
    parts = []
    for _ in range(3):
        part = lax.reduce_precision(value, 8, 7)
        parts.append(part.astype(jnp.bfloat16))
        value = value - part
    return parts


def hand_over(prompt_latents, owners, requests, picks, gates, split):
    n_ep = lax.axis_size("ep")
    stretch, lat = prompt_latents.shape
    cap = 2 * stretch // n_ep
    places = jnp.arange(stretch, dtype=jnp.int32)
    earlier = (owners[:, None] == owners[None, :]) & (places[None, :] < places[:, None])
    target = owners * cap + jnp.sum(earlier.astype(jnp.int32), axis=1)
    slots = jnp.arange(n_ep * cap, dtype=jnp.int32)
    chosen = slots[:, None] == target[None, :]
    packed = jnp.dot(
        chosen.astype(jnp.bfloat16), prompt_latents, preferred_element_type=jnp.float32
    ).astype(jnp.bfloat16)
    mark = jnp.sum(jnp.where(chosen, requests[None, :] + 1, 0), axis=1).astype(jnp.bfloat16)
    planes = n_ep // split
    experts = jnp.arange(planes, dtype=jnp.int32)
    weights = jnp.sum(
        jnp.where(picks[None] == experts[:, None, None], gates[None], jnp.zeros_like(gates)[None]),
        axis=2,
    )
    lanes = weights.shape[1] // cap
    table = jnp.concatenate(
        [part.reshape(planes, 1, cap, lanes) for part in pieces(weights)], axis=3
    )
    table = jnp.broadcast_to(table, (planes, split, cap, 3 * lanes)).reshape(n_ep, cap, 3 * lanes)
    fill = -(lat + 1 + 3 * lanes) % 128
    outgoing = jnp.concatenate(
        [
            packed.reshape(n_ep, cap, lat),
            mark.reshape(n_ep, cap, 1),
            jnp.zeros((n_ep, cap, fill), jnp.bfloat16),
            table,
        ],
        axis=2,
    )
    return outgoing


def row_weights(incoming, count, planes, split):
    n_ep, cap, width = incoming.shape
    lanes = count // cap
    start = width - 3 * lanes
    here = lax.axis_index("ep")
    found = []
    for place in (here, here ^ YBIT):
        for step in range(planes):
            source = (place - step * split + n_ep) % n_ep
            tile = lax.dynamic_slice(incoming, (source, 0, start), (1, cap, 3 * lanes))
            tile = tile.astype(jnp.float32).reshape(cap, 3, lanes)
            found.append((tile[:, 0] + tile[:, 1] + tile[:, 2]).reshape(count, 1))
    return jnp.concatenate(found, axis=0)


def on_device(
    moe_rows,
    routes,
    route_gates,
    gate_proj,
    up_proj,
    down_proj,
    queries,
    cache_latents,
    cache_lens,
    prompt_latents,
    kv_owner,
    kv_request,
):
    sections, count, width = moe_rows.shape
    top = routes.shape[2]
    split = FF_WIN // gate_proj.shape[1]
    outgoing = hand_over(
        prompt_latents,
        kv_owner[:, 0],
        kv_request,
        routes.reshape(sections * count, top),
        route_gates.reshape(sections * count, top),
        split,
    )
    expert_out, incoming, queries = expert_rows(
        moe_rows.reshape(sections * count, width),
        outgoing,
        queries,
        gate_proj,
        up_proj,
        down_proj,
    )
    expert_out = expert_out.reshape(moe_rows.shape)
    lat = prompt_latents.shape[1]
    handed = incoming[:, :, :lat].reshape(-1, lat)
    handed_mark = incoming[:, :, lat].reshape(-1).astype(jnp.float32)
    attended = attend(queries, cache_latents, cache_lens, handed, handed_mark)
    return (expert_out, attended)


def solution(mesh):
    placed = (
        P("section", ("groups", "ep"), None),
        P("section", ("groups", "ep"), None),
        P("section", ("groups", "ep"), None),
        P(None, "ep"),
        P(None, "ep"),
        P("ep", None),
        P(("groups", "ep"), None, None),
        P(("groups", "ep"), None, None),
        P(("groups", "ep")),
        P(("groups", "ep"), None),
        P(("groups", "ep"), None),
        P(("groups", "ep")),
    )
    return jax.shard_map(
        on_device,
        mesh=mesh,
        in_specs=placed,
        out_specs=(P("section", ("groups", "ep"), None), P(("groups", "ep"), None, None)),
        check_vma=False,
    )
```

time: 322 us -> 246 us (0.76)
  waiting for transfers between devices: 234 us -> 153 us
  local copies, waits for them, and re-layouts: 24 us -> 16.6 us
  other arithmetic: 6.56 us -> 11.7 us
  starting transfers between devices: 24.1 us -> 28.1 us
    ppermute x16 -> x26, waiting for transfers between devices: 108 us -> 59.8 us  [swap(): return lax.ppermute(value, 'ep', [(i, i ^ bit) for i in range(count)])]
    all_to_all x1, waiting for transfers between devices: 16.4 us -> 0.01 us  [expert_rows(): lax.all_to_all(outgoing, 'ep', split_axis=0, concat_axis=0, tiled=True)]
    ppermute x6 -> x10, waiting for transfers between devices: 109 us -> 92.9 us  [shift(): lax.ppermute(value, 'ep', [(i, (i + step) % count) for i in range(count)])]
    unnamed x58 -> x40, local copies, waits for them, and re-layouts: 13.4 us -> 4.56 us
    ppermute x16 -> x26, starting transfers between devices: 15.2 us -> 17.4 us  [swap(): return lax.ppermute(value, 'ep', [(i, i ^ bit) for i in range(count)])]
    slice x2 -> x7, local copies, waits for them, and re-layouts: 4.38 us -> 6.56 us  [the longest x1 2.49 us: expert_rows(): up_b = up_proj[cut:]]
    pallas_call x1 -> x2, Pallas kernels: 10.3 us -> 11.9 us  [down_values(): pl.pallas_call(partial(down_kernel, planes), grid=(width // chunk,), in_s...]
  transfers between devices with their start and end apart: 23 -> 37, of which waited for: 14 -> 17; matrix products, arithmetic and copies ran while one was open for 8% -> 12% of each run, Pallas kernels for 4% -> 8%
where the time goes in v9:
time: 246 us; the launch traced here: 243 us
  waiting for transfers between devices  153 us (62%)
  starting transfers between devices  28.1 us (11%)
  Pallas kernels  26.5 us (11%)
  local copies, waits for them, and re-layouts  16.6 us (7%)
  other arithmetic  11.7 us (5%)
  matrix products  6.13 us (2%)
    ppermute x10, waiting for transfers between devices, shift(): lax.ppermute(value, 'ep', [(i, (i + step) % count) for i in range(count)])  92.9 us
    ppermute x26, waiting for transfers between devices, swap(): return lax.ppermute(value, 'ep', [(i, i ^ bit) for i in range(count)])  59.8 us
    ppermute x26, starting transfers between devices, swap(): return lax.ppermute(value, 'ep', [(i, i ^ bit) for i in range(count)])  17.4 us
    pallas_call x1, Pallas kernels, hidden_units(): pl.pallas_call(partial(hidden_kernel, len(units), lead), grid=(width // c...  14.6 us
    pallas_call x2, Pallas kernels, down_values(): pl.pallas_call(partial(down_kernel, planes), grid=(width // chunk,), in_s...  11.9 us
    ppermute x10, starting transfers between devices, shift(): lax.ppermute(value, 'ep', [(i, (i + step) % count) for i in range(count)])  5.71 us
    all_to_all x1, starting transfers between devices, expert_rows(): lax.all_to_all(outgoing, 'ep', split_axis=0, concat_axis=0, tiled=True)  5.02 us
  transfers between devices with their start and end apart: 37, of which 17 were waited for; matrix products, arithmetic and copies ran while one was open for 12% of the time, Pallas kernels for 8%

profile of v9, /device:TPU:16, one launch (start us, length us, event | category | flops | bytes accessed | tf_op | source)
XLA Modules:
  0.0 242.8 jit_solution(9638844722910213982)
XLA Ops:
  11.4 12.4 %collective-permute-done.refs_1_ = bf16[64,7168]{1,0:T(8,128)(2,1)} collective-permute-done((bf16[64,7168]{1,0:T(8,128)(2,1)}, bf16[64,7168]{1,0:T(8,128)(2,1)}, u32[]{:S(2)}, u32[]{:S(2)}) %collective-permute-start) | collective-permute-done | bytes 917536 | tf_op jit(solution)/shard_map/ppermute | solution.py:27
  29.6 2.5 %slice.115 = bf16[5120,128]{1,0:T(8,128)(2,1)} slice(bf16[7168,128]{1,0:T(8,128)(2,1)} %refs_13_), slice={[2048:7168], [0:128]} | slice | bytes 2621440 | tf_op jit(solution)/shard_map/slice | solution.py:160
  33.1 24.2 %collective-permute-done.6.refs_15_ = bf16[2048,128]{1,0:T(8,128)(2,1)} collective-permute-done((bf16[2048,128]{1,0:T(8,128)(2,1)S(1)}, bf16[2048,128]{1,0:T(8,128)(2,1)}, u32[]{:S(2)}, u32[]{:S(2)}) %collective-permute-start.6) | collective-permute-done | bytes 524320 | tf_op jit(solution)/shard_map/ppermute | solution.py:22
  60.5 21.1 %collective-permute-done.8.refs_3_ = bf16[64,7168]{1,0:T(8,128)(2,1)} collective-permute-done((bf16[64,7168]{1,0:T(8,128)(2,1)}, bf16[64,7168]{1,0:T(8,128)(2,1)}, u32[]{:S(2)}, u32[]{:S(2)}) %collective-permute-start.8) | collective-permute-done | bytes 917536 | tf_op jit(solution)/shard_map/ppermute | solution.py:27
  81.6 7.2 %collective-permute-done.10.refs_17_ = bf16[5120,128]{1,0:T(8,128)(2,1)} collective-permute-done((bf16[5120,128]{1,0:T(8,128)(2,1)}, bf16[5120,128]{1,0:T(8,128)(2,1)}, u32[]{:S(2)}, u32[]{:S(2)}) %collective-permute-start.10) | collective-permute-done | bytes 1310752 | tf_op jit(solution)/shard_map/ppermute | solution.py:22
  93.9 9.0 %collective-permute-done.14.refs_7_ = bf16[32,7168]{1,0:T(8,128)(2,1)S(1)} collective-permute-done((bf16[32,7168]{1,0:T(8,128)(2,1)S(1)}, bf16[32,7168]{1,0:T(8,128)(2,1)S(1)}, u32[]{:S(2)}, u32[]{:S(2)}) %collective-permute-start.14) | collective-permute-done | bytes 458784 | tf_op jit(solution)/shard_map/ppermute | solution.py:27
  104.8 5.0 %all-to-all-start = ((bf16[32,8,640]{2,1,0:T(8,128)(2,1)}), bf16[32,8,640]{2,1,0:T(8,128)(2,1)S(1)}, u32[]{:S(2)}, u32[]{:S(2)}) async-start(bf16[32,8,640]{2,1,0:T(8,128)(2,1)} %pad_maximum_fusion), calls=%async_computation | async-start | bytes 655360 | tf_op jit(solution)/shard_map/all_to_all | solution.py:179
  112.0 14.6 %shard_map.131.mine = bf16[512,512]{1,0:T(8,128)(2,1)} custom-call(bf16[64,7168]{1,0:T(8,128)(2,1)} %bitcast.39, bf16[64,7168]{1,0:T(8,128)(2,1)} %collective-permute-done.refs_1_, bf16[64,7168]{1,0:T(8,128)(2,1)} %collective-permute-done.3.refs_2_, bf16[64,7168]{1,0:T(8,128)(2,1)} %collective-permute-done.8.refs_3_, ...), custom_call_target="tpu_custom_call" | custom-call | flops 7516192768 | bytes 22020096 | tf_op jit(solution)/shard_map/pallas_call | solution.py:78
  126.6 9.1 %collective-permute-done.19.refs_4_ = bf16[128,1792]{1,0:T(8,128)(2,1)} collective-permute-done((bf16[128,1792]{1,0:T(8,128)(2,1)S(1)}, bf16[128,1792]{1,0:T(8,128)(2,1)}, u32[]{:S(2)}, u32[]{:S(2)}) %collective-permute-start.19) | collective-permute-done | bytes 458784 | tf_op jit(solution)/shard_map/ppermute | solution.py:22
  138.8 9.2 %collective-permute-done.23.refs_6_ = bf16[128,1792]{1,0:T(8,128)(2,1)} collective-permute-done((bf16[128,1792]{1,0:T(8,128)(2,1)}, bf16[128,1792]{1,0:T(8,128)(2,1)}, u32[]{:S(2)}, u32[]{:S(2)}) %collective-permute-start.23) | collective-permute-done | bytes 458784 | tf_op jit(solution)/shard_map/ppermute | solution.py:22
  150.1 1.6 collective-permute-start.29
  152.6 5.9 %shard_map.132 = (f32[128,1792]{1,0:T(8,128)}, f32[128,1792]{1,0:T(8,128)}, f32[128,1792]{1,0:T(8,128)}, bf16[128,1792]{1,0:T(8,128)(2,1)}) custom-call(bf16[512,512]{1,0:T(8,128)(2,1)} %shard_map.131.mine, bf16[512,512]{1,0:T(8,128)(2,1)} %copy-done.14, f32[512,1]{1,0:T(8,128)} %copy.58.weight, bf16[128,3584]{1,0:T(8,128)(2,1)} %constant_dynamic-slice_fusion.9.refs_0_, ...), custom_call_target="tpu_custom_call" | custom-call | flops 1879048192 | bytes 7340032 | tf_op jit(solution)/shard_map/pallas_call | solution.py:121
  160.3 3.0 %collective-permute-done.29.refs_6_ = bf16[128,1792]{1,0:T(8,128)(2,1)} collective-permute-done((bf16[128,1792]{1,0:T(8,128)(2,1)}, bf16[128,1792]{1,0:T(8,128)(2,1)}, u32[]{:S(2)}, u32[]{:S(2)}) %collective-permute-start.29) | collective-permute-done | bytes 458784 | tf_op jit(solution)/shard_map/ppermute | solution.py:22
  163.4 8.1 %collective-permute-done.25 = bf16[128,1792]{1,0:T(8,128)(2,1)S(1)} collective-permute-done((bf16[128,1792]{1,0:T(8,128)(2,1)}, bf16[128,1792]{1,0:T(8,128)(2,1)S(1)}, u32[]{:S(2)}, u32[]{:S(2)}) %collective-permute-start.25) | collective-permute-done | bytes 458784 | tf_op jit(solution)/shard_map/ppermute | solution.py:27
  171.4 2.0 add_convert_fusion.6
  176.0 6.0 %shard_map.133 = (f32[128,1792]{1,0:T(8,128)}, f32[128,1792]{1,0:T(8,128)}, f32[128,1792]{1,0:T(8,128)}, bf16[128,1792]{1,0:T(8,128)(2,1)}) custom-call(bf16[512,512]{1,0:T(8,128)(2,1)} %shard_map.131.mine, bf16[512,512]{1,0:T(8,128)(2,1)} %copy-done.14, f32[512,1]{1,0:T(8,128)} %copy.58.weight, bf16[128,3584]{1,0:T(8,128)(2,1)} %constant_dynamic-slice_fusion.9.refs_0_, ...), custom_call_target="tpu_custom_call" | custom-call | flops 1879048192 | bytes 7340032 | tf_op jit(solution)/shard_map/pallas_call | solution.py:121
  182.6 1.7 collective-permute-start.26
  185.7 1.7 fusion.35
  190.0 7.2 %collective-permute-done.31 = bf16[128,1792]{1,0:T(8,128)(2,1)} collective-permute-done((bf16[128,1792]{1,0:T(8,128)(2,1)}, bf16[128,1792]{1,0:T(8,128)(2,1)}, u32[]{:S(2)}, u32[]{:S(2)}) %collective-permute-start.31) | collective-permute-done | bytes 458784 | tf_op jit(solution)/shard_map/ppermute | solution.py:27
  198.5 8.6 %collective-permute-done.26 = bf16[128,1792]{1,0:T(8,128)(2,1)} collective-permute-done((bf16[128,1792]{1,0:T(8,128)(2,1)}, bf16[128,1792]{1,0:T(8,128)(2,1)}, u32[]{:S(2)}, u32[]{:S(2)}) %collective-permute-start.26) | collective-permute-done | bytes 458784 | tf_op jit(solution)/shard_map/ppermute | solution.py:27
  208.4 8.5 %collective-permute-done.32 = bf16[128,1792]{1,0:T(8,128)(2,1)S(1)} collective-permute-done((bf16[128,1792]{1,0:T(8,128)(2,1)S(1)}, bf16[128,1792]{1,0:T(8,128)(2,1)S(1)}, u32[]{:S(2)}, u32[]{:S(2)}) %collective-permute-start.32) | collective-permute-done | bytes 458784 | tf_op jit(solution)/shard_map/ppermute | solution.py:27
  217.0 9.7 %collective-permute-done.27 = bf16[128,1792]{1,0:T(8,128)(2,1)S(1)} collective-permute-done((bf16[128,1792]{1,0:T(8,128)(2,1)S(1)}, bf16[128,1792]{1,0:T(8,128)(2,1)S(1)}, u32[]{:S(2)}, u32[]{:S(2)}) %collective-permute-start.27) | collective-permute-done | bytes 458784 | tf_op jit(solution)/shard_map/ppermute | solution.py:27
  226.9 8.3 %collective-permute-done.33 = bf16[128,1792]{1,0:T(8,128)(2,1)S(1)} collective-permute-done((bf16[128,1792]{1,0:T(8,128)(2,1)S(1)}, bf16[128,1792]{1,0:T(8,128)(2,1)S(1)}, u32[]{:S(2)}, u32[]{:S(2)}) %collective-permute-start.33) | collective-permute-done | bytes 458784 | tf_op jit(solution)/shard_map/ppermute | solution.py:27
  236.9 4.8 %collective-permute-done.35 = bf16[64,1792]{1,0:T(8,128)(2,1)S(1)} collective-permute-done((bf16[64,1792]{1,0:T(8,128)(2,1)S(1)}, bf16[64,1792]{1,0:T(8,128)(2,1)S(1)}, u32[]{:S(2)}, u32[]{:S(2)}) %collective-permute-start.35) | collective-permute-done | bytes 229408 | tf_op jit(solution)/shard_map/ppermute | solution.py:22
  (165 shorter events, 50.4 us)
Async XLA Ops:
  0.6 24.4 %collective-permute-start.2 = (bf16[7168,128]{1,0:T(8,128)(2,1)}, bf16[7168,128]{1,0:T(8,128)(2,1)}, u32[]{:S(2)}, u32[]{:S(2)}) collective-permute-start(bf16[7168,128]{1,0:T(8,128)(2,1)} %refs_9_.1), channel_id=1, source_target_pairs={{0,1},{1,0},{2,3},{3,2},{4,5},{5,4},{6,7},{7,6},{8,9},{9,8},{10,11... | collective-permute-start | bytes 5505032 | tf_op jit(solution)/shard_map/ppermute | solution.py:22
  0.7 23.1 %collective-permute-start = (bf16[64,7168]{1,0:T(8,128)(2,1)}, bf16[64,7168]{1,0:T(8,128)(2,1)}, u32[]{:S(2)}, u32[]{:S(2)}) collective-permute-start(bf16[64,7168]{1,0:T(8,128)(2,1)} %bitcast.37), channel_id=1, source_target_pairs={{0,8},{1,9},{2,10},{3,11},{4,12},{5,13},{6,14},{7,15},{8,16},{9,17... | collective-permute-start | bytes 2752520 | tf_op jit(solution)/shard_map/ppermute | solution.py:27
  2.4 22.7 %collective-permute-start.1 = (bf16[64,7168]{1,0:T(8,128)(2,1)}, bf16[64,7168]{1,0:T(8,128)(2,1)}, u32[]{:S(2)}, u32[]{:S(2)}) collective-permute-start(bf16[64,7168]{1,0:T(8,128)(2,1)} %bitcast.38), channel_id=1, source_target_pairs={{0,4},{1,5},{2,6},{3,7},{4,0},{5,1},{6,2},{7,3},{8,12},{9,13},{10,... | collective-permute-start | bytes 2752520 | tf_op jit(solution)/shard_map/ppermute | solution.py:22
  3.9 53.4 %collective-permute-start.5 = (bf16[7168,128]{1,0:T(8,128)(2,1)}, bf16[7168,128]{1,0:T(8,128)(2,1)}, u32[]{:S(2)}, u32[]{:S(2)}) collective-permute-start(bf16[7168,128]{1,0:T(8,128)(2,1)} %refs_9_.1), channel_id=1, source_target_pairs={{0,2},{1,3},{2,0},{3,1},{4,6},{5,7},{6,4},{7,5},{8,10},{9,11},{10,... | collective-permute-start | bytes 5505032 | tf_op jit(solution)/shard_map/ppermute | solution.py:22
  25.1 32.1 %collective-permute-start.7 = (bf16[7168,128]{1,0:T(8,128)(2,1)}, bf16[7168,128]{1,0:T(8,128)(2,1)}, u32[]{:S(2)}, u32[]{:S(2)}) collective-permute-start(bf16[7168,128]{1,0:T(8,128)(2,1)} %refs_13_), channel_id=1, source_target_pairs={{0,1},{1,0},{2,3},{3,2},{4,5},{5,4},{6,7},{7,6},{8,9},{9,8},{10,11... | collective-permute-start | bytes 5505032 | tf_op jit(solution)/shard_map/ppermute | solution.py:22
  25.1 32.1 %collective-permute-start.3 = (bf16[64,7168]{1,0:T(8,128)(2,1)}, bf16[64,7168]{1,0:T(8,128)(2,1)}, u32[]{:S(2)}, u32[]{:S(2)}) collective-permute-start(bf16[64,7168]{1,0:T(8,128)(2,1)} %collective-permute-done.refs_1_), channel_id=1, source_target_pairs={{0,8},{1,9},{2,10},{3,11},{4,12},{5,13},{6,14},{7,15},{8,16},{9,17... | collective-permute-start | bytes 2752520 | tf_op jit(solution)/shard_map/ppermute | solution.py:27
  25.4 31.8 %collective-permute-start.4 = (bf16[64,7168]{1,0:T(8,128)(2,1)}, bf16[64,7168]{1,0:T(8,128)(2,1)}, u32[]{:S(2)}, u32[]{:S(2)}) collective-permute-start(bf16[64,7168]{1,0:T(8,128)(2,1)} %collective-permute-done.refs_1_), channel_id=1, source_target_pairs={{0,4},{1,5},{2,6},{3,7},{4,0},{5,1},{6,2},{7,3},{8,12},{9,13},{10,... | collective-permute-start | bytes 2752520 | tf_op jit(solution)/shard_map/ppermute | solution.py:22
  28.0 29.2 %collective-permute-start.6 = (bf16[2048,128]{1,0:T(8,128)(2,1)S(1)}, bf16[2048,128]{1,0:T(8,128)(2,1)}, u32[]{:S(2)}, u32[]{:S(2)}) collective-permute-start(bf16[2048,128]{1,0:T(8,128)(2,1)S(1)} %slice.114), channel_id=1, source_target_pairs={{0,2},{1,3},{2,0},{3,1},{4,6},{5,7},{6,4},{7,5},{8,10},{9,11},{10,... | collective-permute-start | bytes 1572872 | tf_op jit(solution)/shard_map/ppermute | solution.py:22
  57.2 31.6 %collective-permute-start.11 = (bf16[7168,128]{1,0:T(8,128)(2,1)}, bf16[7168,128]{1,0:T(8,128)(2,1)}, u32[]{:S(2)}, u32[]{:S(2)}) collective-permute-start(bf16[7168,128]{1,0:T(8,128)(2,1)} %collective-permute-done.5.refs_11_), channel_id=1, source_target_pairs={{0,1},{1,0},{2,3},{3,2},{4,5},{5,4},{6,7},{7,6},{8,9},{9,8},{10,11... | collective-permute-start | bytes 5505032 | tf_op jit(solution)/shard_map/ppermute | solution.py:22
  57.3 31.5 %collective-permute-start.10 = (bf16[5120,128]{1,0:T(8,128)(2,1)}, bf16[5120,128]{1,0:T(8,128)(2,1)}, u32[]{:S(2)}, u32[]{:S(2)}) collective-permute-start(bf16[5120,128]{1,0:T(8,128)(2,1)} %slice.115), channel_id=1, source_target_pairs={{0,2},{1,3},{2,0},{3,1},{4,6},{5,7},{6,4},{7,5},{8,10},{9,11},{10,... | collective-permute-start | bytes 3932168 | tf_op jit(solution)/shard_map/ppermute | solution.py:22
  58.9 22.7 %collective-permute-start.8 = (bf16[64,7168]{1,0:T(8,128)(2,1)}, bf16[64,7168]{1,0:T(8,128)(2,1)}, u32[]{:S(2)}, u32[]{:S(2)}) collective-permute-start(bf16[64,7168]{1,0:T(8,128)(2,1)} %collective-permute-done.3.refs_2_), channel_id=1, source_target_pairs={{0,8},{1,9},{2,10},{3,11},{4,12},{5,13},{6,14},{7,15},{8,16},{9,17... | collective-permute-start | bytes 2752520 | tf_op jit(solution)/shard_map/ppermute | solution.py:27
  59.2 22.5 %collective-permute-start.9 = (bf16[64,7168]{1,0:T(8,128)(2,1)}, bf16[64,7168]{1,0:T(8,128)(2,1)}, u32[]{:S(2)}, u32[]{:S(2)}) collective-permute-start(bf16[64,7168]{1,0:T(8,128)(2,1)} %collective-permute-done.3.refs_2_), channel_id=1, source_target_pairs={{0,4},{1,5},{2,6},{3,7},{4,0},{5,1},{6,2},{7,3},{8,12},{9,13},{10,... | collective-permute-start | bytes 2752520 | tf_op jit(solution)/shard_map/ppermute | solution.py:22
  88.8 16.0 %collective-permute-start.13 = (bf16[5120,128]{1,0:T(8,128)(2,1)}, bf16[5120,128]{1,0:T(8,128)(2,1)}, u32[]{:S(2)}, u32[]{:S(2)}) collective-permute-start(bf16[5120,128]{1,0:T(8,128)(2,1)} %collective-permute-done.10.refs_17_), channel_id=1, source_target_pairs={{0,1},{1,0},{2,3},{3,2},{4,5},{5,4},{6,7},{7,6},{8,9},{9,8},{10,11... | collective-permute-start | bytes 3932168 | tf_op jit(solution)/shard_map/ppermute | solution.py:22
  88.8 15.2 %collective-permute-start.12 = (bf16[2048,128]{1,0:T(8,128)(2,1)}, bf16[2048,128]{1,0:T(8,128)(2,1)}, u32[]{:S(2)}, u32[]{:S(2)}) collective-permute-start(bf16[2048,128]{1,0:T(8,128)(2,1)} %collective-permute-done.6.refs_15_), channel_id=1, source_target_pairs={{0,1},{1,0},{2,3},{3,2},{4,5},{5,4},{6,7},{7,6},{8,9},{9,8},{10,11... | collective-permute-start | bytes 1572872 | tf_op jit(solution)/shard_map/ppermute | solution.py:22
  92.4 34.2 %collective-permute-start.16 = (bf16[128,3584]{1,0:T(8,128)(2,1)}, bf16[128,3584]{1,0:T(8,128)(2,1)S(1)}, u32[]{:S(2)}, u32[]{:S(2)}) collective-permute-start(bf16[128,3584]{1,0:T(8,128)(2,1)} %constant_dynamic-slice_fusion.9.refs_0_), channel_id=1, source_target_pairs={{0,2},{1,3},{2,0},{3,1},{4,6},{5,7},{6,4},{7,5},{8,10},{9,11},{10,... | collective-permute-start | bytes 2752520 | tf_op jit(solution)/shard_map/ppermute | solution.py:22
  104.8 30.9 %collective-permute-start.17 = (bf16[128,3584]{1,0:T(8,128)(2,1)}, bf16[128,3584]{1,0:T(8,128)(2,1)}, u32[]{:S(2)}, u32[]{:S(2)}) collective-permute-start(bf16[128,3584]{1,0:T(8,128)(2,1)} %constant_dynamic-slice_fusion.9.refs_0_), channel_id=1, source_target_pairs={{0,1},{1,0},{2,3},{3,2},{4,5},{5,4},{6,7},{7,6},{8,9},{9,8},{10,11... | collective-permute-start | bytes 2752520 | tf_op jit(solution)/shard_map/ppermute | solution.py:22
  104.8 21.7 %all-to-all-start = ((bf16[32,8,640]{2,1,0:T(8,128)(2,1)}), bf16[32,8,640]{2,1,0:T(8,128)(2,1)S(1)}, u32[]{:S(2)}, u32[]{:S(2)}) async-start(bf16[32,8,640]{2,1,0:T(8,128)(2,1)} %pad_maximum_fusion), calls=%async_computation | async-start | bytes 655360 | tf_op jit(solution)/shard_map/all_to_all | solution.py:179
  109.9 16.7 %collective-permute-start.18 = (bf16[128,1792]{1,0:T(8,128)(2,1)S(1)}, bf16[128,1792]{1,0:T(8,128)(2,1)}, u32[]{:S(2)}, u32[]{:S(2)}) collective-permute-start(bf16[128,1792]{1,0:T(8,128)(2,1)S(1)} %copy-done.9), channel_id=1, source_target_pairs={{0,4},{1,5},{2,6},{3,7},{4,0},{5,1},{6,2},{7,3},{8,12},{9,13},{10,... | collective-permute-start | bytes 1376264 | tf_op jit(solution)/shard_map/ppermute | solution.py:22
  111.4 24.3 %collective-permute-start.19 = (bf16[128,1792]{1,0:T(8,128)(2,1)S(1)}, bf16[128,1792]{1,0:T(8,128)(2,1)}, u32[]{:S(2)}, u32[]{:S(2)}) collective-permute-start(bf16[128,1792]{1,0:T(8,128)(2,1)S(1)} %get-tuple-element.77), channel_id=1, source_target_pairs={{0,4},{1,5},{2,6},{3,7},{4,0},{5,1},{6,2},{7,3},{8,12},{9,13},{10,... | collective-permute-start | bytes 1376264 | tf_op jit(solution)/shard_map/ppermute | solution.py:22
  182.0 15.3 %collective-permute-start.31 = (bf16[128,1792]{1,0:T(8,128)(2,1)}, bf16[128,1792]{1,0:T(8,128)(2,1)}, u32[]{:S(2)}, u32[]{:S(2)}) collective-permute-start(bf16[128,1792]{1,0:T(8,128)(2,1)} %get-tuple-element.92), channel_id=1, source_target_pairs={{0,24},{1,25},{2,26},{3,27},{4,28},{5,29},{6,30},{7,31},{8,0},{9,1... | collective-permute-start | bytes 1376264 | tf_op jit(solution)/shard_map/ppermute | solution.py:27
  182.6 24.5 %collective-permute-start.26 = (bf16[128,1792]{1,0:T(8,128)(2,1)}, bf16[128,1792]{1,0:T(8,128)(2,1)}, u32[]{:S(2)}, u32[]{:S(2)}) collective-permute-start(bf16[128,1792]{1,0:T(8,128)(2,1)} %add_convert_fusion.6), channel_id=1, source_target_pairs={{0,24},{1,25},{2,26},{3,27},{4,28},{5,29},{6,30},{7,31},{8,0},{9,1... | collective-permute-start | bytes 1376264 | tf_op jit(solution)/shard_map/ppermute | solution.py:27
  198.5 18.4 %collective-permute-start.32 = (bf16[128,1792]{1,0:T(8,128)(2,1)S(1)}, bf16[128,1792]{1,0:T(8,128)(2,1)S(1)}, u32[]{:S(2)}, u32[]{:S(2)}) collective-permute-start(bf16[128,1792]{1,0:T(8,128)(2,1)S(1)} %add_convert_fusion.3), channel_id=1, source_target_pairs={{0,24},{1,25},{2,26},{3,27},{4,28},{5,29},{6,30},{7,31},{8,0},{9,1... | collective-permute-start | bytes 1376264 | tf_op jit(solution)/shard_map/ppermute | solution.py:27
  208.3 18.4 %collective-permute-start.27 = (bf16[128,1792]{1,0:T(8,128)(2,1)S(1)}, bf16[128,1792]{1,0:T(8,128)(2,1)S(1)}, u32[]{:S(2)}, u32[]{:S(2)}) collective-permute-start(bf16[128,1792]{1,0:T(8,128)(2,1)S(1)} %add_convert_fusion.5), channel_id=1, source_target_pairs={{0,24},{1,25},{2,26},{3,27},{4,28},{5,29},{6,30},{7,31},{8,0},{9,1... | collective-permute-start | bytes 1376264 | tf_op jit(solution)/shard_map/ppermute | solution.py:27
  216.9 18.3 %collective-permute-start.33 = (bf16[128,1792]{1,0:T(8,128)(2,1)S(1)}, bf16[128,1792]{1,0:T(8,128)(2,1)S(1)}, u32[]{:S(2)}, u32[]{:S(2)}) collective-permute-start(bf16[128,1792]{1,0:T(8,128)(2,1)S(1)} %add_convert_fusion.2), channel_id=1, source_target_pairs={{0,24},{1,25},{2,26},{3,27},{4,28},{5,29},{6,30},{7,31},{8,0},{9,1... | collective-permute-start | bytes 1376264 | tf_op jit(solution)/shard_map/ppermute | solution.py:27
  (32 other events, 592.0 us)

commit v10 on v8

--- a/solution.py
+++ b/solution.py
@@ -112,14 +112,14 @@
     )(*units, *weights)
 
 
-def down_kernel(planes, mine, other, own, own_c, side, side_c, *outs):
+def down_kernel(mine, other, own, own_c, side, side_c, *outs):
     deep = own.shape[0] // 2
     parts = (own, own_c, side, side_c)
     table = jnp.concatenate(
         [part[:deep, :] for part in parts] + [part[deep:, :] for part in parts], axis=0
     )
     count = mine.shape[0] // 2
-    rows = count // planes
+    rows = count // len(outs)
     joined = jnp.concatenate(
         [
             jnp.concatenate([mine[:count, :], other[count:, :]], axis=1),
@@ -128,44 +128,30 @@
         axis=0,
     )
     value = jnp.dot(joined, table, preferred_element_type=jnp.float32).astype(jnp.bfloat16)
-
-    def put(targets):
-        for at, out in enumerate(targets):
-            out[:rows, :] = value[at * rows : (at + 1) * rows]
-            out[rows:, :] = value[count + at * rows : count + (at + 1) * rows]
-
-    first = pl.program_id(0) < pl.num_programs(0) // 2
-
-    @pl.when(first)
-    def _():
-        put(outs[:planes])
-
-    @pl.when(jnp.logical_not(first))
-    def _():
-        put(outs[planes:])
-
-
-def down_values(mine, other, tables, planes, chunk):
+    for at, out in enumerate(outs):
+        out[:rows, :] = value[at * rows : (at + 1) * rows]
+        out[rows:, :] = value[count + at * rows : count + (at + 1) * rows]
+
+
+def down_values(mine, other, own, side, planes, chunk, offset):
     count, inner = mine.shape
-    deep, width = tables[0].shape
+    deep, width = side[0].shape
     rows = count // planes
-    steps = width // chunk
-    half = steps // 2
     return pl.pallas_call(
-        partial(down_kernel, planes),
-        grid=(steps,),
+        down_kernel,
+        grid=(width // chunk,),
         in_specs=[pl.BlockSpec((count, inner), lambda k: (0, 0))] * 2
-        + [pl.BlockSpec((deep, chunk), lambda k: (0, k)) for _ in tables],
-        out_specs=[pl.BlockSpec((rows, chunk), lambda k: (0, jnp.minimum(k, half - 1)))] * planes
-        + [pl.BlockSpec((rows, chunk), lambda k: (0, jnp.maximum(k - half, 0)))] * planes,
-        out_shape=[jax.ShapeDtypeStruct((rows, width // 2), jnp.bfloat16)] * (2 * planes),
+        + [pl.BlockSpec((deep, chunk), lambda k: (0, k + offset)) for _ in own]
+        + [pl.BlockSpec((deep, chunk), lambda k: (0, k)) for _ in side],
+        out_specs=[pl.BlockSpec((rows, chunk), lambda k: (0, k))] * planes,
+        out_shape=[jax.ShapeDtypeStruct((rows, width), jnp.bfloat16)] * planes,
         compiler_params=pltpu.CompilerParams(vmem_limit_bytes=VMEM_BYTES),
         cost_estimate=pl.CostEstimate(
             flops=2 * count * 2 * inner * width,
             bytes_accessed=8 * deep * width + 2 * count * width,
             transcendentals=0,
         ),
-    )(mine, other, *tables)
+    )(mine, other, *own, *side)
 
 
 def combine_kernel(high, low, *refs):
@@ -238,11 +224,11 @@
     chosen = (rank[:, None, :] == at[None, :, None]) & named[:, None, :]
     chosen = chosen.astype(jnp.bfloat16)
 
-    own_0, out_1, out_2, out_3 = packs(chosen.reshape(planes * slots, count), rows, planes, span)
-    own_0, out_1, out_3, latents, owners, requests, down_proj = together(
-        own_0, out_1, out_3, latents, owners, requests, down_proj
-    )
-    own_1, own_3, peer_0 = shift(out_1, split), shift(out_3, 3 * split), swap(own_0, YBIT)
+    pack_0, out_1, out_2, out_3 = packs(chosen.reshape(planes * slots, count), rows, planes, span)
+    pack_0, out_1, out_3, latents, owners, requests, down_proj = together(
+        pack_0, out_1, out_3, latents, owners, requests, down_proj
+    )
+    own_1, own_3, peer_0 = shift(out_1, split), shift(out_3, 3 * split), swap(pack_0, YBIT)
     send = lax.dynamic_slice_in_dim(down_proj, (2 - 2 * upper) * span, 2 * span, 1)
     down_y = swap(send, YBIT)
     outgoing = hand_over(latents, owners, requests)
@@ -252,36 +238,32 @@
     )
     own_2, peer_1, peer_3 = shift(out_2, 2 * split), swap(own_1, YBIT), swap(own_3, YBIT)
     up_x, gate_c = swap(up_proj, XBIT), swap(gate_proj, CORE)
-    incoming = lax.all_to_all(outgoing, "ep", split_axis=0, concat_axis=0, tiled=True)
     keep = lax.dynamic_slice_in_dim(down_proj, 2 * upper * span, 2 * span, 1)
     own = jnp.concatenate([keep, down_y], axis=0)
-
-    own_2, peer_1, peer_3, up_x, gate_x, gate_c, up_proj, own, incoming = together(
-        own_2, peer_1, peer_3, up_x, gate_x, gate_c, up_proj, own, incoming
-    )
-    peer_2, side = swap(own_2, YBIT), swap(own, XBIT)
+    own_0, rest = own[:, :span], own[:, span:]
+
+    own_2, peer_1, peer_3, up_x, gate_x, gate_c, up_proj, own, own_0, rest = together(
+        own_2, peer_1, peer_3, up_x, gate_x, gate_c, up_proj, own, own_0, rest
+    )
+    peer_2, side_0 = swap(own_2, YBIT), swap(own_0, XBIT)
     up_c, gate_xc, up_xc = swap(up_proj, CORE), swap(gate_x, CORE), swap(up_x, CORE)
+    incoming = lax.all_to_all(outgoing, "ep", split_axis=0, concat_axis=0, tiled=True)
 
     peer_2, up_c, gate_xc, up_xc = together(peer_2, up_c, gate_xc, up_xc)
-    units = (own_0, own_1, own_2, own_3, peer_0, peer_1, peer_2, peer_3)
+    own_c = swap(own, CORE)
+    units = (pack_0, own_1, own_2, own_3, peer_0, peer_1, peer_2, peer_3)
     weights = (gate_proj, gate_c, gate_x, gate_xc, up_proj, up_c, up_x, up_xc)
     hidden = hidden_units(units, weights, chunk)
-    hidden, own, picks, gates = together(hidden, own, picks, gates)
-    other, own_c = swap(hidden, YBIT), swap(own, CORE)
-    other, own_c, side = together(other, own_c, side)
-    side_c = swap(side, CORE)
+    hidden, own_c, side_0, rest, picks, gates, incoming = together(
+        hidden, own_c, side_0, rest, picks, gates, incoming
+    )
+    other, side_0c, side_1 = swap(hidden, YBIT), swap(side_0, CORE), swap(rest, XBIT)
     info = swap(jnp.concatenate([picks.astype(jnp.float32), gates], axis=1), YBIT)
-    values = down_values(hidden, other, (own, own_c, side, side_c), planes, span // 2)
-
-    def returned(part):
-        return [part[0]] + [shift(part[k], n_ep - k * split) for k in range(1, planes)]
-
-    first = returned(values[:planes])
-    first[1], info, picks, gates, *values = together(
-        first[1], info, picks, gates, *values[planes:]
-    )
-    second = returned(values)
-    backs = (together(*first), together(*second))
+    other, side_0c, info, picks, gates = together(other, side_0c, info, picks, gates)
+    halves = (
+        down_values(hidden, other, (own, own_c), (side_0, side_0c), planes, span // 2, 0),
+        down_values(hidden, other, (own, own_c), (side_1, swap(side_1, CORE)), planes, span // 2, 2),
+    )
 
     top = picks.shape[1]
     tables = [
@@ -296,11 +278,16 @@
     high = lax.reduce_precision(table, 8, 7)
     high, low = high.astype(jnp.bfloat16), (table - high).astype(jnp.bfloat16)
 
+    backs = [
+        [values[0]] + [shift(values[k], n_ep - k * split) for k in range(1, planes)]
+        for values in halves
+    ]
+    backs[1][0], incoming, queries, *backs[0] = together(
+        backs[1][0], incoming, queries, *backs[0]
+    )
     outs, others = [], []
     for back in backs:
         mine, theirs = combine(high, low, back, span // 2)
-        if not outs:
-            mine, theirs, incoming, queries = together(mine, theirs, incoming, queries)
         outs.append(mine)
         others.append(swap(theirs, YBIT))
     low_first = jnp.concatenate(outs + others, axis=1)

time: 237 us -> 226 us (0.954)
  waiting for transfers between devices: 151 us -> 141 us
  local copies, waits for them, and re-layouts: 9.44 us -> 5.4 us
  starting transfers between devices: 26.2 us -> 29.7 us
    ppermute x18 -> x20, waiting for transfers between devices: 71.7 us -> 64 us  [swap(): return lax.ppermute(value, 'ep', [(i, i ^ bit) for i in range(count)])]
    ppermute x9, waiting for transfers between devices: 76.3 us -> 69.1 us  [shift(): lax.ppermute(value, 'ep', [(i, (i + step) % count) for i in range(count)])]
    all_to_all x1, waiting for transfers between devices: 2.78 us -> 8.17 us  [expert_rows(): lax.all_to_all(outgoing, 'ep', split_axis=0, concat_axis=0, tiled=True)]
    ppermute x18 -> x20, starting transfers between devices: 12.1 us -> 16 us  [swap(): return lax.ppermute(value, 'ep', [(i, i ^ bit) for i in range(count)])]
    unnamed x46 -> x44, local copies, waits for them, and re-layouts: 5.04 us -> 2.62 us
    pallas_call x1 -> x2, Pallas kernels: 7.91 us -> 9.33 us  [down_values(): pl.pallas_call(down_kernel, grid=(width // chunk,), in_specs=[pl.BlockSpe...]
  transfers between devices with their start and end apart: 28 -> 30, of which waited for: 15 -> 14; matrix products, arithmetic and copies ran while one was open for 6% -> 7% of each run, Pallas kernels for 8% -> 12%
where the time goes in v10:
time: 226 us; the launch traced here: 223 us
  waiting for transfers between devices  141 us (62%)
  Pallas kernels  30.5 us (13%)
  starting transfers between devices  29.7 us (13%)
  other arithmetic  8.26 us (4%)
  matrix products  7 us (3%)
  local copies, waits for them, and re-layouts  5.4 us (2%)
    ppermute x9, waiting for transfers between devices, shift(): lax.ppermute(value, 'ep', [(i, (i + step) % count) for i in range(count)])  69.1 us
    ppermute x20, waiting for transfers between devices, swap(): return lax.ppermute(value, 'ep', [(i, i ^ bit) for i in range(count)])  64 us
    ppermute x20, starting transfers between devices, swap(): return lax.ppermute(value, 'ep', [(i, i ^ bit) for i in range(count)])  16 us
    pallas_call x1, Pallas kernels, hidden_units(): pl.pallas_call(partial(hidden_kernel, len(units)), grid=(width // chunk,)...  11.1 us
    pallas_call x2, Pallas kernels, down_values(): pl.pallas_call(down_kernel, grid=(width // chunk,), in_specs=[pl.BlockSpe...  9.33 us
    ppermute x9, starting transfers between devices, shift(): lax.ppermute(value, 'ep', [(i, (i + step) % count) for i in range(count)])  8.55 us
    all_to_all x1, waiting for transfers between devices, expert_rows(): lax.all_to_all(outgoing, 'ep', split_axis=0, concat_axis=0, tiled=True)  8.17 us
    pallas_call x2, Pallas kernels, combine(): pl.pallas_call(combine_kernel, grid=(width // chunk,), in_specs=[pl.Block...  5.9 us
  transfers between devices with their start and end apart: 30, of which 14 were waited for; matrix products, arithmetic and copies ran while one was open for 7% of the time, Pallas kernels for 12%

profile of v10, /device:TPU:16, one launch (start us, length us, event | category | flops | bytes accessed | tf_op | source)
XLA Modules:
  0.0 223.2 jit_solution(248734203409949557)
XLA Ops:
  4.0 4.2 %shard_map.131 = (bf16[48,7168]{1,0:T(8,128)(2,1)}, bf16[48,7168]{1,0:T(8,128)(2,1)}, bf16[48,7168]{1,0:T(8,128)(2,1)}, bf16[48,7168]{1,0:T(8,128)(2,1)}) custom-call(bf16[192,64]{1,0:T(8,128)(2,1)} %fusion.20.chosen, bf16[64,7168]{1,0:T(8,128)(2,1)} %bitcast.42), custom_call_target="tpu_custom_call" | custom-call | flops 176160768 | bytes 3670016 | tf_op jit(solution)/shard_map/pallas_call | solution.py:53
  15.2 27.2 %collective-permute-done.refs_1_ = bf16[48,7168]{1,0:T(8,128)(2,1)} collective-permute-done((bf16[48,7168]{1,0:T(8,128)(2,1)}, bf16[48,7168]{1,0:T(8,128)(2,1)}, u32[]{:S(2)}, u32[]{:S(2)}) %collective-permute-start) | collective-permute-done | bytes 688160 | tf_op jit(solution)/shard_map/ppermute | solution.py:26
  43.1 2.9 %collective-permute-done.2.refs_4_ = bf16[48,7168]{1,0:T(8,128)(2,1)} collective-permute-done((bf16[48,7168]{1,0:T(8,128)(2,1)}, bf16[48,7168]{1,0:T(8,128)(2,1)}, u32[]{:S(2)}, u32[]{:S(2)}) %collective-permute-start.2) | collective-permute-done | bytes 688160 | tf_op jit(solution)/shard_map/ppermute | solution.py:21
  51.3 30.8 %collective-permute-done.8.refs_14_ = bf16[7168,128]{1,0:T(8,128)(2,1)} collective-permute-done((bf16[7168,128]{1,0:T(8,128)(2,1)}, bf16[7168,128]{1,0:T(8,128)(2,1)}, u32[]{:S(2)}, u32[]{:S(2)}) %collective-permute-start.8) | collective-permute-done | bytes 1835040 | tf_op jit(solution)/shard_map/ppermute | solution.py:21
  84.8 15.9 %collective-permute-done.10.refs_6_ = bf16[48,7168]{1,0:T(8,128)(2,1)S(1)} collective-permute-done((bf16[48,7168]{1,0:T(8,128)(2,1)S(1)}, bf16[48,7168]{1,0:T(8,128)(2,1)S(1)}, u32[]{:S(2)}, u32[]{:S(2)}) %collective-permute-start.10) | collective-permute-done | bytes 688160 | tf_op jit(solution)/shard_map/ppermute | solution.py:21
  102.3 5.2 %all-to-all-start = ((bf16[32,8,640]{2,1,0:T(8,128)(2,1)}), bf16[32,8,640]{2,1,0:T(8,128)(2,1)S(1)}, u32[]{:S(2)}, u32[]{:S(2)}) async-start(bf16[32,8,640]{2,1,0:T(8,128)(2,1)} %maximum_maximum_fusion), calls=%async_computation | async-start | bytes 655360 | tf_op jit(solution)/shard_map/all_to_all | solution.py:250
  107.6 11.1 %shard_map.132.mine = bf16[384,512]{1,0:T(8,128)(2,1)} custom-call(bf16[48,7168]{1,0:T(8,128)(2,1)} %get-tuple-element.70.refs_0_, bf16[48,7168]{1,0:T(8,128)(2,1)} %collective-permute-done.refs_1_, bf16[48,7168]{1,0:T(8,128)(2,1)} %copy-done.17, bf16[48,7168]{1,0:T(8,128)(2,1)} %collective-permute-done.1.refs_3_, ...), custom_call_target="tpu_custom_call" | custom-call | flops 5637144576 | bytes 20185088 | tf_op jit(solution)/shard_map/pallas_call | solution.py:98
  118.8 8.2 %all-to-all-done = bf16[32,8,640]{2,1,0:T(8,128)(2,1)S(1)} async-done(((bf16[32,8,640]{2,1,0:T(8,128)(2,1)}), bf16[32,8,640]{2,1,0:T(8,128)(2,1)S(1)}, u32[]{:S(2)}, u32[]{:S(2)}) %all-to-all-start) | async-done | bytes 327712 | tf_op jit(solution)/shard_map/all_to_all | solution.py:250
  130.5 8.3 %collective-permute-done.18 = f32[64,4]{0,1:T(4,128)S(1)} collective-permute-done((f32[64,4]{0,1:T(4,128)S(1)}, f32[64,4]{0,1:T(4,128)S(1)}, u32[]{:S(2)}, u32[]{:S(2)}) %collective-permute-start.18) | collective-permute-done | bytes 1056 | tf_op jit(solution)/shard_map/ppermute | solution.py:21
  139.5 4.6 %shard_map.134 = (bf16[96,1792]{1,0:T(8,128)(2,1)}, bf16[96,1792]{1,0:T(8,128)(2,1)}, bf16[96,1792]{1,0:T(8,128)(2,1)}, bf16[96,1792]{1,0:T(8,128)(2,1)}) custom-call(bf16[384,512]{1,0:T(8,128)(2,1)} %shard_map.132.mine, bf16[384,512]{1,0:T(8,128)(2,1)} %copy-done.2, bf16[256,3584]{1,0:T(8,128)(2,1)} %pad_maximum_fusion.own, ...), custom_call_target="tpu_custom_call" | custom-call | flops 1409286144 | bytes 5046272 | tf_op jit(solution)/shard_map/pallas_call | solution.py:140
  144.6 3.5 %collective-permute-start.22 = (bf16[96,1792]{1,0:T(8,128)(2,1)}, bf16[96,1792]{1,0:T(8,128)(2,1)}, u32[]{:S(2)}, u32[]{:S(2)}) collective-permute-start(bf16[96,1792]{1,0:T(8,128)(2,1)} %get-tuple-element.116), channel_id=1, source_target_pairs={{0,16},{1,17},{2,18},{3,19},{4,20},{5,21},{6,22},{7,23},{8,24},{9,... | collective-permute-start | bytes 1032200 | tf_op jit(solution)/shard_map/ppermute | solution.py:26
  151.0 1.6 collective-permute-done.20.side_c
  153.5 4.7 %shard_map.133 = (bf16[96,1792]{1,0:T(8,128)(2,1)}, bf16[96,1792]{1,0:T(8,128)(2,1)}, bf16[96,1792]{1,0:T(8,128)(2,1)}, bf16[96,1792]{1,0:T(8,128)(2,1)}) custom-call(bf16[384,512]{1,0:T(8,128)(2,1)} %shard_map.132.mine, bf16[384,512]{1,0:T(8,128)(2,1)} %copy-done.2, bf16[256,3584]{1,0:T(8,128)(2,1)} %pad_maximum_fusion.own, ...), custom_call_target="tpu_custom_call" | custom-call | flops 1409286144 | bytes 5046272 | tf_op jit(solution)/shard_map/pallas_call | solution.py:140
  158.2 16.1 %collective-permute-done.22.refs_2_ = bf16[96,1792]{1,0:T(8,128)(2,1)} collective-permute-done((bf16[96,1792]{1,0:T(8,128)(2,1)}, bf16[96,1792]{1,0:T(8,128)(2,1)}, u32[]{:S(2)}, u32[]{:S(2)}) %collective-permute-start.22) | collective-permute-done | bytes 344096 | tf_op jit(solution)/shard_map/ppermute | solution.py:26
  174.3 3.3 %collective-permute-done.23.refs_3_ = bf16[96,1792]{1,0:T(8,128)(2,1)} collective-permute-done((bf16[96,1792]{1,0:T(8,128)(2,1)}, bf16[96,1792]{1,0:T(8,128)(2,1)}, u32[]{:S(2)}, u32[]{:S(2)}) %collective-permute-start.23) | collective-permute-done | bytes 344096 | tf_op jit(solution)/shard_map/ppermute | solution.py:26
  178.6 2.9 %shard_map.135 = (bf16[64,1792]{1,0:T(8,128)(2,1)}, bf16[64,1792]{1,0:T(8,128)(2,1)}) custom-call(bf16[128,384]{1,0:T(8,128)(2,1)} %get-tuple-element.143.high, bf16[128,384]{1,0:T(8,128)(2,1)} %get-tuple-element.142.low, bf16[96,1792]{1,0:T(8,128)(2,1)} %get-tuple-element.118.refs_0_, bf16[96,1792]{1,0:T(8,128)(2,1)} %collective-permute-done.21.refs_1_, ...), custom_call_target="tpu_custom_call" | custom-call | flops 352321536 | bytes 1835008 | tf_op jit(solution)/shard_map/pallas_call | solution.py:171
  182.0 2.0 collective-permute-start.26
  186.6 2.2 fusion
  188.8 16.5 %collective-permute-done.24.refs_1_ = bf16[96,1792]{1,0:T(8,128)(2,1)S(1)} collective-permute-done((bf16[96,1792]{1,0:T(8,128)(2,1)}, bf16[96,1792]{1,0:T(8,128)(2,1)S(1)}, u32[]{:S(2)}, u32[]{:S(2)}) %collective-permute-start.24) | collective-permute-done | bytes 344096 | tf_op jit(solution)/shard_map/ppermute | solution.py:26
  205.3 5.8 %collective-permute-done.25.refs_2_ = bf16[96,1792]{1,0:T(8,128)(2,1)} collective-permute-done((bf16[96,1792]{1,0:T(8,128)(2,1)}, bf16[96,1792]{1,0:T(8,128)(2,1)}, u32[]{:S(2)}, u32[]{:S(2)}) %collective-permute-start.25) | collective-permute-done | bytes 344096 | tf_op jit(solution)/shard_map/ppermute | solution.py:26
  211.3 3.0 %shard_map.136 = (bf16[64,1792]{1,0:T(8,128)(2,1)}, bf16[64,1792]{1,0:T(8,128)(2,1)}) custom-call(bf16[128,384]{1,0:T(8,128)(2,1)} %get-tuple-element.143.high, bf16[128,384]{1,0:T(8,128)(2,1)} %get-tuple-element.142.low, bf16[96,1792]{1,0:T(8,128)(2,1)} %get-tuple-element.123.refs_0_, bf16[96,1792]{1,0:T(8,128)(2,1)} %copy-done.8, ...), custom_call_target="tpu_custom_call" | custom-call | flops 352321536 | bytes 1835008 | tf_op jit(solution)/shard_map/pallas_call | solution.py:171
  214.3 1.7 collective-permute-start.28
  216.0 3.1 %add_convert_fusion = bf16[8,128,512]{2,1,0:T(8,128)(2,1)} fusion(f32[8,128,512]{2,1,0:T(8,128)} %fusion, f32[8,128,256]{2,1,0:T(8,128)S(1)} %copy-done.5, f32[8,128]{1,0:T(8,128)S(1)} %add.81, f32[8,128]{1,0:T(8,128)S(1)} %max.7, bf16[256,576]{1,0:T(8,128)(2,1)S(1)} %copy-done.9), kind=kOutput, calls=%fused_computation.5 | convolution fusion | flops 270270464 | bytes 4464640 | tf_op jit(solution)/shard_map/qhr,rv->qhv/dot_general | solution.py:324
  219.1 2.9 %collective-permute-done.28 = bf16[64,1792]{1,0:T(8,128)(2,1)S(1)} collective-permute-done((bf16[64,1792]{1,0:T(8,128)(2,1)}, bf16[64,1792]{1,0:T(8,128)(2,1)S(1)}, u32[]{:S(2)}, u32[]{:S(2)}) %collective-permute-start.28) | collective-permute-done | bytes 229408 | tf_op jit(solution)/shard_map/ppermute | solution.py:21
  (134 shorter events, 34.5 us)
Async XLA Ops:
  0.7 45.4 %collective-permute-start.4 = (bf16[7168,128]{1,0:T(8,128)(2,1)}, bf16[7168,128]{1,0:T(8,128)(2,1)}, u32[]{:S(2)}, u32[]{:S(2)}) collective-permute-start(bf16[7168,128]{1,0:T(8,128)(2,1)} %refs_8_), channel_id=1, source_target_pairs={{0,2},{1,3},{2,0},{3,1},{4,6},{5,7},{6,4},{7,5},{8,10},{9,11},{10,... | collective-permute-start | bytes 5505032 | tf_op jit(solution)/shard_map/ppermute | solution.py:21
  9.2 36.9 %collective-permute-start.3 = (bf16[128,3584]{1,0:T(8,128)(2,1)}, bf16[128,3584]{1,0:T(8,128)(2,1)S(1)}, u32[]{:S(2)}, u32[]{:S(2)}) collective-permute-start(bf16[128,3584]{1,0:T(8,128)(2,1)} %constant_dynamic-slice_fusion.1), channel_id=1, source_target_pairs={{0,4},{1,5},{2,6},{3,7},{4,0},{5,1},{6,2},{7,3},{8,12},{9,13},{10,... | collective-permute-start | bytes 2752520 | tf_op jit(solution)/shard_map/ppermute | solution.py:21
  10.7 31.7 %collective-permute-start = (bf16[48,7168]{1,0:T(8,128)(2,1)}, bf16[48,7168]{1,0:T(8,128)(2,1)}, u32[]{:S(2)}, u32[]{:S(2)}) collective-permute-start(bf16[48,7168]{1,0:T(8,128)(2,1)} %get-tuple-element.71), channel_id=1, source_target_pairs={{0,8},{1,9},{2,10},{3,11},{4,12},{5,13},{6,14},{7,15},{8,16},{9,17... | collective-permute-start | bytes 2064392 | tf_op jit(solution)/shard_map/ppermute | solution.py:26
  12.3 30.8 %collective-permute-start.1 = (bf16[48,7168]{1,0:T(8,128)(2,1)}, bf16[48,7168]{1,0:T(8,128)(2,1)}, u32[]{:S(2)}, u32[]{:S(2)}) collective-permute-start(bf16[48,7168]{1,0:T(8,128)(2,1)} %get-tuple-element.72), channel_id=1, source_target_pairs={{0,24},{1,25},{2,26},{3,27},{4,28},{5,29},{6,30},{7,31},{8,0},{9,1... | collective-permute-start | bytes 2064392 | tf_op jit(solution)/shard_map/ppermute | solution.py:26
  12.7 33.3 %collective-permute-start.2 = (bf16[48,7168]{1,0:T(8,128)(2,1)}, bf16[48,7168]{1,0:T(8,128)(2,1)}, u32[]{:S(2)}, u32[]{:S(2)}) collective-permute-start(bf16[48,7168]{1,0:T(8,128)(2,1)} %get-tuple-element.70.refs_0_), channel_id=1, source_target_pairs={{0,4},{1,5},{2,6},{3,7},{4,0},{5,1},{6,2},{7,3},{8,12},{9,13},{10,... | collective-permute-start | bytes 2064392 | tf_op jit(solution)/shard_map/ppermute | solution.py:21
  42.4 39.7 %collective-permute-start.8 = (bf16[7168,128]{1,0:T(8,128)(2,1)}, bf16[7168,128]{1,0:T(8,128)(2,1)}, u32[]{:S(2)}, u32[]{:S(2)}) collective-permute-start(bf16[7168,128]{1,0:T(8,128)(2,1)} %refs_12_), channel_id=1, source_target_pairs={{0,2},{1,3},{2,0},{3,1},{4,6},{5,7},{6,4},{7,5},{8,10},{9,11},{10,... | collective-permute-start | bytes 5505032 | tf_op jit(solution)/shard_map/ppermute | solution.py:21
  46.1 36.1 %collective-permute-start.9 = (bf16[7168,128]{1,0:T(8,128)(2,1)}, bf16[7168,128]{1,0:T(8,128)(2,1)}, u32[]{:S(2)}, u32[]{:S(2)}) collective-permute-start(bf16[7168,128]{1,0:T(8,128)(2,1)} %refs_8_), channel_id=1, source_target_pairs={{0,1},{1,0},{2,3},{3,2},{4,5},{5,4},{6,7},{7,6},{8,9},{9,8},{10,11... | collective-permute-start | bytes 5505032 | tf_op jit(solution)/shard_map/ppermute | solution.py:21
  46.1 36.0 %collective-permute-start.5 = (bf16[48,7168]{1,0:T(8,128)(2,1)}, bf16[48,7168]{1,0:T(8,128)(2,1)S(1)}, u32[]{:S(2)}, u32[]{:S(2)}) collective-permute-start(bf16[48,7168]{1,0:T(8,128)(2,1)} %get-tuple-element.79), channel_id=1, source_target_pairs={{0,16},{1,17},{2,18},{3,19},{4,20},{5,21},{6,22},{7,23},{8,24},{9,... | collective-permute-start | bytes 2064392 | tf_op jit(solution)/shard_map/ppermute | solution.py:26
  46.5 35.6 %collective-permute-start.6 = (bf16[48,7168]{1,0:T(8,128)(2,1)}, bf16[48,7168]{1,0:T(8,128)(2,1)S(1)}, u32[]{:S(2)}, u32[]{:S(2)}) collective-permute-start(bf16[48,7168]{1,0:T(8,128)(2,1)} %collective-permute-done.refs_1_), channel_id=1, source_target_pairs={{0,4},{1,5},{2,6},{3,7},{4,0},{5,1},{6,2},{7,3},{8,12},{9,13},{10,... | collective-permute-start | bytes 2064392 | tf_op jit(solution)/shard_map/ppermute | solution.py:21
  48.0 34.1 %collective-permute-start.7 = (bf16[48,7168]{1,0:T(8,128)(2,1)}, bf16[48,7168]{1,0:T(8,128)(2,1)S(1)}, u32[]{:S(2)}, u32[]{:S(2)}) collective-permute-start(bf16[48,7168]{1,0:T(8,128)(2,1)} %collective-permute-done.1.refs_3_), channel_id=1, source_target_pairs={{0,4},{1,5},{2,6},{3,7},{4,0},{5,1},{6,2},{7,3},{8,12},{9,13},{10,... | collective-permute-start | bytes 2064392 | tf_op jit(solution)/shard_map/ppermute | solution.py:21
  82.2 25.4 %collective-permute-start.11 = (bf16[7168,128]{1,0:T(8,128)(2,1)}, bf16[7168,128]{1,0:T(8,128)(2,1)}, u32[]{:S(2)}, u32[]{:S(2)}) collective-permute-start(bf16[7168,128]{1,0:T(8,128)(2,1)} %refs_12_), channel_id=1, source_target_pairs={{0,1},{1,0},{2,3},{3,2},{4,5},{5,4},{6,7},{7,6},{8,9},{9,8},{10,11... | collective-permute-start | bytes 5505032 | tf_op jit(solution)/shard_map/ppermute | solution.py:21
  82.3 25.3 %collective-permute-start.12 = (bf16[7168,128]{1,0:T(8,128)(2,1)}, bf16[7168,128]{1,0:T(8,128)(2,1)}, u32[]{:S(2)}, u32[]{:S(2)}) collective-permute-start(bf16[7168,128]{1,0:T(8,128)(2,1)} %collective-permute-done.4.refs_10_), channel_id=1, source_target_pairs={{0,1},{1,0},{2,3},{3,2},{4,5},{5,4},{6,7},{7,6},{8,9},{9,8},{10,11... | collective-permute-start | bytes 5505032 | tf_op jit(solution)/shard_map/ppermute | solution.py:21
  82.8 24.9 %collective-permute-start.13 = (bf16[7168,128]{1,0:T(8,128)(2,1)}, bf16[7168,128]{1,0:T(8,128)(2,1)}, u32[]{:S(2)}, u32[]{:S(2)}) collective-permute-start(bf16[7168,128]{1,0:T(8,128)(2,1)} %collective-permute-done.8.refs_14_), channel_id=1, source_target_pairs={{0,1},{1,0},{2,3},{3,2},{4,5},{5,4},{6,7},{7,6},{8,9},{9,8},{10,11... | collective-permute-start | bytes 5505032 | tf_op jit(solution)/shard_map/ppermute | solution.py:21
  82.8 44.1 %collective-permute-start.14 = (bf16[256,3584]{1,0:T(8,128)(2,1)}, bf16[256,3584]{1,0:T(8,128)(2,1)}, u32[]{:S(2)}, u32[]{:S(2)}) collective-permute-start(bf16[256,3584]{1,0:T(8,128)(2,1)} %pad_maximum_fusion.own), channel_id=1, source_target_pairs={{0,1},{1,0},{2,3},{3,2},{4,5},{5,4},{6,7},{7,6},{8,9},{9,8},{10,11... | collective-permute-start | bytes 5505032 | tf_op jit(solution)/shard_map/ppermute | solution.py:21
  83.3 17.4 %collective-permute-start.10 = (bf16[48,7168]{1,0:T(8,128)(2,1)S(1)}, bf16[48,7168]{1,0:T(8,128)(2,1)S(1)}, u32[]{:S(2)}, u32[]{:S(2)}) collective-permute-start(bf16[48,7168]{1,0:T(8,128)(2,1)S(1)} %collective-permute-done.5.refs_2_), channel_id=1, source_target_pairs={{0,4},{1,5},{2,6},{3,7},{4,0},{5,1},{6,2},{7,3},{8,12},{9,13},{10,... | collective-permute-start | bytes 2064392 | tf_op jit(solution)/shard_map/ppermute | solution.py:21
  100.7 26.2 %collective-permute-start.15 = (bf16[256,1792]{1,0:T(8,128)(2,1)}, bf16[256,1792]{1,0:T(8,128)(2,1)}, u32[]{:S(2)}, u32[]{:S(2)}) collective-permute-start(bf16[256,1792]{1,0:T(8,128)(2,1)} %get-tuple-element.98), channel_id=1, source_target_pairs={{0,2},{1,3},{2,0},{3,1},{4,6},{5,7},{6,4},{7,5},{8,10},{9,11},{10,... | collective-permute-start | bytes 2752520 | tf_op jit(solution)/shard_map/ppermute | solution.py:21
  102.3 24.7 %all-to-all-start = ((bf16[32,8,640]{2,1,0:T(8,128)(2,1)}), bf16[32,8,640]{2,1,0:T(8,128)(2,1)S(1)}, u32[]{:S(2)}, u32[]{:S(2)}) async-start(bf16[32,8,640]{2,1,0:T(8,128)(2,1)} %maximum_maximum_fusion), calls=%async_computation | async-start | bytes 655360 | tf_op jit(solution)/shard_map/all_to_all | solution.py:250
  127.4 22.4 %collective-permute-start.19 = (bf16[256,1792]{1,0:T(8,128)(2,1)S(1)}, bf16[256,1792]{1,0:T(8,128)(2,1)}, u32[]{:S(2)}, u32[]{:S(2)}) collective-permute-start(bf16[256,1792]{1,0:T(8,128)(2,1)S(1)} %copy-done.6), channel_id=1, source_target_pairs={{0,2},{1,3},{2,0},{3,1},{4,6},{5,7},{6,4},{7,5},{8,10},{9,11},{10,... | collective-permute-start | bytes 2752520 | tf_op jit(solution)/shard_map/ppermute | solution.py:21
  144.6 29.7 %collective-permute-start.22 = (bf16[96,1792]{1,0:T(8,128)(2,1)}, bf16[96,1792]{1,0:T(8,128)(2,1)}, u32[]{:S(2)}, u32[]{:S(2)}) collective-permute-start(bf16[96,1792]{1,0:T(8,128)(2,1)} %get-tuple-element.116), channel_id=1, source_target_pairs={{0,16},{1,17},{2,18},{3,19},{4,20},{5,21},{6,22},{7,23},{8,24},{9,... | collective-permute-start | bytes 1032200 | tf_op jit(solution)/shard_map/ppermute | solution.py:26
  148.1 29.4 %collective-permute-start.23 = (bf16[96,1792]{1,0:T(8,128)(2,1)}, bf16[96,1792]{1,0:T(8,128)(2,1)}, u32[]{:S(2)}, u32[]{:S(2)}) collective-permute-start(bf16[96,1792]{1,0:T(8,128)(2,1)} %get-tuple-element.117), channel_id=1, source_target_pairs={{0,8},{1,9},{2,10},{3,11},{4,12},{5,13},{6,14},{7,15},{8,16},{9,17... | collective-permute-start | bytes 1032200 | tf_op jit(solution)/shard_map/ppermute | solution.py:26
  181.5 37.6 %collective-permute-start.27 = (bf16[64,1792]{1,0:T(8,128)(2,1)}, bf16[64,1792]{1,0:T(8,128)(2,1)S(1)}, u32[]{:S(2)}, u32[]{:S(2)}) collective-permute-start(bf16[64,1792]{1,0:T(8,128)(2,1)} %get-tuple-element.128), channel_id=1, source_target_pairs={{0,4},{1,5},{2,6},{3,7},{4,0},{5,1},{6,2},{7,3},{8,12},{9,13},{10,... | collective-permute-start | bytes 688136 | tf_op jit(solution)/shard_map/ppermute | solution.py:21
  181.8 23.4 %collective-permute-start.24 = (bf16[96,1792]{1,0:T(8,128)(2,1)}, bf16[96,1792]{1,0:T(8,128)(2,1)S(1)}, u32[]{:S(2)}, u32[]{:S(2)}) collective-permute-start(bf16[96,1792]{1,0:T(8,128)(2,1)} %get-tuple-element.124), channel_id=1, source_target_pairs={{0,24},{1,25},{2,26},{3,27},{4,28},{5,29},{6,30},{7,31},{8,0},{9,1... | collective-permute-start | bytes 1032200 | tf_op jit(solution)/shard_map/ppermute | solution.py:26
  181.8 29.2 %collective-permute-start.25 = (bf16[96,1792]{1,0:T(8,128)(2,1)}, bf16[96,1792]{1,0:T(8,128)(2,1)}, u32[]{:S(2)}, u32[]{:S(2)}) collective-permute-start(bf16[96,1792]{1,0:T(8,128)(2,1)} %get-tuple-element.125), channel_id=1, source_target_pairs={{0,16},{1,17},{2,18},{3,19},{4,20},{5,21},{6,22},{7,23},{8,24},{9,... | collective-permute-start | bytes 1032200 | tf_op jit(solution)/shard_map/ppermute | solution.py:26
  182.0 29.4 %collective-permute-start.26 = (bf16[96,1792]{1,0:T(8,128)(2,1)}, bf16[96,1792]{1,0:T(8,128)(2,1)}, u32[]{:S(2)}, u32[]{:S(2)}) collective-permute-start(bf16[96,1792]{1,0:T(8,128)(2,1)} %get-tuple-element.126), channel_id=1, source_target_pairs={{0,8},{1,9},{2,10},{3,11},{4,12},{5,13},{6,14},{7,15},{8,16},{9,17... | collective-permute-start | bytes 1032200 | tf_op jit(solution)/shard_map/ppermute | solution.py:26
  (27 other events, 354.3 us)

commit v11 on v10

--- a/solution.py
+++ b/solution.py
@@ -206,8 +206,19 @@
     return jnp.where(found, weight.T[:, :, None], 0.0)
 
 
-def expert_rows(
-    rows, picks, gates, latents, owners, requests, queries, gate_proj, up_proj, down_proj
+def layer(
+    rows,
+    picks,
+    gates,
+    latents,
+    owners,
+    requests,
+    queries,
+    cache_latents,
+    cache_lens,
+    gate_proj,
+    up_proj,
+    down_proj,
 ):
     n_ep = lax.axis_size("ep")
     split = FF_WIN // gate_proj.shape[1]
@@ -224,7 +235,9 @@
     chosen = (rank[:, None, :] == at[None, :, None]) & named[:, None, :]
     chosen = chosen.astype(jnp.bfloat16)
 
-    pack_0, out_1, out_2, out_3 = packs(chosen.reshape(planes * slots, count), rows, planes, span)
+    pack_0, out_1, out_2, out_3 = packs(
+        chosen.reshape(planes * slots, count), rows, planes, 2 * span
+    )
     pack_0, out_1, out_3, latents, owners, requests, down_proj = together(
         pack_0, out_1, out_3, latents, owners, requests, down_proj
     )
@@ -233,29 +246,32 @@
     down_y = swap(send, YBIT)
     outgoing = hand_over(latents, owners, requests)
 
-    own_1, own_3, peer_0, down_y, gate_x, out_2, outgoing, down_proj, gate_proj = together(
-        own_1, own_3, peer_0, down_y, gate_x, out_2, outgoing, down_proj, gate_proj
-    )
+    incoming = lax.all_to_all(outgoing, "ep", split_axis=0, concat_axis=0, tiled=True)
+    own_1, own_3, peer_0, down_y, gate_x, out_2, incoming, down_proj, gate_proj = together(
+        own_1, own_3, peer_0, down_y, gate_x, out_2, incoming, down_proj, gate_proj
+    )
+    handed = incoming.reshape(-1, incoming.shape[2])
+    marks = handed[:, latents.shape[1]].astype(jnp.float32)[None, :]
+    attended = attend(queries, cache_latents, cache_lens, handed, marks)
     own_2, peer_1, peer_3 = shift(out_2, 2 * split), swap(own_1, YBIT), swap(own_3, YBIT)
     up_x, gate_c = swap(up_proj, XBIT), swap(gate_proj, CORE)
     keep = lax.dynamic_slice_in_dim(down_proj, 2 * upper * span, 2 * span, 1)
     own = jnp.concatenate([keep, down_y], axis=0)
     own_0, rest = own[:, :span], own[:, span:]
 
-    own_2, peer_1, peer_3, up_x, gate_x, gate_c, up_proj, own, own_0, rest = together(
-        own_2, peer_1, peer_3, up_x, gate_x, gate_c, up_proj, own, own_0, rest
+    own_2, peer_1, peer_3, up_x, gate_x, gate_c, up_proj, own, own_0, rest, attended = together(
+        own_2, peer_1, peer_3, up_x, gate_x, gate_c, up_proj, own, own_0, rest, attended
     )
     peer_2, side_0 = swap(own_2, YBIT), swap(own_0, XBIT)
     up_c, gate_xc, up_xc = swap(up_proj, CORE), swap(gate_x, CORE), swap(up_x, CORE)
-    incoming = lax.all_to_all(outgoing, "ep", split_axis=0, concat_axis=0, tiled=True)
-
-    peer_2, up_c, gate_xc, up_xc = together(peer_2, up_c, gate_xc, up_xc)
+
+    peer_2, up_c, gate_xc, up_xc, own = together(peer_2, up_c, gate_xc, up_xc, own)
     own_c = swap(own, CORE)
     units = (pack_0, own_1, own_2, own_3, peer_0, peer_1, peer_2, peer_3)
     weights = (gate_proj, gate_c, gate_x, gate_xc, up_proj, up_c, up_x, up_xc)
     hidden = hidden_units(units, weights, chunk)
-    hidden, own_c, side_0, rest, picks, gates, incoming = together(
-        hidden, own_c, side_0, rest, picks, gates, incoming
+    hidden, own_c, side_0, rest, picks, gates = together(
+        hidden, own_c, side_0, rest, picks, gates
     )
     other, side_0c, side_1 = swap(hidden, YBIT), swap(side_0, CORE), swap(rest, XBIT)
     info = swap(jnp.concatenate([picks.astype(jnp.float32), gates], axis=1), YBIT)
@@ -282,49 +298,71 @@
         [values[0]] + [shift(values[k], n_ep - k * split) for k in range(1, planes)]
         for values in halves
     ]
-    backs[1][0], incoming, queries, *backs[0] = together(
-        backs[1][0], incoming, queries, *backs[0]
-    )
+    flat = together(*backs[0], *backs[1])
     outs, others = [], []
-    for back in backs:
+    for back in (flat[:planes], flat[planes:]):
         mine, theirs = combine(high, low, back, span // 2)
         outs.append(mine)
         others.append(swap(theirs, YBIT))
     low_first = jnp.concatenate(outs + others, axis=1)
     high_first = jnp.concatenate(others + outs, axis=1)
-    return jnp.where(upper == 0, low_first, high_first), incoming, queries
-
-
-def attend(query_part, cache_latents, cache_lens, handed, handed_mark):
-    requests = query_part.shape[0]
-    cache_scores = (
-        jnp.einsum("qhl,qcl->qhc", query_part, cache_latents, preferred_element_type=jnp.float32)
-        * score_scale
-    )
-    hand_scores = (
-        jnp.einsum("qhl,rl->qhr", query_part, handed, preferred_element_type=jnp.float32)
-        * score_scale
-    )
-    cache_mask = (
-        jnp.arange(cache_latents.shape[1], dtype=jnp.int32)[None, :] < cache_lens[:, None]
-    )[:, None, :]
-    marks = jnp.arange(1, requests + 1, dtype=jnp.int32).astype(jnp.float32)
-    hand_mask = (handed_mark[None, :] == marks[:, None])[:, None, :]
-    cache_scores = jnp.where(cache_mask, cache_scores, -jnp.inf)
-    hand_scores = jnp.where(hand_mask, hand_scores, -jnp.inf)
-    top = jnp.maximum(jnp.max(cache_scores, axis=2), jnp.max(hand_scores, axis=2))[:, :, None]
-    cache_expo = jnp.exp(cache_scores - top)
-    hand_expo = jnp.exp(hand_scores - top)
-    denom = (jnp.sum(cache_expo, axis=2) + jnp.sum(hand_expo, axis=2))[:, :, None]
-    cache_prob = (cache_expo / denom).astype(jnp.bfloat16)
-    hand_prob = (hand_expo / denom).astype(jnp.bfloat16)
-    result = jnp.einsum(
-        "qhc,qcv->qhv", cache_prob, cache_latents[:, :, :VDIM], preferred_element_type=jnp.float32
-    )
-    result = result + jnp.einsum(
-        "qhr,rv->qhv", hand_prob, handed[:, :VDIM], preferred_element_type=jnp.float32
-    )
-    return result.astype(jnp.bfloat16)
+    return jnp.where(upper == 0, low_first, high_first), attended
+
+
+def attend_kernel(lens, query, cache, handed, marks, out):
+    request = pl.program_id(0)
+    heads = query.shape[2]
+    wide = out.shape[2]
+    lat = query.shape[1]
+    asked = query[0].astype(jnp.float32).T.astype(jnp.bfloat16)
+    given = handed[:, :lat]
+    near = jnp.dot(asked, cache[0], preferred_element_type=jnp.float32) * score_scale
+    over_last = (((1,), (1,)), ((), ()))
+    far = lax.dot_general(asked, given, over_last, preferred_element_type=jnp.float32)
+    far = far * score_scale
+    place = lax.broadcasted_iota(jnp.int32, (heads, near.shape[1]), 1)
+    near = jnp.where(place < lens[request], near, -jnp.inf)
+    mark = (request + 1).astype(jnp.float32)
+    far = jnp.where(jnp.broadcast_to(marks[...], far.shape) == mark, far, -jnp.inf)
+    top = jnp.maximum(
+        jnp.max(near, axis=1, keepdims=True), jnp.max(far, axis=1, keepdims=True)
+    )
+    near, far = jnp.exp(near - top), jnp.exp(far - top)
+    total = jnp.sum(near, axis=1, keepdims=True) + jnp.sum(far, axis=1, keepdims=True)
+    near, far = (near / total).astype(jnp.bfloat16), (far / total).astype(jnp.bfloat16)
+    result = lax.dot_general(near, cache[0, :wide], over_last, preferred_element_type=jnp.float32)
+    result = result + jnp.dot(far, given[:, :wide], preferred_element_type=jnp.float32)
+    out[0] = result.astype(jnp.bfloat16)
+
+
+def attend(queries, cache_latents, cache_lens, handed, marks):
+    requests, heads, lat = queries.shape
+    cached = cache_latents.shape[1]
+    return pl.pallas_call(
+        attend_kernel,
+        grid=(requests,),
+        in_specs=[
+            pl.BlockSpec(memory_space=pltpu.SMEM),
+            pl.BlockSpec((1, lat, heads), lambda k: (k, 0, 0)),
+            pl.BlockSpec((1, lat, cached), lambda k: (k, 0, 0)),
+            pl.BlockSpec(handed.shape, lambda k: (0, 0)),
+            pl.BlockSpec(marks.shape, lambda k: (0, 0)),
+        ],
+        out_specs=pl.BlockSpec((1, heads, VDIM), lambda k: (k, 0, 0)),
+        out_shape=jax.ShapeDtypeStruct((requests, heads, VDIM), jnp.bfloat16),
+        compiler_params=pltpu.CompilerParams(vmem_limit_bytes=VMEM_BYTES),
+        cost_estimate=pl.CostEstimate(
+            flops=2 * requests * heads * (cached + handed.shape[0]) * (lat + VDIM),
+            bytes_accessed=2 * requests * (heads * (lat + VDIM) + cached * lat),
+            transcendentals=requests * heads * (cached + handed.shape[0]),
+        ),
+    )(
+        cache_lens,
+        jnp.swapaxes(queries, 1, 2),
+        jnp.swapaxes(cache_latents, 1, 2),
+        handed,
+        marks,
+    )
 
 
 def hand_over(prompt_latents, owners, requests):
@@ -363,7 +401,7 @@
 ):
     sections, count, width = moe_rows.shape
     top = routes.shape[2]
-    expert_out, incoming, queries = expert_rows(
+    expert_out, attended = layer(
         moe_rows.reshape(sections * count, width),
         routes.reshape(sections * count, top),
         route_gates.reshape(sections * count, top),
@@ -371,15 +409,13 @@
         kv_owner[:, 0],
         kv_request,
         queries,
+        cache_latents,
+        cache_lens,
         gate_proj,
         up_proj,
         down_proj,
     )
     expert_out = expert_out.reshape(moe_rows.shape)
-    lat = prompt_latents.shape[1]
-    handed = incoming[:, :, :lat].reshape(-1, lat)
-    handed_mark = incoming[:, :, lat].reshape(-1).astype(jnp.float32)
-    attended = attend(queries, cache_latents, cache_lens, handed, handed_mark)
     return (expert_out, attended)
 
 

time: 226 us -> 237 us (1.049)
  Pallas kernels: 30.5 us -> 38.5 us
  matrix products: 7 us -> 0.24 us
  waiting for transfers between devices: 141 us -> 146 us
  starting transfers between devices: 29.7 us -> 32.8 us
    pallas_call x0 -> x1, Pallas kernels: none -> 9.06 us  [attend(): pl.pallas_call(attend_kernel, grid=(requests,), in_specs=[pl.BlockSpec(me...]
    dot_general x4 -> x0, matrix products: 6.76 us -> none  [the longest x1 3.11 us: attend(): jnp.einsum('qhr,rv->qhv', hand_prob, handed[:, :VDIM], preferred_element_...]
    all_to_all x1, waiting for transfers between devices: 8.17 us -> 13 us  [layer(): lax.all_to_all(outgoing, 'ep', split_axis=0, concat_axis=0, tiled=True)]
    ppermute x9, starting transfers between devices: 8.55 us -> 12.3 us  [shift(): lax.ppermute(value, 'ep', [(i, (i + step) % count) for i in range(count)])]
    unnamed x44 -> x38, local copies, waits for them, and re-layouts: 2.62 us -> 5.54 us
  transfers between devices with their start and end apart: 30 -> 30, of which waited for: 14 -> 15; matrix products, arithmetic and copies ran while one was open for 7% -> 3% of each run, Pallas kernels for 12% -> 14%
where the time goes in v11:
time: 237 us; the launch traced here: 235 us
  waiting for transfers between devices  146 us (62%)
  Pallas kernels  38.5 us (16%)
  starting transfers between devices  32.8 us (14%)
  other arithmetic  9.13 us (4%)
  local copies, waits for them, and re-layouts  7.49 us (3%)
    ppermute x9, waiting for transfers between devices, shift(): lax.ppermute(value, 'ep', [(i, (i + step) % count) for i in range(count)])  67.3 us
    ppermute x20, waiting for transfers between devices, swap(): return lax.ppermute(value, 'ep', [(i, i ^ bit) for i in range(count)])  66 us
    ppermute x20, starting transfers between devices, swap(): return lax.ppermute(value, 'ep', [(i, i ^ bit) for i in range(count)])  15.5 us
    all_to_all x1, waiting for transfers between devices, layer(): lax.all_to_all(outgoing, 'ep', split_axis=0, concat_axis=0, tiled=True)  13 us
    ppermute x9, starting transfers between devices, shift(): lax.ppermute(value, 'ep', [(i, (i + step) % count) for i in range(count)])  12.3 us
    pallas_call x1, Pallas kernels, hidden_units(): pl.pallas_call(partial(hidden_kernel, len(units)), grid=(width // chunk,)...  11.1 us
    pallas_call x2, Pallas kernels, down_values(): pl.pallas_call(down_kernel, grid=(width // chunk,), in_specs=[pl.BlockSpe...  9.4 us
    pallas_call x1, Pallas kernels, attend(): pl.pallas_call(attend_kernel, grid=(requests,), in_specs=[pl.BlockSpec(me...  9.06 us
  transfers between devices with their start and end apart: 30, of which 15 were waited for; matrix products, arithmetic and copies ran while one was open for 3% of the time, Pallas kernels for 14%

profile of v11, /device:TPU:16, one launch (start us, length us, event | category | flops | bytes accessed | tf_op | source)
XLA Modules:
  0.0 235.5 jit_solution(3930971581347822218)
XLA Ops:
  2.6 3.1 %shard_map.131 = (bf16[48,7168]{1,0:T(8,128)(2,1)}, bf16[48,7168]{1,0:T(8,128)(2,1)}, bf16[48,7168]{1,0:T(8,128)(2,1)}, bf16[48,7168]{1,0:T(8,128)(2,1)}) custom-call(bf16[192,64]{1,0:T(8,128)(2,1)} %fusion.8.chosen, bf16[64,7168]{1,0:T(8,128)(2,1)} %bitcast.36), custom_call_target="tpu_custom_call" | custom-call | flops 176160768 | bytes 3670016 | tf_op jit(solution)/shard_map/pallas_call | solution.py:53
  14.2 5.0 %all-to-all-start = ((bf16[32,8,640]{2,1,0:T(8,128)(2,1)}), bf16[32,8,640]{2,1,0:T(8,128)(2,1)S(1)}, u32[]{:S(2)}, u32[]{:S(2)}) async-start(bf16[32,8,640]{2,1,0:T(8,128)(2,1)} %maximum_maximum_fusion), calls=%async_computation | async-start | bytes 655360 | tf_op jit(solution)/shard_map/all_to_all | solution.py:249
  19.2 22.2 %collective-permute-done.refs_1_ = bf16[48,7168]{1,0:T(8,128)(2,1)} collective-permute-done((bf16[48,7168]{1,0:T(8,128)(2,1)}, bf16[48,7168]{1,0:T(8,128)(2,1)}, u32[]{:S(2)}, u32[]{:S(2)}) %collective-permute-start) | collective-permute-done | bytes 688160 | tf_op jit(solution)/shard_map/ppermute | solution.py:26
  42.9 13.0 %all-to-all-done = bf16[32,8,640]{2,1,0:T(8,128)(2,1)S(1)} async-done(((bf16[32,8,640]{2,1,0:T(8,128)(2,1)}), bf16[32,8,640]{2,1,0:T(8,128)(2,1)S(1)}, u32[]{:S(2)}, u32[]{:S(2)}) %all-to-all-start) | async-done | bytes 327712 | tf_op jit(solution)/shard_map/all_to_all | solution.py:249
  62.2 9.1 %shard_map.132 = bf16[8,128,512]{2,1,0:T(8,128)(2,1)} custom-call(s32[8]{0:T(128)} %lens.1, bf16[8,576,128]{2,1,0:T(8,128)(2,1)} %bitcast.35, bf16[8,576,256]{2,1,0:T(8,128)(2,1)} %bitcast.31, bf16[256,640]{1,0:T(8,128)(2,1)} %bitcast.33, f32[1,256]{1,0:T(1,128)} %bitcast.48), custom_call_target="tpu_custom_call" | custom-call | flops 1140850688 | bytes 4587520 | tf_op jit(solution)/shard_map/pallas_call | solution.py:341
  72.7 20.6 %collective-permute-done.8.refs_14_ = bf16[7168,128]{1,0:T(8,128)(2,1)} collective-permute-done((bf16[7168,128]{1,0:T(8,128)(2,1)}, bf16[7168,128]{1,0:T(8,128)(2,1)}, u32[]{:S(2)}, u32[]{:S(2)}) %collective-permute-start.8) | collective-permute-done | bytes 1835040 | tf_op jit(solution)/shard_map/ppermute | solution.py:21
  94.5 17.5 %collective-permute-done.10.refs_6_ = bf16[48,7168]{1,0:T(8,128)(2,1)S(1)} collective-permute-done((bf16[48,7168]{1,0:T(8,128)(2,1)}, bf16[48,7168]{1,0:T(8,128)(2,1)S(1)}, u32[]{:S(2)}, u32[]{:S(2)}) %collective-permute-start.10) | collective-permute-done | bytes 688160 | tf_op jit(solution)/shard_map/ppermute | solution.py:21
  116.0 11.1 %shard_map.133.mine = bf16[384,512]{1,0:T(8,128)(2,1)} custom-call(bf16[48,7168]{1,0:T(8,128)(2,1)} %get-tuple-element.72.refs_0_, bf16[48,7168]{1,0:T(8,128)(2,1)} %collective-permute-done.refs_1_, bf16[48,7168]{1,0:T(8,128)(2,1)} %collective-permute-done.5.refs_2_, bf16[48,7168]{1,0:T(8,128)(2,1)} %collective-permute-done.1.refs_3_, ...), custom_call_target="tpu_custom_call" | custom-call | flops 5637144576 | bytes 20185088 | tf_op jit(solution)/shard_map/pallas_call | solution.py:98
  127.1 9.5 %collective-permute-done.15.side = bf16[256,1792]{1,0:T(8,128)(2,1)} collective-permute-done((bf16[256,1792]{1,0:T(8,128)(2,1)}, bf16[256,1792]{1,0:T(8,128)(2,1)}, u32[]{:S(2)}, u32[]{:S(2)}) %collective-permute-start.15) | collective-permute-done | bytes 917536 | tf_op jit(solution)/shard_map/ppermute | solution.py:21
  140.3 9.3 %collective-permute-done.18 = f32[64,4]{0,1:T(4,128)S(1)} collective-permute-done((f32[64,4]{0,1:T(4,128)S(1)}, f32[64,4]{0,1:T(4,128)S(1)}, u32[]{:S(2)}, u32[]{:S(2)}) %collective-permute-start.18) | collective-permute-done | bytes 1056 | tf_op jit(solution)/shard_map/ppermute | solution.py:21
  150.4 4.7 %shard_map.134 = (bf16[96,1792]{1,0:T(8,128)(2,1)}, bf16[96,1792]{1,0:T(8,128)(2,1)}, bf16[96,1792]{1,0:T(8,128)(2,1)}, bf16[96,1792]{1,0:T(8,128)(2,1)}) custom-call(bf16[384,512]{1,0:T(8,128)(2,1)} %shard_map.133.mine, bf16[384,512]{1,0:T(8,128)(2,1)} %copy-done.2, bf16[256,3584]{1,0:T(8,128)(2,1)} %pad_maximum_fusion.own, ...), custom_call_target="tpu_custom_call" | custom-call | flops 1409286144 | bytes 5046272 | tf_op jit(solution)/shard_map/pallas_call | solution.py:140
  155.6 3.5 %collective-permute-start.20 = (bf16[96,1792]{1,0:T(8,128)(2,1)}, bf16[96,1792]{1,0:T(8,128)(2,1)}, u32[]{:S(2)}, u32[]{:S(2)}) collective-permute-start(bf16[96,1792]{1,0:T(8,128)(2,1)} %get-tuple-element.116), channel_id=1, source_target_pairs={{0,16},{1,17},{2,18},{3,19},{4,20},{5,21},{6,22},{7,23},{8,24},{9,... | collective-permute-start | bytes 1032200 | tf_op jit(solution)/shard_map/ppermute | solution.py:26
  162.8 4.7 %shard_map.135 = (bf16[96,1792]{1,0:T(8,128)(2,1)}, bf16[96,1792]{1,0:T(8,128)(2,1)}, bf16[96,1792]{1,0:T(8,128)(2,1)}, bf16[96,1792]{1,0:T(8,128)(2,1)}) custom-call(bf16[384,512]{1,0:T(8,128)(2,1)} %shard_map.133.mine, bf16[384,512]{1,0:T(8,128)(2,1)} %copy-done.2, bf16[256,3584]{1,0:T(8,128)(2,1)} %pad_maximum_fusion.own, ...), custom_call_target="tpu_custom_call" | custom-call | flops 1409286144 | bytes 5046272 | tf_op jit(solution)/shard_map/pallas_call | solution.py:140
  171.4 6.2 %collective-permute-done.19.refs_1_ = bf16[96,1792]{1,0:T(8,128)(2,1)} collective-permute-done((bf16[96,1792]{1,0:T(8,128)(2,1)}, bf16[96,1792]{1,0:T(8,128)(2,1)}, u32[]{:S(2)}, u32[]{:S(2)}) %collective-permute-start.19) | collective-permute-done | bytes 344096 | tf_op jit(solution)/shard_map/ppermute | solution.py:26
  178.6 22.6 %collective-permute-done.20.refs_2_ = bf16[96,1792]{1,0:T(8,128)(2,1)} collective-permute-done((bf16[96,1792]{1,0:T(8,128)(2,1)}, bf16[96,1792]{1,0:T(8,128)(2,1)}, u32[]{:S(2)}, u32[]{:S(2)}) %collective-permute-start.20) | collective-permute-done | bytes 344096 | tf_op jit(solution)/shard_map/ppermute | solution.py:26
  201.2 2.6 %collective-permute-done.21.refs_3_ = bf16[96,1792]{1,0:T(8,128)(2,1)} collective-permute-done((bf16[96,1792]{1,0:T(8,128)(2,1)}, bf16[96,1792]{1,0:T(8,128)(2,1)}, u32[]{:S(2)}, u32[]{:S(2)}) %collective-permute-start.21) | collective-permute-done | bytes 344096 | tf_op jit(solution)/shard_map/ppermute | solution.py:26
  203.7 4.9 %collective-permute-done.24.refs_1_ = bf16[96,1792]{1,0:T(8,128)(2,1)S(1)} collective-permute-done((bf16[96,1792]{1,0:T(8,128)(2,1)}, bf16[96,1792]{1,0:T(8,128)(2,1)S(1)}, u32[]{:S(2)}, u32[]{:S(2)}) %collective-permute-start.24) | collective-permute-done | bytes 344096 | tf_op jit(solution)/shard_map/ppermute | solution.py:26
  208.7 5.7 %collective-permute-done.25.refs_2_ = bf16[96,1792]{1,0:T(8,128)(2,1)S(1)} collective-permute-done((bf16[96,1792]{1,0:T(8,128)(2,1)}, bf16[96,1792]{1,0:T(8,128)(2,1)S(1)}, u32[]{:S(2)}, u32[]{:S(2)}) %collective-permute-start.25) | collective-permute-done | bytes 344096 | tf_op jit(solution)/shard_map/ppermute | solution.py:26
  214.4 3.1 %collective-permute-done.26.refs_3_ = bf16[96,1792]{1,0:T(8,128)(2,1)S(1)} collective-permute-done((bf16[96,1792]{1,0:T(8,128)(2,1)}, bf16[96,1792]{1,0:T(8,128)(2,1)S(1)}, u32[]{:S(2)}, u32[]{:S(2)}) %collective-permute-start.26) | collective-permute-done | bytes 344096 | tf_op jit(solution)/shard_map/ppermute | solution.py:26
  218.2 2.9 %shard_map.137 = (bf16[64,1792]{1,0:T(8,128)(2,1)}, bf16[64,1792]{1,0:T(8,128)(2,1)}) custom-call(bf16[128,384]{1,0:T(8,128)(2,1)} %get-tuple-element.145.high, bf16[128,384]{1,0:T(8,128)(2,1)} %get-tuple-element.144.low, bf16[96,1792]{1,0:T(8,128)(2,1)} %get-tuple-element.128.refs_0_, bf16[96,1792]{1,0:T(8,128)(2,1)} %copy-done.6, ...), custom_call_target="tpu_custom_call" | custom-call | flops 352321536 | bytes 1835008 | tf_op jit(solution)/shard_map/pallas_call | solution.py:171
  221.7 2.9 %shard_map.136 = (bf16[64,1792]{1,0:T(8,128)(2,1)}, bf16[64,1792]{1,0:T(8,128)(2,1)}) custom-call(bf16[128,384]{1,0:T(8,128)(2,1)} %get-tuple-element.145.high, bf16[128,384]{1,0:T(8,128)(2,1)} %get-tuple-element.144.low, bf16[96,1792]{1,0:T(8,128)(2,1)} %get-tuple-element.123.refs_0_, bf16[96,1792]{1,0:T(8,128)(2,1)} %collective-permute-done.19.refs_1_, ...), custom_call_target="tpu_custom_call" | custom-call | flops 352321536 | bytes 1835008 | tf_op jit(solution)/shard_map/pallas_call | solution.py:171
  226.1 3.7 %collective-permute-done.28 = bf16[64,1792]{1,0:T(8,128)(2,1)S(1)} collective-permute-done((bf16[64,1792]{1,0:T(8,128)(2,1)}, bf16[64,1792]{1,0:T(8,128)(2,1)S(1)}, u32[]{:S(2)}, u32[]{:S(2)}) %collective-permute-start.28) | collective-permute-done | bytes 229408 | tf_op jit(solution)/shard_map/ppermute | solution.py:21
  229.8 3.2 %collective-permute-done.27 = bf16[64,1792]{1,0:T(8,128)(2,1)S(1)} collective-permute-done((bf16[64,1792]{1,0:T(8,128)(2,1)}, bf16[64,1792]{1,0:T(8,128)(2,1)S(1)}, u32[]{:S(2)}, u32[]{:S(2)}) %collective-permute-start.27) | collective-permute-done | bytes 229408 | tf_op jit(solution)/shard_map/ppermute | solution.py:21
  233.0 2.4 %maximum_select_fusion = bf16[2,32,7168]{2,1,0:T(8,128)(2,1)} fusion(bf16[2,32,1792]{2,1,0:T(8,128)(2,1)S(1)} %bitcast.39, bf16[2,32,1792]{2,1,0:T(8,128)(2,1)S(1)} %bitcast.41, bf16[2,32,1792]{2,1,0:T(8,128)(2,1)} %bitcast.38, bf16[2,32,1792]{2,1,0:T(8,128)(2,1)} %bitcast.40, pred[]{:T(512)S(6)} %eq.61), kind=kLoop, calls=%fused_computation.8 | loop fusion | flops 7798784 | bytes 1835009 | tf_op jit(solution)/shard_map/jit(_where)/select_n | solution.py:309
  (117 shorter events, 41.0 us)
Async XLA Ops:
  5.7 35.7 %collective-permute-start = (bf16[48,7168]{1,0:T(8,128)(2,1)}, bf16[48,7168]{1,0:T(8,128)(2,1)}, u32[]{:S(2)}, u32[]{:S(2)}) collective-permute-start(bf16[48,7168]{1,0:T(8,128)(2,1)} %get-tuple-element.73), channel_id=1, source_target_pairs={{0,8},{1,9},{2,10},{3,11},{4,12},{5,13},{6,14},{7,15},{8,16},{9,17... | collective-permute-start | bytes 2064392 | tf_op jit(solution)/shard_map/ppermute | solution.py:26
  7.3 48.6 %collective-permute-start.1 = (bf16[48,7168]{1,0:T(8,128)(2,1)}, bf16[48,7168]{1,0:T(8,128)(2,1)}, u32[]{:S(2)}, u32[]{:S(2)}) collective-permute-start(bf16[48,7168]{1,0:T(8,128)(2,1)} %get-tuple-element.74), channel_id=1, source_target_pairs={{0,24},{1,25},{2,26},{3,27},{4,28},{5,29},{6,30},{7,31},{8,0},{9,1... | collective-permute-start | bytes 2064392 | tf_op jit(solution)/shard_map/ppermute | solution.py:26
  7.7 48.1 %collective-permute-start.2 = (bf16[48,7168]{1,0:T(8,128)(2,1)}, bf16[48,7168]{1,0:T(8,128)(2,1)}, u32[]{:S(2)}, u32[]{:S(2)}) collective-permute-start(bf16[48,7168]{1,0:T(8,128)(2,1)} %get-tuple-element.72.refs_0_), channel_id=1, source_target_pairs={{0,4},{1,5},{2,6},{3,7},{4,0},{5,1},{6,2},{7,3},{8,12},{9,13},{10,... | collective-permute-start | bytes 2064392 | tf_op jit(solution)/shard_map/ppermute | solution.py:21
  9.2 46.6 %collective-permute-start.4 = (bf16[7168,128]{1,0:T(8,128)(2,1)}, bf16[7168,128]{1,0:T(8,128)(2,1)}, u32[]{:S(2)}, u32[]{:S(2)}) collective-permute-start(bf16[7168,128]{1,0:T(8,128)(2,1)} %refs_8_), channel_id=1, source_target_pairs={{0,2},{1,3},{2,0},{3,1},{4,6},{5,7},{6,4},{7,5},{8,10},{9,11},{10,... | collective-permute-start | bytes 5505032 | tf_op jit(solution)/shard_map/ppermute | solution.py:21
  11.7 44.1 %collective-permute-start.3 = (bf16[128,3584]{1,0:T(8,128)(2,1)}, bf16[128,3584]{1,0:T(8,128)(2,1)S(1)}, u32[]{:S(2)}, u32[]{:S(2)}) collective-permute-start(bf16[128,3584]{1,0:T(8,128)(2,1)} %constant_dynamic-slice_fusion.1), channel_id=1, source_target_pairs={{0,4},{1,5},{2,6},{3,7},{4,0},{5,1},{6,2},{7,3},{8,12},{9,13},{10,... | collective-permute-start | bytes 2752520 | tf_op jit(solution)/shard_map/ppermute | solution.py:21
  14.2 41.7 %all-to-all-start = ((bf16[32,8,640]{2,1,0:T(8,128)(2,1)}), bf16[32,8,640]{2,1,0:T(8,128)(2,1)S(1)}, u32[]{:S(2)}, u32[]{:S(2)}) async-start(bf16[32,8,640]{2,1,0:T(8,128)(2,1)} %maximum_maximum_fusion), calls=%async_computation | async-start | bytes 655360 | tf_op jit(solution)/shard_map/all_to_all | solution.py:249
  41.4 51.9 %collective-permute-start.8 = (bf16[7168,128]{1,0:T(8,128)(2,1)}, bf16[7168,128]{1,0:T(8,128)(2,1)}, u32[]{:S(2)}, u32[]{:S(2)}) collective-permute-start(bf16[7168,128]{1,0:T(8,128)(2,1)} %refs_12_), channel_id=1, source_target_pairs={{0,2},{1,3},{2,0},{3,1},{4,6},{5,7},{6,4},{7,5},{8,10},{9,11},{10,... | collective-permute-start | bytes 5505032 | tf_op jit(solution)/shard_map/ppermute | solution.py:21
  55.9 37.4 %collective-permute-start.9 = (bf16[7168,128]{1,0:T(8,128)(2,1)}, bf16[7168,128]{1,0:T(8,128)(2,1)}, u32[]{:S(2)}, u32[]{:S(2)}) collective-permute-start(bf16[7168,128]{1,0:T(8,128)(2,1)} %refs_8_), channel_id=1, source_target_pairs={{0,1},{1,0},{2,3},{3,2},{4,5},{5,4},{6,7},{7,6},{8,9},{9,8},{10,11... | collective-permute-start | bytes 5505032 | tf_op jit(solution)/shard_map/ppermute | solution.py:21
  56.0 37.3 %collective-permute-start.5 = (bf16[48,7168]{1,0:T(8,128)(2,1)}, bf16[48,7168]{1,0:T(8,128)(2,1)}, u32[]{:S(2)}, u32[]{:S(2)}) collective-permute-start(bf16[48,7168]{1,0:T(8,128)(2,1)} %get-tuple-element.81), channel_id=1, source_target_pairs={{0,16},{1,17},{2,18},{3,19},{4,20},{5,21},{6,22},{7,23},{8,24},{9,... | collective-permute-start | bytes 2064392 | tf_op jit(solution)/shard_map/ppermute | solution.py:26
  58.0 35.3 %collective-permute-start.6 = (bf16[48,7168]{1,0:T(8,128)(2,1)}, bf16[48,7168]{1,0:T(8,128)(2,1)}, u32[]{:S(2)}, u32[]{:S(2)}) collective-permute-start(bf16[48,7168]{1,0:T(8,128)(2,1)} %collective-permute-done.refs_1_), channel_id=1, source_target_pairs={{0,4},{1,5},{2,6},{3,7},{4,0},{5,1},{6,2},{7,3},{8,12},{9,13},{10,... | collective-permute-start | bytes 2064392 | tf_op jit(solution)/shard_map/ppermute | solution.py:21
  59.4 33.9 %collective-permute-start.7 = (bf16[48,7168]{1,0:T(8,128)(2,1)}, bf16[48,7168]{1,0:T(8,128)(2,1)}, u32[]{:S(2)}, u32[]{:S(2)}) collective-permute-start(bf16[48,7168]{1,0:T(8,128)(2,1)} %collective-permute-done.1.refs_3_), channel_id=1, source_target_pairs={{0,4},{1,5},{2,6},{3,7},{4,0},{5,1},{6,2},{7,3},{8,12},{9,13},{10,... | collective-permute-start | bytes 2064392 | tf_op jit(solution)/shard_map/ppermute | solution.py:21
  93.3 18.7 %collective-permute-start.11 = (bf16[7168,128]{1,0:T(8,128)(2,1)S(1)}, bf16[7168,128]{1,0:T(8,128)(2,1)S(1)}, u32[]{:S(2)}, u32[]{:S(2)}) collective-permute-start(bf16[7168,128]{1,0:T(8,128)(2,1)S(1)} %copy-done.13), channel_id=1, source_target_pairs={{0,1},{1,0},{2,3},{3,2},{4,5},{5,4},{6,7},{7,6},{8,9},{9,8},{10,11... | collective-permute-start | bytes 5505032 | tf_op jit(solution)/shard_map/ppermute | solution.py:21
  93.4 18.6 %collective-permute-start.12 = (bf16[7168,128]{1,0:T(8,128)(2,1)}, bf16[7168,128]{1,0:T(8,128)(2,1)S(1)}, u32[]{:S(2)}, u32[]{:S(2)}) collective-permute-start(bf16[7168,128]{1,0:T(8,128)(2,1)} %collective-permute-done.4.refs_10_), channel_id=1, source_target_pairs={{0,1},{1,0},{2,3},{3,2},{4,5},{5,4},{6,7},{7,6},{8,9},{9,8},{10,11... | collective-permute-start | bytes 5505032 | tf_op jit(solution)/shard_map/ppermute | solution.py:21
  93.9 18.1 %collective-permute-start.13 = (bf16[7168,128]{1,0:T(8,128)(2,1)}, bf16[7168,128]{1,0:T(8,128)(2,1)S(1)}, u32[]{:S(2)}, u32[]{:S(2)}) collective-permute-start(bf16[7168,128]{1,0:T(8,128)(2,1)} %collective-permute-done.8.refs_14_), channel_id=1, source_target_pairs={{0,1},{1,0},{2,3},{3,2},{4,5},{5,4},{6,7},{7,6},{8,9},{9,8},{10,11... | collective-permute-start | bytes 5505032 | tf_op jit(solution)/shard_map/ppermute | solution.py:21
  94.0 18.0 %collective-permute-start.10 = (bf16[48,7168]{1,0:T(8,128)(2,1)}, bf16[48,7168]{1,0:T(8,128)(2,1)S(1)}, u32[]{:S(2)}, u32[]{:S(2)}) collective-permute-start(bf16[48,7168]{1,0:T(8,128)(2,1)} %collective-permute-done.5.refs_2_), channel_id=1, source_target_pairs={{0,4},{1,5},{2,6},{3,7},{4,0},{5,1},{6,2},{7,3},{8,12},{9,13},{10,... | collective-permute-start | bytes 2064392 | tf_op jit(solution)/shard_map/ppermute | solution.py:21
  112.0 24.6 %collective-permute-start.14 = (bf16[256,3584]{1,0:T(8,128)(2,1)}, bf16[256,3584]{1,0:T(8,128)(2,1)}, u32[]{:S(2)}, u32[]{:S(2)}) collective-permute-start(bf16[256,3584]{1,0:T(8,128)(2,1)} %pad_maximum_fusion.own), channel_id=1, source_target_pairs={{0,1},{1,0},{2,3},{3,2},{4,5},{5,4},{6,7},{7,6},{8,9},{9,8},{10,11... | collective-permute-start | bytes 5505032 | tf_op jit(solution)/shard_map/ppermute | solution.py:21
  114.4 22.2 %collective-permute-start.15 = (bf16[256,1792]{1,0:T(8,128)(2,1)}, bf16[256,1792]{1,0:T(8,128)(2,1)}, u32[]{:S(2)}, u32[]{:S(2)}) collective-permute-start(bf16[256,1792]{1,0:T(8,128)(2,1)} %get-tuple-element.102), channel_id=1, source_target_pairs={{0,2},{1,3},{2,0},{3,1},{4,6},{5,7},{6,4},{7,5},{8,10},{9,11},{10,... | collective-permute-start | bytes 2752520 | tf_op jit(solution)/shard_map/ppermute | solution.py:21
  136.6 22.8 %collective-permute-start.22 = (bf16[256,1792]{1,0:T(8,128)(2,1)S(1)}, bf16[256,1792]{1,0:T(8,128)(2,1)S(1)}, u32[]{:S(2)}, u32[]{:S(2)}) collective-permute-start(bf16[256,1792]{1,0:T(8,128)(2,1)S(1)} %copy-done.3), channel_id=1, source_target_pairs={{0,2},{1,3},{2,0},{3,1},{4,6},{5,7},{6,4},{7,5},{8,10},{9,11},{10,... | collective-permute-start | bytes 2752520 | tf_op jit(solution)/shard_map/ppermute | solution.py:21
  155.1 22.5 %collective-permute-start.19 = (bf16[96,1792]{1,0:T(8,128)(2,1)}, bf16[96,1792]{1,0:T(8,128)(2,1)}, u32[]{:S(2)}, u32[]{:S(2)}) collective-permute-start(bf16[96,1792]{1,0:T(8,128)(2,1)} %get-tuple-element.115), channel_id=1, source_target_pairs={{0,24},{1,25},{2,26},{3,27},{4,28},{5,29},{6,30},{7,31},{8,0},{9,1... | collective-permute-start | bytes 1032200 | tf_op jit(solution)/shard_map/ppermute | solution.py:26
  155.6 45.6 %collective-permute-start.20 = (bf16[96,1792]{1,0:T(8,128)(2,1)}, bf16[96,1792]{1,0:T(8,128)(2,1)}, u32[]{:S(2)}, u32[]{:S(2)}) collective-permute-start(bf16[96,1792]{1,0:T(8,128)(2,1)} %get-tuple-element.116), channel_id=1, source_target_pairs={{0,16},{1,17},{2,18},{3,19},{4,20},{5,21},{6,22},{7,23},{8,24},{9,... | collective-permute-start | bytes 1032200 | tf_op jit(solution)/shard_map/ppermute | solution.py:26
  159.0 44.7 %collective-permute-start.21 = (bf16[96,1792]{1,0:T(8,128)(2,1)}, bf16[96,1792]{1,0:T(8,128)(2,1)}, u32[]{:S(2)}, u32[]{:S(2)}) collective-permute-start(bf16[96,1792]{1,0:T(8,128)(2,1)} %get-tuple-element.117), channel_id=1, source_target_pairs={{0,8},{1,9},{2,10},{3,11},{4,12},{5,13},{6,14},{7,15},{8,16},{9,17... | collective-permute-start | bytes 1032200 | tf_op jit(solution)/shard_map/ppermute | solution.py:26
  167.5 41.2 %collective-permute-start.24 = (bf16[96,1792]{1,0:T(8,128)(2,1)}, bf16[96,1792]{1,0:T(8,128)(2,1)S(1)}, u32[]{:S(2)}, u32[]{:S(2)}) collective-permute-start(bf16[96,1792]{1,0:T(8,128)(2,1)} %get-tuple-element.120), channel_id=1, source_target_pairs={{0,24},{1,25},{2,26},{3,27},{4,28},{5,29},{6,30},{7,31},{8,0},{9,1... | collective-permute-start | bytes 1032200 | tf_op jit(solution)/shard_map/ppermute | solution.py:26
  169.2 45.2 %collective-permute-start.25 = (bf16[96,1792]{1,0:T(8,128)(2,1)}, bf16[96,1792]{1,0:T(8,128)(2,1)S(1)}, u32[]{:S(2)}, u32[]{:S(2)}) collective-permute-start(bf16[96,1792]{1,0:T(8,128)(2,1)} %get-tuple-element.121), channel_id=1, source_target_pairs={{0,16},{1,17},{2,18},{3,19},{4,20},{5,21},{6,22},{7,23},{8,24},{9,... | collective-permute-start | bytes 1032200 | tf_op jit(solution)/shard_map/ppermute | solution.py:26
  177.6 39.9 %collective-permute-start.26 = (bf16[96,1792]{1,0:T(8,128)(2,1)}, bf16[96,1792]{1,0:T(8,128)(2,1)S(1)}, u32[]{:S(2)}, u32[]{:S(2)}) collective-permute-start(bf16[96,1792]{1,0:T(8,128)(2,1)} %get-tuple-element.122), channel_id=1, source_target_pairs={{0,8},{1,9},{2,10},{3,11},{4,12},{5,13},{6,14},{7,15},{8,16},{9,17... | collective-permute-start | bytes 1032200 | tf_op jit(solution)/shard_map/ppermute | solution.py:26
  (24 other events, 219.3 us)

commit v12 on v11

--- a/solution.py
+++ b/solution.py
@@ -11,6 +11,7 @@
 FF_WIN = 1024
 CORE, XBIT, YBIT = 1, 2, 4
 VMEM_BYTES = 60 * 1024 * 1024
+SMALL_BYTES = 14 * 1024 * 1024
 
 
 score_scale = 0.07216878364870323
@@ -59,7 +60,7 @@
         ],
         out_specs=[pl.BlockSpec((slots, chunk), lambda k: (0, k))] * planes,
         out_shape=[jax.ShapeDtypeStruct((slots, width), jnp.bfloat16)] * planes,
-        compiler_params=pltpu.CompilerParams(vmem_limit_bytes=VMEM_BYTES),
+        compiler_params=pltpu.CompilerParams(vmem_limit_bytes=SMALL_BYTES),
         cost_estimate=pl.CostEstimate(
             flops=2 * chosen.size * width,
             bytes_accessed=2 * width * (count + planes * slots),
@@ -145,7 +146,7 @@
         + [pl.BlockSpec((deep, chunk), lambda k: (0, k)) for _ in side],
         out_specs=[pl.BlockSpec((rows, chunk), lambda k: (0, k))] * planes,
         out_shape=[jax.ShapeDtypeStruct((rows, width), jnp.bfloat16)] * planes,
-        compiler_params=pltpu.CompilerParams(vmem_limit_bytes=VMEM_BYTES),
+        compiler_params=pltpu.CompilerParams(vmem_limit_bytes=SMALL_BYTES),
         cost_estimate=pl.CostEstimate(
             flops=2 * count * 2 * inner * width,
             bytes_accessed=8 * deep * width + 2 * count * width,
@@ -175,7 +176,7 @@
         + [pl.BlockSpec((rows, chunk), lambda k: (0, k)) for _ in parts],
         out_specs=[pl.BlockSpec((count, chunk), lambda k: (0, k))] * 2,
         out_shape=[out, out],
-        compiler_params=pltpu.CompilerParams(vmem_limit_bytes=VMEM_BYTES),
+        compiler_params=pltpu.CompilerParams(vmem_limit_bytes=SMALL_BYTES),
         cost_estimate=pl.CostEstimate(
             flops=4 * high.size * width,
             bytes_accessed=2 * width * (len(parts) * rows + 2 * count),
@@ -236,7 +237,7 @@
     chosen = chosen.astype(jnp.bfloat16)
 
     pack_0, out_1, out_2, out_3 = packs(
-        chosen.reshape(planes * slots, count), rows, planes, 2 * span
+        chosen.reshape(planes * slots, count), rows, planes, span
     )
     pack_0, out_1, out_3, latents, owners, requests, down_proj = together(
         pack_0, out_1, out_3, latents, owners, requests, down_proj
@@ -246,40 +247,47 @@
     down_y = swap(send, YBIT)
     outgoing = hand_over(latents, owners, requests)
 
-    incoming = lax.all_to_all(outgoing, "ep", split_axis=0, concat_axis=0, tiled=True)
-    own_1, own_3, peer_0, down_y, gate_x, out_2, incoming, down_proj, gate_proj = together(
-        own_1, own_3, peer_0, down_y, gate_x, out_2, incoming, down_proj, gate_proj
-    )
-    handed = incoming.reshape(-1, incoming.shape[2])
-    marks = handed[:, latents.shape[1]].astype(jnp.float32)[None, :]
-    attended = attend(queries, cache_latents, cache_lens, handed, marks)
+    own_1, own_3, peer_0, down_y, gate_x, out_2, outgoing, down_proj, gate_proj = together(
+        own_1, own_3, peer_0, down_y, gate_x, out_2, outgoing, down_proj, gate_proj
+    )
     own_2, peer_1, peer_3 = shift(out_2, 2 * split), swap(own_1, YBIT), swap(own_3, YBIT)
     up_x, gate_c = swap(up_proj, XBIT), swap(gate_proj, CORE)
     keep = lax.dynamic_slice_in_dim(down_proj, 2 * upper * span, 2 * span, 1)
     own = jnp.concatenate([keep, down_y], axis=0)
     own_0, rest = own[:, :span], own[:, span:]
 
-    own_2, peer_1, peer_3, up_x, gate_x, gate_c, up_proj, own, own_0, rest, attended = together(
-        own_2, peer_1, peer_3, up_x, gate_x, gate_c, up_proj, own, own_0, rest, attended
+    own_2, peer_1, peer_3, up_x, gate_x, gate_c, up_proj, own, own_0, rest = together(
+        own_2, peer_1, peer_3, up_x, gate_x, gate_c, up_proj, own, own_0, rest
     )
     peer_2, side_0 = swap(own_2, YBIT), swap(own_0, XBIT)
     up_c, gate_xc, up_xc = swap(up_proj, CORE), swap(gate_x, CORE), swap(up_x, CORE)
 
-    peer_2, up_c, gate_xc, up_xc, own = together(peer_2, up_c, gate_xc, up_xc, own)
-    own_c = swap(own, CORE)
+    peer_2, up_c, gate_xc, up_xc, side_0, own = together(
+        peer_2, up_c, gate_xc, up_xc, side_0, own
+    )
+    own_c, side_0c = swap(own, CORE), swap(side_0, CORE)
     units = (pack_0, own_1, own_2, own_3, peer_0, peer_1, peer_2, peer_3)
     weights = (gate_proj, gate_c, gate_x, gate_xc, up_proj, up_c, up_x, up_xc)
     hidden = hidden_units(units, weights, chunk)
-    hidden, own_c, side_0, rest, picks, gates = together(
-        hidden, own_c, side_0, rest, picks, gates
-    )
-    other, side_0c, side_1 = swap(hidden, YBIT), swap(side_0, CORE), swap(rest, XBIT)
+    hidden, own_c, side_0c, rest, picks, gates = together(
+        hidden, own_c, side_0c, rest, picks, gates
+    )
+    other, side_1 = swap(hidden, YBIT), swap(rest, XBIT)
     info = swap(jnp.concatenate([picks.astype(jnp.float32), gates], axis=1), YBIT)
-    other, side_0c, info, picks, gates = together(other, side_0c, info, picks, gates)
-    halves = (
-        down_values(hidden, other, (own, own_c), (side_0, side_0c), planes, span // 2, 0),
-        down_values(hidden, other, (own, own_c), (side_1, swap(side_1, CORE)), planes, span // 2, 2),
-    )
+    first = down_values(
+        hidden, other, (own, own_c), (side_0, side_0c), planes, span // 2, 0
+    )
+    first = list(first)
+    side_1, info, picks, gates, first[0] = together(side_1, info, picks, gates, first[0])
+    second = down_values(
+        hidden, other, (own, own_c), (side_1, swap(side_1, CORE)), planes, span // 2, 2
+    )
+    second = list(second)
+    outgoing, second[0] = together(outgoing, second[0])
+    incoming = lax.all_to_all(outgoing, "ep", split_axis=0, concat_axis=0, tiled=True)
+    handed = incoming.reshape(-1, incoming.shape[2])
+    marks = handed[:, latents.shape[1]].astype(jnp.float32)[None, :]
+    attended = attend(queries, cache_latents, cache_lens, handed, marks)
 
     top = picks.shape[1]
     tables = [
@@ -296,9 +304,9 @@
 
     backs = [
         [values[0]] + [shift(values[k], n_ep - k * split) for k in range(1, planes)]
-        for values in halves
+        for values in (first, second)
     ]
-    flat = together(*backs[0], *backs[1])
+    *flat, attended = together(*backs[0], *backs[1], attended)
     outs, others = [], []
     for back in (flat[:planes], flat[planes:]):
         mine, theirs = combine(high, low, back, span // 2)

time: 237 us -> 231 us (0.975)
  waiting for transfers between devices: 146 us -> 122 us
  starting transfers between devices: 32.8 us -> 46.9 us
  other arithmetic: 9.13 us -> 12.6 us
  Pallas kernels: 38.5 us -> 35.1 us
  local copies, waits for them, and re-layouts: 7.49 us -> 10.1 us
    ppermute x9, waiting for transfers between devices: 67.3 us -> 11.5 us  [shift(): lax.ppermute(value, 'ep', [(i, (i + step) % count) for i in range(count)])]
    all_to_all x1, waiting for transfers between devices: 13 us -> 36.3 us  [layer(): lax.all_to_all(outgoing, 'ep', split_axis=0, concat_axis=0, tiled=True)]
    ppermute x20, starting transfers between devices: 15.5 us -> 29 us  [swap(): return lax.ppermute(value, 'ep', [(i, i ^ bit) for i in range(count)])]
    ppermute x20, waiting for transfers between devices: 66 us -> 74.5 us  [swap(): return lax.ppermute(value, 'ep', [(i, i ^ bit) for i in range(count)])]
    unnamed x38 -> x40, local copies, waits for them, and re-layouts: 5.54 us -> 5.92 us
  transfers between devices with their start and end apart: 30 -> 30, of which waited for: 15 -> 11; matrix products, arithmetic and copies ran while one was open for 3% -> 7% of each run, Pallas kernels for 14% -> 15%
where the time goes in v12:
time: 231 us; the launch traced here: 229 us
  waiting for transfers between devices  122 us (53%)
  starting transfers between devices  46.9 us (20%)
  Pallas kernels  35.1 us (15%)
  other arithmetic  12.6 us (5%)
  local copies, waits for them, and re-layouts  10.1 us (4%)
    ppermute x20, waiting for transfers between devices, swap(): return lax.ppermute(value, 'ep', [(i, i ^ bit) for i in range(count)])  74.5 us
    all_to_all x1, waiting for transfers between devices, layer(): lax.all_to_all(outgoing, 'ep', split_axis=0, concat_axis=0, tiled=True)  36.3 us
    ppermute x20, starting transfers between devices, swap(): return lax.ppermute(value, 'ep', [(i, i ^ bit) for i in range(count)])  29 us
    ppermute x9, starting transfers between devices, shift(): lax.ppermute(value, 'ep', [(i, (i + step) % count) for i in range(count)])  12.1 us
    ppermute x9, waiting for transfers between devices, shift(): lax.ppermute(value, 'ep', [(i, (i + step) % count) for i in range(count)])  11.5 us
    pallas_call x1, Pallas kernels, hidden_units(): pl.pallas_call(partial(hidden_kernel, len(units)), grid=(width // chunk,)...  11 us
    pallas_call x1, Pallas kernels, attend(): pl.pallas_call(attend_kernel, grid=(requests,), in_specs=[pl.BlockSpec(me...  9.1 us
    pallas_call x2, Pallas kernels, down_values(): pl.pallas_call(down_kernel, grid=(width // chunk,), in_specs=[pl.BlockSpe...  8.07 us
  transfers between devices with their start and end apart: 30, of which 11 were waited for; matrix products, arithmetic and copies ran while one was open for 7% of the time, Pallas kernels for 15%

profile of v12, /device:TPU:16, one launch (start us, length us, event | category | flops | bytes accessed | tf_op | source)
XLA Modules:
  0.0 229.1 jit_solution(11764043342701867764)
XLA Ops:
  4.6 2.5 %shard_map.131 = (bf16[48,7168]{1,0:T(8,128)(2,1)S(1)}, bf16[48,7168]{1,0:T(8,128)(2,1)}, bf16[48,7168]{1,0:T(8,128)(2,1)S(1)}, bf16[48,7168]{1,0:T(8,128)(2,1)}) custom-call(bf16[192,64]{1,0:T(8,128)(2,1)S(1)} %fusion.8.chosen, bf16[64,7168]{1,0:T(8,128)(2,1)S(1)} %bitcast.31), custom_call_target="tpu_custom_call" | custom-call | flops 176160768 | bytes 3670016 | tf_op jit(solution)/shard_map/pallas_call | solution.py:54
  17.2 8.6 %collective-permute-done.refs_1_ = bf16[48,7168]{1,0:T(8,128)(2,1)} collective-permute-done((bf16[48,7168]{1,0:T(8,128)(2,1)}, bf16[48,7168]{1,0:T(8,128)(2,1)}, u32[]{:S(2)}, u32[]{:S(2)}) %collective-permute-start) | collective-permute-done | bytes 688160 | tf_op jit(solution)/shard_map/ppermute | solution.py:27
  25.8 14.0 %collective-permute-start.8 = (bf16[7168,128]{1,0:T(8,128)(2,1)}, bf16[7168,128]{1,0:T(8,128)(2,1)}, u32[]{:S(2)}, u32[]{:S(2)}) collective-permute-start(bf16[7168,128]{1,0:T(8,128)(2,1)} %refs_12_), channel_id=1, source_target_pairs={{0,2},{1,3},{2,0},{3,1},{4,6},{5,7},{6,4},{7,5},{8,10},{9,11},{10,... | collective-permute-start | bytes 5505032 | tf_op jit(solution)/shard_map/ppermute | solution.py:22
  39.8 5.4 %collective-permute-done.3 = bf16[128,3584]{1,0:T(8,128)(2,1)} collective-permute-done((bf16[128,3584]{1,0:T(8,128)(2,1)}, bf16[128,3584]{1,0:T(8,128)(2,1)}, u32[]{:S(2)}, u32[]{:S(2)}) %collective-permute-start.3) | collective-permute-done | bytes 917536 | tf_op jit(solution)/shard_map/ppermute | solution.py:22
  45.2 2.2 collective-permute-start.5
  51.7 2.7 %pad_maximum_fusion.own = bf16[256,3584]{1,0:T(8,128)(2,1)} fusion(bf16[128,3584]{1,0:T(8,128)(2,1)} %collective-permute-done.3, bf16[128,3584]{1,0:T(8,128)(2,1)S(1)} %constant_dynamic-slice_fusion), kind=kLoop, calls=%fused_computation.2 | loop fusion | flops 3670016 | bytes 3670016 | tf_op jit(solution)/shard_map/concatenate | solution.py:256
  54.4 27.7 %collective-permute-done.8.refs_14_ = bf16[7168,128]{1,0:T(8,128)(2,1)} collective-permute-done((bf16[7168,128]{1,0:T(8,128)(2,1)}, bf16[7168,128]{1,0:T(8,128)(2,1)}, u32[]{:S(2)}, u32[]{:S(2)}) %collective-permute-start.8) | collective-permute-done | bytes 1835040 | tf_op jit(solution)/shard_map/ppermute | solution.py:22
  85.9 16.0 %collective-permute-done.10.refs_6_ = bf16[48,7168]{1,0:T(8,128)(2,1)S(1)} collective-permute-done((bf16[48,7168]{1,0:T(8,128)(2,1)S(1)}, bf16[48,7168]{1,0:T(8,128)(2,1)S(1)}, u32[]{:S(2)}, u32[]{:S(2)}) %collective-permute-start.10) | collective-permute-done | bytes 688160 | tf_op jit(solution)/shard_map/ppermute | solution.py:22
  101.8 3.7 %collective-permute-done.14.side = bf16[256,1792]{1,0:T(8,128)(2,1)S(1)} collective-permute-done((bf16[256,1792]{1,0:T(8,128)(2,1)S(1)}, bf16[256,1792]{1,0:T(8,128)(2,1)S(1)}, u32[]{:S(2)}, u32[]{:S(2)}) %collective-permute-start.14) | collective-permute-done | bytes 917536 | tf_op jit(solution)/shard_map/ppermute | solution.py:22
  108.1 11.0 %shard_map.132.mine = bf16[384,512]{1,0:T(8,128)(2,1)} custom-call(bf16[48,7168]{1,0:T(8,128)(2,1)} %copy-done.6, bf16[48,7168]{1,0:T(8,128)(2,1)} %collective-permute-done.refs_1_, bf16[48,7168]{1,0:T(8,128)(2,1)} %copy-done.15, bf16[48,7168]{1,0:T(8,128)(2,1)} %collective-permute-done.1.refs_3_, bf16[48,7168]{1,0:T(8,128)(2,1)} %collective-permute-done.2.refs_4_, ...), custom_call_target="tpu_custom_call" | custom-call | flops 5637144576 | bytes 20185088 | tf_op jit(solution)/shard_map/pallas_call | solution.py:99
  122.8 9.4 %collective-permute-done.19.other = bf16[384,512]{1,0:T(8,128)(2,1)S(1)} collective-permute-done((bf16[384,512]{1,0:T(8,128)(2,1)}, bf16[384,512]{1,0:T(8,128)(2,1)S(1)}, u32[]{:S(2)}, u32[]{:S(2)}) %collective-permute-start.19) | collective-permute-done | bytes 393248 | tf_op jit(solution)/shard_map/ppermute | solution.py:22
  133.2 4.1 %shard_map.133 = (bf16[96,1792]{1,0:T(8,128)(2,1)S(1)}, bf16[96,1792]{1,0:T(8,128)(2,1)}, bf16[96,1792]{1,0:T(8,128)(2,1)}, bf16[96,1792]{1,0:T(8,128)(2,1)}) custom-call(bf16[384,512]{1,0:T(8,128)(2,1)S(1)} %copy-done.1, bf16[384,512]{1,0:T(8,128)(2,1)S(1)} %collective-permute-done.19.other, bf16[256,3584]{1,0:T(8,128)(2,1)} %pad_maximum_fusion.own, ...), custom_call_target="tpu_custom_call" | custom-call | flops 1409286144 | bytes 5046272 | tf_op jit(solution)/shard_map/pallas_call | solution.py:141
  137.3 4.9 %collective-permute-done.17.side = bf16[256,1792]{1,0:T(8,128)(2,1)S(1)} collective-permute-done((bf16[256,1792]{1,0:T(8,128)(2,1)}, bf16[256,1792]{1,0:T(8,128)(2,1)S(1)}, u32[]{:S(2)}, u32[]{:S(2)}) %collective-permute-start.17) | collective-permute-done | bytes 917536 | tf_op jit(solution)/shard_map/ppermute | solution.py:22
  142.6 3.5 %collective-permute-start.21 = (bf16[96,1792]{1,0:T(8,128)(2,1)}, bf16[96,1792]{1,0:T(8,128)(2,1)S(1)}, u32[]{:S(2)}, u32[]{:S(2)}) collective-permute-start(bf16[96,1792]{1,0:T(8,128)(2,1)} %get-tuple-element.119), channel_id=1, source_target_pairs={{0,16},{1,17},{2,18},{3,19},{4,20},{5,21},{6,22},{7,23},{8,24},{9,... | collective-permute-start | bytes 1032200 | tf_op jit(solution)/shard_map/ppermute | solution.py:27
  146.4 4.0 %shard_map.134 = (bf16[96,1792]{1,0:T(8,128)(2,1)S(1)}, bf16[96,1792]{1,0:T(8,128)(2,1)}, bf16[96,1792]{1,0:T(8,128)(2,1)}, bf16[96,1792]{1,0:T(8,128)(2,1)}) custom-call(bf16[384,512]{1,0:T(8,128)(2,1)S(1)} %copy-done.1, bf16[384,512]{1,0:T(8,128)(2,1)S(1)} %collective-permute-done.19.other, bf16[256,3584]{1,0:T(8,128)(2,1)} %pad_maximum_fusion.own, ...), custom_call_target="tpu_custom_call" | custom-call | flops 1409286144 | bytes 5046272 | tf_op jit(solution)/shard_map/pallas_call | solution.py:141
  151.1 5.9 %all-to-all-start = ((bf16[32,8,640]{2,1,0:T(8,128)(2,1)}), bf16[32,8,640]{2,1,0:T(8,128)(2,1)}, u32[]{:S(2)}, u32[]{:S(2)}) async-start(bf16[32,8,640]{2,1,0:T(8,128)(2,1)} %maximum_maximum_fusion), calls=%async_computation | async-start | bytes 655360 | tf_op jit(solution)/shard_map/all_to_all | solution.py:287
  158.5 3.3 %collective-permute-start.25 = (bf16[96,1792]{1,0:T(8,128)(2,1)}, bf16[96,1792]{1,0:T(8,128)(2,1)}, u32[]{:S(2)}, u32[]{:S(2)}) collective-permute-start(bf16[96,1792]{1,0:T(8,128)(2,1)} %get-tuple-element.126), channel_id=1, source_target_pairs={{0,16},{1,17},{2,18},{3,19},{4,20},{5,21},{6,22},{7,23},{8,24},{9,... | collective-permute-start | bytes 1032200 | tf_op jit(solution)/shard_map/ppermute | solution.py:27
  162.8 36.3 %all-to-all-done = bf16[32,8,640]{2,1,0:T(8,128)(2,1)} async-done(((bf16[32,8,640]{2,1,0:T(8,128)(2,1)}), bf16[32,8,640]{2,1,0:T(8,128)(2,1)}, u32[]{:S(2)}, u32[]{:S(2)}) %all-to-all-start) | async-done | bytes 327712 | tf_op jit(solution)/shard_map/all_to_all | solution.py:287
  200.8 9.1 %shard_map.135 = bf16[8,128,512]{2,1,0:T(8,128)(2,1)} custom-call(s32[8]{0:T(128)} %lens.1, bf16[8,576,128]{2,1,0:T(8,128)(2,1)} %bitcast.36, bf16[8,576,256]{2,1,0:T(8,128)(2,1)} %bitcast.34, bf16[256,640]{1,0:T(8,128)(2,1)} %bitcast.14.handed, f32[1,256]{1,0:T(1,128)} %bitcast.45), custom_call_target="tpu_custom_call" | custom-call | flops 1140850688 | bytes 4587520 | tf_op jit(solution)/shard_map/pallas_call | solution.py:349
  209.9 3.0 %collective-permute-done.26.refs_3_ = bf16[96,1792]{1,0:T(8,128)(2,1)} collective-permute-done((bf16[96,1792]{1,0:T(8,128)(2,1)}, bf16[96,1792]{1,0:T(8,128)(2,1)}, u32[]{:S(2)}, u32[]{:S(2)}) %collective-permute-start.26) | collective-permute-done | bytes 344096 | tf_op jit(solution)/shard_map/ppermute | solution.py:27
  216.1 2.7 %shard_map.137 = (bf16[64,1792]{1,0:T(8,128)(2,1)S(1)}, bf16[64,1792]{1,0:T(8,128)(2,1)}) custom-call(bf16[128,384]{1,0:T(8,128)(2,1)S(1)} %get-tuple-element.151.high, bf16[128,384]{1,0:T(8,128)(2,1)S(1)} %get-tuple-element.150.low, bf16[96,1792]{1,0:T(8,128)(2,1)S(1)} %copy-done.4, bf16[96,1792]{1,0:T(8,128)(2,1)} %collective-permute-done.24.refs_1_, ...), custom_call_target="tpu_custom_call" | custom-call | flops 352321536 | bytes 1835008 | tf_op jit(solution)/shard_map/pallas_call | solution.py:172
  219.3 3.5 %collective-permute-done.27 = bf16[64,1792]{1,0:T(8,128)(2,1)} collective-permute-done((bf16[64,1792]{1,0:T(8,128)(2,1)}, bf16[64,1792]{1,0:T(8,128)(2,1)}, u32[]{:S(2)}, u32[]{:S(2)}) %collective-permute-start.27) | collective-permute-done | bytes 229408 | tf_op jit(solution)/shard_map/ppermute | solution.py:22
  222.8 3.9 %collective-permute-done.28 = bf16[64,1792]{1,0:T(8,128)(2,1)S(1)} collective-permute-done((bf16[64,1792]{1,0:T(8,128)(2,1)}, bf16[64,1792]{1,0:T(8,128)(2,1)S(1)}, u32[]{:S(2)}, u32[]{:S(2)}) %collective-permute-start.28) | collective-permute-done | bytes 229408 | tf_op jit(solution)/shard_map/ppermute | solution.py:22
  226.6 2.4 %maximum_select_fusion = bf16[2,32,7168]{2,1,0:T(8,128)(2,1)} fusion(bf16[2,32,1792]{2,1,0:T(8,128)(2,1)S(1)} %bitcast.38, bf16[2,32,1792]{2,1,0:T(8,128)(2,1)} %bitcast.17, bf16[2,32,1792]{2,1,0:T(8,128)(2,1)S(1)} %bitcast.33, bf16[2,32,1792]{2,1,0:T(8,128)(2,1)} %bitcast.32, pred[]{:T(512)S(6)} %eq.61), kind=kLoop, calls=%fused_computation.8 | loop fusion | flops 7798784 | bytes 1835009 | tf_op jit(solution)/shard_map/jit(_where)/select_n | solution.py:317
  (119 shorter events, 38.4 us)
Async XLA Ops:
  0.7 44.5 %collective-permute-start.4 = (bf16[7168,128]{1,0:T(8,128)(2,1)}, bf16[7168,128]{1,0:T(8,128)(2,1)}, u32[]{:S(2)}, u32[]{:S(2)}) collective-permute-start(bf16[7168,128]{1,0:T(8,128)(2,1)} %refs_8_), channel_id=1, source_target_pairs={{0,2},{1,3},{2,0},{3,1},{4,6},{5,7},{6,4},{7,5},{8,10},{9,11},{10,... | collective-permute-start | bytes 5505032 | tf_op jit(solution)/shard_map/ppermute | solution.py:22
  7.1 18.7 %collective-permute-start = (bf16[48,7168]{1,0:T(8,128)(2,1)}, bf16[48,7168]{1,0:T(8,128)(2,1)}, u32[]{:S(2)}, u32[]{:S(2)}) collective-permute-start(bf16[48,7168]{1,0:T(8,128)(2,1)} %get-tuple-element.76), channel_id=1, source_target_pairs={{0,8},{1,9},{2,10},{3,11},{4,12},{5,13},{6,14},{7,15},{8,16},{9,17... | collective-permute-start | bytes 2064392 | tf_op jit(solution)/shard_map/ppermute | solution.py:27
  8.7 31.1 %collective-permute-start.1 = (bf16[48,7168]{1,0:T(8,128)(2,1)}, bf16[48,7168]{1,0:T(8,128)(2,1)}, u32[]{:S(2)}, u32[]{:S(2)}) collective-permute-start(bf16[48,7168]{1,0:T(8,128)(2,1)} %get-tuple-element.77), channel_id=1, source_target_pairs={{0,24},{1,25},{2,26},{3,27},{4,28},{5,29},{6,30},{7,31},{8,0},{9,1... | collective-permute-start | bytes 2064392 | tf_op jit(solution)/shard_map/ppermute | solution.py:27
  9.1 30.6 %collective-permute-start.2 = (bf16[48,7168]{1,0:T(8,128)(2,1)S(1)}, bf16[48,7168]{1,0:T(8,128)(2,1)}, u32[]{:S(2)}, u32[]{:S(2)}) collective-permute-start(bf16[48,7168]{1,0:T(8,128)(2,1)S(1)} %get-tuple-element.75.refs_0_), channel_id=1, source_target_pairs={{0,4},{1,5},{2,6},{3,7},{4,0},{5,1},{6,2},{7,3},{8,12},{9,13},{10,... | collective-permute-start | bytes 2064392 | tf_op jit(solution)/shard_map/ppermute | solution.py:22
  11.6 33.6 %collective-permute-start.3 = (bf16[128,3584]{1,0:T(8,128)(2,1)}, bf16[128,3584]{1,0:T(8,128)(2,1)}, u32[]{:S(2)}, u32[]{:S(2)}) collective-permute-start(bf16[128,3584]{1,0:T(8,128)(2,1)} %constant_dynamic-slice_fusion.1), channel_id=1, source_target_pairs={{0,4},{1,5},{2,6},{3,7},{4,0},{5,1},{6,2},{7,3},{8,12},{9,13},{10,... | collective-permute-start | bytes 2752520 | tf_op jit(solution)/shard_map/ppermute | solution.py:22
  25.8 56.4 %collective-permute-start.8 = (bf16[7168,128]{1,0:T(8,128)(2,1)}, bf16[7168,128]{1,0:T(8,128)(2,1)}, u32[]{:S(2)}, u32[]{:S(2)}) collective-permute-start(bf16[7168,128]{1,0:T(8,128)(2,1)} %refs_12_), channel_id=1, source_target_pairs={{0,2},{1,3},{2,0},{3,1},{4,6},{5,7},{6,4},{7,5},{8,10},{9,11},{10,... | collective-permute-start | bytes 5505032 | tf_op jit(solution)/shard_map/ppermute | solution.py:22
  45.2 37.0 %collective-permute-start.9 = (bf16[7168,128]{1,0:T(8,128)(2,1)}, bf16[7168,128]{1,0:T(8,128)(2,1)}, u32[]{:S(2)}, u32[]{:S(2)}) collective-permute-start(bf16[7168,128]{1,0:T(8,128)(2,1)} %refs_8_), channel_id=1, source_target_pairs={{0,1},{1,0},{2,3},{3,2},{4,5},{5,4},{6,7},{7,6},{8,9},{9,8},{10,11... | collective-permute-start | bytes 5505032 | tf_op jit(solution)/shard_map/ppermute | solution.py:22
  45.2 36.9 %collective-permute-start.5 = (bf16[48,7168]{1,0:T(8,128)(2,1)S(1)}, bf16[48,7168]{1,0:T(8,128)(2,1)S(1)}, u32[]{:S(2)}, u32[]{:S(2)}) collective-permute-start(bf16[48,7168]{1,0:T(8,128)(2,1)S(1)} %get-tuple-element.84), channel_id=1, source_target_pairs={{0,16},{1,17},{2,18},{3,19},{4,20},{5,21},{6,22},{7,23},{8,24},{9,... | collective-permute-start | bytes 2064392 | tf_op jit(solution)/shard_map/ppermute | solution.py:27
  47.4 34.7 %collective-permute-start.6 = (bf16[48,7168]{1,0:T(8,128)(2,1)}, bf16[48,7168]{1,0:T(8,128)(2,1)S(1)}, u32[]{:S(2)}, u32[]{:S(2)}) collective-permute-start(bf16[48,7168]{1,0:T(8,128)(2,1)} %collective-permute-done.refs_1_), channel_id=1, source_target_pairs={{0,4},{1,5},{2,6},{3,7},{4,0},{5,1},{6,2},{7,3},{8,12},{9,13},{10,... | collective-permute-start | bytes 2064392 | tf_op jit(solution)/shard_map/ppermute | solution.py:22
  49.0 33.2 %collective-permute-start.7 = (bf16[48,7168]{1,0:T(8,128)(2,1)}, bf16[48,7168]{1,0:T(8,128)(2,1)S(1)}, u32[]{:S(2)}, u32[]{:S(2)}) collective-permute-start(bf16[48,7168]{1,0:T(8,128)(2,1)} %collective-permute-done.1.refs_3_), channel_id=1, source_target_pairs={{0,4},{1,5},{2,6},{3,7},{4,0},{5,1},{6,2},{7,3},{8,12},{9,13},{10,... | collective-permute-start | bytes 2064392 | tf_op jit(solution)/shard_map/ppermute | solution.py:22
  82.2 23.4 %collective-permute-start.11 = (bf16[7168,128]{1,0:T(8,128)(2,1)S(1)}, bf16[7168,128]{1,0:T(8,128)(2,1)S(1)}, u32[]{:S(2)}, u32[]{:S(2)}) collective-permute-start(bf16[7168,128]{1,0:T(8,128)(2,1)S(1)} %copy-done.11), channel_id=1, source_target_pairs={{0,1},{1,0},{2,3},{3,2},{4,5},{5,4},{6,7},{7,6},{8,9},{9,8},{10,11... | collective-permute-start | bytes 5505032 | tf_op jit(solution)/shard_map/ppermute | solution.py:22
  82.3 23.3 %collective-permute-start.12 = (bf16[7168,128]{1,0:T(8,128)(2,1)}, bf16[7168,128]{1,0:T(8,128)(2,1)S(1)}, u32[]{:S(2)}, u32[]{:S(2)}) collective-permute-start(bf16[7168,128]{1,0:T(8,128)(2,1)} %collective-permute-done.4.refs_10_), channel_id=1, source_target_pairs={{0,1},{1,0},{2,3},{3,2},{4,5},{5,4},{6,7},{7,6},{8,9},{9,8},{10,11... | collective-permute-start | bytes 5505032 | tf_op jit(solution)/shard_map/ppermute | solution.py:22
  82.8 22.8 %collective-permute-start.13 = (bf16[7168,128]{1,0:T(8,128)(2,1)}, bf16[7168,128]{1,0:T(8,128)(2,1)S(1)}, u32[]{:S(2)}, u32[]{:S(2)}) collective-permute-start(bf16[7168,128]{1,0:T(8,128)(2,1)} %collective-permute-done.8.refs_14_), channel_id=1, source_target_pairs={{0,1},{1,0},{2,3},{3,2},{4,5},{5,4},{6,7},{7,6},{8,9},{9,8},{10,11... | collective-permute-start | bytes 5505032 | tf_op jit(solution)/shard_map/ppermute | solution.py:22
  82.8 22.7 %collective-permute-start.14 = (bf16[256,1792]{1,0:T(8,128)(2,1)S(1)}, bf16[256,1792]{1,0:T(8,128)(2,1)S(1)}, u32[]{:S(2)}, u32[]{:S(2)}) collective-permute-start(bf16[256,1792]{1,0:T(8,128)(2,1)S(1)} %get-tuple-element.96), channel_id=1, source_target_pairs={{0,2},{1,3},{2,0},{3,1},{4,6},{5,7},{6,4},{7,5},{8,10},{9,11},{10,... | collective-permute-start | bytes 2752520 | tf_op jit(solution)/shard_map/ppermute | solution.py:22
  84.3 17.5 %collective-permute-start.10 = (bf16[48,7168]{1,0:T(8,128)(2,1)S(1)}, bf16[48,7168]{1,0:T(8,128)(2,1)S(1)}, u32[]{:S(2)}, u32[]{:S(2)}) collective-permute-start(bf16[48,7168]{1,0:T(8,128)(2,1)S(1)} %collective-permute-done.5.refs_2_), channel_id=1, source_target_pairs={{0,4},{1,5},{2,6},{3,7},{4,0},{5,1},{6,2},{7,3},{8,12},{9,13},{10,... | collective-permute-start | bytes 2064392 | tf_op jit(solution)/shard_map/ppermute | solution.py:22
  119.1 23.0 %collective-permute-start.17 = (bf16[256,1792]{1,0:T(8,128)(2,1)}, bf16[256,1792]{1,0:T(8,128)(2,1)S(1)}, u32[]{:S(2)}, u32[]{:S(2)}) collective-permute-start(bf16[256,1792]{1,0:T(8,128)(2,1)} %get-tuple-element.107), channel_id=1, source_target_pairs={{0,2},{1,3},{2,0},{3,1},{4,6},{5,7},{6,4},{7,5},{8,10},{9,11},{10,... | collective-permute-start | bytes 2752520 | tf_op jit(solution)/shard_map/ppermute | solution.py:22
  122.2 15.0 %collective-permute-start.18 = (f32[64,4]{0,1:T(4,128)S(1)}, f32[64,4]{0,1:T(4,128)S(1)}, u32[]{:S(2)}, u32[]{:S(2)}) collective-permute-start(f32[64,4]{0,1:T(4,128)S(1)} %pad_maximum_fusion.1), channel_id=1, source_target_pairs={{0,4},{1,5},{2,6},{3,7},{4,0},{5,1},{6,2},{7,3},{8,12},{9,13},{10,... | collective-permute-start | bytes 3080 | tf_op jit(solution)/shard_map/ppermute | solution.py:22
  142.2 19.7 %collective-permute-start.20 = (bf16[96,1792]{1,0:T(8,128)(2,1)}, bf16[96,1792]{1,0:T(8,128)(2,1)S(1)}, u32[]{:S(2)}, u32[]{:S(2)}) collective-permute-start(bf16[96,1792]{1,0:T(8,128)(2,1)} %get-tuple-element.118), channel_id=1, source_target_pairs={{0,24},{1,25},{2,26},{3,27},{4,28},{5,29},{6,30},{7,31},{8,0},{9,1... | collective-permute-start | bytes 1032200 | tf_op jit(solution)/shard_map/ppermute | solution.py:27
  142.6 67.3 %collective-permute-start.21 = (bf16[96,1792]{1,0:T(8,128)(2,1)}, bf16[96,1792]{1,0:T(8,128)(2,1)S(1)}, u32[]{:S(2)}, u32[]{:S(2)}) collective-permute-start(bf16[96,1792]{1,0:T(8,128)(2,1)} %get-tuple-element.119), channel_id=1, source_target_pairs={{0,16},{1,17},{2,18},{3,19},{4,20},{5,21},{6,22},{7,23},{8,24},{9,... | collective-permute-start | bytes 1032200 | tf_op jit(solution)/shard_map/ppermute | solution.py:27
  146.1 63.8 %collective-permute-start.22 = (bf16[96,1792]{1,0:T(8,128)(2,1)}, bf16[96,1792]{1,0:T(8,128)(2,1)S(1)}, u32[]{:S(2)}, u32[]{:S(2)}) collective-permute-start(bf16[96,1792]{1,0:T(8,128)(2,1)} %get-tuple-element.120), channel_id=1, source_target_pairs={{0,8},{1,9},{2,10},{3,11},{4,12},{5,13},{6,14},{7,15},{8,16},{9,17... | collective-permute-start | bytes 1032200 | tf_op jit(solution)/shard_map/ppermute | solution.py:27
  151.1 48.0 %all-to-all-start = ((bf16[32,8,640]{2,1,0:T(8,128)(2,1)}), bf16[32,8,640]{2,1,0:T(8,128)(2,1)}, u32[]{:S(2)}, u32[]{:S(2)}) async-start(bf16[32,8,640]{2,1,0:T(8,128)(2,1)} %maximum_maximum_fusion), calls=%async_computation | async-start | bytes 655360 | tf_op jit(solution)/shard_map/all_to_all | solution.py:287
  158.0 51.9 %collective-permute-start.24 = (bf16[96,1792]{1,0:T(8,128)(2,1)}, bf16[96,1792]{1,0:T(8,128)(2,1)}, u32[]{:S(2)}, u32[]{:S(2)}) collective-permute-start(bf16[96,1792]{1,0:T(8,128)(2,1)} %get-tuple-element.125), channel_id=1, source_target_pairs={{0,24},{1,25},{2,26},{3,27},{4,28},{5,29},{6,30},{7,31},{8,0},{9,1... | collective-permute-start | bytes 1032200 | tf_op jit(solution)/shard_map/ppermute | solution.py:27
  158.5 51.4 %collective-permute-start.25 = (bf16[96,1792]{1,0:T(8,128)(2,1)}, bf16[96,1792]{1,0:T(8,128)(2,1)}, u32[]{:S(2)}, u32[]{:S(2)}) collective-permute-start(bf16[96,1792]{1,0:T(8,128)(2,1)} %get-tuple-element.126), channel_id=1, source_target_pairs={{0,16},{1,17},{2,18},{3,19},{4,20},{5,21},{6,22},{7,23},{8,24},{9,... | collective-permute-start | bytes 1032200 | tf_op jit(solution)/shard_map/ppermute | solution.py:27
  161.8 51.0 %collective-permute-start.26 = (bf16[96,1792]{1,0:T(8,128)(2,1)}, bf16[96,1792]{1,0:T(8,128)(2,1)}, u32[]{:S(2)}, u32[]{:S(2)}) collective-permute-start(bf16[96,1792]{1,0:T(8,128)(2,1)} %get-tuple-element.127), channel_id=1, source_target_pairs={{0,8},{1,9},{2,10},{3,11},{4,12},{5,13},{6,14},{7,15},{8,16},{9,17... | collective-permute-start | bytes 1032200 | tf_op jit(solution)/shard_map/ppermute | solution.py:27
  (25 other events, 306.6 us)

commit v13 on v12

--- a/solution.py
+++ b/solution.py
@@ -25,6 +25,12 @@
 def shift(value, step):
     count = lax.axis_size("ep")
     return lax.ppermute(value, "ep", [(i, (i + step) % count) for i in range(count)])
+
+
+def cross(value, step):
+    count = lax.axis_size("ep")
+    pairs = [(i, (i + step) % count ^ YBIT) for i in range(count)]
+    return lax.ppermute(value, "ep", pairs)
 
 
 def together(*values):
@@ -113,76 +119,115 @@
     )(*units, *weights)
 
 
-def down_kernel(mine, other, own, own_c, side, side_c, *outs):
+def down_kernel(mine, other, own, own_c, side_0, side_0c, side_1, side_1c, *outs):
     deep = own.shape[0] // 2
-    parts = (own, own_c, side, side_c)
-    table = jnp.concatenate(
-        [part[:deep, :] for part in parts] + [part[deep:, :] for part in parts], axis=0
-    )
     count = mine.shape[0] // 2
-    rows = count // len(outs)
-    joined = jnp.concatenate(
-        [
-            jnp.concatenate([mine[:count, :], other[count:, :]], axis=1),
-            jnp.concatenate([mine[count:, :], other[:count, :]], axis=1),
-        ],
-        axis=0,
-    )
-    value = jnp.dot(joined, table, preferred_element_type=jnp.float32).astype(jnp.bfloat16)
-    for at, out in enumerate(outs):
-        out[:rows, :] = value[at * rows : (at + 1) * rows]
-        out[rows:, :] = value[count + at * rows : count + (at + 1) * rows]
-
-
-def down_values(mine, other, own, side, planes, chunk, offset):
+    rows = 2 * count // len(outs)
+
+    def fill(side, side_c):
+        parts = (own, own_c, side, side_c)
+        table = jnp.concatenate(
+            [part[:deep, :] for part in parts] + [part[deep:, :] for part in parts], axis=0
+        )
+        joined = jnp.concatenate(
+            [
+                jnp.concatenate([mine[:count, :], other[count:, :]], axis=1),
+                jnp.concatenate([mine[count:, :], other[:count, :]], axis=1),
+            ],
+            axis=0,
+        )
+        value = jnp.dot(joined, table, preferred_element_type=jnp.float32).astype(jnp.bfloat16)
+        for at, out in enumerate(outs):
+            out[...] = value[at * rows : (at + 1) * rows]
+
+    first = pl.program_id(0) < pl.num_programs(0) // 2
+
+    @pl.when(first)
+    def _():
+        fill(side_0, side_0c)
+
+    @pl.when(jnp.logical_not(first))
+    def _():
+        fill(side_1, side_1c)
+
+
+def down_values(mine, other, own, firsts, seconds, planes, chunk):
     count, inner = mine.shape
-    deep, width = side[0].shape
-    rows = count // planes
+    deep, width = own[0].shape
+    rows = count // (2 * planes)
+    steps = width // chunk
+    half = steps // 2
     return pl.pallas_call(
         down_kernel,
-        grid=(width // chunk,),
+        grid=(steps,),
         in_specs=[pl.BlockSpec((count, inner), lambda k: (0, 0))] * 2
-        + [pl.BlockSpec((deep, chunk), lambda k: (0, k + offset)) for _ in own]
-        + [pl.BlockSpec((deep, chunk), lambda k: (0, k)) for _ in side],
-        out_specs=[pl.BlockSpec((rows, chunk), lambda k: (0, k))] * planes,
-        out_shape=[jax.ShapeDtypeStruct((rows, width), jnp.bfloat16)] * planes,
+        + [pl.BlockSpec((deep, chunk), lambda k: (0, k)) for _ in own]
+        + [pl.BlockSpec((deep, chunk), lambda k: (0, jnp.minimum(k, half - 1))) for _ in firsts]
+        + [pl.BlockSpec((deep, chunk), lambda k: (0, jnp.maximum(k - half, 0))) for _ in seconds],
+        out_specs=[pl.BlockSpec((rows, chunk), lambda k: (0, k))] * (2 * planes),
+        out_shape=[jax.ShapeDtypeStruct((rows, width), jnp.bfloat16)] * (2 * planes),
         compiler_params=pltpu.CompilerParams(vmem_limit_bytes=SMALL_BYTES),
         cost_estimate=pl.CostEstimate(
             flops=2 * count * 2 * inner * width,
             bytes_accessed=8 * deep * width + 2 * count * width,
             transcendentals=0,
         ),
-    )(mine, other, *own, *side)
-
-
-def combine_kernel(high, low, *refs):
-    parts, (mine, theirs) = refs[:-2], refs[-2:]
-    values = jnp.concatenate([part[...] for part in parts], axis=0)
-    total = jnp.dot(high[...], values, preferred_element_type=jnp.float32)
-    total = total + jnp.dot(low[...], values, preferred_element_type=jnp.float32)
-    rows = mine.shape[0]
-    mine[...] = total[:rows].astype(jnp.bfloat16)
-    theirs[...] = total[rows:].astype(jnp.bfloat16)
-
-
-def combine(high, low, parts, chunk):
-    rows, width = parts[0].shape
-    count = high.shape[0] // 2
-    out = jax.ShapeDtypeStruct((count, width), jnp.bfloat16)
+    )(mine, other, *own, *firsts, *seconds)
+
+
+def combine_kernel(upper, high, low, *refs):
+    parts, out = refs[:-1], refs[-1]
+    planes = len(parts) // 2
+
+    def mix(chosen):
+        values = jnp.concatenate([part[...] for part in chosen], axis=0)
+        total = jnp.dot(high[...], values, preferred_element_type=jnp.float32)
+        total = total + jnp.dot(low[...], values, preferred_element_type=jnp.float32)
+        out[...] = total.astype(jnp.bfloat16)
+
+    side = pl.program_id(0)
+
+    @pl.when(side == 0)
+    def _():
+        mix(parts[:planes])
+
+    @pl.when(side == 1)
+    def _():
+        mix(parts[planes:])
+
+
+def combine(upper, high, low, mine, theirs, chunk):
+    rows, width = mine[0].shape
+    count = high.shape[0]
+    steps = width // chunk
+
+    def own_block(g, k, upper):
+        return 0, jnp.where(g == 0, k, steps - 1)
+
+    def other_block(g, k, upper):
+        return 0, jnp.where(g == 0, 0, k)
+
+    def out_block(g, k, upper):
+        return 0, (upper[0] + g) % 2 * steps + k
+
     return pl.pallas_call(
         combine_kernel,
-        grid=(width // chunk,),
-        in_specs=[pl.BlockSpec(high.shape, lambda k: (0, 0))] * 2
-        + [pl.BlockSpec((rows, chunk), lambda k: (0, k)) for _ in parts],
-        out_specs=[pl.BlockSpec((count, chunk), lambda k: (0, k))] * 2,
-        out_shape=[out, out],
+        grid_spec=pltpu.PrefetchScalarGridSpec(
+            num_scalar_prefetch=1,
+            grid=(2, steps),
+            in_specs=[pl.BlockSpec(high.shape, lambda g, k, upper: (0, 0))] * 2
+            + [pl.BlockSpec((rows, chunk), own_block) for _ in mine]
+            + [pl.BlockSpec((rows, chunk), other_block) for _ in theirs],
+            out_specs=pl.BlockSpec((count, chunk), out_block),
+        ),
+        out_shape=jax.ShapeDtypeStruct((count, 2 * width), jnp.bfloat16),
         compiler_params=pltpu.CompilerParams(vmem_limit_bytes=SMALL_BYTES),
         cost_estimate=pl.CostEstimate(
-            flops=4 * high.size * width,
-            bytes_accessed=2 * width * (len(parts) * rows + 2 * count),
+            flops=8 * high.size * width,
+            bytes_accessed=4 * width * (len(mine) * rows + count),
             transcendentals=0,
         ),
-    )(high, low, *parts)
+    )(upper.reshape(1), high, low, *mine, *theirs)
 
 
 def places(picks, planes, split):
@@ -252,69 +297,38 @@
     )
     own_2, peer_1, peer_3 = shift(out_2, 2 * split), swap(own_1, YBIT), swap(own_3, YBIT)
     up_x, gate_c = swap(up_proj, XBIT), swap(gate_proj, CORE)
+    incoming = lax.all_to_all(outgoing, "ep", split_axis=0, concat_axis=0, tiled=True)
     keep = lax.dynamic_slice_in_dim(down_proj, 2 * upper * span, 2 * span, 1)
     own = jnp.concatenate([keep, down_y], axis=0)
-    own_0, rest = own[:, :span], own[:, span:]
-
-    own_2, peer_1, peer_3, up_x, gate_x, gate_c, up_proj, own, own_0, rest = together(
-        own_2, peer_1, peer_3, up_x, gate_x, gate_c, up_proj, own, own_0, rest
-    )
-    peer_2, side_0 = swap(own_2, YBIT), swap(own_0, XBIT)
+    begin, rest = own[:, :span], own[:, span:]
+
+    own_2, peer_1, peer_3, up_x, gate_x, gate_c, up_proj, own, begin, rest, incoming = together(
+        own_2, peer_1, peer_3, up_x, gate_x, gate_c, up_proj, own, begin, rest, incoming
+    )
+    peer_2, side_0 = swap(own_2, YBIT), swap(begin, XBIT)
     up_c, gate_xc, up_xc = swap(up_proj, CORE), swap(gate_x, CORE), swap(up_x, CORE)
-
-    peer_2, up_c, gate_xc, up_xc, side_0, own = together(
-        peer_2, up_c, gate_xc, up_xc, side_0, own
-    )
-    own_c, side_0c = swap(own, CORE), swap(side_0, CORE)
+    handed = incoming.reshape(-1, incoming.shape[2])
+    marks = handed[:, latents.shape[1]].astype(jnp.float32)[None, :]
+    attended = attend(queries, cache_latents, cache_lens, handed, marks)
+    peer_2, up_c, gate_xc, up_xc, side_0, rest, own, attended, picks, gates = together(
+        peer_2, up_c, gate_xc, up_xc, side_0, rest, own, attended, picks, gates
+    )
+    own_c, side_0c, side_1 = swap(own, CORE), swap(side_0, CORE), swap(rest, XBIT)
     units = (pack_0, own_1, own_2, own_3, peer_0, peer_1, peer_2, peer_3)
     weights = (gate_proj, gate_c, gate_x, gate_xc, up_proj, up_c, up_x, up_xc)
     hidden = hidden_units(units, weights, chunk)
-    hidden, own_c, side_0c, rest, picks, gates = together(
-        hidden, own_c, side_0c, rest, picks, gates
-    )
-    other, side_1 = swap(hidden, YBIT), swap(rest, XBIT)
-    info = swap(jnp.concatenate([picks.astype(jnp.float32), gates], axis=1), YBIT)
-    first = down_values(
-        hidden, other, (own, own_c), (side_0, side_0c), planes, span // 2, 0
-    )
-    first = list(first)
-    side_1, info, picks, gates, first[0] = together(side_1, info, picks, gates, first[0])
-    second = down_values(
-        hidden, other, (own, own_c), (side_1, swap(side_1, CORE)), planes, span // 2, 2
-    )
-    second = list(second)
-    outgoing, second[0] = together(outgoing, second[0])
-    incoming = lax.all_to_all(outgoing, "ep", split_axis=0, concat_axis=0, tiled=True)
-    handed = incoming.reshape(-1, incoming.shape[2])
-    marks = handed[:, latents.shape[1]].astype(jnp.float32)[None, :]
-    attended = attend(queries, cache_latents, cache_lens, handed, marks)
-
-    top = picks.shape[1]
-    tables = [
-        gate_table(picks, gates, planes, split, slots),
-        gate_table(info[:, :top].astype(jnp.int32), info[:, top:], planes, split, slots),
-    ]
-    tables = [
-        jnp.pad(tables[0], ((0, 0), (0, 0), (0, slots))),
-        jnp.pad(tables[1], ((0, 0), (0, 0), (slots, 0))),
-    ]
-    table = jnp.concatenate(tables, axis=0).reshape(2 * count, planes * 2 * slots)
+    hidden, own_c, side_0c, picks, gates = together(hidden, own_c, side_0c, picks, gates)
+    table = gate_table(picks, gates, planes, split, slots).reshape(count, planes * slots)
     high = lax.reduce_precision(table, 8, 7)
     high, low = high.astype(jnp.bfloat16), (table - high).astype(jnp.bfloat16)
-
-    backs = [
-        [values[0]] + [shift(values[k], n_ep - k * split) for k in range(1, planes)]
-        for values in (first, second)
+    other, side_1, high, low = together(swap(hidden, YBIT), side_1, high, low)
+    firsts, seconds = (side_0, side_0c), (side_1, swap(side_1, CORE))
+    values = down_values(hidden, other, (own, own_c), firsts, seconds, planes, span // 2)
+    mine = [values[0]] + [shift(values[k], n_ep - k * split) for k in range(1, planes)]
+    theirs = [swap(values[planes], YBIT)] + [
+        cross(values[planes + k], n_ep - k * split) for k in range(1, planes)
     ]
-    *flat, attended = together(*backs[0], *backs[1], attended)
-    outs, others = [], []
-    for back in (flat[:planes], flat[planes:]):
-        mine, theirs = combine(high, low, back, span // 2)
-        outs.append(mine)
-        others.append(swap(theirs, YBIT))
-    low_first = jnp.concatenate(outs + others, axis=1)
-    high_first = jnp.concatenate(others + outs, axis=1)
-    return jnp.where(upper == 0, low_first, high_first), attended
+    return combine(upper, high, low, mine, theirs, span), attended
 
 
 def attend_kernel(lens, query, cache, handed, marks, out):

time: 231 us -> 217 us (0.939)
  starting transfers between devices: 46.9 us -> 35.4 us
  waiting for transfers between devices: 122 us -> 129 us
  other arithmetic: 12.6 us -> 8.36 us
  Pallas kernels: 35.1 us -> 31.7 us
    ppermute x9 -> x6, waiting for transfers between devices: 11.5 us -> 59.3 us  [shift(): lax.ppermute(value, 'ep', [(i, (i + step) % count) for i in range(count)])]
    all_to_all x1, waiting for transfers between devices: 36.3 us -> 1.3 us  [layer(): lax.all_to_all(outgoing, 'ep', split_axis=0, concat_axis=0, tiled=True)]
    ppermute x20 -> x18, waiting for transfers between devices: 74.5 us -> 53.7 us  [swap(): return lax.ppermute(value, 'ep', [(i, i ^ bit) for i in range(count)])]
    ppermute x0 -> x3, waiting for transfers between devices: none -> 14.8 us  [cross(): return lax.ppermute(value, 'ep', pairs)]
    ppermute x20 -> x18, starting transfers between devices: 29 us -> 15 us  [swap(): return lax.ppermute(value, 'ep', [(i, i ^ bit) for i in range(count)])]
    ppermute x0 -> x3, starting transfers between devices: none -> 7.17 us  [cross(): return lax.ppermute(value, 'ep', pairs)]
    ppermute x9 -> x6, starting transfers between devices: 12.1 us -> 7.91 us  [shift(): lax.ppermute(value, 'ep', [(i, (i + step) % count) for i in range(count)])]
    pallas_call x4 -> x2, Pallas kernels: 12.5 us -> 8.94 us  [the longest x1 6.08 us: down_values(): pl.pallas_call(down_kernel, grid=(steps,), in_specs=[pl.BlockSpec((count,...]
  transfers between devices with their start and end apart: 30 -> 28, of which waited for: 11 -> 16; matrix products, arithmetic and copies ran while one was open for 7% -> 6% of each run, Pallas kernels for 15% -> 11%
where the time goes in v13:
time: 217 us; the launch traced here: 215 us
  waiting for transfers between devices  129 us (59%)
  starting transfers between devices  35.4 us (16%)
  Pallas kernels  31.7 us (15%)
  local copies, waits for them, and re-layouts  8.59 us (4%)
  other arithmetic  8.36 us (4%)
    ppermute x6, waiting for transfers between devices, shift(): lax.ppermute(value, 'ep', [(i, (i + step) % count) for i in range(count)])  59.3 us
    ppermute x18, waiting for transfers between devices, swap(): return lax.ppermute(value, 'ep', [(i, i ^ bit) for i in range(count)])  53.7 us
    ppermute x18, starting transfers between devices, swap(): return lax.ppermute(value, 'ep', [(i, i ^ bit) for i in range(count)])  15 us
    ppermute x3, waiting for transfers between devices, cross(): return lax.ppermute(value, 'ep', pairs)  14.8 us
    pallas_call x1, Pallas kernels, hidden_units(): pl.pallas_call(partial(hidden_kernel, len(units)), grid=(width // chunk,)...  11.1 us
    pallas_call x1, Pallas kernels, attend(): pl.pallas_call(attend_kernel, grid=(requests,), in_specs=[pl.BlockSpec(me...  9.2 us
    ppermute x6, starting transfers between devices, shift(): lax.ppermute(value, 'ep', [(i, (i + step) % count) for i in range(count)])  7.91 us
    ppermute x3, starting transfers between devices, cross(): return lax.ppermute(value, 'ep', pairs)  7.17 us
  transfers between devices with their start and end apart: 28, of which 16 were waited for; matrix products, arithmetic and copies ran while one was open for 6% of the time, Pallas kernels for 11%

profile of v13, /device:TPU:16, one launch (start us, length us, event | category | flops | bytes accessed | tf_op | source)
XLA Modules:
  0.0 215.1 jit_solution(3838380271008735313)
XLA Ops:
  5.1 2.5 %shard_map.131 = (bf16[48,7168]{1,0:T(8,128)(2,1)S(1)}, bf16[48,7168]{1,0:T(8,128)(2,1)}, bf16[48,7168]{1,0:T(8,128)(2,1)S(1)}, bf16[48,7168]{1,0:T(8,128)(2,1)}) custom-call(bf16[192,64]{1,0:T(8,128)(2,1)S(1)} %fusion.3.chosen, bf16[64,7168]{1,0:T(8,128)(2,1)S(1)} %bitcast.28), custom_call_target="tpu_custom_call" | custom-call | flops 176160768 | bytes 3670016 | tf_op jit(solution)/shard_map/pallas_call | solution.py:60
  17.8 21.9 %collective-permute-done.refs_1_ = bf16[48,7168]{1,0:T(8,128)(2,1)} collective-permute-done((bf16[48,7168]{1,0:T(8,128)(2,1)}, bf16[48,7168]{1,0:T(8,128)(2,1)}, u32[]{:S(2)}, u32[]{:S(2)}) %collective-permute-start) | collective-permute-done | bytes 688160 | tf_op jit(solution)/shard_map/ppermute | solution.py:27
  40.3 5.5 %collective-permute-done.3 = bf16[128,3584]{1,0:T(8,128)(2,1)} collective-permute-done((bf16[128,3584]{1,0:T(8,128)(2,1)}, bf16[128,3584]{1,0:T(8,128)(2,1)}, u32[]{:S(2)}, u32[]{:S(2)}) %collective-permute-start.3) | collective-permute-done | bytes 917536 | tf_op jit(solution)/shard_map/ppermute | solution.py:22
  45.8 5.3 %all-to-all-start = ((bf16[32,8,640]{2,1,0:T(8,128)(2,1)}), bf16[32,8,640]{2,1,0:T(8,128)(2,1)S(1)}, u32[]{:S(2)}, u32[]{:S(2)}) async-start(bf16[32,8,640]{2,1,0:T(8,128)(2,1)} %maximum_maximum_fusion), calls=%async_computation | async-start | bytes 655360 | tf_op jit(solution)/shard_map/all_to_all | solution.py:300
  51.4 1.8 collective-permute-start.6
  53.5 2.5 %fusion.1 = (bf16[256,1792]{1,0:T(8,128)(2,1)}, bf16[256,1792]{1,0:T(8,128)(2,1)}) fusion(bf16[128,3584]{1,0:T(8,128)(2,1)S(1)} %constant_dynamic-slice_fusion, bf16[128,3584]{1,0:T(8,128)(2,1)} %collective-permute-done.3), kind=kLoop, calls=%fused_computation.7 | loop fusion | flops 3670016 | bytes 3670016 | tf_op jit(solution)/shard_map/concatenate | solution.py:302
  56.0 2.5 %pad_maximum_fusion.own = bf16[256,3584]{1,0:T(8,128)(2,1)} fusion(bf16[128,3584]{1,0:T(8,128)(2,1)} %collective-permute-done.3, bf16[128,3584]{1,0:T(8,128)(2,1)S(1)} %constant_dynamic-slice_fusion), kind=kLoop, calls=%fused_computation.2 | loop fusion | flops 3670016 | bytes 3670016 | tf_op jit(solution)/shard_map/concatenate | solution.py:302
  58.5 26.7 %collective-permute-done.8.refs_14_ = bf16[7168,128]{1,0:T(8,128)(2,1)} collective-permute-done((bf16[7168,128]{1,0:T(8,128)(2,1)}, bf16[7168,128]{1,0:T(8,128)(2,1)}, u32[]{:S(2)}, u32[]{:S(2)}) %collective-permute-start.8) | collective-permute-done | bytes 1835040 | tf_op jit(solution)/shard_map/ppermute | solution.py:22
  92.7 9.2 %shard_map.132 = bf16[8,128,512]{2,1,0:T(8,128)(2,1)} custom-call(s32[8]{0:T(128)} %lens.1, bf16[8,576,128]{2,1,0:T(8,128)(2,1)} %bitcast.33, bf16[8,576,256]{2,1,0:T(8,128)(2,1)} %bitcast.29, bf16[256,640]{1,0:T(8,128)(2,1)} %bitcast.31, f32[1,256]{1,0:T(1,128)} %bitcast.41), custom_call_target="tpu_custom_call" | custom-call | flops 1140850688 | bytes 4587520 | tf_op jit(solution)/shard_map/pallas_call | solution.py:363
  101.9 6.3 %collective-permute-done.10.refs_6_ = bf16[48,7168]{1,0:T(8,128)(2,1)} collective-permute-done((bf16[48,7168]{1,0:T(8,128)(2,1)}, bf16[48,7168]{1,0:T(8,128)(2,1)}, u32[]{:S(2)}, u32[]{:S(2)}) %collective-permute-start.10) | collective-permute-done | bytes 688160 | tf_op jit(solution)/shard_map/ppermute | solution.py:22
  108.2 3.7 %collective-permute-done.14.side_0 = bf16[256,1792]{1,0:T(8,128)(2,1)} collective-permute-done((bf16[256,1792]{1,0:T(8,128)(2,1)}, bf16[256,1792]{1,0:T(8,128)(2,1)}, u32[]{:S(2)}, u32[]{:S(2)}) %collective-permute-start.14) | collective-permute-done | bytes 917536 | tf_op jit(solution)/shard_map/ppermute | solution.py:22
  114.0 11.1 %shard_map.133.mine = bf16[384,512]{1,0:T(8,128)(2,1)} custom-call(bf16[48,7168]{1,0:T(8,128)(2,1)} %copy-done.4, bf16[48,7168]{1,0:T(8,128)(2,1)} %collective-permute-done.refs_1_, bf16[48,7168]{1,0:T(8,128)(2,1)} %collective-permute-done.5.refs_2_, bf16[48,7168]{1,0:T(8,128)(2,1)} %collective-permute-done.1.refs_3_, ...), custom_call_target="tpu_custom_call" | custom-call | flops 5637144576 | bytes 20185088 | tf_op jit(solution)/shard_map/pallas_call | solution.py:105
  127.3 7.9 %collective-permute-done.18.side_1 = bf16[256,1792]{1,0:T(8,128)(2,1)} collective-permute-done((bf16[256,1792]{1,0:T(8,128)(2,1)}, bf16[256,1792]{1,0:T(8,128)(2,1)}, u32[]{:S(2)}, u32[]{:S(2)}) %collective-permute-start.18) | collective-permute-done | bytes 917536 | tf_op jit(solution)/shard_map/ppermute | solution.py:22
  136.2 2.7 %collective-permute-done.19.side_1c = bf16[256,1792]{1,0:T(8,128)(2,1)S(1)} collective-permute-done((bf16[256,1792]{1,0:T(8,128)(2,1)}, bf16[256,1792]{1,0:T(8,128)(2,1)S(1)}, u32[]{:S(2)}, u32[]{:S(2)}) %collective-permute-start.19) | collective-permute-done | bytes 917536 | tf_op jit(solution)/shard_map/ppermute | solution.py:22
  141.4 6.1 %shard_map.134 = (bf16[48,3584]{1,0:T(8,128)(2,1)S(1)}, bf16[48,3584]{1,0:T(8,128)(2,1)S(1)}, bf16[48,3584]{1,0:T(8,128)(2,1)S(1)}, bf16[48,3584]{1,0:T(8,128)(2...) custom-call(bf16[384,512]{1,0:T(8,128)(2,1)S(1)} %copy-done.5, ...), custom_call_target="tpu_custom_call" | custom-call | flops 2818572288 | bytes 10092544 | tf_op jit(solution)/shard_map/pallas_call | solution.py:160
  148.1 4.4 %collective-permute-start.21 = (bf16[48,3584]{1,0:T(8,128)(2,1)S(1)}, bf16[48,3584]{1,0:T(8,128)(2,1)S(1)}, u32[]{:S(2)}, u32[]{:S(2)}) collective-permute-start(bf16[48,3584]{1,0:T(8,128)(2,1)S(1)} %get-tuple-element.111), channel_id=1, source_target_pairs={{0,16},{1,17},{2,18},{3,19},{4,20},{5,21},{6,22},{7,23},{8,24},{9,... | collective-permute-start | bytes 1032200 | tf_op jit(solution)/shard_map/ppermute | solution.py:27
  155.9 3.0 %collective-permute-done.20.refs_1_ = bf16[48,3584]{1,0:T(8,128)(2,1)S(1)} collective-permute-done((bf16[48,3584]{1,0:T(8,128)(2,1)S(1)}, bf16[48,3584]{1,0:T(8,128)(2,1)S(1)}, u32[]{:S(2)}, u32[]{:S(2)}) %collective-permute-start.20) | collective-permute-done | bytes 344096 | tf_op jit(solution)/shard_map/ppermute | solution.py:27
  158.9 5.7 %collective-permute-start.25 = (bf16[48,3584]{1,0:T(8,128)(2,1)S(1)}, bf16[48,3584]{1,0:T(8,128)(2,1)S(1)}, u32[]{:S(2)}, u32[]{:S(2)}) collective-permute-start(bf16[48,3584]{1,0:T(8,128)(2,1)S(1)} %get-tuple-element.115), channel_id=1, source_target_pairs={{0,20},{1,21},{2,22},{3,23},{4,16},{5,17},{6,18},{7,19},{8,28},{9,... | collective-permute-start | bytes 1032200 | tf_op jit(solution)/shard_map/ppermute | solution.py:33
  164.7 14.0 %collective-permute-done.21.refs_2_ = bf16[48,3584]{1,0:T(8,128)(2,1)S(1)} collective-permute-done((bf16[48,3584]{1,0:T(8,128)(2,1)S(1)}, bf16[48,3584]{1,0:T(8,128)(2,1)S(1)}, u32[]{:S(2)}, u32[]{:S(2)}) %collective-permute-start.21) | collective-permute-done | bytes 344096 | tf_op jit(solution)/shard_map/ppermute | solution.py:27
  178.6 18.7 %collective-permute-done.22.refs_3_ = bf16[48,3584]{1,0:T(8,128)(2,1)S(1)} collective-permute-done((bf16[48,3584]{1,0:T(8,128)(2,1)S(1)}, bf16[48,3584]{1,0:T(8,128)(2,1)S(1)}, u32[]{:S(2)}, u32[]{:S(2)}) %collective-permute-start.22) | collective-permute-done | bytes 344096 | tf_op jit(solution)/shard_map/ppermute | solution.py:27
  197.4 4.5 %collective-permute-done.24.refs_5_ = bf16[48,3584]{1,0:T(8,128)(2,1)S(1)} collective-permute-done((bf16[48,3584]{1,0:T(8,128)(2,1)S(1)}, bf16[48,3584]{1,0:T(8,128)(2,1)S(1)}, u32[]{:S(2)}, u32[]{:S(2)}) %collective-permute-start.24) | collective-permute-done | bytes 344096 | tf_op jit(solution)/shard_map/ppermute | solution.py:33
  201.9 6.6 %collective-permute-done.25.refs_6_ = bf16[48,3584]{1,0:T(8,128)(2,1)S(1)} collective-permute-done((bf16[48,3584]{1,0:T(8,128)(2,1)S(1)}, bf16[48,3584]{1,0:T(8,128)(2,1)S(1)}, u32[]{:S(2)}, u32[]{:S(2)}) %collective-permute-start.25) | collective-permute-done | bytes 344096 | tf_op jit(solution)/shard_map/ppermute | solution.py:33
  208.4 3.8 %collective-permute-done.26.refs_7_ = bf16[48,3584]{1,0:T(8,128)(2,1)S(1)} collective-permute-done((bf16[48,3584]{1,0:T(8,128)(2,1)S(1)}, bf16[48,3584]{1,0:T(8,128)(2,1)S(1)}, u32[]{:S(2)}, u32[]{:S(2)}) %collective-permute-start.26) | collective-permute-done | bytes 344096 | tf_op jit(solution)/shard_map/ppermute | solution.py:33
  212.2 2.9 %shard_map.135 = bf16[64,7168]{1,0:T(8,128)(2,1)} custom-call(s32[1]{0:T(128)} %bitcast.upper, bf16[64,192]{1,0:T(8,128)(2,1)S(1)} %get-tuple-element.103.high, bf16[64,192]{1,0:T(8,128)(2,1)S(1)} %get-tuple-element.104.low, bf16[48,3584]{1,0:T(8,128)(2,1)S(1)} %get-tuple-element.109.refs_0_, bf16[48,3584]{1,0:T(8,128)(2,1)S(1)} %collective-permute-done.20.refs_1_, ...), custom_call_target="tpu_custom_call" | custom-call | flops 352321536 | bytes 3670016 | tf_op jit(solution)/shard_map/pallas_call | solution.py:213
  (99 shorter events, 35.2 us)
Async XLA Ops:
  0.7 45.1 %collective-permute-start.4 = (bf16[7168,128]{1,0:T(8,128)(2,1)}, bf16[7168,128]{1,0:T(8,128)(2,1)}, u32[]{:S(2)}, u32[]{:S(2)}) collective-permute-start(bf16[7168,128]{1,0:T(8,128)(2,1)} %refs_8_), channel_id=1, source_target_pairs={{0,2},{1,3},{2,0},{3,1},{4,6},{5,7},{6,4},{7,5},{8,10},{9,11},{10,... | collective-permute-start | bytes 5505032 | tf_op jit(solution)/shard_map/ppermute | solution.py:22
  7.7 32.0 %collective-permute-start = (bf16[48,7168]{1,0:T(8,128)(2,1)}, bf16[48,7168]{1,0:T(8,128)(2,1)}, u32[]{:S(2)}, u32[]{:S(2)}) collective-permute-start(bf16[48,7168]{1,0:T(8,128)(2,1)} %get-tuple-element.64), channel_id=1, source_target_pairs={{0,8},{1,9},{2,10},{3,11},{4,12},{5,13},{6,14},{7,15},{8,16},{9,17... | collective-permute-start | bytes 2064392 | tf_op jit(solution)/shard_map/ppermute | solution.py:27
  9.2 31.1 %collective-permute-start.1 = (bf16[48,7168]{1,0:T(8,128)(2,1)}, bf16[48,7168]{1,0:T(8,128)(2,1)}, u32[]{:S(2)}, u32[]{:S(2)}) collective-permute-start(bf16[48,7168]{1,0:T(8,128)(2,1)} %get-tuple-element.65), channel_id=1, source_target_pairs={{0,24},{1,25},{2,26},{3,27},{4,28},{5,29},{6,30},{7,31},{8,0},{9,1... | collective-permute-start | bytes 2064392 | tf_op jit(solution)/shard_map/ppermute | solution.py:27
  9.7 30.7 %collective-permute-start.2 = (bf16[48,7168]{1,0:T(8,128)(2,1)S(1)}, bf16[48,7168]{1,0:T(8,128)(2,1)}, u32[]{:S(2)}, u32[]{:S(2)}) collective-permute-start(bf16[48,7168]{1,0:T(8,128)(2,1)S(1)} %get-tuple-element.63.refs_0_), channel_id=1, source_target_pairs={{0,4},{1,5},{2,6},{3,7},{4,0},{5,1},{6,2},{7,3},{8,12},{9,13},{10,... | collective-permute-start | bytes 2064392 | tf_op jit(solution)/shard_map/ppermute | solution.py:22
  12.2 33.6 %collective-permute-start.3 = (bf16[128,3584]{1,0:T(8,128)(2,1)}, bf16[128,3584]{1,0:T(8,128)(2,1)}, u32[]{:S(2)}, u32[]{:S(2)}) collective-permute-start(bf16[128,3584]{1,0:T(8,128)(2,1)} %constant_dynamic-slice_fusion.1), channel_id=1, source_target_pairs={{0,4},{1,5},{2,6},{3,7},{4,0},{5,1},{6,2},{7,3},{8,12},{9,13},{10,... | collective-permute-start | bytes 2752520 | tf_op jit(solution)/shard_map/ppermute | solution.py:22
  39.6 45.6 %collective-permute-start.8 = (bf16[7168,128]{1,0:T(8,128)(2,1)}, bf16[7168,128]{1,0:T(8,128)(2,1)}, u32[]{:S(2)}, u32[]{:S(2)}) collective-permute-start(bf16[7168,128]{1,0:T(8,128)(2,1)} %refs_12_), channel_id=1, source_target_pairs={{0,2},{1,3},{2,0},{3,1},{4,6},{5,7},{6,4},{7,5},{8,10},{9,11},{10,... | collective-permute-start | bytes 5505032 | tf_op jit(solution)/shard_map/ppermute | solution.py:22
  45.8 42.4 %collective-permute-start.9 = (bf16[7168,128]{1,0:T(8,128)(2,1)}, bf16[7168,128]{1,0:T(8,128)(2,1)}, u32[]{:S(2)}, u32[]{:S(2)}) collective-permute-start(bf16[7168,128]{1,0:T(8,128)(2,1)} %refs_8_), channel_id=1, source_target_pairs={{0,1},{1,0},{2,3},{3,2},{4,5},{5,4},{6,7},{7,6},{8,9},{9,8},{10,11... | collective-permute-start | bytes 5505032 | tf_op jit(solution)/shard_map/ppermute | solution.py:22
  45.8 40.7 %all-to-all-start = ((bf16[32,8,640]{2,1,0:T(8,128)(2,1)}), bf16[32,8,640]{2,1,0:T(8,128)(2,1)S(1)}, u32[]{:S(2)}, u32[]{:S(2)}) async-start(bf16[32,8,640]{2,1,0:T(8,128)(2,1)} %maximum_maximum_fusion), calls=%async_computation | async-start | bytes 655360 | tf_op jit(solution)/shard_map/all_to_all | solution.py:300
  51.1 37.2 %collective-permute-start.5 = (bf16[48,7168]{1,0:T(8,128)(2,1)S(1)}, bf16[48,7168]{1,0:T(8,128)(2,1)}, u32[]{:S(2)}, u32[]{:S(2)}) collective-permute-start(bf16[48,7168]{1,0:T(8,128)(2,1)S(1)} %get-tuple-element.72), channel_id=1, source_target_pairs={{0,16},{1,17},{2,18},{3,19},{4,20},{5,21},{6,22},{7,23},{8,24},{9,... | collective-permute-start | bytes 2064392 | tf_op jit(solution)/shard_map/ppermute | solution.py:27
  51.4 36.8 %collective-permute-start.6 = (bf16[48,7168]{1,0:T(8,128)(2,1)}, bf16[48,7168]{1,0:T(8,128)(2,1)}, u32[]{:S(2)}, u32[]{:S(2)}) collective-permute-start(bf16[48,7168]{1,0:T(8,128)(2,1)} %collective-permute-done.refs_1_), channel_id=1, source_target_pairs={{0,4},{1,5},{2,6},{3,7},{4,0},{5,1},{6,2},{7,3},{8,12},{9,13},{10,... | collective-permute-start | bytes 2064392 | tf_op jit(solution)/shard_map/ppermute | solution.py:22
  53.2 35.1 %collective-permute-start.7 = (bf16[48,7168]{1,0:T(8,128)(2,1)}, bf16[48,7168]{1,0:T(8,128)(2,1)}, u32[]{:S(2)}, u32[]{:S(2)}) collective-permute-start(bf16[48,7168]{1,0:T(8,128)(2,1)} %collective-permute-done.1.refs_3_), channel_id=1, source_target_pairs={{0,4},{1,5},{2,6},{3,7},{4,0},{5,1},{6,2},{7,3},{8,12},{9,13},{10,... | collective-permute-start | bytes 2064392 | tf_op jit(solution)/shard_map/ppermute | solution.py:22
  88.2 23.7 %collective-permute-start.11 = (bf16[7168,128]{1,0:T(8,128)(2,1)}, bf16[7168,128]{1,0:T(8,128)(2,1)}, u32[]{:S(2)}, u32[]{:S(2)}) collective-permute-start(bf16[7168,128]{1,0:T(8,128)(2,1)} %refs_12_), channel_id=1, source_target_pairs={{0,1},{1,0},{2,3},{3,2},{4,5},{5,4},{6,7},{7,6},{8,9},{9,8},{10,11... | collective-permute-start | bytes 5505032 | tf_op jit(solution)/shard_map/ppermute | solution.py:22
  88.3 23.6 %collective-permute-start.12 = (bf16[7168,128]{1,0:T(8,128)(2,1)}, bf16[7168,128]{1,0:T(8,128)(2,1)}, u32[]{:S(2)}, u32[]{:S(2)}) collective-permute-start(bf16[7168,128]{1,0:T(8,128)(2,1)} %collective-permute-done.4.refs_10_), channel_id=1, source_target_pairs={{0,1},{1,0},{2,3},{3,2},{4,5},{5,4},{6,7},{7,6},{8,9},{9,8},{10,11... | collective-permute-start | bytes 5505032 | tf_op jit(solution)/shard_map/ppermute | solution.py:22
  88.8 23.1 %collective-permute-start.13 = (bf16[7168,128]{1,0:T(8,128)(2,1)}, bf16[7168,128]{1,0:T(8,128)(2,1)}, u32[]{:S(2)}, u32[]{:S(2)}) collective-permute-start(bf16[7168,128]{1,0:T(8,128)(2,1)} %collective-permute-done.8.refs_14_), channel_id=1, source_target_pairs={{0,1},{1,0},{2,3},{3,2},{4,5},{5,4},{6,7},{7,6},{8,9},{9,8},{10,11... | collective-permute-start | bytes 5505032 | tf_op jit(solution)/shard_map/ppermute | solution.py:22
  88.9 23.0 %collective-permute-start.14 = (bf16[256,1792]{1,0:T(8,128)(2,1)}, bf16[256,1792]{1,0:T(8,128)(2,1)}, u32[]{:S(2)}, u32[]{:S(2)}) collective-permute-start(bf16[256,1792]{1,0:T(8,128)(2,1)} %get-tuple-element.85), channel_id=1, source_target_pairs={{0,2},{1,3},{2,0},{3,1},{4,6},{5,7},{6,4},{7,5},{8,10},{9,11},{10,... | collective-permute-start | bytes 2752520 | tf_op jit(solution)/shard_map/ppermute | solution.py:22
  90.4 17.8 %collective-permute-start.10 = (bf16[48,7168]{1,0:T(8,128)(2,1)}, bf16[48,7168]{1,0:T(8,128)(2,1)}, u32[]{:S(2)}, u32[]{:S(2)}) collective-permute-start(bf16[48,7168]{1,0:T(8,128)(2,1)} %collective-permute-done.5.refs_2_), channel_id=1, source_target_pairs={{0,4},{1,5},{2,6},{3,7},{4,0},{5,1},{6,2},{7,3},{8,12},{9,13},{10,... | collective-permute-start | bytes 2064392 | tf_op jit(solution)/shard_map/ppermute | solution.py:22
  111.9 13.1 %collective-permute-start.15 = (bf16[256,3584]{1,0:T(8,128)(2,1)S(1)}, bf16[256,3584]{1,0:T(8,128)(2,1)}, u32[]{:S(2)}, u32[]{:S(2)}) collective-permute-start(bf16[256,3584]{1,0:T(8,128)(2,1)S(1)} %copy-done.1), channel_id=1, source_target_pairs={{0,1},{1,0},{2,3},{3,2},{4,5},{5,4},{6,7},{7,6},{8,9},{9,8},{10,11... | collective-permute-start | bytes 5505032 | tf_op jit(solution)/shard_map/ppermute | solution.py:22
  112.5 22.7 %collective-permute-start.18 = (bf16[256,1792]{1,0:T(8,128)(2,1)}, bf16[256,1792]{1,0:T(8,128)(2,1)}, u32[]{:S(2)}, u32[]{:S(2)}) collective-permute-start(bf16[256,1792]{1,0:T(8,128)(2,1)} %get-tuple-element.100), channel_id=1, source_target_pairs={{0,2},{1,3},{2,0},{3,1},{4,6},{5,7},{6,4},{7,5},{8,10},{9,11},{10,... | collective-permute-start | bytes 2752520 | tf_op jit(solution)/shard_map/ppermute | solution.py:22
  148.1 30.6 %collective-permute-start.21 = (bf16[48,3584]{1,0:T(8,128)(2,1)S(1)}, bf16[48,3584]{1,0:T(8,128)(2,1)S(1)}, u32[]{:S(2)}, u32[]{:S(2)}) collective-permute-start(bf16[48,3584]{1,0:T(8,128)(2,1)S(1)} %get-tuple-element.111), channel_id=1, source_target_pairs={{0,16},{1,17},{2,18},{3,19},{4,20},{5,21},{6,22},{7,23},{8,24},{9,... | collective-permute-start | bytes 1032200 | tf_op jit(solution)/shard_map/ppermute | solution.py:27
  152.4 45.0 %collective-permute-start.22 = (bf16[48,3584]{1,0:T(8,128)(2,1)S(1)}, bf16[48,3584]{1,0:T(8,128)(2,1)S(1)}, u32[]{:S(2)}, u32[]{:S(2)}) collective-permute-start(bf16[48,3584]{1,0:T(8,128)(2,1)S(1)} %get-tuple-element.112), channel_id=1, source_target_pairs={{0,8},{1,9},{2,10},{3,11},{4,12},{5,13},{6,14},{7,15},{8,16},{9,17... | collective-permute-start | bytes 1032200 | tf_op jit(solution)/shard_map/ppermute | solution.py:27
  153.0 44.4 %collective-permute-start.23 = (bf16[48,3584]{1,0:T(8,128)(2,1)S(1)}, bf16[48,3584]{1,0:T(8,128)(2,1)S(1)}, u32[]{:S(2)}, u32[]{:S(2)}) collective-permute-start(bf16[48,3584]{1,0:T(8,128)(2,1)S(1)} %get-tuple-element.113), channel_id=1, source_target_pairs={{0,4},{1,5},{2,6},{3,7},{4,0},{5,1},{6,2},{7,3},{8,12},{9,13},{10,... | collective-permute-start | bytes 1032200 | tf_op jit(solution)/shard_map/ppermute | solution.py:22
  154.5 47.4 %collective-permute-start.24 = (bf16[48,3584]{1,0:T(8,128)(2,1)S(1)}, bf16[48,3584]{1,0:T(8,128)(2,1)S(1)}, u32[]{:S(2)}, u32[]{:S(2)}) collective-permute-start(bf16[48,3584]{1,0:T(8,128)(2,1)S(1)} %get-tuple-element.114), channel_id=1, source_target_pairs={{0,28},{1,29},{2,30},{3,31},{4,24},{5,25},{6,26},{7,27},{8,4},{9,5... | collective-permute-start | bytes 1032200 | tf_op jit(solution)/shard_map/ppermute | solution.py:33
  158.9 49.5 %collective-permute-start.25 = (bf16[48,3584]{1,0:T(8,128)(2,1)S(1)}, bf16[48,3584]{1,0:T(8,128)(2,1)S(1)}, u32[]{:S(2)}, u32[]{:S(2)}) collective-permute-start(bf16[48,3584]{1,0:T(8,128)(2,1)S(1)} %get-tuple-element.115), channel_id=1, source_target_pairs={{0,20},{1,21},{2,22},{3,23},{4,16},{5,17},{6,18},{7,19},{8,28},{9,... | collective-permute-start | bytes 1032200 | tf_op jit(solution)/shard_map/ppermute | solution.py:33
  178.6 33.6 %collective-permute-start.26 = (bf16[48,3584]{1,0:T(8,128)(2,1)S(1)}, bf16[48,3584]{1,0:T(8,128)(2,1)S(1)}, u32[]{:S(2)}, u32[]{:S(2)}) collective-permute-start(bf16[48,3584]{1,0:T(8,128)(2,1)S(1)} %get-tuple-element.116), channel_id=1, source_target_pairs={{0,12},{1,13},{2,14},{3,15},{4,8},{5,9},{6,10},{7,11},{8,20},{9,21... | collective-permute-start | bytes 1032200 | tf_op jit(solution)/shard_map/ppermute | solution.py:33
  (17 other events, 182.3 us)

commit v14 on v13

--- a/solution.py
+++ b/solution.py
@@ -297,21 +297,17 @@
     )
     own_2, peer_1, peer_3 = shift(out_2, 2 * split), swap(own_1, YBIT), swap(own_3, YBIT)
     up_x, gate_c = swap(up_proj, XBIT), swap(gate_proj, CORE)
-    incoming = lax.all_to_all(outgoing, "ep", split_axis=0, concat_axis=0, tiled=True)
     keep = lax.dynamic_slice_in_dim(down_proj, 2 * upper * span, 2 * span, 1)
     own = jnp.concatenate([keep, down_y], axis=0)
     begin, rest = own[:, :span], own[:, span:]
 
-    own_2, peer_1, peer_3, up_x, gate_x, gate_c, up_proj, own, begin, rest, incoming = together(
-        own_2, peer_1, peer_3, up_x, gate_x, gate_c, up_proj, own, begin, rest, incoming
+    own_2, peer_1, peer_3, up_x, gate_x, gate_c, up_proj, own, begin, rest = together(
+        own_2, peer_1, peer_3, up_x, gate_x, gate_c, up_proj, own, begin, rest
     )
     peer_2, side_0 = swap(own_2, YBIT), swap(begin, XBIT)
     up_c, gate_xc, up_xc = swap(up_proj, CORE), swap(gate_x, CORE), swap(up_x, CORE)
-    handed = incoming.reshape(-1, incoming.shape[2])
-    marks = handed[:, latents.shape[1]].astype(jnp.float32)[None, :]
-    attended = attend(queries, cache_latents, cache_lens, handed, marks)
-    peer_2, up_c, gate_xc, up_xc, side_0, rest, own, attended, picks, gates = together(
-        peer_2, up_c, gate_xc, up_xc, side_0, rest, own, attended, picks, gates
+    peer_2, up_c, gate_xc, up_xc, side_0, rest, own, picks, gates = together(
+        peer_2, up_c, gate_xc, up_xc, side_0, rest, own, picks, gates
     )
     own_c, side_0c, side_1 = swap(own, CORE), swap(side_0, CORE), swap(rest, XBIT)
     units = (pack_0, own_1, own_2, own_3, peer_0, peer_1, peer_2, peer_3)
@@ -321,13 +317,26 @@
     table = gate_table(picks, gates, planes, split, slots).reshape(count, planes * slots)
     high = lax.reduce_precision(table, 8, 7)
     high, low = high.astype(jnp.bfloat16), (table - high).astype(jnp.bfloat16)
-    other, side_1, high, low = together(swap(hidden, YBIT), side_1, high, low)
+    other, side_1, high, low, outgoing = together(
+        swap(hidden, YBIT), side_1, high, low, outgoing
+    )
     firsts, seconds = (side_0, side_0c), (side_1, swap(side_1, CORE))
     values = down_values(hidden, other, (own, own_c), firsts, seconds, planes, span // 2)
-    mine = [values[0]] + [shift(values[k], n_ep - k * split) for k in range(1, planes)]
-    theirs = [swap(values[planes], YBIT)] + [
-        cross(values[planes + k], n_ep - k * split) for k in range(1, planes)
-    ]
+    mine, theirs = list(values[:planes]), list(values[planes:])
+    theirs[0] = swap(theirs[0], YBIT)
+    mine[1] = shift(mine[1], n_ep - split)
+    mine[2], theirs[2] = shift(mine[2], n_ep - 2 * split), cross(theirs[2], n_ep - 2 * split)
+    theirs[3] = cross(theirs[3], n_ep - 3 * split)
+    theirs[1] = cross(theirs[1], n_ep - split)
+    mine[3] = shift(mine[3], n_ep - 3 * split)
+    incoming = lax.all_to_all(outgoing, "ep", split_axis=0, concat_axis=0, tiled=True)
+    theirs[0], incoming = together(theirs[0], incoming)
+    handed = incoming.reshape(-1, incoming.shape[2])
+    marks = handed[:, latents.shape[1]].astype(jnp.float32)[None, :]
+    attended = attend(queries, cache_latents, cache_lens, handed, marks)
+    mine[1], mine[2], theirs[2], theirs[3], theirs[1], mine[3], attended = together(
+        mine[1], mine[2], theirs[2], theirs[3], theirs[1], mine[3], attended
+    )
     return combine(upper, high, low, mine, theirs, span), attended
 
 

time: 217 us -> 218 us (level)
  local copies, waits for them, and re-layouts: 8.59 us -> 13.4 us
  waiting for transfers between devices: 129 us -> 125 us
    ppermute x6, waiting for transfers between devices: 59.3 us -> 42.9 us  [shift(): lax.ppermute(value, 'ep', [(i, (i + step) % count) for i in range(count)])]
    ppermute x18, waiting for transfers between devices: 53.7 us -> 60.4 us  [swap(): return lax.ppermute(value, 'ep', [(i, i ^ bit) for i in range(count)])]
    ppermute x3, waiting for transfers between devices: 14.8 us -> 21.2 us  [cross(): return lax.ppermute(value, 'ep', pairs)]
    unnamed x28 -> x40, local copies, waits for them, and re-layouts: 4.9 us -> 9.7 us
    ppermute x3, starting transfers between devices: 7.17 us -> 4.08 us  [cross(): return lax.ppermute(value, 'ep', pairs)]
  transfers between devices with their start and end apart: 28 -> 28, of which waited for: 16 -> 13; matrix products, arithmetic and copies ran while one was open for 6% -> 7% of each run, Pallas kernels for 11% -> 13%
where the time goes in v14:
time: 218 us; the launch traced here: 217 us
  waiting for transfers between devices  125 us (57%)
  starting transfers between devices  33.7 us (15%)
  Pallas kernels  33.5 us (15%)
  local copies, waits for them, and re-layouts  13.4 us (6%)
  other arithmetic  9.86 us (5%)
    ppermute x18, waiting for transfers between devices, swap(): return lax.ppermute(value, 'ep', [(i, i ^ bit) for i in range(count)])  60.4 us
    ppermute x6, waiting for transfers between devices, shift(): lax.ppermute(value, 'ep', [(i, (i + step) % count) for i in range(count)])  42.9 us
    ppermute x3, waiting for transfers between devices, cross(): return lax.ppermute(value, 'ep', pairs)  21.2 us
    ppermute x18, starting transfers between devices, swap(): return lax.ppermute(value, 'ep', [(i, i ^ bit) for i in range(count)])  15 us
    pallas_call x1, Pallas kernels, hidden_units(): pl.pallas_call(partial(hidden_kernel, len(units)), grid=(width // chunk,)...  11 us
    unnamed x40, local copies, waits for them, and re-layouts  9.7 us
    ppermute x6, starting transfers between devices, shift(): lax.ppermute(value, 'ep', [(i, (i + step) % count) for i in range(count)])  9.47 us
    pallas_call x1, Pallas kernels, attend(): pl.pallas_call(attend_kernel, grid=(requests,), in_specs=[pl.BlockSpec(me...  9.09 us
  transfers between devices with their start and end apart: 28, of which 13 were waited for; matrix products, arithmetic and copies ran while one was open for 7% of the time, Pallas kernels for 13%

profile of v14, /device:TPU:16, one launch (start us, length us, event | category | flops | bytes accessed | tf_op | source)
XLA Modules:
  0.0 216.8 jit_solution(779664018980263805)
XLA Ops:
  5.1 2.6 %shard_map.131 = (bf16[48,7168]{1,0:T(8,128)(2,1)S(1)}, bf16[48,7168]{1,0:T(8,128)(2,1)}, bf16[48,7168]{1,0:T(8,128)(2,1)S(1)}, bf16[48,7168]{1,0:T(8,128)(2,1)}) custom-call(bf16[192,64]{1,0:T(8,128)(2,1)S(1)} %fusion.3.chosen, bf16[64,7168]{1,0:T(8,128)(2,1)S(1)} %bitcast.28), custom_call_target="tpu_custom_call" | custom-call | flops 176160768 | bytes 3670016 | tf_op jit(solution)/shard_map/pallas_call | solution.py:60
  17.8 21.9 %collective-permute-done.refs_1_ = bf16[48,7168]{1,0:T(8,128)(2,1)} collective-permute-done((bf16[48,7168]{1,0:T(8,128)(2,1)}, bf16[48,7168]{1,0:T(8,128)(2,1)}, u32[]{:S(2)}, u32[]{:S(2)}) %collective-permute-start) | collective-permute-done | bytes 688160 | tf_op jit(solution)/shard_map/ppermute | solution.py:27
  40.4 5.4 %collective-permute-done.3 = bf16[128,3584]{1,0:T(8,128)(2,1)} collective-permute-done((bf16[128,3584]{1,0:T(8,128)(2,1)}, bf16[128,3584]{1,0:T(8,128)(2,1)}, u32[]{:S(2)}, u32[]{:S(2)}) %collective-permute-start.3) | collective-permute-done | bytes 917536 | tf_op jit(solution)/shard_map/ppermute | solution.py:22
  45.8 2.2 %collective-permute-start.5 = (bf16[48,7168]{1,0:T(8,128)(2,1)S(1)}, bf16[48,7168]{1,0:T(8,128)(2,1)}, u32[]{:S(2)}, u32[]{:S(2)}) collective-permute-start(bf16[48,7168]{1,0:T(8,128)(2,1)S(1)} %get-tuple-element.80), channel_id=1, source_target_pairs={{0,16},{1,17},{2,18},{3,19},{4,20},{5,21},{6,22},{7,23},{8,24},{9,... | collective-permute-start | bytes 2064392 | tf_op jit(solution)/shard_map/ppermute | solution.py:27
  50.1 2.5 %fusion.1 = (bf16[256,1792]{1,0:T(8,128)(2,1)}, bf16[256,1792]{1,0:T(8,128)(2,1)}) fusion(bf16[128,3584]{1,0:T(8,128)(2,1)S(1)} %constant_dynamic-slice_fusion, bf16[128,3584]{1,0:T(8,128)(2,1)} %collective-permute-done.3), kind=kLoop, calls=%fused_computation.7 | loop fusion | flops 3670016 | bytes 3670016 | tf_op jit(solution)/shard_map/concatenate | solution.py:301
  52.6 2.6 %pad_maximum_fusion.own = bf16[256,3584]{1,0:T(8,128)(2,1)} fusion(bf16[128,3584]{1,0:T(8,128)(2,1)} %collective-permute-done.3, bf16[128,3584]{1,0:T(8,128)(2,1)S(1)} %constant_dynamic-slice_fusion), kind=kLoop, calls=%fused_computation.2 | loop fusion | flops 3670016 | bytes 3670016 | tf_op jit(solution)/shard_map/concatenate | solution.py:301
  55.2 27.0 %collective-permute-done.8.refs_14_ = bf16[7168,128]{1,0:T(8,128)(2,1)} collective-permute-done((bf16[7168,128]{1,0:T(8,128)(2,1)}, bf16[7168,128]{1,0:T(8,128)(2,1)}, u32[]{:S(2)}, u32[]{:S(2)}) %collective-permute-start.8) | collective-permute-done | bytes 1835040 | tf_op jit(solution)/shard_map/ppermute | solution.py:22
  85.9 16.2 %collective-permute-done.10.refs_6_ = bf16[48,7168]{1,0:T(8,128)(2,1)} collective-permute-done((bf16[48,7168]{1,0:T(8,128)(2,1)}, bf16[48,7168]{1,0:T(8,128)(2,1)}, u32[]{:S(2)}, u32[]{:S(2)}) %collective-permute-start.10) | collective-permute-done | bytes 688160 | tf_op jit(solution)/shard_map/ppermute | solution.py:22
  102.1 3.6 %collective-permute-done.14.side_0 = bf16[256,1792]{1,0:T(8,128)(2,1)S(1)} collective-permute-done((bf16[256,1792]{1,0:T(8,128)(2,1)}, bf16[256,1792]{1,0:T(8,128)(2,1)S(1)}, u32[]{:S(2)}, u32[]{:S(2)}) %collective-permute-start.14) | collective-permute-done | bytes 917536 | tf_op jit(solution)/shard_map/ppermute | solution.py:22
  108.7 11.0 %shard_map.132.mine = bf16[384,512]{1,0:T(8,128)(2,1)} custom-call(bf16[48,7168]{1,0:T(8,128)(2,1)} %copy-done.9, bf16[48,7168]{1,0:T(8,128)(2,1)} %collective-permute-done.refs_1_, bf16[48,7168]{1,0:T(8,128)(2,1)} %collective-permute-done.5.refs_2_, bf16[48,7168]{1,0:T(8,128)(2,1)} %collective-permute-done.1.refs_3_, ...), custom_call_target="tpu_custom_call" | custom-call | flops 5637144576 | bytes 20185088 | tf_op jit(solution)/shard_map/pallas_call | solution.py:105
  123.7 6.0 %collective-permute-done.18.side_1 = bf16[256,1792]{1,0:T(8,128)(2,1)} collective-permute-done((bf16[256,1792]{1,0:T(8,128)(2,1)}, bf16[256,1792]{1,0:T(8,128)(2,1)}, u32[]{:S(2)}, u32[]{:S(2)}) %collective-permute-start.18) | collective-permute-done | bytes 917536 | tf_op jit(solution)/shard_map/ppermute | solution.py:22
  129.7 2.2 collective-permute-done.17.other
  131.9 5.2 %all-to-all-start = ((bf16[32,8,640]{2,1,0:T(8,128)(2,1)}), bf16[32,8,640]{2,1,0:T(8,128)(2,1)}, u32[]{:S(2)}, u32[]{:S(2)}) async-start(bf16[32,8,640]{2,1,0:T(8,128)(2,1)} %maximum_maximum_fusion), calls=%async_computation | async-start | bytes 655360 | tf_op jit(solution)/shard_map/all_to_all | solution.py:332
  142.3 6.5 %shard_map.133 = (bf16[48,3584]{1,0:T(8,128)(2,1)S(1)}, bf16[48,3584]{1,0:T(8,128)(2,1)S(1)}, bf16[48,3584]{1,0:T(8,128)(2,1)}, bf16[48,3584]{1,0:T(8,128)(2,1)}...) custom-call(bf16[384,512]{1,0:T(8,128)(2,1)S(1)} %copy-done.10, ...), custom_call_target="tpu_custom_call" | custom-call | flops 2818572288 | bytes 10092544 | tf_op jit(solution)/shard_map/pallas_call | solution.py:160
  150.8 3.3 %collective-permute-start.21 = (bf16[48,3584]{1,0:T(8,128)(2,1)}, bf16[48,3584]{1,0:T(8,128)(2,1)S(1)}, u32[]{:S(2)}, u32[]{:S(2)}) collective-permute-start(bf16[48,3584]{1,0:T(8,128)(2,1)} %get-tuple-element.118), channel_id=1, source_target_pairs={{0,16},{1,17},{2,18},{3,19},{4,20},{5,21},{6,22},{7,23},{8,24},{9,... | collective-permute-start | bytes 1032200 | tf_op jit(solution)/shard_map/ppermute | solution.py:27
  156.1 3.6 %collective-permute-done.20.refs_1_ = bf16[48,3584]{1,0:T(8,128)(2,1)S(1)} collective-permute-done((bf16[48,3584]{1,0:T(8,128)(2,1)S(1)}, bf16[48,3584]{1,0:T(8,128)(2,1)S(1)}, u32[]{:S(2)}, u32[]{:S(2)}) %collective-permute-start.20) | collective-permute-done | bytes 344096 | tf_op jit(solution)/shard_map/ppermute | solution.py:27
  159.7 2.1 collective-permute-start.24
  164.8 9.1 %shard_map.134 = bf16[8,128,512]{2,1,0:T(8,128)(2,1)} custom-call(s32[8]{0:T(128)} %lens.1, bf16[8,576,128]{2,1,0:T(8,128)(2,1)} %bitcast.31, bf16[8,576,256]{2,1,0:T(8,128)(2,1)} %bitcast.29, bf16[256,640]{1,0:T(8,128)(2,1)} %bitcast.14.handed, f32[1,256]{1,0:T(1,128)} %bitcast.39), custom_call_target="tpu_custom_call" | custom-call | flops 1140850688 | bytes 4587520 | tf_op jit(solution)/shard_map/pallas_call | solution.py:372
  173.9 13.6 %collective-permute-done.21.refs_2_ = bf16[48,3584]{1,0:T(8,128)(2,1)S(1)} collective-permute-done((bf16[48,3584]{1,0:T(8,128)(2,1)}, bf16[48,3584]{1,0:T(8,128)(2,1)S(1)}, u32[]{:S(2)}, u32[]{:S(2)}) %collective-permute-start.21) | collective-permute-done | bytes 344096 | tf_op jit(solution)/shard_map/ppermute | solution.py:27
  187.5 14.6 %collective-permute-done.22.refs_6_ = bf16[48,3584]{1,0:T(8,128)(2,1)S(1)} collective-permute-done((bf16[48,3584]{1,0:T(8,128)(2,1)}, bf16[48,3584]{1,0:T(8,128)(2,1)S(1)}, u32[]{:S(2)}, u32[]{:S(2)}) %collective-permute-start.22) | collective-permute-done | bytes 344096 | tf_op jit(solution)/shard_map/ppermute | solution.py:33
  202.1 4.1 %collective-permute-done.23.refs_7_ = bf16[48,3584]{1,0:T(8,128)(2,1)} collective-permute-done((bf16[48,3584]{1,0:T(8,128)(2,1)}, bf16[48,3584]{1,0:T(8,128)(2,1)}, u32[]{:S(2)}, u32[]{:S(2)}) %collective-permute-start.23) | collective-permute-done | bytes 344096 | tf_op jit(solution)/shard_map/ppermute | solution.py:33
  206.2 2.5 %collective-permute-done.24.refs_5_ = bf16[48,3584]{1,0:T(8,128)(2,1)} collective-permute-done((bf16[48,3584]{1,0:T(8,128)(2,1)}, bf16[48,3584]{1,0:T(8,128)(2,1)}, u32[]{:S(2)}, u32[]{:S(2)}) %collective-permute-start.24) | collective-permute-done | bytes 344096 | tf_op jit(solution)/shard_map/ppermute | solution.py:33
  208.7 3.8 %collective-permute-done.25.refs_3_ = bf16[48,3584]{1,0:T(8,128)(2,1)} collective-permute-done((bf16[48,3584]{1,0:T(8,128)(2,1)}, bf16[48,3584]{1,0:T(8,128)(2,1)}, u32[]{:S(2)}, u32[]{:S(2)}) %collective-permute-start.25) | collective-permute-done | bytes 344096 | tf_op jit(solution)/shard_map/ppermute | solution.py:27
  212.5 4.3 %shard_map.135 = bf16[64,7168]{1,0:T(8,128)(2,1)} custom-call(s32[1]{0:T(128)} %bitcast.upper, bf16[64,192]{1,0:T(8,128)(2,1)S(1)} %copy-done.4, bf16[64,192]{1,0:T(8,128)(2,1)S(1)} %copy-done.3, bf16[48,3584]{1,0:T(8,128)(2,1)S(1)} %get-tuple-element.116.refs_0_, bf16[48,3584]{1,0:T(8,128)(2,1)S(1)} %collective-permute-done.20.refs_1_, ...), custom_call_target="tpu_custom_call" | custom-call | flops 352321536 | bytes 3670016 | tf_op jit(solution)/shard_map/pallas_call | solution.py:213
  (111 shorter events, 40.1 us)
Async XLA Ops:
  0.7 45.1 %collective-permute-start.4 = (bf16[7168,128]{1,0:T(8,128)(2,1)}, bf16[7168,128]{1,0:T(8,128)(2,1)}, u32[]{:S(2)}, u32[]{:S(2)}) collective-permute-start(bf16[7168,128]{1,0:T(8,128)(2,1)} %refs_8_), channel_id=1, source_target_pairs={{0,2},{1,3},{2,0},{3,1},{4,6},{5,7},{6,4},{7,5},{8,10},{9,11},{10,... | collective-permute-start | bytes 5505032 | tf_op jit(solution)/shard_map/ppermute | solution.py:22
  7.7 32.0 %collective-permute-start = (bf16[48,7168]{1,0:T(8,128)(2,1)}, bf16[48,7168]{1,0:T(8,128)(2,1)}, u32[]{:S(2)}, u32[]{:S(2)}) collective-permute-start(bf16[48,7168]{1,0:T(8,128)(2,1)} %get-tuple-element.72), channel_id=1, source_target_pairs={{0,8},{1,9},{2,10},{3,11},{4,12},{5,13},{6,14},{7,15},{8,16},{9,17... | collective-permute-start | bytes 2064392 | tf_op jit(solution)/shard_map/ppermute | solution.py:27
  9.2 31.1 %collective-permute-start.1 = (bf16[48,7168]{1,0:T(8,128)(2,1)}, bf16[48,7168]{1,0:T(8,128)(2,1)}, u32[]{:S(2)}, u32[]{:S(2)}) collective-permute-start(bf16[48,7168]{1,0:T(8,128)(2,1)} %get-tuple-element.73), channel_id=1, source_target_pairs={{0,24},{1,25},{2,26},{3,27},{4,28},{5,29},{6,30},{7,31},{8,0},{9,1... | collective-permute-start | bytes 2064392 | tf_op jit(solution)/shard_map/ppermute | solution.py:27
  9.7 30.7 %collective-permute-start.2 = (bf16[48,7168]{1,0:T(8,128)(2,1)S(1)}, bf16[48,7168]{1,0:T(8,128)(2,1)}, u32[]{:S(2)}, u32[]{:S(2)}) collective-permute-start(bf16[48,7168]{1,0:T(8,128)(2,1)S(1)} %get-tuple-element.71.refs_0_), channel_id=1, source_target_pairs={{0,4},{1,5},{2,6},{3,7},{4,0},{5,1},{6,2},{7,3},{8,12},{9,13},{10,... | collective-permute-start | bytes 2064392 | tf_op jit(solution)/shard_map/ppermute | solution.py:22
  12.2 33.6 %collective-permute-start.3 = (bf16[128,3584]{1,0:T(8,128)(2,1)}, bf16[128,3584]{1,0:T(8,128)(2,1)}, u32[]{:S(2)}, u32[]{:S(2)}) collective-permute-start(bf16[128,3584]{1,0:T(8,128)(2,1)} %constant_dynamic-slice_fusion.1), channel_id=1, source_target_pairs={{0,4},{1,5},{2,6},{3,7},{4,0},{5,1},{6,2},{7,3},{8,12},{9,13},{10,... | collective-permute-start | bytes 2752520 | tf_op jit(solution)/shard_map/ppermute | solution.py:22
  39.6 42.5 %collective-permute-start.8 = (bf16[7168,128]{1,0:T(8,128)(2,1)}, bf16[7168,128]{1,0:T(8,128)(2,1)}, u32[]{:S(2)}, u32[]{:S(2)}) collective-permute-start(bf16[7168,128]{1,0:T(8,128)(2,1)} %refs_12_), channel_id=1, source_target_pairs={{0,2},{1,3},{2,0},{3,1},{4,6},{5,7},{6,4},{7,5},{8,10},{9,11},{10,... | collective-permute-start | bytes 5505032 | tf_op jit(solution)/shard_map/ppermute | solution.py:22
  45.8 36.4 %collective-permute-start.9 = (bf16[7168,128]{1,0:T(8,128)(2,1)}, bf16[7168,128]{1,0:T(8,128)(2,1)}, u32[]{:S(2)}, u32[]{:S(2)}) collective-permute-start(bf16[7168,128]{1,0:T(8,128)(2,1)} %refs_8_), channel_id=1, source_target_pairs={{0,1},{1,0},{2,3},{3,2},{4,5},{5,4},{6,7},{7,6},{8,9},{9,8},{10,11... | collective-permute-start | bytes 5505032 | tf_op jit(solution)/shard_map/ppermute | solution.py:22
  45.8 36.3 %collective-permute-start.5 = (bf16[48,7168]{1,0:T(8,128)(2,1)S(1)}, bf16[48,7168]{1,0:T(8,128)(2,1)}, u32[]{:S(2)}, u32[]{:S(2)}) collective-permute-start(bf16[48,7168]{1,0:T(8,128)(2,1)S(1)} %get-tuple-element.80), channel_id=1, source_target_pairs={{0,16},{1,17},{2,18},{3,19},{4,20},{5,21},{6,22},{7,23},{8,24},{9,... | collective-permute-start | bytes 2064392 | tf_op jit(solution)/shard_map/ppermute | solution.py:27
  48.0 34.1 %collective-permute-start.6 = (bf16[48,7168]{1,0:T(8,128)(2,1)}, bf16[48,7168]{1,0:T(8,128)(2,1)S(1)}, u32[]{:S(2)}, u32[]{:S(2)}) collective-permute-start(bf16[48,7168]{1,0:T(8,128)(2,1)} %collective-permute-done.refs_1_), channel_id=1, source_target_pairs={{0,4},{1,5},{2,6},{3,7},{4,0},{5,1},{6,2},{7,3},{8,12},{9,13},{10,... | collective-permute-start | bytes 2064392 | tf_op jit(solution)/shard_map/ppermute | solution.py:22
  49.5 32.6 %collective-permute-start.7 = (bf16[48,7168]{1,0:T(8,128)(2,1)}, bf16[48,7168]{1,0:T(8,128)(2,1)S(1)}, u32[]{:S(2)}, u32[]{:S(2)}) collective-permute-start(bf16[48,7168]{1,0:T(8,128)(2,1)} %collective-permute-done.1.refs_3_), channel_id=1, source_target_pairs={{0,4},{1,5},{2,6},{3,7},{4,0},{5,1},{6,2},{7,3},{8,12},{9,13},{10,... | collective-permute-start | bytes 2064392 | tf_op jit(solution)/shard_map/ppermute | solution.py:22
  82.2 23.6 %collective-permute-start.11 = (bf16[7168,128]{1,0:T(8,128)(2,1)}, bf16[7168,128]{1,0:T(8,128)(2,1)}, u32[]{:S(2)}, u32[]{:S(2)}) collective-permute-start(bf16[7168,128]{1,0:T(8,128)(2,1)} %refs_12_), channel_id=1, source_target_pairs={{0,1},{1,0},{2,3},{3,2},{4,5},{5,4},{6,7},{7,6},{8,9},{9,8},{10,11... | collective-permute-start | bytes 5505032 | tf_op jit(solution)/shard_map/ppermute | solution.py:22
  82.2 23.5 %collective-permute-start.12 = (bf16[7168,128]{1,0:T(8,128)(2,1)}, bf16[7168,128]{1,0:T(8,128)(2,1)}, u32[]{:S(2)}, u32[]{:S(2)}) collective-permute-start(bf16[7168,128]{1,0:T(8,128)(2,1)} %collective-permute-done.4.refs_10_), channel_id=1, source_target_pairs={{0,1},{1,0},{2,3},{3,2},{4,5},{5,4},{6,7},{7,6},{8,9},{9,8},{10,11... | collective-permute-start | bytes 5505032 | tf_op jit(solution)/shard_map/ppermute | solution.py:22
  82.7 23.9 %collective-permute-start.13 = (bf16[7168,128]{1,0:T(8,128)(2,1)}, bf16[7168,128]{1,0:T(8,128)(2,1)}, u32[]{:S(2)}, u32[]{:S(2)}) collective-permute-start(bf16[7168,128]{1,0:T(8,128)(2,1)} %collective-permute-done.8.refs_14_), channel_id=1, source_target_pairs={{0,1},{1,0},{2,3},{3,2},{4,5},{5,4},{6,7},{7,6},{8,9},{9,8},{10,11... | collective-permute-start | bytes 5505032 | tf_op jit(solution)/shard_map/ppermute | solution.py:22
  82.8 22.9 %collective-permute-start.14 = (bf16[256,1792]{1,0:T(8,128)(2,1)}, bf16[256,1792]{1,0:T(8,128)(2,1)S(1)}, u32[]{:S(2)}, u32[]{:S(2)}) collective-permute-start(bf16[256,1792]{1,0:T(8,128)(2,1)} %get-tuple-element.92), channel_id=1, source_target_pairs={{0,2},{1,3},{2,0},{3,1},{4,6},{5,7},{6,4},{7,5},{8,10},{9,11},{10,... | collective-permute-start | bytes 2752520 | tf_op jit(solution)/shard_map/ppermute | solution.py:22
  84.3 17.8 %collective-permute-start.10 = (bf16[48,7168]{1,0:T(8,128)(2,1)}, bf16[48,7168]{1,0:T(8,128)(2,1)}, u32[]{:S(2)}, u32[]{:S(2)}) collective-permute-start(bf16[48,7168]{1,0:T(8,128)(2,1)} %collective-permute-done.5.refs_2_), channel_id=1, source_target_pairs={{0,4},{1,5},{2,6},{3,7},{4,0},{5,1},{6,2},{7,3},{8,12},{9,13},{10,... | collective-permute-start | bytes 2064392 | tf_op jit(solution)/shard_map/ppermute | solution.py:22
  106.7 13.1 %collective-permute-start.15 = (bf16[256,3584]{1,0:T(8,128)(2,1)}, bf16[256,3584]{1,0:T(8,128)(2,1)S(1)}, u32[]{:S(2)}, u32[]{:S(2)}) collective-permute-start(bf16[256,3584]{1,0:T(8,128)(2,1)} %pad_maximum_fusion.own), channel_id=1, source_target_pairs={{0,1},{1,0},{2,3},{3,2},{4,5},{5,4},{6,7},{7,6},{8,9},{9,8},{10,11... | collective-permute-start | bytes 5505032 | tf_op jit(solution)/shard_map/ppermute | solution.py:22
  106.7 13.1 %collective-permute-start.16 = (bf16[256,1792]{1,0:T(8,128)(2,1)}, bf16[256,1792]{1,0:T(8,128)(2,1)}, u32[]{:S(2)}, u32[]{:S(2)}) collective-permute-start(bf16[256,1792]{1,0:T(8,128)(2,1)} %copy-done.7), channel_id=1, source_target_pairs={{0,1},{1,0},{2,3},{3,2},{4,5},{5,4},{6,7},{7,6},{8,9},{9,8},{10,11... | collective-permute-start | bytes 2752520 | tf_op jit(solution)/shard_map/ppermute | solution.py:22
  107.2 22.6 %collective-permute-start.18 = (bf16[256,1792]{1,0:T(8,128)(2,1)}, bf16[256,1792]{1,0:T(8,128)(2,1)}, u32[]{:S(2)}, u32[]{:S(2)}) collective-permute-start(bf16[256,1792]{1,0:T(8,128)(2,1)} %get-tuple-element.106), channel_id=1, source_target_pairs={{0,2},{1,3},{2,0},{3,1},{4,6},{5,7},{6,4},{7,5},{8,10},{9,11},{10,... | collective-permute-start | bytes 2752520 | tf_op jit(solution)/shard_map/ppermute | solution.py:22
  131.9 31.2 %all-to-all-start = ((bf16[32,8,640]{2,1,0:T(8,128)(2,1)}), bf16[32,8,640]{2,1,0:T(8,128)(2,1)}, u32[]{:S(2)}, u32[]{:S(2)}) async-start(bf16[32,8,640]{2,1,0:T(8,128)(2,1)} %maximum_maximum_fusion), calls=%async_computation | async-start | bytes 655360 | tf_op jit(solution)/shard_map/all_to_all | solution.py:332
  150.8 36.7 %collective-permute-start.21 = (bf16[48,3584]{1,0:T(8,128)(2,1)}, bf16[48,3584]{1,0:T(8,128)(2,1)S(1)}, u32[]{:S(2)}, u32[]{:S(2)}) collective-permute-start(bf16[48,3584]{1,0:T(8,128)(2,1)} %get-tuple-element.118), channel_id=1, source_target_pairs={{0,16},{1,17},{2,18},{3,19},{4,20},{5,21},{6,22},{7,23},{8,24},{9,... | collective-permute-start | bytes 1032200 | tf_op jit(solution)/shard_map/ppermute | solution.py:27
  154.2 48.0 %collective-permute-start.22 = (bf16[48,3584]{1,0:T(8,128)(2,1)}, bf16[48,3584]{1,0:T(8,128)(2,1)S(1)}, u32[]{:S(2)}, u32[]{:S(2)}) collective-permute-start(bf16[48,3584]{1,0:T(8,128)(2,1)} %get-tuple-element.119), channel_id=1, source_target_pairs={{0,20},{1,21},{2,22},{3,23},{4,16},{5,17},{6,18},{7,19},{8,28},{9,... | collective-permute-start | bytes 1032200 | tf_op jit(solution)/shard_map/ppermute | solution.py:33
  154.2 52.0 %collective-permute-start.23 = (bf16[48,3584]{1,0:T(8,128)(2,1)}, bf16[48,3584]{1,0:T(8,128)(2,1)}, u32[]{:S(2)}, u32[]{:S(2)}) collective-permute-start(bf16[48,3584]{1,0:T(8,128)(2,1)} %get-tuple-element.120), channel_id=1, source_target_pairs={{0,12},{1,13},{2,14},{3,15},{4,8},{5,9},{6,10},{7,11},{8,20},{9,21... | collective-permute-start | bytes 1032200 | tf_op jit(solution)/shard_map/ppermute | solution.py:33
  159.7 49.0 %collective-permute-start.24 = (bf16[48,3584]{1,0:T(8,128)(2,1)}, bf16[48,3584]{1,0:T(8,128)(2,1)}, u32[]{:S(2)}, u32[]{:S(2)}) collective-permute-start(bf16[48,3584]{1,0:T(8,128)(2,1)} %get-tuple-element.121), channel_id=1, source_target_pairs={{0,28},{1,29},{2,30},{3,31},{4,24},{5,25},{6,26},{7,27},{8,4},{9,5... | collective-permute-start | bytes 1032200 | tf_op jit(solution)/shard_map/ppermute | solution.py:33
  161.8 50.7 %collective-permute-start.25 = (bf16[48,3584]{1,0:T(8,128)(2,1)}, bf16[48,3584]{1,0:T(8,128)(2,1)}, u32[]{:S(2)}, u32[]{:S(2)}) collective-permute-start(bf16[48,3584]{1,0:T(8,128)(2,1)} %get-tuple-element.122), channel_id=1, source_target_pairs={{0,8},{1,9},{2,10},{3,11},{4,12},{5,13},{6,14},{7,15},{8,16},{9,17... | collective-permute-start | bytes 1032200 | tf_op jit(solution)/shard_map/ppermute | solution.py:27
  (23 other events, 275.0 us)

commit v15 on v14

--- a/solution.py
+++ b/solution.py
@@ -166,7 +166,7 @@
         + [pl.BlockSpec((deep, chunk), lambda k: (0, jnp.maximum(k - half, 0))) for _ in seconds],
         out_specs=[pl.BlockSpec((rows, chunk), lambda k: (0, k))] * (2 * planes),
         out_shape=[jax.ShapeDtypeStruct((rows, width), jnp.bfloat16)] * (2 * planes),
-        compiler_params=pltpu.CompilerParams(vmem_limit_bytes=SMALL_BYTES),
+        compiler_params=pltpu.CompilerParams(vmem_limit_bytes=VMEM_BYTES),
         cost_estimate=pl.CostEstimate(
             flops=2 * count * 2 * inner * width,
             bytes_accessed=8 * deep * width + 2 * count * width,
@@ -313,13 +313,13 @@
     units = (pack_0, own_1, own_2, own_3, peer_0, peer_1, peer_2, peer_3)
     weights = (gate_proj, gate_c, gate_x, gate_xc, up_proj, up_c, up_x, up_xc)
     hidden = hidden_units(units, weights, chunk)
-    hidden, own_c, side_0c, picks, gates = together(hidden, own_c, side_0c, picks, gates)
+    hidden, own_c, side_0c, picks, gates, outgoing = together(
+        hidden, own_c, side_0c, picks, gates, outgoing
+    )
     table = gate_table(picks, gates, planes, split, slots).reshape(count, planes * slots)
     high = lax.reduce_precision(table, 8, 7)
     high, low = high.astype(jnp.bfloat16), (table - high).astype(jnp.bfloat16)
-    other, side_1, high, low, outgoing = together(
-        swap(hidden, YBIT), side_1, high, low, outgoing
-    )
+    other, side_1, high, low = together(swap(hidden, YBIT), side_1, high, low)
     firsts, seconds = (side_0, side_0c), (side_1, swap(side_1, CORE))
     values = down_values(hidden, other, (own, own_c), firsts, seconds, planes, span // 2)
     mine, theirs = list(values[:planes]), list(values[planes:])
@@ -334,9 +334,7 @@
     handed = incoming.reshape(-1, incoming.shape[2])
     marks = handed[:, latents.shape[1]].astype(jnp.float32)[None, :]
     attended = attend(queries, cache_latents, cache_lens, handed, marks)
-    mine[1], mine[2], theirs[2], theirs[3], theirs[1], mine[3], attended = together(
-        mine[1], mine[2], theirs[2], theirs[3], theirs[1], mine[3], attended
-    )
+    mine[3], attended = together(mine[3], attended)
     return combine(upper, high, low, mine, theirs, span), attended
 
 

time: 218 us -> 217 us (level)
  the two profiles are of different devices: /device:TPU:16 before, /device:TPU:0 now
where the time goes in v15:
time: 217 us; the launch traced here: 216 us
  waiting for transfers between devices  102 us (47%)
  starting transfers between devices  59.9 us (28%)
  Pallas kernels  34.9 us (16%)
  other arithmetic  9.57 us (4%)
  local copies, waits for them, and re-layouts  7.82 us (4%)
    ppermute x18, waiting for transfers between devices, swap(): return lax.ppermute(value, 'ep', [(i, i ^ bit) for i in range(count)])  61.3 us
    ppermute x3, starting transfers between devices, cross(): return lax.ppermute(value, 'ep', pairs)  28.9 us
    ppermute x6, waiting for transfers between devices, shift(): lax.ppermute(value, 'ep', [(i, (i + step) % count) for i in range(count)])  26.5 us
    ppermute x18, starting transfers between devices, swap(): return lax.ppermute(value, 'ep', [(i, i ^ bit) for i in range(count)])  16.6 us
    ppermute x3, waiting for transfers between devices, cross(): return lax.ppermute(value, 'ep', pairs)  14.2 us
    pallas_call x1, Pallas kernels, hidden_units(): pl.pallas_call(partial(hidden_kernel, len(units)), grid=(width // chunk,)...  11 us
    ppermute x6, starting transfers between devices, shift(): lax.ppermute(value, 'ep', [(i, (i + step) % count) for i in range(count)])  9.22 us
    pallas_call x1, Pallas kernels, attend(): pl.pallas_call(attend_kernel, grid=(requests,), in_specs=[pl.BlockSpec(me...  9.12 us
  transfers between devices with their start and end apart: 28, of which 10 were waited for; matrix products, arithmetic and copies ran while one was open for 7% of the time, Pallas kernels for 14%

profile of v15, /device:TPU:0, one launch (start us, length us, event | category | flops | bytes accessed | tf_op | source)
XLA Modules:
  0.0 216.1 jit_solution(15541509180570722762)
XLA Ops:
  0.7 3.0 %collective-permute-start.4 = (bf16[7168,128]{1,0:T(8,128)(2,1)}, bf16[7168,128]{1,0:T(8,128)(2,1)}, u32[]{:S(2)}, u32[]{:S(2)}) collective-permute-start(bf16[7168,128]{1,0:T(8,128)(2,1)} %refs_8_), channel_id=1, source_target_pairs={{0,2},{1,3},{2,0},{3,1},{4,6},{5,7},{6,4},{7,5},{8,10},{9,11},{10,... | collective-permute-start | bytes 5505032 | tf_op jit(solution)/shard_map/ppermute | solution.py:22
  6.6 2.5 %shard_map.131 = (bf16[48,7168]{1,0:T(8,128)(2,1)S(1)}, bf16[48,7168]{1,0:T(8,128)(2,1)}, bf16[48,7168]{1,0:T(8,128)(2,1)S(1)}, bf16[48,7168]{1,0:T(8,128)(2,1)}) custom-call(bf16[192,64]{1,0:T(8,128)(2,1)S(1)} %fusion.3.chosen, bf16[64,7168]{1,0:T(8,128)(2,1)S(1)} %bitcast.28), custom_call_target="tpu_custom_call" | custom-call | flops 176160768 | bytes 3670016 | tf_op jit(solution)/shard_map/pallas_call | solution.py:60
  10.7 2.2 %collective-permute-start.1 = (bf16[48,7168]{1,0:T(8,128)(2,1)}, bf16[48,7168]{1,0:T(8,128)(2,1)}, u32[]{:S(2)}, u32[]{:S(2)}) collective-permute-start(bf16[48,7168]{1,0:T(8,128)(2,1)} %get-tuple-element.68), channel_id=1, source_target_pairs={{0,24},{1,25},{2,26},{3,27},{4,28},{5,29},{6,30},{7,31},{8,0},{9,1... | collective-permute-start | bytes 2064392 | tf_op jit(solution)/shard_map/ppermute | solution.py:27
  21.0 8.6 %collective-permute-done.refs_1_ = bf16[48,7168]{1,0:T(8,128)(2,1)} collective-permute-done((bf16[48,7168]{1,0:T(8,128)(2,1)}, bf16[48,7168]{1,0:T(8,128)(2,1)}, u32[]{:S(2)}, u32[]{:S(2)}) %collective-permute-start) | collective-permute-done | bytes 688160 | tf_op jit(solution)/shard_map/ppermute | solution.py:27
  29.9 12.5 %collective-permute-done.1.refs_3_ = bf16[48,7168]{1,0:T(8,128)(2,1)} collective-permute-done((bf16[48,7168]{1,0:T(8,128)(2,1)}, bf16[48,7168]{1,0:T(8,128)(2,1)}, u32[]{:S(2)}, u32[]{:S(2)}) %collective-permute-start.1) | collective-permute-done | bytes 688160 | tf_op jit(solution)/shard_map/ppermute | solution.py:27
  42.4 6.7 %collective-permute-done.3 = bf16[128,3584]{1,0:T(8,128)(2,1)} collective-permute-done((bf16[128,3584]{1,0:T(8,128)(2,1)}, bf16[128,3584]{1,0:T(8,128)(2,1)}, u32[]{:S(2)}, u32[]{:S(2)}) %collective-permute-start.3) | collective-permute-done | bytes 917536 | tf_op jit(solution)/shard_map/ppermute | solution.py:22
  51.9 2.2 %fusion.1 = (bf16[256,1792]{1,0:T(8,128)(2,1)S(1)}, bf16[256,1792]{1,0:T(8,128)(2,1)}) fusion(bf16[128,3584]{1,0:T(8,128)(2,1)S(1)} %constant_dynamic-slice_fusion, bf16[128,3584]{1,0:T(8,128)(2,1)} %collective-permute-done.3), kind=kLoop, calls=%fused_computation.7 | loop fusion | flops 3670016 | bytes 3670016 | tf_op jit(solution)/shard_map/concatenate | solution.py:301
  54.1 2.6 %pad_maximum_fusion.own = bf16[256,3584]{1,0:T(8,128)(2,1)} fusion(bf16[128,3584]{1,0:T(8,128)(2,1)} %collective-permute-done.3, bf16[128,3584]{1,0:T(8,128)(2,1)S(1)} %constant_dynamic-slice_fusion), kind=kLoop, calls=%fused_computation.2 | loop fusion | flops 3670016 | bytes 3670016 | tf_op jit(solution)/shard_map/concatenate | solution.py:301
  56.7 26.6 %collective-permute-done.8.refs_14_ = bf16[7168,128]{1,0:T(8,128)(2,1)} collective-permute-done((bf16[7168,128]{1,0:T(8,128)(2,1)}, bf16[7168,128]{1,0:T(8,128)(2,1)}, u32[]{:S(2)}, u32[]{:S(2)}) %collective-permute-start.8) | collective-permute-done | bytes 1835040 | tf_op jit(solution)/shard_map/ppermute | solution.py:22
  84.0 1.7 collective-permute-start.14
  87.4 16.2 %collective-permute-done.10.refs_6_ = bf16[48,7168]{1,0:T(8,128)(2,1)} collective-permute-done((bf16[48,7168]{1,0:T(8,128)(2,1)}, bf16[48,7168]{1,0:T(8,128)(2,1)}, u32[]{:S(2)}, u32[]{:S(2)}) %collective-permute-start.10) | collective-permute-done | bytes 688160 | tf_op jit(solution)/shard_map/ppermute | solution.py:22
  103.6 3.5 %collective-permute-done.14.side_0 = bf16[256,1792]{1,0:T(8,128)(2,1)} collective-permute-done((bf16[256,1792]{1,0:T(8,128)(2,1)}, bf16[256,1792]{1,0:T(8,128)(2,1)}, u32[]{:S(2)}, u32[]{:S(2)}) %collective-permute-start.14) | collective-permute-done | bytes 917536 | tf_op jit(solution)/shard_map/ppermute | solution.py:22
  107.6 1.7 collective-permute-start.18
  109.4 11.0 %shard_map.132.mine = bf16[384,512]{1,0:T(8,128)(2,1)} custom-call(bf16[48,7168]{1,0:T(8,128)(2,1)} %copy-done.5, bf16[48,7168]{1,0:T(8,128)(2,1)} %collective-permute-done.refs_1_, bf16[48,7168]{1,0:T(8,128)(2,1)} %collective-permute-done.5.refs_2_, bf16[48,7168]{1,0:T(8,128)(2,1)} %collective-permute-done.1.refs_3_, ...), custom_call_target="tpu_custom_call" | custom-call | flops 5637144576 | bytes 20185088 | tf_op jit(solution)/shard_map/pallas_call | solution.py:105
  123.3 6.8 %collective-permute-done.18.side_1 = bf16[256,1792]{1,0:T(8,128)(2,1)} collective-permute-done((bf16[256,1792]{1,0:T(8,128)(2,1)S(1)}, bf16[256,1792]{1,0:T(8,128)(2,1)}, u32[]{:S(2)}, u32[]{:S(2)}) %collective-permute-start.18) | collective-permute-done | bytes 917536 | tf_op jit(solution)/shard_map/ppermute | solution.py:22
  132.3 5.1 %all-to-all-start = ((bf16[32,8,640]{2,1,0:T(8,128)(2,1)}), bf16[32,8,640]{2,1,0:T(8,128)(2,1)}, u32[]{:S(2)}, u32[]{:S(2)}) async-start(bf16[32,8,640]{2,1,0:T(8,128)(2,1)} %maximum_maximum_fusion), calls=%async_computation | async-start | bytes 655360 | tf_op jit(solution)/shard_map/all_to_all | solution.py:332
  138.4 8.0 %shard_map.133 = (bf16[48,3584]{1,0:T(8,128)(2,1)}, bf16[48,3584]{1,0:T(8,128)(2,1)}, bf16[48,3584]{1,0:T(8,128)(2,1)}, bf16[48,3584]{1,0:T(8,128)(2,1)}, bf16[4...) custom-call(bf16[384,512]{1,0:T(8,128)(2,1)} %shard_map.132.mine, ...), custom_call_target="tpu_custom_call" | custom-call | flops 2818572288 | bytes 10092544 | tf_op jit(solution)/shard_map/pallas_call | solution.py:160
  146.4 1.8 collective-permute-start.22
  149.6 2.4 %collective-permute-start.20 = (bf16[48,3584]{1,0:T(8,128)(2,1)}, bf16[48,3584]{1,0:T(8,128)(2,1)S(1)}, u32[]{:S(2)}, u32[]{:S(2)}) collective-permute-start(bf16[48,3584]{1,0:T(8,128)(2,1)} %get-tuple-element.112), channel_id=1, source_target_pairs={{0,24},{1,25},{2,26},{3,27},{4,28},{5,29},{6,30},{7,31},{8,0},{9,1... | collective-permute-start | bytes 1032200 | tf_op jit(solution)/shard_map/ppermute | solution.py:27
  154.0 5.4 %collective-permute-done.22.refs_3_ = bf16[48,3584]{1,0:T(8,128)(2,1)S(1)} collective-permute-done((bf16[48,3584]{1,0:T(8,128)(2,1)}, bf16[48,3584]{1,0:T(8,128)(2,1)S(1)}, u32[]{:S(2)}, u32[]{:S(2)}) %collective-permute-start.22) | collective-permute-done | bytes 344096 | tf_op jit(solution)/shard_map/ppermute | solution.py:27
  159.4 27.5 %collective-permute-start.25 = (bf16[48,3584]{1,0:T(8,128)(2,1)}, bf16[48,3584]{1,0:T(8,128)(2,1)}, u32[]{:S(2)}, u32[]{:S(2)}) collective-permute-start(bf16[48,3584]{1,0:T(8,128)(2,1)} %get-tuple-element.121), channel_id=1, source_target_pairs={{0,20},{1,21},{2,22},{3,23},{4,16},{5,17},{6,18},{7,19},{8,28},{9,... | collective-permute-start | bytes 1032200 | tf_op jit(solution)/shard_map/ppermute | solution.py:33
  188.5 9.1 %shard_map.134 = bf16[8,128,512]{2,1,0:T(8,128)(2,1)} custom-call(s32[8]{0:T(128)} %lens.1, bf16[8,576,128]{2,1,0:T(8,128)(2,1)} %bitcast.31, bf16[8,576,256]{2,1,0:T(8,128)(2,1)} %bitcast.29, bf16[256,640]{1,0:T(8,128)(2,1)} %bitcast.14.handed, f32[1,256]{1,0:T(1,128)} %bitcast.39), custom_call_target="tpu_custom_call" | custom-call | flops 1140850688 | bytes 4587520 | tf_op jit(solution)/shard_map/pallas_call | solution.py:370
  197.6 14.2 %collective-permute-done.25.refs_6_ = bf16[48,3584]{1,0:T(8,128)(2,1)} collective-permute-done((bf16[48,3584]{1,0:T(8,128)(2,1)}, bf16[48,3584]{1,0:T(8,128)(2,1)}, u32[]{:S(2)}, u32[]{:S(2)}) %collective-permute-start.25) | collective-permute-done | bytes 344096 | tf_op jit(solution)/shard_map/ppermute | solution.py:33
  211.8 4.3 %shard_map.135 = bf16[64,7168]{1,0:T(8,128)(2,1)} custom-call(s32[1]{0:T(128)} %bitcast.upper, bf16[64,192]{1,0:T(8,128)(2,1)S(1)} %copy-done.4, bf16[64,192]{1,0:T(8,128)(2,1)S(1)} %copy-done.3, bf16[48,3584]{1,0:T(8,128)(2,1)S(1)} %copy-done.2, bf16[48,3584]{1,0:T(8,128)(2,1)S(1)} %collective-permute-done.20.refs_1_, ...), custom_call_target="tpu_custom_call" | custom-call | flops 352321536 | bytes 3670016 | tf_op jit(solution)/shard_map/pallas_call | solution.py:213
  (105 shorter events, 29.5 us)
Async XLA Ops:
  0.7 48.5 %collective-permute-start.4 = (bf16[7168,128]{1,0:T(8,128)(2,1)}, bf16[7168,128]{1,0:T(8,128)(2,1)}, u32[]{:S(2)}, u32[]{:S(2)}) collective-permute-start(bf16[7168,128]{1,0:T(8,128)(2,1)} %refs_8_), channel_id=1, source_target_pairs={{0,2},{1,3},{2,0},{3,1},{4,6},{5,7},{6,4},{7,5},{8,10},{9,11},{10,... | collective-permute-start | bytes 5505032 | tf_op jit(solution)/shard_map/ppermute | solution.py:22
  9.1 20.5 %collective-permute-start = (bf16[48,7168]{1,0:T(8,128)(2,1)}, bf16[48,7168]{1,0:T(8,128)(2,1)}, u32[]{:S(2)}, u32[]{:S(2)}) collective-permute-start(bf16[48,7168]{1,0:T(8,128)(2,1)} %get-tuple-element.67), channel_id=1, source_target_pairs={{0,8},{1,9},{2,10},{3,11},{4,12},{5,13},{6,14},{7,15},{8,16},{9,17... | collective-permute-start | bytes 2064392 | tf_op jit(solution)/shard_map/ppermute | solution.py:27
  10.7 31.7 %collective-permute-start.1 = (bf16[48,7168]{1,0:T(8,128)(2,1)}, bf16[48,7168]{1,0:T(8,128)(2,1)}, u32[]{:S(2)}, u32[]{:S(2)}) collective-permute-start(bf16[48,7168]{1,0:T(8,128)(2,1)} %get-tuple-element.68), channel_id=1, source_target_pairs={{0,24},{1,25},{2,26},{3,27},{4,28},{5,29},{6,30},{7,31},{8,0},{9,1... | collective-permute-start | bytes 2064392 | tf_op jit(solution)/shard_map/ppermute | solution.py:27
  12.9 29.4 %collective-permute-start.2 = (bf16[48,7168]{1,0:T(8,128)(2,1)S(1)}, bf16[48,7168]{1,0:T(8,128)(2,1)}, u32[]{:S(2)}, u32[]{:S(2)}) collective-permute-start(bf16[48,7168]{1,0:T(8,128)(2,1)S(1)} %get-tuple-element.66.refs_0_), channel_id=1, source_target_pairs={{0,4},{1,5},{2,6},{3,7},{4,0},{5,1},{6,2},{7,3},{8,12},{9,13},{10,... | collective-permute-start | bytes 2064392 | tf_op jit(solution)/shard_map/ppermute | solution.py:22
  15.5 33.7 %collective-permute-start.3 = (bf16[128,3584]{1,0:T(8,128)(2,1)}, bf16[128,3584]{1,0:T(8,128)(2,1)}, u32[]{:S(2)}, u32[]{:S(2)}) collective-permute-start(bf16[128,3584]{1,0:T(8,128)(2,1)} %constant_dynamic-slice_fusion.1), channel_id=1, source_target_pairs={{0,4},{1,5},{2,6},{3,7},{4,0},{5,1},{6,2},{7,3},{8,12},{9,13},{10,... | collective-permute-start | bytes 2752520 | tf_op jit(solution)/shard_map/ppermute | solution.py:22
  29.6 53.7 %collective-permute-start.8 = (bf16[7168,128]{1,0:T(8,128)(2,1)}, bf16[7168,128]{1,0:T(8,128)(2,1)}, u32[]{:S(2)}, u32[]{:S(2)}) collective-permute-start(bf16[7168,128]{1,0:T(8,128)(2,1)} %refs_12_), channel_id=1, source_target_pairs={{0,2},{1,3},{2,0},{3,1},{4,6},{5,7},{6,4},{7,5},{8,10},{9,11},{10,... | collective-permute-start | bytes 5505032 | tf_op jit(solution)/shard_map/ppermute | solution.py:22
  49.1 34.2 %collective-permute-start.9 = (bf16[7168,128]{1,0:T(8,128)(2,1)}, bf16[7168,128]{1,0:T(8,128)(2,1)}, u32[]{:S(2)}, u32[]{:S(2)}) collective-permute-start(bf16[7168,128]{1,0:T(8,128)(2,1)} %refs_8_), channel_id=1, source_target_pairs={{0,1},{1,0},{2,3},{3,2},{4,5},{5,4},{6,7},{7,6},{8,9},{9,8},{10,11... | collective-permute-start | bytes 5505032 | tf_op jit(solution)/shard_map/ppermute | solution.py:22
  49.1 34.2 %collective-permute-start.5 = (bf16[48,7168]{1,0:T(8,128)(2,1)S(1)}, bf16[48,7168]{1,0:T(8,128)(2,1)}, u32[]{:S(2)}, u32[]{:S(2)}) collective-permute-start(bf16[48,7168]{1,0:T(8,128)(2,1)S(1)} %get-tuple-element.75), channel_id=1, source_target_pairs={{0,16},{1,17},{2,18},{3,19},{4,20},{5,21},{6,22},{7,23},{8,24},{9,... | collective-permute-start | bytes 2064392 | tf_op jit(solution)/shard_map/ppermute | solution.py:27
  49.9 33.5 %collective-permute-start.6 = (bf16[48,7168]{1,0:T(8,128)(2,1)}, bf16[48,7168]{1,0:T(8,128)(2,1)S(1)}, u32[]{:S(2)}, u32[]{:S(2)}) collective-permute-start(bf16[48,7168]{1,0:T(8,128)(2,1)} %collective-permute-done.refs_1_), channel_id=1, source_target_pairs={{0,4},{1,5},{2,6},{3,7},{4,0},{5,1},{6,2},{7,3},{8,12},{9,13},{10,... | collective-permute-start | bytes 2064392 | tf_op jit(solution)/shard_map/ppermute | solution.py:22
  51.4 32.0 %collective-permute-start.7 = (bf16[48,7168]{1,0:T(8,128)(2,1)}, bf16[48,7168]{1,0:T(8,128)(2,1)S(1)}, u32[]{:S(2)}, u32[]{:S(2)}) collective-permute-start(bf16[48,7168]{1,0:T(8,128)(2,1)} %collective-permute-done.1.refs_3_), channel_id=1, source_target_pairs={{0,4},{1,5},{2,6},{3,7},{4,0},{5,1},{6,2},{7,3},{8,12},{9,13},{10,... | collective-permute-start | bytes 2064392 | tf_op jit(solution)/shard_map/ppermute | solution.py:22
  83.4 23.7 %collective-permute-start.11 = (bf16[7168,128]{1,0:T(8,128)(2,1)}, bf16[7168,128]{1,0:T(8,128)(2,1)}, u32[]{:S(2)}, u32[]{:S(2)}) collective-permute-start(bf16[7168,128]{1,0:T(8,128)(2,1)} %refs_12_), channel_id=1, source_target_pairs={{0,1},{1,0},{2,3},{3,2},{4,5},{5,4},{6,7},{7,6},{8,9},{9,8},{10,11... | collective-permute-start | bytes 5505032 | tf_op jit(solution)/shard_map/ppermute | solution.py:22
  83.4 23.6 %collective-permute-start.12 = (bf16[7168,128]{1,0:T(8,128)(2,1)}, bf16[7168,128]{1,0:T(8,128)(2,1)}, u32[]{:S(2)}, u32[]{:S(2)}) collective-permute-start(bf16[7168,128]{1,0:T(8,128)(2,1)} %collective-permute-done.4.refs_10_), channel_id=1, source_target_pairs={{0,1},{1,0},{2,3},{3,2},{4,5},{5,4},{6,7},{7,6},{8,9},{9,8},{10,11... | collective-permute-start | bytes 5505032 | tf_op jit(solution)/shard_map/ppermute | solution.py:22
  83.9 23.1 %collective-permute-start.13 = (bf16[7168,128]{1,0:T(8,128)(2,1)}, bf16[7168,128]{1,0:T(8,128)(2,1)}, u32[]{:S(2)}, u32[]{:S(2)}) collective-permute-start(bf16[7168,128]{1,0:T(8,128)(2,1)} %collective-permute-done.8.refs_14_), channel_id=1, source_target_pairs={{0,1},{1,0},{2,3},{3,2},{4,5},{5,4},{6,7},{7,6},{8,9},{9,8},{10,11... | collective-permute-start | bytes 5505032 | tf_op jit(solution)/shard_map/ppermute | solution.py:22
  84.0 23.0 %collective-permute-start.14 = (bf16[256,1792]{1,0:T(8,128)(2,1)}, bf16[256,1792]{1,0:T(8,128)(2,1)}, u32[]{:S(2)}, u32[]{:S(2)}) collective-permute-start(bf16[256,1792]{1,0:T(8,128)(2,1)} %get-tuple-element.87), channel_id=1, source_target_pairs={{0,2},{1,3},{2,0},{3,1},{4,6},{5,7},{6,4},{7,5},{8,10},{9,11},{10,... | collective-permute-start | bytes 2752520 | tf_op jit(solution)/shard_map/ppermute | solution.py:22
  85.8 17.8 %collective-permute-start.10 = (bf16[48,7168]{1,0:T(8,128)(2,1)}, bf16[48,7168]{1,0:T(8,128)(2,1)}, u32[]{:S(2)}, u32[]{:S(2)}) collective-permute-start(bf16[48,7168]{1,0:T(8,128)(2,1)} %collective-permute-done.5.refs_2_), channel_id=1, source_target_pairs={{0,4},{1,5},{2,6},{3,7},{4,0},{5,1},{6,2},{7,3},{8,12},{9,13},{10,... | collective-permute-start | bytes 2064392 | tf_op jit(solution)/shard_map/ppermute | solution.py:22
  107.1 13.4 %collective-permute-start.15 = (bf16[256,3584]{1,0:T(8,128)(2,1)}, bf16[256,3584]{1,0:T(8,128)(2,1)}, u32[]{:S(2)}, u32[]{:S(2)}) collective-permute-start(bf16[256,3584]{1,0:T(8,128)(2,1)} %pad_maximum_fusion.own), channel_id=1, source_target_pairs={{0,1},{1,0},{2,3},{3,2},{4,5},{5,4},{6,7},{7,6},{8,9},{9,8},{10,11... | collective-permute-start | bytes 5505032 | tf_op jit(solution)/shard_map/ppermute | solution.py:22
  107.6 22.4 %collective-permute-start.18 = (bf16[256,1792]{1,0:T(8,128)(2,1)S(1)}, bf16[256,1792]{1,0:T(8,128)(2,1)}, u32[]{:S(2)}, u32[]{:S(2)}) collective-permute-start(bf16[256,1792]{1,0:T(8,128)(2,1)S(1)} %get-tuple-element.102), channel_id=1, source_target_pairs={{0,2},{1,3},{2,0},{3,1},{4,6},{5,7},{6,4},{7,5},{8,10},{9,11},{10,... | collective-permute-start | bytes 2752520 | tf_op jit(solution)/shard_map/ppermute | solution.py:22
  132.3 54.6 %all-to-all-start = ((bf16[32,8,640]{2,1,0:T(8,128)(2,1)}), bf16[32,8,640]{2,1,0:T(8,128)(2,1)}, u32[]{:S(2)}, u32[]{:S(2)}) async-start(bf16[32,8,640]{2,1,0:T(8,128)(2,1)} %maximum_maximum_fusion), calls=%async_computation | async-start | bytes 655360 | tf_op jit(solution)/shard_map/all_to_all | solution.py:332
  148.1 38.7 %collective-permute-start.23 = (bf16[48,3584]{1,0:T(8,128)(2,1)}, bf16[48,3584]{1,0:T(8,128)(2,1)S(1)}, u32[]{:S(2)}, u32[]{:S(2)}) collective-permute-start(bf16[48,3584]{1,0:T(8,128)(2,1)} %get-tuple-element.115), channel_id=1, source_target_pairs={{0,4},{1,5},{2,6},{3,7},{4,0},{5,1},{6,2},{7,3},{8,12},{9,13},{10,... | collective-permute-start | bytes 1032200 | tf_op jit(solution)/shard_map/ppermute | solution.py:22
  149.6 48.0 %collective-permute-start.20 = (bf16[48,3584]{1,0:T(8,128)(2,1)}, bf16[48,3584]{1,0:T(8,128)(2,1)S(1)}, u32[]{:S(2)}, u32[]{:S(2)}) collective-permute-start(bf16[48,3584]{1,0:T(8,128)(2,1)} %get-tuple-element.112), channel_id=1, source_target_pairs={{0,24},{1,25},{2,26},{3,27},{4,28},{5,29},{6,30},{7,31},{8,0},{9,1... | collective-permute-start | bytes 1032200 | tf_op jit(solution)/shard_map/ppermute | solution.py:27
  152.0 45.6 %collective-permute-start.21 = (bf16[48,3584]{1,0:T(8,128)(2,1)}, bf16[48,3584]{1,0:T(8,128)(2,1)S(1)}, u32[]{:S(2)}, u32[]{:S(2)}) collective-permute-start(bf16[48,3584]{1,0:T(8,128)(2,1)} %get-tuple-element.113), channel_id=1, source_target_pairs={{0,16},{1,17},{2,18},{3,19},{4,20},{5,21},{6,22},{7,23},{8,24},{9,... | collective-permute-start | bytes 1032200 | tf_op jit(solution)/shard_map/ppermute | solution.py:27
  152.5 45.1 %collective-permute-start.24 = (bf16[48,3584]{1,0:T(8,128)(2,1)}, bf16[48,3584]{1,0:T(8,128)(2,1)S(1)}, u32[]{:S(2)}, u32[]{:S(2)}) collective-permute-start(bf16[48,3584]{1,0:T(8,128)(2,1)} %get-tuple-element.120), channel_id=1, source_target_pairs={{0,28},{1,29},{2,30},{3,31},{4,24},{5,25},{6,26},{7,27},{8,4},{9,5... | collective-permute-start | bytes 1032200 | tf_op jit(solution)/shard_map/ppermute | solution.py:33
  159.4 52.4 %collective-permute-start.25 = (bf16[48,3584]{1,0:T(8,128)(2,1)}, bf16[48,3584]{1,0:T(8,128)(2,1)}, u32[]{:S(2)}, u32[]{:S(2)}) collective-permute-start(bf16[48,3584]{1,0:T(8,128)(2,1)} %get-tuple-element.121), channel_id=1, source_target_pairs={{0,20},{1,21},{2,22},{3,23},{4,16},{5,17},{6,18},{7,19},{8,28},{9,... | collective-permute-start | bytes 1032200 | tf_op jit(solution)/shard_map/ppermute | solution.py:33
  186.9 24.9 %collective-permute-start.26 = (bf16[48,3584]{1,0:T(8,128)(2,1)}, bf16[48,3584]{1,0:T(8,128)(2,1)}, u32[]{:S(2)}, u32[]{:S(2)}) collective-permute-start(bf16[48,3584]{1,0:T(8,128)(2,1)} %get-tuple-element.122), channel_id=1, source_target_pairs={{0,12},{1,13},{2,14},{3,15},{4,8},{5,9},{6,10},{7,11},{8,20},{9,21... | collective-permute-start | bytes 1032200 | tf_op jit(solution)/shard_map/ppermute | solution.py:33
  (20 other events, 258.8 us)

commit v16 on v15

--- a/solution.py
+++ b/solution.py
@@ -175,9 +175,13 @@
     )(mine, other, *own, *firsts, *seconds)
 
 
+ARRIVAL = (4, 1, 2, 6, 7, 5, 3, 0)
+
+
 def combine_kernel(upper, high, low, *refs):
-    parts, out = refs[:-1], refs[-1]
-    planes = len(parts) // 2
+    out = refs[-1]
+    planes = len(ARRIVAL) // 2
+    parts = [refs[ARRIVAL.index(at)] for at in range(2 * planes)]
 
     def mix(chosen):
         values = jnp.concatenate([part[...] for part in chosen], axis=0)
@@ -216,8 +220,10 @@
             num_scalar_prefetch=1,
             grid=(2, steps),
             in_specs=[pl.BlockSpec(high.shape, lambda g, k, upper: (0, 0))] * 2
-            + [pl.BlockSpec((rows, chunk), own_block) for _ in mine]
-            + [pl.BlockSpec((rows, chunk), other_block) for _ in theirs],
+            + [
+                pl.BlockSpec((rows, chunk), own_block if at < len(mine) else other_block)
+                for at in ARRIVAL
+            ],
             out_specs=pl.BlockSpec((count, chunk), out_block),
         ),
         out_shape=jax.ShapeDtypeStruct((count, 2 * width), jnp.bfloat16),
@@ -227,7 +233,7 @@
             bytes_accessed=4 * width * (len(mine) * rows + count),
             transcendentals=0,
         ),
-    )(upper.reshape(1), high, low, *mine, *theirs)
+    )(upper.reshape(1), high, low, *[(*mine, *theirs)[at] for at in ARRIVAL])
 
 
 def places(picks, planes, split):
@@ -304,18 +310,18 @@
     own_2, peer_1, peer_3, up_x, gate_x, gate_c, up_proj, own, begin, rest = together(
         own_2, peer_1, peer_3, up_x, gate_x, gate_c, up_proj, own, begin, rest
     )
+    outgoing, own_2 = together(outgoing, own_2)
     peer_2, side_0 = swap(own_2, YBIT), swap(begin, XBIT)
     up_c, gate_xc, up_xc = swap(up_proj, CORE), swap(gate_x, CORE), swap(up_x, CORE)
-    peer_2, up_c, gate_xc, up_xc, side_0, rest, own, picks, gates = together(
-        peer_2, up_c, gate_xc, up_xc, side_0, rest, own, picks, gates
+    incoming = lax.all_to_all(outgoing, "ep", split_axis=0, concat_axis=0, tiled=True)
+    peer_2, up_c, gate_xc, up_xc, side_0, rest, own, picks, gates, incoming = together(
+        peer_2, up_c, gate_xc, up_xc, side_0, rest, own, picks, gates, incoming
     )
     own_c, side_0c, side_1 = swap(own, CORE), swap(side_0, CORE), swap(rest, XBIT)
     units = (pack_0, own_1, own_2, own_3, peer_0, peer_1, peer_2, peer_3)
     weights = (gate_proj, gate_c, gate_x, gate_xc, up_proj, up_c, up_x, up_xc)
     hidden = hidden_units(units, weights, chunk)
-    hidden, own_c, side_0c, picks, gates, outgoing = together(
-        hidden, own_c, side_0c, picks, gates, outgoing
-    )
+    hidden, own_c, side_0c, picks, gates = together(hidden, own_c, side_0c, picks, gates)
     table = gate_table(picks, gates, planes, split, slots).reshape(count, planes * slots)
     high = lax.reduce_precision(table, 8, 7)
     high, low = high.astype(jnp.bfloat16), (table - high).astype(jnp.bfloat16)
@@ -329,12 +335,11 @@
     theirs[3] = cross(theirs[3], n_ep - 3 * split)
     theirs[1] = cross(theirs[1], n_ep - split)
     mine[3] = shift(mine[3], n_ep - 3 * split)
-    incoming = lax.all_to_all(outgoing, "ep", split_axis=0, concat_axis=0, tiled=True)
-    theirs[0], incoming = together(theirs[0], incoming)
     handed = incoming.reshape(-1, incoming.shape[2])
+    mine[0], handed = together(mine[0], handed)
     marks = handed[:, latents.shape[1]].astype(jnp.float32)[None, :]
     attended = attend(queries, cache_latents, cache_lens, handed, marks)
-    mine[3], attended = together(mine[3], attended)
+    theirs[0], attended = together(theirs[0], attended)
     return combine(upper, high, low, mine, theirs, span), attended
 
 

time: 217 us -> 214 us (0.986)
  the two profiles are of different devices: /device:TPU:0 before, /device:TPU:16 now
where the time goes in v16:
time: 214 us
  waiting for transfers between devices  131 us (61%)
  Pallas kernels  34.8 us (16%)
  starting transfers between devices  31.4 us (15%)
  other arithmetic  8.1 us (4%)
  local copies, waits for them, and re-layouts  7 us (3%)
    ppermute x18, waiting for transfers between devices, swap(): return lax.ppermute(value, 'ep', [(i, i ^ bit) for i in range(count)])  49.1 us
    ppermute x6, waiting for transfers between devices, shift(): lax.ppermute(value, 'ep', [(i, (i + step) % count) for i in range(count)])  41 us
    ppermute x3, waiting for transfers between devices, cross(): return lax.ppermute(value, 'ep', pairs)  20.3 us
    all_to_all x1, waiting for transfers between devices, layer(): lax.all_to_all(outgoing, 'ep', split_axis=0, concat_axis=0, tiled=True)  20.2 us
    ppermute x18, starting transfers between devices, swap(): return lax.ppermute(value, 'ep', [(i, i ^ bit) for i in range(count)])  13.2 us
    ppermute x6, starting transfers between devices, shift(): lax.ppermute(value, 'ep', [(i, (i + step) % count) for i in range(count)])  11.6 us
    pallas_call x1, Pallas kernels, hidden_units(): pl.pallas_call(partial(hidden_kernel, len(units)), grid=(width // chunk,)...  11 us
    pallas_call x1, Pallas kernels, attend(): pl.pallas_call(attend_kernel, grid=(requests,), in_specs=[pl.BlockSpec(me...  9.1 us
  transfers between devices with their start and end apart: 28, of which 14 were waited for; matrix products, arithmetic and copies ran while one was open for 6% of the time, Pallas kernels for 11%

profile of v16, /device:TPU:16, one launch (start us, length us, event | category | flops | bytes accessed | tf_op | source)
XLA Modules:
  0.0 213.7 jit_solution(8419282494908048101)
XLA Ops:
  5.1 2.5 %shard_map.131 = (bf16[48,7168]{1,0:T(8,128)(2,1)S(1)}, bf16[48,7168]{1,0:T(8,128)(2,1)}, bf16[48,7168]{1,0:T(8,128)(2,1)S(1)}, bf16[48,7168]{1,0:T(8,128)(2,1)}) custom-call(bf16[192,64]{1,0:T(8,128)(2,1)S(1)} %fusion.3.chosen, bf16[64,7168]{1,0:T(8,128)(2,1)S(1)} %bitcast.28), custom_call_target="tpu_custom_call" | custom-call | flops 176160768 | bytes 3670016 | tf_op jit(solution)/shard_map/pallas_call | solution.py:60
  16.1 1.7 maximum_maximum_fusion
  17.7 21.9 %collective-permute-done.refs_1_ = bf16[48,7168]{1,0:T(8,128)(2,1)} collective-permute-done((bf16[48,7168]{1,0:T(8,128)(2,1)}, bf16[48,7168]{1,0:T(8,128)(2,1)}, u32[]{:S(2)}, u32[]{:S(2)}) %collective-permute-start) | collective-permute-done | bytes 688160 | tf_op jit(solution)/shard_map/ppermute | solution.py:27
  40.3 5.4 %collective-permute-done.3 = bf16[128,3584]{1,0:T(8,128)(2,1)} collective-permute-done((bf16[128,3584]{1,0:T(8,128)(2,1)}, bf16[128,3584]{1,0:T(8,128)(2,1)}, u32[]{:S(2)}, u32[]{:S(2)}) %collective-permute-start.3) | collective-permute-done | bytes 917536 | tf_op jit(solution)/shard_map/ppermute | solution.py:22
  45.8 2.2 %collective-permute-start.5 = (bf16[48,7168]{1,0:T(8,128)(2,1)S(1)}, bf16[48,7168]{1,0:T(8,128)(2,1)}, u32[]{:S(2)}, u32[]{:S(2)}) collective-permute-start(bf16[48,7168]{1,0:T(8,128)(2,1)S(1)} %get-tuple-element.78), channel_id=1, source_target_pairs={{0,16},{1,17},{2,18},{3,19},{4,20},{5,21},{6,22},{7,23},{8,24},{9,... | collective-permute-start | bytes 2064392 | tf_op jit(solution)/shard_map/ppermute | solution.py:27
  50.1 2.2 %fusion.1 = (bf16[256,1792]{1,0:T(8,128)(2,1)S(1)}, bf16[256,1792]{1,0:T(8,128)(2,1)}) fusion(bf16[128,3584]{1,0:T(8,128)(2,1)S(1)} %constant_dynamic-slice_fusion, bf16[128,3584]{1,0:T(8,128)(2,1)} %collective-permute-done.3), kind=kLoop, calls=%fused_computation.7 | loop fusion | flops 3670016 | bytes 3670016 | tf_op jit(solution)/shard_map/concatenate | solution.py:307
  52.3 2.6 %pad_maximum_fusion.own = bf16[256,3584]{1,0:T(8,128)(2,1)} fusion(bf16[128,3584]{1,0:T(8,128)(2,1)} %collective-permute-done.3, bf16[128,3584]{1,0:T(8,128)(2,1)S(1)} %constant_dynamic-slice_fusion), kind=kLoop, calls=%fused_computation.2 | loop fusion | flops 3670016 | bytes 3670016 | tf_op jit(solution)/shard_map/concatenate | solution.py:307
  54.8 27.3 %collective-permute-done.8.refs_14_ = bf16[7168,128]{1,0:T(8,128)(2,1)} collective-permute-done((bf16[7168,128]{1,0:T(8,128)(2,1)}, bf16[7168,128]{1,0:T(8,128)(2,1)}, u32[]{:S(2)}, u32[]{:S(2)}) %collective-permute-start.8) | collective-permute-done | bytes 1835040 | tf_op jit(solution)/shard_map/ppermute | solution.py:22
  85.8 4.1 %all-to-all-start = ((bf16[32,8,640]{2,1,0:T(8,128)(2,1)}), bf16[32,8,640]{2,1,0:T(8,128)(2,1)S(1)}, u32[]{:S(2)}, u32[]{:S(2)}) async-start(bf16[32,8,640]{2,1,0:T(8,128)(2,1)} %maximum_maximum_fusion), calls=%async_computation | async-start | bytes 655360 | tf_op jit(solution)/shard_map/all_to_all | solution.py:316
  90.0 20.2 %all-to-all-done = bf16[32,8,640]{2,1,0:T(8,128)(2,1)S(1)} async-done(((bf16[32,8,640]{2,1,0:T(8,128)(2,1)}), bf16[32,8,640]{2,1,0:T(8,128)(2,1)S(1)}, u32[]{:S(2)}, u32[]{:S(2)}) %all-to-all-start) | async-done | bytes 327712 | tf_op jit(solution)/shard_map/all_to_all | solution.py:316
  112.0 11.0 %shard_map.132.mine = bf16[384,512]{1,0:T(8,128)(2,1)} custom-call(bf16[48,7168]{1,0:T(8,128)(2,1)} %copy-done.3, bf16[48,7168]{1,0:T(8,128)(2,1)} %collective-permute-done.refs_1_, bf16[48,7168]{1,0:T(8,128)(2,1)} %collective-permute-done.5.refs_2_, bf16[48,7168]{1,0:T(8,128)(2,1)} %collective-permute-done.1.refs_3_, ...), custom_call_target="tpu_custom_call" | custom-call | flops 5637144576 | bytes 20185088 | tf_op jit(solution)/shard_map/pallas_call | solution.py:105
  124.4 8.8 %collective-permute-done.18.side_1 = bf16[256,1792]{1,0:T(8,128)(2,1)} collective-permute-done((bf16[256,1792]{1,0:T(8,128)(2,1)S(1)}, bf16[256,1792]{1,0:T(8,128)(2,1)}, u32[]{:S(2)}, u32[]{:S(2)}) %collective-permute-start.18) | collective-permute-done | bytes 917536 | tf_op jit(solution)/shard_map/ppermute | solution.py:22
  134.3 2.7 %collective-permute-done.19.side_1c = bf16[256,1792]{1,0:T(8,128)(2,1)S(1)} collective-permute-done((bf16[256,1792]{1,0:T(8,128)(2,1)}, bf16[256,1792]{1,0:T(8,128)(2,1)S(1)}, u32[]{:S(2)}, u32[]{:S(2)}) %collective-permute-start.19) | collective-permute-done | bytes 917536 | tf_op jit(solution)/shard_map/ppermute | solution.py:22
  137.9 8.0 %shard_map.133 = (bf16[48,3584]{1,0:T(8,128)(2,1)}, bf16[48,3584]{1,0:T(8,128)(2,1)}, bf16[48,3584]{1,0:T(8,128)(2,1)}, bf16[48,3584]{1,0:T(8,128)(2,1)}, bf16[4...) custom-call(bf16[384,512]{1,0:T(8,128)(2,1)} %shard_map.132.mine, ...), custom_call_target="tpu_custom_call" | custom-call | flops 2818572288 | bytes 10092544 | tf_op jit(solution)/shard_map/pallas_call | solution.py:160
  147.0 3.5 %collective-permute-start.22 = (bf16[48,3584]{1,0:T(8,128)(2,1)}, bf16[48,3584]{1,0:T(8,128)(2,1)S(1)}, u32[]{:S(2)}, u32[]{:S(2)}) collective-permute-start(bf16[48,3584]{1,0:T(8,128)(2,1)} %get-tuple-element.121), channel_id=1, source_target_pairs={{0,16},{1,17},{2,18},{3,19},{4,20},{5,21},{6,22},{7,23},{8,24},{9,... | collective-permute-start | bytes 1032200 | tf_op jit(solution)/shard_map/ppermute | solution.py:27
  152.4 3.8 %collective-permute-done.20.refs_0_ = bf16[48,3584]{1,0:T(8,128)(2,1)S(1)} collective-permute-done((bf16[48,3584]{1,0:T(8,128)(2,1)}, bf16[48,3584]{1,0:T(8,128)(2,1)S(1)}, u32[]{:S(2)}, u32[]{:S(2)}) %collective-permute-start.20) | collective-permute-done | bytes 344096 | tf_op jit(solution)/shard_map/ppermute | solution.py:22
  157.7 3.5 %collective-permute-start.26 = (bf16[48,3584]{1,0:T(8,128)(2,1)}, bf16[48,3584]{1,0:T(8,128)(2,1)}, u32[]{:S(2)}, u32[]{:S(2)}) collective-permute-start(bf16[48,3584]{1,0:T(8,128)(2,1)} %get-tuple-element.125), channel_id=1, source_target_pairs={{0,8},{1,9},{2,10},{3,11},{4,12},{5,13},{6,14},{7,15},{8,16},{9,17... | collective-permute-start | bytes 1032200 | tf_op jit(solution)/shard_map/ppermute | solution.py:27
  162.0 9.1 %shard_map.134 = bf16[8,128,512]{2,1,0:T(8,128)(2,1)} custom-call(s32[8]{0:T(128)} %lens.1, bf16[8,576,128]{2,1,0:T(8,128)(2,1)} %bitcast.33, bf16[8,576,256]{2,1,0:T(8,128)(2,1)} %bitcast.29, bf16[256,640]{1,0:T(8,128)(2,1)} %bitcast.31, f32[1,256]{1,0:T(1,128)} %bitcast.41), custom_call_target="tpu_custom_call" | custom-call | flops 1140850688 | bytes 4587520 | tf_op jit(solution)/shard_map/pallas_call | solution.py:375
  171.1 14.9 %collective-permute-done.22.refs_2_ = bf16[48,3584]{1,0:T(8,128)(2,1)S(1)} collective-permute-done((bf16[48,3584]{1,0:T(8,128)(2,1)}, bf16[48,3584]{1,0:T(8,128)(2,1)S(1)}, u32[]{:S(2)}, u32[]{:S(2)}) %collective-permute-start.22) | collective-permute-done | bytes 344096 | tf_op jit(solution)/shard_map/ppermute | solution.py:27
  186.0 14.1 %collective-permute-done.23.refs_3_ = bf16[48,3584]{1,0:T(8,128)(2,1)S(1)} collective-permute-done((bf16[48,3584]{1,0:T(8,128)(2,1)}, bf16[48,3584]{1,0:T(8,128)(2,1)S(1)}, u32[]{:S(2)}, u32[]{:S(2)}) %collective-permute-start.23) | collective-permute-done | bytes 344096 | tf_op jit(solution)/shard_map/ppermute | solution.py:33
  200.0 3.7 %collective-permute-done.24.refs_4_ = bf16[48,3584]{1,0:T(8,128)(2,1)S(1)} collective-permute-done((bf16[48,3584]{1,0:T(8,128)(2,1)}, bf16[48,3584]{1,0:T(8,128)(2,1)S(1)}, u32[]{:S(2)}, u32[]{:S(2)}) %collective-permute-start.24) | collective-permute-done | bytes 344096 | tf_op jit(solution)/shard_map/ppermute | solution.py:33
  203.7 2.6 %collective-permute-done.25.refs_5_ = bf16[48,3584]{1,0:T(8,128)(2,1)} collective-permute-done((bf16[48,3584]{1,0:T(8,128)(2,1)}, bf16[48,3584]{1,0:T(8,128)(2,1)}, u32[]{:S(2)}, u32[]{:S(2)}) %collective-permute-start.25) | collective-permute-done | bytes 344096 | tf_op jit(solution)/shard_map/ppermute | solution.py:33
  206.3 3.3 %collective-permute-done.26.refs_6_ = bf16[48,3584]{1,0:T(8,128)(2,1)} collective-permute-done((bf16[48,3584]{1,0:T(8,128)(2,1)}, bf16[48,3584]{1,0:T(8,128)(2,1)}, u32[]{:S(2)}, u32[]{:S(2)}) %collective-permute-start.26) | collective-permute-done | bytes 344096 | tf_op jit(solution)/shard_map/ppermute | solution.py:27
  209.6 4.2 %shard_map.135 = bf16[64,7168]{1,0:T(8,128)(2,1)} custom-call(s32[1]{0:T(128)} %bitcast.upper, bf16[64,192]{1,0:T(8,128)(2,1)S(1)} %get-tuple-element.109.high, bf16[64,192]{1,0:T(8,128)(2,1)S(1)} %get-tuple-element.110.low, bf16[48,3584]{1,0:T(8,128)(2,1)S(1)} %collective-permute-done.20.refs_0_, bf16[48,3584]{1,0:T(8,128)(2,1)S(1)} %collective-permute-done.21.refs_1_, ...), custom_call_target="tpu_custom_call" | custom-call | flops 352321536 | bytes 3670016 | tf_op jit(solution)/shard_map/pallas_call | solution.py:217
  (97 shorter events, 29.8 us)
Async XLA Ops:
  0.7 45.1 %collective-permute-start.4 = (bf16[7168,128]{1,0:T(8,128)(2,1)}, bf16[7168,128]{1,0:T(8,128)(2,1)}, u32[]{:S(2)}, u32[]{:S(2)}) collective-permute-start(bf16[7168,128]{1,0:T(8,128)(2,1)} %refs_8_), channel_id=1, source_target_pairs={{0,2},{1,3},{2,0},{3,1},{4,6},{5,7},{6,4},{7,5},{8,10},{9,11},{10,... | collective-permute-start | bytes 5505032 | tf_op jit(solution)/shard_map/ppermute | solution.py:22
  7.6 32.0 %collective-permute-start = (bf16[48,7168]{1,0:T(8,128)(2,1)}, bf16[48,7168]{1,0:T(8,128)(2,1)}, u32[]{:S(2)}, u32[]{:S(2)}) collective-permute-start(bf16[48,7168]{1,0:T(8,128)(2,1)} %get-tuple-element.69), channel_id=1, source_target_pairs={{0,8},{1,9},{2,10},{3,11},{4,12},{5,13},{6,14},{7,15},{8,16},{9,17... | collective-permute-start | bytes 2064392 | tf_op jit(solution)/shard_map/ppermute | solution.py:27
  9.2 31.1 %collective-permute-start.1 = (bf16[48,7168]{1,0:T(8,128)(2,1)}, bf16[48,7168]{1,0:T(8,128)(2,1)}, u32[]{:S(2)}, u32[]{:S(2)}) collective-permute-start(bf16[48,7168]{1,0:T(8,128)(2,1)} %get-tuple-element.70), channel_id=1, source_target_pairs={{0,24},{1,25},{2,26},{3,27},{4,28},{5,29},{6,30},{7,31},{8,0},{9,1... | collective-permute-start | bytes 2064392 | tf_op jit(solution)/shard_map/ppermute | solution.py:27
  9.6 30.7 %collective-permute-start.2 = (bf16[48,7168]{1,0:T(8,128)(2,1)S(1)}, bf16[48,7168]{1,0:T(8,128)(2,1)}, u32[]{:S(2)}, u32[]{:S(2)}) collective-permute-start(bf16[48,7168]{1,0:T(8,128)(2,1)S(1)} %get-tuple-element.68.refs_0_), channel_id=1, source_target_pairs={{0,4},{1,5},{2,6},{3,7},{4,0},{5,1},{6,2},{7,3},{8,12},{9,13},{10,... | collective-permute-start | bytes 2064392 | tf_op jit(solution)/shard_map/ppermute | solution.py:22
  12.2 33.6 %collective-permute-start.3 = (bf16[128,3584]{1,0:T(8,128)(2,1)}, bf16[128,3584]{1,0:T(8,128)(2,1)}, u32[]{:S(2)}, u32[]{:S(2)}) collective-permute-start(bf16[128,3584]{1,0:T(8,128)(2,1)} %constant_dynamic-slice_fusion.1), channel_id=1, source_target_pairs={{0,4},{1,5},{2,6},{3,7},{4,0},{5,1},{6,2},{7,3},{8,12},{9,13},{10,... | collective-permute-start | bytes 2752520 | tf_op jit(solution)/shard_map/ppermute | solution.py:22
  39.6 42.5 %collective-permute-start.8 = (bf16[7168,128]{1,0:T(8,128)(2,1)}, bf16[7168,128]{1,0:T(8,128)(2,1)}, u32[]{:S(2)}, u32[]{:S(2)}) collective-permute-start(bf16[7168,128]{1,0:T(8,128)(2,1)} %refs_12_), channel_id=1, source_target_pairs={{0,2},{1,3},{2,0},{3,1},{4,6},{5,7},{6,4},{7,5},{8,10},{9,11},{10,... | collective-permute-start | bytes 5505032 | tf_op jit(solution)/shard_map/ppermute | solution.py:22
  45.8 36.4 %collective-permute-start.9 = (bf16[7168,128]{1,0:T(8,128)(2,1)}, bf16[7168,128]{1,0:T(8,128)(2,1)}, u32[]{:S(2)}, u32[]{:S(2)}) collective-permute-start(bf16[7168,128]{1,0:T(8,128)(2,1)} %refs_8_), channel_id=1, source_target_pairs={{0,1},{1,0},{2,3},{3,2},{4,5},{5,4},{6,7},{7,6},{8,9},{9,8},{10,11... | collective-permute-start | bytes 5505032 | tf_op jit(solution)/shard_map/ppermute | solution.py:22
  45.8 36.4 %collective-permute-start.5 = (bf16[48,7168]{1,0:T(8,128)(2,1)S(1)}, bf16[48,7168]{1,0:T(8,128)(2,1)}, u32[]{:S(2)}, u32[]{:S(2)}) collective-permute-start(bf16[48,7168]{1,0:T(8,128)(2,1)S(1)} %get-tuple-element.78), channel_id=1, source_target_pairs={{0,16},{1,17},{2,18},{3,19},{4,20},{5,21},{6,22},{7,23},{8,24},{9,... | collective-permute-start | bytes 2064392 | tf_op jit(solution)/shard_map/ppermute | solution.py:27
  48.0 34.2 %collective-permute-start.6 = (bf16[48,7168]{1,0:T(8,128)(2,1)}, bf16[48,7168]{1,0:T(8,128)(2,1)}, u32[]{:S(2)}, u32[]{:S(2)}) collective-permute-start(bf16[48,7168]{1,0:T(8,128)(2,1)} %collective-permute-done.refs_1_), channel_id=1, source_target_pairs={{0,4},{1,5},{2,6},{3,7},{4,0},{5,1},{6,2},{7,3},{8,12},{9,13},{10,... | collective-permute-start | bytes 2064392 | tf_op jit(solution)/shard_map/ppermute | solution.py:22
  49.5 32.6 %collective-permute-start.7 = (bf16[48,7168]{1,0:T(8,128)(2,1)}, bf16[48,7168]{1,0:T(8,128)(2,1)}, u32[]{:S(2)}, u32[]{:S(2)}) collective-permute-start(bf16[48,7168]{1,0:T(8,128)(2,1)} %collective-permute-done.1.refs_3_), channel_id=1, source_target_pairs={{0,4},{1,5},{2,6},{3,7},{4,0},{5,1},{6,2},{7,3},{8,12},{9,13},{10,... | collective-permute-start | bytes 2064392 | tf_op jit(solution)/shard_map/ppermute | solution.py:22
  82.1 28.0 %collective-permute-start.11 = (bf16[7168,128]{1,0:T(8,128)(2,1)}, bf16[7168,128]{1,0:T(8,128)(2,1)}, u32[]{:S(2)}, u32[]{:S(2)}) collective-permute-start(bf16[7168,128]{1,0:T(8,128)(2,1)} %refs_12_), channel_id=1, source_target_pairs={{0,1},{1,0},{2,3},{3,2},{4,5},{5,4},{6,7},{7,6},{8,9},{9,8},{10,11... | collective-permute-start | bytes 5505032 | tf_op jit(solution)/shard_map/ppermute | solution.py:22
  82.2 28.0 %collective-permute-start.12 = (bf16[7168,128]{1,0:T(8,128)(2,1)}, bf16[7168,128]{1,0:T(8,128)(2,1)}, u32[]{:S(2)}, u32[]{:S(2)}) collective-permute-start(bf16[7168,128]{1,0:T(8,128)(2,1)} %collective-permute-done.4.refs_10_), channel_id=1, source_target_pairs={{0,1},{1,0},{2,3},{3,2},{4,5},{5,4},{6,7},{7,6},{8,9},{9,8},{10,11... | collective-permute-start | bytes 5505032 | tf_op jit(solution)/shard_map/ppermute | solution.py:22
  82.7 27.5 %collective-permute-start.13 = (bf16[7168,128]{1,0:T(8,128)(2,1)}, bf16[7168,128]{1,0:T(8,128)(2,1)}, u32[]{:S(2)}, u32[]{:S(2)}) collective-permute-start(bf16[7168,128]{1,0:T(8,128)(2,1)} %collective-permute-done.8.refs_14_), channel_id=1, source_target_pairs={{0,1},{1,0},{2,3},{3,2},{4,5},{5,4},{6,7},{7,6},{8,9},{9,8},{10,11... | collective-permute-start | bytes 5505032 | tf_op jit(solution)/shard_map/ppermute | solution.py:22
  82.8 27.4 %collective-permute-start.14 = (bf16[256,1792]{1,0:T(8,128)(2,1)}, bf16[256,1792]{1,0:T(8,128)(2,1)}, u32[]{:S(2)}, u32[]{:S(2)}) collective-permute-start(bf16[256,1792]{1,0:T(8,128)(2,1)} %get-tuple-element.91), channel_id=1, source_target_pairs={{0,2},{1,3},{2,0},{3,1},{4,6},{5,7},{6,4},{7,5},{8,10},{9,11},{10,... | collective-permute-start | bytes 2752520 | tf_op jit(solution)/shard_map/ppermute | solution.py:22
  84.3 25.9 %collective-permute-start.10 = (bf16[48,7168]{1,0:T(8,128)(2,1)}, bf16[48,7168]{1,0:T(8,128)(2,1)}, u32[]{:S(2)}, u32[]{:S(2)}) collective-permute-start(bf16[48,7168]{1,0:T(8,128)(2,1)} %collective-permute-done.5.refs_2_), channel_id=1, source_target_pairs={{0,4},{1,5},{2,6},{3,7},{4,0},{5,1},{6,2},{7,3},{8,12},{9,13},{10,... | collective-permute-start | bytes 2064392 | tf_op jit(solution)/shard_map/ppermute | solution.py:22
  85.8 24.4 %all-to-all-start = ((bf16[32,8,640]{2,1,0:T(8,128)(2,1)}), bf16[32,8,640]{2,1,0:T(8,128)(2,1)S(1)}, u32[]{:S(2)}, u32[]{:S(2)}) async-start(bf16[32,8,640]{2,1,0:T(8,128)(2,1)} %maximum_maximum_fusion), calls=%async_computation | async-start | bytes 655360 | tf_op jit(solution)/shard_map/all_to_all | solution.py:316
  110.2 12.8 %collective-permute-start.15 = (bf16[256,3584]{1,0:T(8,128)(2,1)}, bf16[256,3584]{1,0:T(8,128)(2,1)}, u32[]{:S(2)}, u32[]{:S(2)}) collective-permute-start(bf16[256,3584]{1,0:T(8,128)(2,1)} %pad_maximum_fusion.own), channel_id=1, source_target_pairs={{0,1},{1,0},{2,3},{3,2},{4,5},{5,4},{6,7},{7,6},{8,9},{9,8},{10,11... | collective-permute-start | bytes 5505032 | tf_op jit(solution)/shard_map/ppermute | solution.py:22
  110.3 12.7 %collective-permute-start.16 = (bf16[256,1792]{1,0:T(8,128)(2,1)}, bf16[256,1792]{1,0:T(8,128)(2,1)}, u32[]{:S(2)}, u32[]{:S(2)}) collective-permute-start(bf16[256,1792]{1,0:T(8,128)(2,1)} %collective-permute-done.14.side_0), channel_id=1, source_target_pairs={{0,1},{1,0},{2,3},{3,2},{4,5},{5,4},{6,7},{7,6},{8,9},{9,8},{10,11... | collective-permute-start | bytes 2752520 | tf_op jit(solution)/shard_map/ppermute | solution.py:22
  110.8 22.4 %collective-permute-start.18 = (bf16[256,1792]{1,0:T(8,128)(2,1)S(1)}, bf16[256,1792]{1,0:T(8,128)(2,1)}, u32[]{:S(2)}, u32[]{:S(2)}) collective-permute-start(bf16[256,1792]{1,0:T(8,128)(2,1)S(1)} %get-tuple-element.106), channel_id=1, source_target_pairs={{0,2},{1,3},{2,0},{3,1},{4,6},{5,7},{6,4},{7,5},{8,10},{9,11},{10,... | collective-permute-start | bytes 2752520 | tf_op jit(solution)/shard_map/ppermute | solution.py:22
  147.0 39.0 %collective-permute-start.22 = (bf16[48,3584]{1,0:T(8,128)(2,1)}, bf16[48,3584]{1,0:T(8,128)(2,1)S(1)}, u32[]{:S(2)}, u32[]{:S(2)}) collective-permute-start(bf16[48,3584]{1,0:T(8,128)(2,1)} %get-tuple-element.121), channel_id=1, source_target_pairs={{0,16},{1,17},{2,18},{3,19},{4,20},{5,21},{6,22},{7,23},{8,24},{9,... | collective-permute-start | bytes 1032200 | tf_op jit(solution)/shard_map/ppermute | solution.py:27
  150.5 49.5 %collective-permute-start.23 = (bf16[48,3584]{1,0:T(8,128)(2,1)}, bf16[48,3584]{1,0:T(8,128)(2,1)S(1)}, u32[]{:S(2)}, u32[]{:S(2)}) collective-permute-start(bf16[48,3584]{1,0:T(8,128)(2,1)} %get-tuple-element.122), channel_id=1, source_target_pairs={{0,20},{1,21},{2,22},{3,23},{4,16},{5,17},{6,18},{7,19},{8,28},{9,... | collective-permute-start | bytes 1032200 | tf_op jit(solution)/shard_map/ppermute | solution.py:33
  151.3 52.4 %collective-permute-start.24 = (bf16[48,3584]{1,0:T(8,128)(2,1)}, bf16[48,3584]{1,0:T(8,128)(2,1)S(1)}, u32[]{:S(2)}, u32[]{:S(2)}) collective-permute-start(bf16[48,3584]{1,0:T(8,128)(2,1)} %get-tuple-element.123), channel_id=1, source_target_pairs={{0,12},{1,13},{2,14},{3,15},{4,8},{5,9},{6,10},{7,11},{8,20},{9,21... | collective-permute-start | bytes 1032200 | tf_op jit(solution)/shard_map/ppermute | solution.py:33
  156.2 50.1 %collective-permute-start.25 = (bf16[48,3584]{1,0:T(8,128)(2,1)}, bf16[48,3584]{1,0:T(8,128)(2,1)}, u32[]{:S(2)}, u32[]{:S(2)}) collective-permute-start(bf16[48,3584]{1,0:T(8,128)(2,1)} %get-tuple-element.124), channel_id=1, source_target_pairs={{0,28},{1,29},{2,30},{3,31},{4,24},{5,25},{6,26},{7,27},{8,4},{9,5... | collective-permute-start | bytes 1032200 | tf_op jit(solution)/shard_map/ppermute | solution.py:33
  157.7 51.8 %collective-permute-start.26 = (bf16[48,3584]{1,0:T(8,128)(2,1)}, bf16[48,3584]{1,0:T(8,128)(2,1)}, u32[]{:S(2)}, u32[]{:S(2)}) collective-permute-start(bf16[48,3584]{1,0:T(8,128)(2,1)} %get-tuple-element.125), channel_id=1, source_target_pairs={{0,8},{1,9},{2,10},{3,11},{4,12},{5,13},{6,14},{7,15},{8,16},{9,17... | collective-permute-start | bytes 1032200 | tf_op jit(solution)/shard_map/ppermute | solution.py:27
  (16 other events, 261.7 us)

commit v17 on v16

--- a/solution.py
+++ b/solution.py
@@ -327,7 +327,7 @@
     high, low = high.astype(jnp.bfloat16), (table - high).astype(jnp.bfloat16)
     other, side_1, high, low = together(swap(hidden, YBIT), side_1, high, low)
     firsts, seconds = (side_0, side_0c), (side_1, swap(side_1, CORE))
-    values = down_values(hidden, other, (own, own_c), firsts, seconds, planes, span // 2)
+    values = down_values(hidden, other, (own, own_c), firsts, seconds, planes, span)
     mine, theirs = list(values[:planes]), list(values[planes:])
     theirs[0] = swap(theirs[0], YBIT)
     mine[1] = shift(mine[1], n_ep - split)
@@ -340,7 +340,7 @@
     marks = handed[:, latents.shape[1]].astype(jnp.float32)[None, :]
     attended = attend(queries, cache_latents, cache_lens, handed, marks)
     theirs[0], attended = together(theirs[0], attended)
-    return combine(upper, high, low, mine, theirs, span), attended
+    return combine(upper, high, low, mine, theirs, 2 * span), attended
 
 
 def attend_kernel(lens, query, cache, handed, marks, out):

time: 214 us -> 213 us (level)
  no operation moved by 1% of the time
where the time goes in v17:
time: 213 us; the launch traced here: 212 us
  waiting for transfers between devices  131 us (62%)
  Pallas kernels  33.5 us (16%)
  starting transfers between devices  31.4 us (15%)
  other arithmetic  8.1 us (4%)
  local copies, waits for them, and re-layouts  7 us (3%)
    ppermute x18, waiting for transfers between devices, swap(): return lax.ppermute(value, 'ep', [(i, i ^ bit) for i in range(count)])  49.1 us
    ppermute x6, waiting for transfers between devices, shift(): lax.ppermute(value, 'ep', [(i, (i + step) % count) for i in range(count)])  41 us
    ppermute x3, waiting for transfers between devices, cross(): return lax.ppermute(value, 'ep', pairs)  20.3 us
    all_to_all x1, waiting for transfers between devices, layer(): lax.all_to_all(outgoing, 'ep', split_axis=0, concat_axis=0, tiled=True)  20.2 us
    ppermute x18, starting transfers between devices, swap(): return lax.ppermute(value, 'ep', [(i, i ^ bit) for i in range(count)])  13.2 us
    ppermute x6, starting transfers between devices, shift(): lax.ppermute(value, 'ep', [(i, (i + step) % count) for i in range(count)])  11.6 us
    pallas_call x1, Pallas kernels, hidden_units(): pl.pallas_call(partial(hidden_kernel, len(units)), grid=(width // chunk,)...  11 us
    pallas_call x1, Pallas kernels, attend(): pl.pallas_call(attend_kernel, grid=(requests,), in_specs=[pl.BlockSpec(me...  9.1 us
  transfers between devices with their start and end apart: 28, of which 14 were waited for; matrix products, arithmetic and copies ran while one was open for 6% of the time, Pallas kernels for 11%

profile of v17, /device:TPU:16, one launch (start us, length us, event | category | flops | bytes accessed | tf_op | source)
XLA Modules:
  0.0 212.5 jit_solution(17801572799266752692)
XLA Ops:
  5.1 2.5 %shard_map.131 = (bf16[48,7168]{1,0:T(8,128)(2,1)S(1)}, bf16[48,7168]{1,0:T(8,128)(2,1)}, bf16[48,7168]{1,0:T(8,128)(2,1)S(1)}, bf16[48,7168]{1,0:T(8,128)(2,1)}) custom-call(bf16[192,64]{1,0:T(8,128)(2,1)S(1)} %fusion.3.chosen, bf16[64,7168]{1,0:T(8,128)(2,1)S(1)} %bitcast.28), custom_call_target="tpu_custom_call" | custom-call | flops 176160768 | bytes 3670016 | tf_op jit(solution)/shard_map/pallas_call | solution.py:60
  16.1 1.7 maximum_maximum_fusion
  17.7 21.9 %collective-permute-done.refs_1_ = bf16[48,7168]{1,0:T(8,128)(2,1)} collective-permute-done((bf16[48,7168]{1,0:T(8,128)(2,1)}, bf16[48,7168]{1,0:T(8,128)(2,1)}, u32[]{:S(2)}, u32[]{:S(2)}) %collective-permute-start) | collective-permute-done | bytes 688160 | tf_op jit(solution)/shard_map/ppermute | solution.py:27
  40.3 5.4 %collective-permute-done.3 = bf16[128,3584]{1,0:T(8,128)(2,1)} collective-permute-done((bf16[128,3584]{1,0:T(8,128)(2,1)}, bf16[128,3584]{1,0:T(8,128)(2,1)}, u32[]{:S(2)}, u32[]{:S(2)}) %collective-permute-start.3) | collective-permute-done | bytes 917536 | tf_op jit(solution)/shard_map/ppermute | solution.py:22
  45.8 2.2 %collective-permute-start.5 = (bf16[48,7168]{1,0:T(8,128)(2,1)S(1)}, bf16[48,7168]{1,0:T(8,128)(2,1)}, u32[]{:S(2)}, u32[]{:S(2)}) collective-permute-start(bf16[48,7168]{1,0:T(8,128)(2,1)S(1)} %get-tuple-element.78), channel_id=1, source_target_pairs={{0,16},{1,17},{2,18},{3,19},{4,20},{5,21},{6,22},{7,23},{8,24},{9,... | collective-permute-start | bytes 2064392 | tf_op jit(solution)/shard_map/ppermute | solution.py:27
  50.1 2.2 %fusion.1 = (bf16[256,1792]{1,0:T(8,128)(2,1)S(1)}, bf16[256,1792]{1,0:T(8,128)(2,1)}) fusion(bf16[128,3584]{1,0:T(8,128)(2,1)S(1)} %constant_dynamic-slice_fusion, bf16[128,3584]{1,0:T(8,128)(2,1)} %collective-permute-done.3), kind=kLoop, calls=%fused_computation.7 | loop fusion | flops 3670016 | bytes 3670016 | tf_op jit(solution)/shard_map/concatenate | solution.py:307
  52.3 2.6 %pad_maximum_fusion.own = bf16[256,3584]{1,0:T(8,128)(2,1)} fusion(bf16[128,3584]{1,0:T(8,128)(2,1)} %collective-permute-done.3, bf16[128,3584]{1,0:T(8,128)(2,1)S(1)} %constant_dynamic-slice_fusion), kind=kLoop, calls=%fused_computation.2 | loop fusion | flops 3670016 | bytes 3670016 | tf_op jit(solution)/shard_map/concatenate | solution.py:307
  54.8 27.3 %collective-permute-done.8.refs_14_ = bf16[7168,128]{1,0:T(8,128)(2,1)} collective-permute-done((bf16[7168,128]{1,0:T(8,128)(2,1)}, bf16[7168,128]{1,0:T(8,128)(2,1)}, u32[]{:S(2)}, u32[]{:S(2)}) %collective-permute-start.8) | collective-permute-done | bytes 1835040 | tf_op jit(solution)/shard_map/ppermute | solution.py:22
  85.8 4.1 %all-to-all-start = ((bf16[32,8,640]{2,1,0:T(8,128)(2,1)}), bf16[32,8,640]{2,1,0:T(8,128)(2,1)S(1)}, u32[]{:S(2)}, u32[]{:S(2)}) async-start(bf16[32,8,640]{2,1,0:T(8,128)(2,1)} %maximum_maximum_fusion), calls=%async_computation | async-start | bytes 655360 | tf_op jit(solution)/shard_map/all_to_all | solution.py:316
  90.0 20.2 %all-to-all-done = bf16[32,8,640]{2,1,0:T(8,128)(2,1)S(1)} async-done(((bf16[32,8,640]{2,1,0:T(8,128)(2,1)}), bf16[32,8,640]{2,1,0:T(8,128)(2,1)S(1)}, u32[]{:S(2)}, u32[]{:S(2)}) %all-to-all-start) | async-done | bytes 327712 | tf_op jit(solution)/shard_map/all_to_all | solution.py:316
  112.0 11.0 %shard_map.132.mine = bf16[384,512]{1,0:T(8,128)(2,1)} custom-call(bf16[48,7168]{1,0:T(8,128)(2,1)} %copy-done.3, bf16[48,7168]{1,0:T(8,128)(2,1)} %collective-permute-done.refs_1_, bf16[48,7168]{1,0:T(8,128)(2,1)} %collective-permute-done.5.refs_2_, bf16[48,7168]{1,0:T(8,128)(2,1)} %collective-permute-done.1.refs_3_, ...), custom_call_target="tpu_custom_call" | custom-call | flops 5637144576 | bytes 20185088 | tf_op jit(solution)/shard_map/pallas_call | solution.py:105
  124.4 8.8 %collective-permute-done.18.side_1 = bf16[256,1792]{1,0:T(8,128)(2,1)} collective-permute-done((bf16[256,1792]{1,0:T(8,128)(2,1)S(1)}, bf16[256,1792]{1,0:T(8,128)(2,1)}, u32[]{:S(2)}, u32[]{:S(2)}) %collective-permute-start.18) | collective-permute-done | bytes 917536 | tf_op jit(solution)/shard_map/ppermute | solution.py:22
  134.3 2.7 %collective-permute-done.19.side_1c = bf16[256,1792]{1,0:T(8,128)(2,1)S(1)} collective-permute-done((bf16[256,1792]{1,0:T(8,128)(2,1)}, bf16[256,1792]{1,0:T(8,128)(2,1)S(1)}, u32[]{:S(2)}, u32[]{:S(2)}) %collective-permute-start.19) | collective-permute-done | bytes 917536 | tf_op jit(solution)/shard_map/ppermute | solution.py:22
  137.9 7.7 %shard_map.133 = (bf16[48,3584]{1,0:T(8,128)(2,1)}, bf16[48,3584]{1,0:T(8,128)(2,1)}, bf16[48,3584]{1,0:T(8,128)(2,1)}, bf16[48,3584]{1,0:T(8,128)(2,1)}, bf16[4...) custom-call(bf16[384,512]{1,0:T(8,128)(2,1)} %shard_map.132.mine, ...), custom_call_target="tpu_custom_call" | custom-call | flops 2818572288 | bytes 10092544 | tf_op jit(solution)/shard_map/pallas_call | solution.py:160
  146.8 3.5 %collective-permute-start.22 = (bf16[48,3584]{1,0:T(8,128)(2,1)}, bf16[48,3584]{1,0:T(8,128)(2,1)S(1)}, u32[]{:S(2)}, u32[]{:S(2)}) collective-permute-start(bf16[48,3584]{1,0:T(8,128)(2,1)} %get-tuple-element.121), channel_id=1, source_target_pairs={{0,16},{1,17},{2,18},{3,19},{4,20},{5,21},{6,22},{7,23},{8,24},{9,... | collective-permute-start | bytes 1032200 | tf_op jit(solution)/shard_map/ppermute | solution.py:27
  152.2 3.8 %collective-permute-done.20.refs_0_ = bf16[48,3584]{1,0:T(8,128)(2,1)S(1)} collective-permute-done((bf16[48,3584]{1,0:T(8,128)(2,1)}, bf16[48,3584]{1,0:T(8,128)(2,1)S(1)}, u32[]{:S(2)}, u32[]{:S(2)}) %collective-permute-start.20) | collective-permute-done | bytes 344096 | tf_op jit(solution)/shard_map/ppermute | solution.py:22
  157.5 3.5 %collective-permute-start.26 = (bf16[48,3584]{1,0:T(8,128)(2,1)}, bf16[48,3584]{1,0:T(8,128)(2,1)}, u32[]{:S(2)}, u32[]{:S(2)}) collective-permute-start(bf16[48,3584]{1,0:T(8,128)(2,1)} %get-tuple-element.125), channel_id=1, source_target_pairs={{0,8},{1,9},{2,10},{3,11},{4,12},{5,13},{6,14},{7,15},{8,16},{9,17... | collective-permute-start | bytes 1032200 | tf_op jit(solution)/shard_map/ppermute | solution.py:27
  161.7 9.1 %shard_map.134 = bf16[8,128,512]{2,1,0:T(8,128)(2,1)} custom-call(s32[8]{0:T(128)} %lens.1, bf16[8,576,128]{2,1,0:T(8,128)(2,1)} %bitcast.33, bf16[8,576,256]{2,1,0:T(8,128)(2,1)} %bitcast.29, bf16[256,640]{1,0:T(8,128)(2,1)} %bitcast.31, f32[1,256]{1,0:T(1,128)} %bitcast.41), custom_call_target="tpu_custom_call" | custom-call | flops 1140850688 | bytes 4587520 | tf_op jit(solution)/shard_map/pallas_call | solution.py:375
  170.8 14.9 %collective-permute-done.22.refs_2_ = bf16[48,3584]{1,0:T(8,128)(2,1)S(1)} collective-permute-done((bf16[48,3584]{1,0:T(8,128)(2,1)}, bf16[48,3584]{1,0:T(8,128)(2,1)S(1)}, u32[]{:S(2)}, u32[]{:S(2)}) %collective-permute-start.22) | collective-permute-done | bytes 344096 | tf_op jit(solution)/shard_map/ppermute | solution.py:27
  185.8 14.0 %collective-permute-done.23.refs_3_ = bf16[48,3584]{1,0:T(8,128)(2,1)S(1)} collective-permute-done((bf16[48,3584]{1,0:T(8,128)(2,1)}, bf16[48,3584]{1,0:T(8,128)(2,1)S(1)}, u32[]{:S(2)}, u32[]{:S(2)}) %collective-permute-start.23) | collective-permute-done | bytes 344096 | tf_op jit(solution)/shard_map/ppermute | solution.py:33
  199.8 3.7 %collective-permute-done.24.refs_4_ = bf16[48,3584]{1,0:T(8,128)(2,1)S(1)} collective-permute-done((bf16[48,3584]{1,0:T(8,128)(2,1)}, bf16[48,3584]{1,0:T(8,128)(2,1)S(1)}, u32[]{:S(2)}, u32[]{:S(2)}) %collective-permute-start.24) | collective-permute-done | bytes 344096 | tf_op jit(solution)/shard_map/ppermute | solution.py:33
  203.5 2.6 %collective-permute-done.25.refs_5_ = bf16[48,3584]{1,0:T(8,128)(2,1)} collective-permute-done((bf16[48,3584]{1,0:T(8,128)(2,1)}, bf16[48,3584]{1,0:T(8,128)(2,1)}, u32[]{:S(2)}, u32[]{:S(2)}) %collective-permute-start.25) | collective-permute-done | bytes 344096 | tf_op jit(solution)/shard_map/ppermute | solution.py:33
  206.1 3.3 %collective-permute-done.26.refs_6_ = bf16[48,3584]{1,0:T(8,128)(2,1)} collective-permute-done((bf16[48,3584]{1,0:T(8,128)(2,1)}, bf16[48,3584]{1,0:T(8,128)(2,1)}, u32[]{:S(2)}, u32[]{:S(2)}) %collective-permute-start.26) | collective-permute-done | bytes 344096 | tf_op jit(solution)/shard_map/ppermute | solution.py:27
  209.3 3.1 %shard_map.135 = bf16[64,7168]{1,0:T(8,128)(2,1)} custom-call(s32[1]{0:T(128)} %bitcast.upper, bf16[64,192]{1,0:T(8,128)(2,1)S(1)} %get-tuple-element.109.high, bf16[64,192]{1,0:T(8,128)(2,1)S(1)} %get-tuple-element.110.low, bf16[48,3584]{1,0:T(8,128)(2,1)S(1)} %collective-permute-done.20.refs_0_, bf16[48,3584]{1,0:T(8,128)(2,1)S(1)} %collective-permute-done.21.refs_1_, ...), custom_call_target="tpu_custom_call" | custom-call | flops 352321536 | bytes 3670016 | tf_op jit(solution)/shard_map/pallas_call | solution.py:217
  (97 shorter events, 29.8 us)
Async XLA Ops:
  0.7 45.1 %collective-permute-start.4 = (bf16[7168,128]{1,0:T(8,128)(2,1)}, bf16[7168,128]{1,0:T(8,128)(2,1)}, u32[]{:S(2)}, u32[]{:S(2)}) collective-permute-start(bf16[7168,128]{1,0:T(8,128)(2,1)} %refs_8_), channel_id=1, source_target_pairs={{0,2},{1,3},{2,0},{3,1},{4,6},{5,7},{6,4},{7,5},{8,10},{9,11},{10,... | collective-permute-start | bytes 5505032 | tf_op jit(solution)/shard_map/ppermute | solution.py:22
  7.6 32.0 %collective-permute-start = (bf16[48,7168]{1,0:T(8,128)(2,1)}, bf16[48,7168]{1,0:T(8,128)(2,1)}, u32[]{:S(2)}, u32[]{:S(2)}) collective-permute-start(bf16[48,7168]{1,0:T(8,128)(2,1)} %get-tuple-element.69), channel_id=1, source_target_pairs={{0,8},{1,9},{2,10},{3,11},{4,12},{5,13},{6,14},{7,15},{8,16},{9,17... | collective-permute-start | bytes 2064392 | tf_op jit(solution)/shard_map/ppermute | solution.py:27
  9.2 31.1 %collective-permute-start.1 = (bf16[48,7168]{1,0:T(8,128)(2,1)}, bf16[48,7168]{1,0:T(8,128)(2,1)}, u32[]{:S(2)}, u32[]{:S(2)}) collective-permute-start(bf16[48,7168]{1,0:T(8,128)(2,1)} %get-tuple-element.70), channel_id=1, source_target_pairs={{0,24},{1,25},{2,26},{3,27},{4,28},{5,29},{6,30},{7,31},{8,0},{9,1... | collective-permute-start | bytes 2064392 | tf_op jit(solution)/shard_map/ppermute | solution.py:27
  9.6 30.7 %collective-permute-start.2 = (bf16[48,7168]{1,0:T(8,128)(2,1)S(1)}, bf16[48,7168]{1,0:T(8,128)(2,1)}, u32[]{:S(2)}, u32[]{:S(2)}) collective-permute-start(bf16[48,7168]{1,0:T(8,128)(2,1)S(1)} %get-tuple-element.68.refs_0_), channel_id=1, source_target_pairs={{0,4},{1,5},{2,6},{3,7},{4,0},{5,1},{6,2},{7,3},{8,12},{9,13},{10,... | collective-permute-start | bytes 2064392 | tf_op jit(solution)/shard_map/ppermute | solution.py:22
  12.2 33.6 %collective-permute-start.3 = (bf16[128,3584]{1,0:T(8,128)(2,1)}, bf16[128,3584]{1,0:T(8,128)(2,1)}, u32[]{:S(2)}, u32[]{:S(2)}) collective-permute-start(bf16[128,3584]{1,0:T(8,128)(2,1)} %constant_dynamic-slice_fusion.1), channel_id=1, source_target_pairs={{0,4},{1,5},{2,6},{3,7},{4,0},{5,1},{6,2},{7,3},{8,12},{9,13},{10,... | collective-permute-start | bytes 2752520 | tf_op jit(solution)/shard_map/ppermute | solution.py:22
  39.6 42.5 %collective-permute-start.8 = (bf16[7168,128]{1,0:T(8,128)(2,1)}, bf16[7168,128]{1,0:T(8,128)(2,1)}, u32[]{:S(2)}, u32[]{:S(2)}) collective-permute-start(bf16[7168,128]{1,0:T(8,128)(2,1)} %refs_12_), channel_id=1, source_target_pairs={{0,2},{1,3},{2,0},{3,1},{4,6},{5,7},{6,4},{7,5},{8,10},{9,11},{10,... | collective-permute-start | bytes 5505032 | tf_op jit(solution)/shard_map/ppermute | solution.py:22
  45.8 36.4 %collective-permute-start.9 = (bf16[7168,128]{1,0:T(8,128)(2,1)}, bf16[7168,128]{1,0:T(8,128)(2,1)}, u32[]{:S(2)}, u32[]{:S(2)}) collective-permute-start(bf16[7168,128]{1,0:T(8,128)(2,1)} %refs_8_), channel_id=1, source_target_pairs={{0,1},{1,0},{2,3},{3,2},{4,5},{5,4},{6,7},{7,6},{8,9},{9,8},{10,11... | collective-permute-start | bytes 5505032 | tf_op jit(solution)/shard_map/ppermute | solution.py:22
  45.8 36.4 %collective-permute-start.5 = (bf16[48,7168]{1,0:T(8,128)(2,1)S(1)}, bf16[48,7168]{1,0:T(8,128)(2,1)}, u32[]{:S(2)}, u32[]{:S(2)}) collective-permute-start(bf16[48,7168]{1,0:T(8,128)(2,1)S(1)} %get-tuple-element.78), channel_id=1, source_target_pairs={{0,16},{1,17},{2,18},{3,19},{4,20},{5,21},{6,22},{7,23},{8,24},{9,... | collective-permute-start | bytes 2064392 | tf_op jit(solution)/shard_map/ppermute | solution.py:27
  48.0 34.2 %collective-permute-start.6 = (bf16[48,7168]{1,0:T(8,128)(2,1)}, bf16[48,7168]{1,0:T(8,128)(2,1)}, u32[]{:S(2)}, u32[]{:S(2)}) collective-permute-start(bf16[48,7168]{1,0:T(8,128)(2,1)} %collective-permute-done.refs_1_), channel_id=1, source_target_pairs={{0,4},{1,5},{2,6},{3,7},{4,0},{5,1},{6,2},{7,3},{8,12},{9,13},{10,... | collective-permute-start | bytes 2064392 | tf_op jit(solution)/shard_map/ppermute | solution.py:22
  49.5 32.6 %collective-permute-start.7 = (bf16[48,7168]{1,0:T(8,128)(2,1)}, bf16[48,7168]{1,0:T(8,128)(2,1)}, u32[]{:S(2)}, u32[]{:S(2)}) collective-permute-start(bf16[48,7168]{1,0:T(8,128)(2,1)} %collective-permute-done.1.refs_3_), channel_id=1, source_target_pairs={{0,4},{1,5},{2,6},{3,7},{4,0},{5,1},{6,2},{7,3},{8,12},{9,13},{10,... | collective-permute-start | bytes 2064392 | tf_op jit(solution)/shard_map/ppermute | solution.py:22
  82.1 28.0 %collective-permute-start.11 = (bf16[7168,128]{1,0:T(8,128)(2,1)}, bf16[7168,128]{1,0:T(8,128)(2,1)}, u32[]{:S(2)}, u32[]{:S(2)}) collective-permute-start(bf16[7168,128]{1,0:T(8,128)(2,1)} %refs_12_), channel_id=1, source_target_pairs={{0,1},{1,0},{2,3},{3,2},{4,5},{5,4},{6,7},{7,6},{8,9},{9,8},{10,11... | collective-permute-start | bytes 5505032 | tf_op jit(solution)/shard_map/ppermute | solution.py:22
  82.2 28.0 %collective-permute-start.12 = (bf16[7168,128]{1,0:T(8,128)(2,1)}, bf16[7168,128]{1,0:T(8,128)(2,1)}, u32[]{:S(2)}, u32[]{:S(2)}) collective-permute-start(bf16[7168,128]{1,0:T(8,128)(2,1)} %collective-permute-done.4.refs_10_), channel_id=1, source_target_pairs={{0,1},{1,0},{2,3},{3,2},{4,5},{5,4},{6,7},{7,6},{8,9},{9,8},{10,11... | collective-permute-start | bytes 5505032 | tf_op jit(solution)/shard_map/ppermute | solution.py:22
  82.7 27.5 %collective-permute-start.13 = (bf16[7168,128]{1,0:T(8,128)(2,1)}, bf16[7168,128]{1,0:T(8,128)(2,1)}, u32[]{:S(2)}, u32[]{:S(2)}) collective-permute-start(bf16[7168,128]{1,0:T(8,128)(2,1)} %collective-permute-done.8.refs_14_), channel_id=1, source_target_pairs={{0,1},{1,0},{2,3},{3,2},{4,5},{5,4},{6,7},{7,6},{8,9},{9,8},{10,11... | collective-permute-start | bytes 5505032 | tf_op jit(solution)/shard_map/ppermute | solution.py:22
  82.8 27.4 %collective-permute-start.14 = (bf16[256,1792]{1,0:T(8,128)(2,1)}, bf16[256,1792]{1,0:T(8,128)(2,1)}, u32[]{:S(2)}, u32[]{:S(2)}) collective-permute-start(bf16[256,1792]{1,0:T(8,128)(2,1)} %get-tuple-element.91), channel_id=1, source_target_pairs={{0,2},{1,3},{2,0},{3,1},{4,6},{5,7},{6,4},{7,5},{8,10},{9,11},{10,... | collective-permute-start | bytes 2752520 | tf_op jit(solution)/shard_map/ppermute | solution.py:22
  84.3 25.9 %collective-permute-start.10 = (bf16[48,7168]{1,0:T(8,128)(2,1)}, bf16[48,7168]{1,0:T(8,128)(2,1)}, u32[]{:S(2)}, u32[]{:S(2)}) collective-permute-start(bf16[48,7168]{1,0:T(8,128)(2,1)} %collective-permute-done.5.refs_2_), channel_id=1, source_target_pairs={{0,4},{1,5},{2,6},{3,7},{4,0},{5,1},{6,2},{7,3},{8,12},{9,13},{10,... | collective-permute-start | bytes 2064392 | tf_op jit(solution)/shard_map/ppermute | solution.py:22
  85.8 24.4 %all-to-all-start = ((bf16[32,8,640]{2,1,0:T(8,128)(2,1)}), bf16[32,8,640]{2,1,0:T(8,128)(2,1)S(1)}, u32[]{:S(2)}, u32[]{:S(2)}) async-start(bf16[32,8,640]{2,1,0:T(8,128)(2,1)} %maximum_maximum_fusion), calls=%async_computation | async-start | bytes 655360 | tf_op jit(solution)/shard_map/all_to_all | solution.py:316
  110.2 12.8 %collective-permute-start.15 = (bf16[256,3584]{1,0:T(8,128)(2,1)}, bf16[256,3584]{1,0:T(8,128)(2,1)}, u32[]{:S(2)}, u32[]{:S(2)}) collective-permute-start(bf16[256,3584]{1,0:T(8,128)(2,1)} %pad_maximum_fusion.own), channel_id=1, source_target_pairs={{0,1},{1,0},{2,3},{3,2},{4,5},{5,4},{6,7},{7,6},{8,9},{9,8},{10,11... | collective-permute-start | bytes 5505032 | tf_op jit(solution)/shard_map/ppermute | solution.py:22
  110.3 12.7 %collective-permute-start.16 = (bf16[256,1792]{1,0:T(8,128)(2,1)}, bf16[256,1792]{1,0:T(8,128)(2,1)}, u32[]{:S(2)}, u32[]{:S(2)}) collective-permute-start(bf16[256,1792]{1,0:T(8,128)(2,1)} %collective-permute-done.14.side_0), channel_id=1, source_target_pairs={{0,1},{1,0},{2,3},{3,2},{4,5},{5,4},{6,7},{7,6},{8,9},{9,8},{10,11... | collective-permute-start | bytes 2752520 | tf_op jit(solution)/shard_map/ppermute | solution.py:22
  110.8 22.4 %collective-permute-start.18 = (bf16[256,1792]{1,0:T(8,128)(2,1)S(1)}, bf16[256,1792]{1,0:T(8,128)(2,1)}, u32[]{:S(2)}, u32[]{:S(2)}) collective-permute-start(bf16[256,1792]{1,0:T(8,128)(2,1)S(1)} %get-tuple-element.106), channel_id=1, source_target_pairs={{0,2},{1,3},{2,0},{3,1},{4,6},{5,7},{6,4},{7,5},{8,10},{9,11},{10,... | collective-permute-start | bytes 2752520 | tf_op jit(solution)/shard_map/ppermute | solution.py:22
  146.8 39.0 %collective-permute-start.22 = (bf16[48,3584]{1,0:T(8,128)(2,1)}, bf16[48,3584]{1,0:T(8,128)(2,1)S(1)}, u32[]{:S(2)}, u32[]{:S(2)}) collective-permute-start(bf16[48,3584]{1,0:T(8,128)(2,1)} %get-tuple-element.121), channel_id=1, source_target_pairs={{0,16},{1,17},{2,18},{3,19},{4,20},{5,21},{6,22},{7,23},{8,24},{9,... | collective-permute-start | bytes 1032200 | tf_op jit(solution)/shard_map/ppermute | solution.py:27
  150.3 49.5 %collective-permute-start.23 = (bf16[48,3584]{1,0:T(8,128)(2,1)}, bf16[48,3584]{1,0:T(8,128)(2,1)S(1)}, u32[]{:S(2)}, u32[]{:S(2)}) collective-permute-start(bf16[48,3584]{1,0:T(8,128)(2,1)} %get-tuple-element.122), channel_id=1, source_target_pairs={{0,20},{1,21},{2,22},{3,23},{4,16},{5,17},{6,18},{7,19},{8,28},{9,... | collective-permute-start | bytes 1032200 | tf_op jit(solution)/shard_map/ppermute | solution.py:33
  151.1 52.4 %collective-permute-start.24 = (bf16[48,3584]{1,0:T(8,128)(2,1)}, bf16[48,3584]{1,0:T(8,128)(2,1)S(1)}, u32[]{:S(2)}, u32[]{:S(2)}) collective-permute-start(bf16[48,3584]{1,0:T(8,128)(2,1)} %get-tuple-element.123), channel_id=1, source_target_pairs={{0,12},{1,13},{2,14},{3,15},{4,8},{5,9},{6,10},{7,11},{8,20},{9,21... | collective-permute-start | bytes 1032200 | tf_op jit(solution)/shard_map/ppermute | solution.py:33
  156.0 50.1 %collective-permute-start.25 = (bf16[48,3584]{1,0:T(8,128)(2,1)}, bf16[48,3584]{1,0:T(8,128)(2,1)}, u32[]{:S(2)}, u32[]{:S(2)}) collective-permute-start(bf16[48,3584]{1,0:T(8,128)(2,1)} %get-tuple-element.124), channel_id=1, source_target_pairs={{0,28},{1,29},{2,30},{3,31},{4,24},{5,25},{6,26},{7,27},{8,4},{9,5... | collective-permute-start | bytes 1032200 | tf_op jit(solution)/shard_map/ppermute | solution.py:33
  157.5 51.8 %collective-permute-start.26 = (bf16[48,3584]{1,0:T(8,128)(2,1)}, bf16[48,3584]{1,0:T(8,128)(2,1)}, u32[]{:S(2)}, u32[]{:S(2)}) collective-permute-start(bf16[48,3584]{1,0:T(8,128)(2,1)} %get-tuple-element.125), channel_id=1, source_target_pairs={{0,8},{1,9},{2,10},{3,11},{4,12},{5,13},{6,14},{7,15},{8,16},{9,17... | collective-permute-start | bytes 1032200 | tf_op jit(solution)/shard_map/ppermute | solution.py:27
  (16 other events, 261.5 us)

commit v18 on v17

--- a/solution.py
+++ b/solution.py
@@ -290,8 +290,8 @@
     pack_0, out_1, out_2, out_3 = packs(
         chosen.reshape(planes * slots, count), rows, planes, span
     )
-    pack_0, out_1, out_3, latents, owners, requests, down_proj = together(
-        pack_0, out_1, out_3, latents, owners, requests, down_proj
+    pack_0, out_1, out_3, latents, owners, requests = together(
+        pack_0, out_1, out_3, latents, owners, requests
     )
     own_1, own_3, peer_0 = shift(out_1, split), shift(out_3, 3 * split), swap(pack_0, YBIT)
     send = lax.dynamic_slice_in_dim(down_proj, (2 - 2 * upper) * span, 2 * span, 1)

time: 213 us -> 213 us (level)
    ppermute x6, starting transfers between devices: 11.6 us -> 9.43 us  [shift(): lax.ppermute(value, 'ep', [(i, (i + step) % count) for i in range(count)])]
  transfers between devices with their start and end apart: 28 -> 28, of which waited for: 14 -> 14; matrix products, arithmetic and copies ran while one was open for 6% -> 7% of each run, Pallas kernels for 11% -> 11%
where the time goes in v18:
time: 213 us; the launch traced here: 212 us
  waiting for transfers between devices  132 us (62%)
  Pallas kernels  33.5 us (16%)
  starting transfers between devices  30 us (14%)
  other arithmetic  8.61 us (4%)
  local copies, waits for them, and re-layouts  5.61 us (3%)
    ppermute x18, waiting for transfers between devices, swap(): return lax.ppermute(value, 'ep', [(i, i ^ bit) for i in range(count)])  49.1 us
    ppermute x6, waiting for transfers between devices, shift(): lax.ppermute(value, 'ep', [(i, (i + step) % count) for i in range(count)])  42.3 us
    ppermute x3, waiting for transfers between devices, cross(): return lax.ppermute(value, 'ep', pairs)  20.3 us
    all_to_all x1, waiting for transfers between devices, layer(): lax.all_to_all(outgoing, 'ep', split_axis=0, concat_axis=0, tiled=True)  20.2 us
    ppermute x18, starting transfers between devices, swap(): return lax.ppermute(value, 'ep', [(i, i ^ bit) for i in range(count)])  14 us
    pallas_call x1, Pallas kernels, hidden_units(): pl.pallas_call(partial(hidden_kernel, len(units)), grid=(width // chunk,)...  11 us
    ppermute x6, starting transfers between devices, shift(): lax.ppermute(value, 'ep', [(i, (i + step) % count) for i in range(count)])  9.43 us
    pallas_call x1, Pallas kernels, attend(): pl.pallas_call(attend_kernel, grid=(requests,), in_specs=[pl.BlockSpec(me...  9.1 us
  transfers between devices with their start and end apart: 28, of which 14 were waited for; matrix products, arithmetic and copies ran while one was open for 7% of the time, Pallas kernels for 11%

profile of v18, /device:TPU:16, one launch (start us, length us, event | category | flops | bytes accessed | tf_op | source)
XLA Modules:
  0.0 212.5 jit_solution(7136466255353080338)
XLA Ops:
  5.3 2.5 %shard_map.131 = (bf16[48,7168]{1,0:T(8,128)(2,1)S(1)}, bf16[48,7168]{1,0:T(8,128)(2,1)}, bf16[48,7168]{1,0:T(8,128)(2,1)S(1)}, bf16[48,7168]{1,0:T(8,128)(2,1)}) custom-call(bf16[192,64]{1,0:T(8,128)(2,1)S(1)} %fusion.3.chosen, bf16[64,7168]{1,0:T(8,128)(2,1)S(1)} %bitcast.28), custom_call_target="tpu_custom_call" | custom-call | flops 176160768 | bytes 3670016 | tf_op jit(solution)/shard_map/pallas_call | solution.py:60
  11.8 1.9 convolution_convert_fusion
  13.6 1.9 copy.32
  17.4 23.2 %collective-permute-done.refs_1_ = bf16[48,7168]{1,0:T(8,128)(2,1)} collective-permute-done((bf16[48,7168]{1,0:T(8,128)(2,1)}, bf16[48,7168]{1,0:T(8,128)(2,1)}, u32[]{:S(2)}, u32[]{:S(2)}) %collective-permute-start) | collective-permute-done | bytes 688160 | tf_op jit(solution)/shard_map/ppermute | solution.py:27
  42.1 1.9 collective-permute-done.4.refs_10_
  46.1 2.5 %fusion.1 = (bf16[256,1792]{1,0:T(8,128)(2,1)}, bf16[256,1792]{1,0:T(8,128)(2,1)}) fusion(bf16[128,3584]{1,0:T(8,128)(2,1)S(1)} %constant_dynamic-slice_fusion, bf16[128,3584]{1,0:T(8,128)(2,1)} %collective-permute-done.3), kind=kLoop, calls=%fused_computation.7 | loop fusion | flops 3670016 | bytes 3670016 | tf_op jit(solution)/shard_map/concatenate | solution.py:307
  48.7 2.6 %pad_maximum_fusion.own = bf16[256,3584]{1,0:T(8,128)(2,1)} fusion(bf16[128,3584]{1,0:T(8,128)(2,1)} %collective-permute-done.3, bf16[128,3584]{1,0:T(8,128)(2,1)S(1)} %constant_dynamic-slice_fusion), kind=kLoop, calls=%fused_computation.2 | loop fusion | flops 3670016 | bytes 3670016 | tf_op jit(solution)/shard_map/concatenate | solution.py:307
  51.3 30.8 %collective-permute-done.8.refs_14_ = bf16[7168,128]{1,0:T(8,128)(2,1)} collective-permute-done((bf16[7168,128]{1,0:T(8,128)(2,1)}, bf16[7168,128]{1,0:T(8,128)(2,1)}, u32[]{:S(2)}, u32[]{:S(2)}) %collective-permute-start.8) | collective-permute-done | bytes 1835040 | tf_op jit(solution)/shard_map/ppermute | solution.py:22
  85.8 4.1 %all-to-all-start = ((bf16[32,8,640]{2,1,0:T(8,128)(2,1)}), bf16[32,8,640]{2,1,0:T(8,128)(2,1)S(1)}, u32[]{:S(2)}, u32[]{:S(2)}) async-start(bf16[32,8,640]{2,1,0:T(8,128)(2,1)} %maximum_maximum_fusion), calls=%async_computation | async-start | bytes 655360 | tf_op jit(solution)/shard_map/all_to_all | solution.py:316
  90.0 20.2 %all-to-all-done = bf16[32,8,640]{2,1,0:T(8,128)(2,1)S(1)} async-done(((bf16[32,8,640]{2,1,0:T(8,128)(2,1)}), bf16[32,8,640]{2,1,0:T(8,128)(2,1)S(1)}, u32[]{:S(2)}, u32[]{:S(2)}) %all-to-all-start) | async-done | bytes 327712 | tf_op jit(solution)/shard_map/all_to_all | solution.py:316
  112.0 11.0 %shard_map.132.mine = bf16[384,512]{1,0:T(8,128)(2,1)} custom-call(bf16[48,7168]{1,0:T(8,128)(2,1)} %copy-done.3, bf16[48,7168]{1,0:T(8,128)(2,1)} %collective-permute-done.refs_1_, bf16[48,7168]{1,0:T(8,128)(2,1)} %collective-permute-done.5.refs_2_, bf16[48,7168]{1,0:T(8,128)(2,1)} %collective-permute-done.1.refs_3_, ...), custom_call_target="tpu_custom_call" | custom-call | flops 5637144576 | bytes 20185088 | tf_op jit(solution)/shard_map/pallas_call | solution.py:105
  124.4 8.8 %collective-permute-done.18.side_1 = bf16[256,1792]{1,0:T(8,128)(2,1)} collective-permute-done((bf16[256,1792]{1,0:T(8,128)(2,1)S(1)}, bf16[256,1792]{1,0:T(8,128)(2,1)}, u32[]{:S(2)}, u32[]{:S(2)}) %collective-permute-start.18) | collective-permute-done | bytes 917536 | tf_op jit(solution)/shard_map/ppermute | solution.py:22
  134.3 2.7 %collective-permute-done.19.side_1c = bf16[256,1792]{1,0:T(8,128)(2,1)S(1)} collective-permute-done((bf16[256,1792]{1,0:T(8,128)(2,1)}, bf16[256,1792]{1,0:T(8,128)(2,1)S(1)}, u32[]{:S(2)}, u32[]{:S(2)}) %collective-permute-start.19) | collective-permute-done | bytes 917536 | tf_op jit(solution)/shard_map/ppermute | solution.py:22
  137.9 7.7 %shard_map.133 = (bf16[48,3584]{1,0:T(8,128)(2,1)}, bf16[48,3584]{1,0:T(8,128)(2,1)}, bf16[48,3584]{1,0:T(8,128)(2,1)}, bf16[48,3584]{1,0:T(8,128)(2,1)}, bf16[4...) custom-call(bf16[384,512]{1,0:T(8,128)(2,1)} %shard_map.132.mine, ...), custom_call_target="tpu_custom_call" | custom-call | flops 2818572288 | bytes 10092544 | tf_op jit(solution)/shard_map/pallas_call | solution.py:160
  146.8 3.5 %collective-permute-start.22 = (bf16[48,3584]{1,0:T(8,128)(2,1)}, bf16[48,3584]{1,0:T(8,128)(2,1)S(1)}, u32[]{:S(2)}, u32[]{:S(2)}) collective-permute-start(bf16[48,3584]{1,0:T(8,128)(2,1)} %get-tuple-element.119), channel_id=1, source_target_pairs={{0,16},{1,17},{2,18},{3,19},{4,20},{5,21},{6,22},{7,23},{8,24},{9,... | collective-permute-start | bytes 1032200 | tf_op jit(solution)/shard_map/ppermute | solution.py:27
  152.2 3.8 %collective-permute-done.20.refs_0_ = bf16[48,3584]{1,0:T(8,128)(2,1)S(1)} collective-permute-done((bf16[48,3584]{1,0:T(8,128)(2,1)}, bf16[48,3584]{1,0:T(8,128)(2,1)S(1)}, u32[]{:S(2)}, u32[]{:S(2)}) %collective-permute-start.20) | collective-permute-done | bytes 344096 | tf_op jit(solution)/shard_map/ppermute | solution.py:22
  157.5 3.5 %collective-permute-start.26 = (bf16[48,3584]{1,0:T(8,128)(2,1)}, bf16[48,3584]{1,0:T(8,128)(2,1)}, u32[]{:S(2)}, u32[]{:S(2)}) collective-permute-start(bf16[48,3584]{1,0:T(8,128)(2,1)} %get-tuple-element.123), channel_id=1, source_target_pairs={{0,8},{1,9},{2,10},{3,11},{4,12},{5,13},{6,14},{7,15},{8,16},{9,17... | collective-permute-start | bytes 1032200 | tf_op jit(solution)/shard_map/ppermute | solution.py:27
  161.7 9.1 %shard_map.134 = bf16[8,128,512]{2,1,0:T(8,128)(2,1)} custom-call(s32[8]{0:T(128)} %lens.1, bf16[8,576,128]{2,1,0:T(8,128)(2,1)} %bitcast.33, bf16[8,576,256]{2,1,0:T(8,128)(2,1)} %bitcast.29, bf16[256,640]{1,0:T(8,128)(2,1)} %bitcast.31, f32[1,256]{1,0:T(1,128)} %bitcast.41), custom_call_target="tpu_custom_call" | custom-call | flops 1140850688 | bytes 4587520 | tf_op jit(solution)/shard_map/pallas_call | solution.py:375
  170.8 14.9 %collective-permute-done.22.refs_2_ = bf16[48,3584]{1,0:T(8,128)(2,1)S(1)} collective-permute-done((bf16[48,3584]{1,0:T(8,128)(2,1)}, bf16[48,3584]{1,0:T(8,128)(2,1)S(1)}, u32[]{:S(2)}, u32[]{:S(2)}) %collective-permute-start.22) | collective-permute-done | bytes 344096 | tf_op jit(solution)/shard_map/ppermute | solution.py:27
  185.8 14.0 %collective-permute-done.23.refs_3_ = bf16[48,3584]{1,0:T(8,128)(2,1)S(1)} collective-permute-done((bf16[48,3584]{1,0:T(8,128)(2,1)}, bf16[48,3584]{1,0:T(8,128)(2,1)S(1)}, u32[]{:S(2)}, u32[]{:S(2)}) %collective-permute-start.23) | collective-permute-done | bytes 344096 | tf_op jit(solution)/shard_map/ppermute | solution.py:33
  199.8 3.7 %collective-permute-done.24.refs_4_ = bf16[48,3584]{1,0:T(8,128)(2,1)S(1)} collective-permute-done((bf16[48,3584]{1,0:T(8,128)(2,1)}, bf16[48,3584]{1,0:T(8,128)(2,1)S(1)}, u32[]{:S(2)}, u32[]{:S(2)}) %collective-permute-start.24) | collective-permute-done | bytes 344096 | tf_op jit(solution)/shard_map/ppermute | solution.py:33
  203.5 2.5 %collective-permute-done.25.refs_5_ = bf16[48,3584]{1,0:T(8,128)(2,1)} collective-permute-done((bf16[48,3584]{1,0:T(8,128)(2,1)}, bf16[48,3584]{1,0:T(8,128)(2,1)}, u32[]{:S(2)}, u32[]{:S(2)}) %collective-permute-start.25) | collective-permute-done | bytes 344096 | tf_op jit(solution)/shard_map/ppermute | solution.py:33
  206.1 3.3 %collective-permute-done.26.refs_6_ = bf16[48,3584]{1,0:T(8,128)(2,1)} collective-permute-done((bf16[48,3584]{1,0:T(8,128)(2,1)}, bf16[48,3584]{1,0:T(8,128)(2,1)}, u32[]{:S(2)}, u32[]{:S(2)}) %collective-permute-start.26) | collective-permute-done | bytes 344096 | tf_op jit(solution)/shard_map/ppermute | solution.py:27
  209.3 3.1 %shard_map.135 = bf16[64,7168]{1,0:T(8,128)(2,1)} custom-call(s32[1]{0:T(128)} %bitcast.upper, bf16[64,192]{1,0:T(8,128)(2,1)S(1)} %get-tuple-element.107.high, bf16[64,192]{1,0:T(8,128)(2,1)S(1)} %get-tuple-element.108.low, bf16[48,3584]{1,0:T(8,128)(2,1)S(1)} %collective-permute-done.20.refs_0_, bf16[48,3584]{1,0:T(8,128)(2,1)S(1)} %collective-permute-done.21.refs_1_, ...), custom_call_target="tpu_custom_call" | custom-call | flops 352321536 | bytes 3670016 | tf_op jit(solution)/shard_map/pallas_call | solution.py:217
  (99 shorter events, 28.2 us)
Async XLA Ops:
  0.7 43.3 %collective-permute-start.4 = (bf16[7168,128]{1,0:T(8,128)(2,1)}, bf16[7168,128]{1,0:T(8,128)(2,1)}, u32[]{:S(2)}, u32[]{:S(2)}) collective-permute-start(bf16[7168,128]{1,0:T(8,128)(2,1)} %refs_8_), channel_id=1, source_target_pairs={{0,2},{1,3},{2,0},{3,1},{4,6},{5,7},{6,4},{7,5},{8,10},{9,11},{10,... | collective-permute-start | bytes 5505032 | tf_op jit(solution)/shard_map/ppermute | solution.py:22
  3.2 38.8 %collective-permute-start.3 = (bf16[128,3584]{1,0:T(8,128)(2,1)}, bf16[128,3584]{1,0:T(8,128)(2,1)}, u32[]{:S(2)}, u32[]{:S(2)}) collective-permute-start(bf16[128,3584]{1,0:T(8,128)(2,1)} %constant_dynamic-slice_fusion.1), channel_id=1, source_target_pairs={{0,4},{1,5},{2,6},{3,7},{4,0},{5,1},{6,2},{7,3},{8,12},{9,13},{10,... | collective-permute-start | bytes 2752520 | tf_op jit(solution)/shard_map/ppermute | solution.py:22
  8.7 31.9 %collective-permute-start = (bf16[48,7168]{1,0:T(8,128)(2,1)}, bf16[48,7168]{1,0:T(8,128)(2,1)}, u32[]{:S(2)}, u32[]{:S(2)}) collective-permute-start(bf16[48,7168]{1,0:T(8,128)(2,1)} %get-tuple-element.68), channel_id=1, source_target_pairs={{0,8},{1,9},{2,10},{3,11},{4,12},{5,13},{6,14},{7,15},{8,16},{9,17... | collective-permute-start | bytes 2064392 | tf_op jit(solution)/shard_map/ppermute | solution.py:27
  10.3 31.8 %collective-permute-start.1 = (bf16[48,7168]{1,0:T(8,128)(2,1)}, bf16[48,7168]{1,0:T(8,128)(2,1)}, u32[]{:S(2)}, u32[]{:S(2)}) collective-permute-start(bf16[48,7168]{1,0:T(8,128)(2,1)} %get-tuple-element.69), channel_id=1, source_target_pairs={{0,24},{1,25},{2,26},{3,27},{4,28},{5,29},{6,30},{7,31},{8,0},{9,1... | collective-permute-start | bytes 2064392 | tf_op jit(solution)/shard_map/ppermute | solution.py:27
  10.7 31.3 %collective-permute-start.2 = (bf16[48,7168]{1,0:T(8,128)(2,1)S(1)}, bf16[48,7168]{1,0:T(8,128)(2,1)}, u32[]{:S(2)}, u32[]{:S(2)}) collective-permute-start(bf16[48,7168]{1,0:T(8,128)(2,1)S(1)} %get-tuple-element.67.refs_0_), channel_id=1, source_target_pairs={{0,4},{1,5},{2,6},{3,7},{4,0},{5,1},{6,2},{7,3},{8,12},{9,13},{10,... | collective-permute-start | bytes 2064392 | tf_op jit(solution)/shard_map/ppermute | solution.py:22
  40.5 41.6 %collective-permute-start.8 = (bf16[7168,128]{1,0:T(8,128)(2,1)}, bf16[7168,128]{1,0:T(8,128)(2,1)}, u32[]{:S(2)}, u32[]{:S(2)}) collective-permute-start(bf16[7168,128]{1,0:T(8,128)(2,1)} %refs_12_), channel_id=1, source_target_pairs={{0,2},{1,3},{2,0},{3,1},{4,6},{5,7},{6,4},{7,5},{8,10},{9,11},{10,... | collective-permute-start | bytes 5505032 | tf_op jit(solution)/shard_map/ppermute | solution.py:22
  44.0 38.2 %collective-permute-start.9 = (bf16[7168,128]{1,0:T(8,128)(2,1)}, bf16[7168,128]{1,0:T(8,128)(2,1)}, u32[]{:S(2)}, u32[]{:S(2)}) collective-permute-start(bf16[7168,128]{1,0:T(8,128)(2,1)} %refs_8_), channel_id=1, source_target_pairs={{0,1},{1,0},{2,3},{3,2},{4,5},{5,4},{6,7},{7,6},{8,9},{9,8},{10,11... | collective-permute-start | bytes 5505032 | tf_op jit(solution)/shard_map/ppermute | solution.py:22
  44.0 38.2 %collective-permute-start.5 = (bf16[48,7168]{1,0:T(8,128)(2,1)S(1)}, bf16[48,7168]{1,0:T(8,128)(2,1)}, u32[]{:S(2)}, u32[]{:S(2)}) collective-permute-start(bf16[48,7168]{1,0:T(8,128)(2,1)S(1)} %copy-done.5), channel_id=1, source_target_pairs={{0,16},{1,17},{2,18},{3,19},{4,20},{5,21},{6,22},{7,23},{8,24},{9,... | collective-permute-start | bytes 2064392 | tf_op jit(solution)/shard_map/ppermute | solution.py:27
  44.0 38.2 %collective-permute-start.6 = (bf16[48,7168]{1,0:T(8,128)(2,1)}, bf16[48,7168]{1,0:T(8,128)(2,1)}, u32[]{:S(2)}, u32[]{:S(2)}) collective-permute-start(bf16[48,7168]{1,0:T(8,128)(2,1)} %collective-permute-done.refs_1_), channel_id=1, source_target_pairs={{0,4},{1,5},{2,6},{3,7},{4,0},{5,1},{6,2},{7,3},{8,12},{9,13},{10,... | collective-permute-start | bytes 2064392 | tf_op jit(solution)/shard_map/ppermute | solution.py:22
  45.8 36.3 %collective-permute-start.7 = (bf16[48,7168]{1,0:T(8,128)(2,1)}, bf16[48,7168]{1,0:T(8,128)(2,1)}, u32[]{:S(2)}, u32[]{:S(2)}) collective-permute-start(bf16[48,7168]{1,0:T(8,128)(2,1)} %collective-permute-done.1.refs_3_), channel_id=1, source_target_pairs={{0,4},{1,5},{2,6},{3,7},{4,0},{5,1},{6,2},{7,3},{8,12},{9,13},{10,... | collective-permute-start | bytes 2064392 | tf_op jit(solution)/shard_map/ppermute | solution.py:22
  82.2 28.0 %collective-permute-start.11 = (bf16[7168,128]{1,0:T(8,128)(2,1)}, bf16[7168,128]{1,0:T(8,128)(2,1)}, u32[]{:S(2)}, u32[]{:S(2)}) collective-permute-start(bf16[7168,128]{1,0:T(8,128)(2,1)} %refs_12_), channel_id=1, source_target_pairs={{0,1},{1,0},{2,3},{3,2},{4,5},{5,4},{6,7},{7,6},{8,9},{9,8},{10,11... | collective-permute-start | bytes 5505032 | tf_op jit(solution)/shard_map/ppermute | solution.py:22
  82.2 28.0 %collective-permute-start.12 = (bf16[7168,128]{1,0:T(8,128)(2,1)}, bf16[7168,128]{1,0:T(8,128)(2,1)}, u32[]{:S(2)}, u32[]{:S(2)}) collective-permute-start(bf16[7168,128]{1,0:T(8,128)(2,1)} %collective-permute-done.4.refs_10_), channel_id=1, source_target_pairs={{0,1},{1,0},{2,3},{3,2},{4,5},{5,4},{6,7},{7,6},{8,9},{9,8},{10,11... | collective-permute-start | bytes 5505032 | tf_op jit(solution)/shard_map/ppermute | solution.py:22
  82.7 27.5 %collective-permute-start.13 = (bf16[7168,128]{1,0:T(8,128)(2,1)}, bf16[7168,128]{1,0:T(8,128)(2,1)}, u32[]{:S(2)}, u32[]{:S(2)}) collective-permute-start(bf16[7168,128]{1,0:T(8,128)(2,1)} %collective-permute-done.8.refs_14_), channel_id=1, source_target_pairs={{0,1},{1,0},{2,3},{3,2},{4,5},{5,4},{6,7},{7,6},{8,9},{9,8},{10,11... | collective-permute-start | bytes 5505032 | tf_op jit(solution)/shard_map/ppermute | solution.py:22
  82.8 27.4 %collective-permute-start.14 = (bf16[256,1792]{1,0:T(8,128)(2,1)}, bf16[256,1792]{1,0:T(8,128)(2,1)}, u32[]{:S(2)}, u32[]{:S(2)}) collective-permute-start(bf16[256,1792]{1,0:T(8,128)(2,1)} %get-tuple-element.89), channel_id=1, source_target_pairs={{0,2},{1,3},{2,0},{3,1},{4,6},{5,7},{6,4},{7,5},{8,10},{9,11},{10,... | collective-permute-start | bytes 2752520 | tf_op jit(solution)/shard_map/ppermute | solution.py:22
  84.3 25.9 %collective-permute-start.10 = (bf16[48,7168]{1,0:T(8,128)(2,1)}, bf16[48,7168]{1,0:T(8,128)(2,1)}, u32[]{:S(2)}, u32[]{:S(2)}) collective-permute-start(bf16[48,7168]{1,0:T(8,128)(2,1)} %collective-permute-done.5.refs_2_), channel_id=1, source_target_pairs={{0,4},{1,5},{2,6},{3,7},{4,0},{5,1},{6,2},{7,3},{8,12},{9,13},{10,... | collective-permute-start | bytes 2064392 | tf_op jit(solution)/shard_map/ppermute | solution.py:22
  85.8 24.4 %all-to-all-start = ((bf16[32,8,640]{2,1,0:T(8,128)(2,1)}), bf16[32,8,640]{2,1,0:T(8,128)(2,1)S(1)}, u32[]{:S(2)}, u32[]{:S(2)}) async-start(bf16[32,8,640]{2,1,0:T(8,128)(2,1)} %maximum_maximum_fusion), calls=%async_computation | async-start | bytes 655360 | tf_op jit(solution)/shard_map/all_to_all | solution.py:316
  110.2 12.8 %collective-permute-start.15 = (bf16[256,3584]{1,0:T(8,128)(2,1)}, bf16[256,3584]{1,0:T(8,128)(2,1)}, u32[]{:S(2)}, u32[]{:S(2)}) collective-permute-start(bf16[256,3584]{1,0:T(8,128)(2,1)} %pad_maximum_fusion.own), channel_id=1, source_target_pairs={{0,1},{1,0},{2,3},{3,2},{4,5},{5,4},{6,7},{7,6},{8,9},{9,8},{10,11... | collective-permute-start | bytes 5505032 | tf_op jit(solution)/shard_map/ppermute | solution.py:22
  110.3 12.7 %collective-permute-start.16 = (bf16[256,1792]{1,0:T(8,128)(2,1)}, bf16[256,1792]{1,0:T(8,128)(2,1)}, u32[]{:S(2)}, u32[]{:S(2)}) collective-permute-start(bf16[256,1792]{1,0:T(8,128)(2,1)} %collective-permute-done.14.side_0), channel_id=1, source_target_pairs={{0,1},{1,0},{2,3},{3,2},{4,5},{5,4},{6,7},{7,6},{8,9},{9,8},{10,11... | collective-permute-start | bytes 2752520 | tf_op jit(solution)/shard_map/ppermute | solution.py:22
  110.8 22.4 %collective-permute-start.18 = (bf16[256,1792]{1,0:T(8,128)(2,1)S(1)}, bf16[256,1792]{1,0:T(8,128)(2,1)}, u32[]{:S(2)}, u32[]{:S(2)}) collective-permute-start(bf16[256,1792]{1,0:T(8,128)(2,1)S(1)} %copy-done.7), channel_id=1, source_target_pairs={{0,2},{1,3},{2,0},{3,1},{4,6},{5,7},{6,4},{7,5},{8,10},{9,11},{10,... | collective-permute-start | bytes 2752520 | tf_op jit(solution)/shard_map/ppermute | solution.py:22
  146.8 39.0 %collective-permute-start.22 = (bf16[48,3584]{1,0:T(8,128)(2,1)}, bf16[48,3584]{1,0:T(8,128)(2,1)S(1)}, u32[]{:S(2)}, u32[]{:S(2)}) collective-permute-start(bf16[48,3584]{1,0:T(8,128)(2,1)} %get-tuple-element.119), channel_id=1, source_target_pairs={{0,16},{1,17},{2,18},{3,19},{4,20},{5,21},{6,22},{7,23},{8,24},{9,... | collective-permute-start | bytes 1032200 | tf_op jit(solution)/shard_map/ppermute | solution.py:27
  150.3 49.5 %collective-permute-start.23 = (bf16[48,3584]{1,0:T(8,128)(2,1)}, bf16[48,3584]{1,0:T(8,128)(2,1)S(1)}, u32[]{:S(2)}, u32[]{:S(2)}) collective-permute-start(bf16[48,3584]{1,0:T(8,128)(2,1)} %get-tuple-element.120), channel_id=1, source_target_pairs={{0,20},{1,21},{2,22},{3,23},{4,16},{5,17},{6,18},{7,19},{8,28},{9,... | collective-permute-start | bytes 1032200 | tf_op jit(solution)/shard_map/ppermute | solution.py:33
  151.1 52.4 %collective-permute-start.24 = (bf16[48,3584]{1,0:T(8,128)(2,1)}, bf16[48,3584]{1,0:T(8,128)(2,1)S(1)}, u32[]{:S(2)}, u32[]{:S(2)}) collective-permute-start(bf16[48,3584]{1,0:T(8,128)(2,1)} %get-tuple-element.121), channel_id=1, source_target_pairs={{0,12},{1,13},{2,14},{3,15},{4,8},{5,9},{6,10},{7,11},{8,20},{9,21... | collective-permute-start | bytes 1032200 | tf_op jit(solution)/shard_map/ppermute | solution.py:33
  156.0 50.1 %collective-permute-start.25 = (bf16[48,3584]{1,0:T(8,128)(2,1)}, bf16[48,3584]{1,0:T(8,128)(2,1)}, u32[]{:S(2)}, u32[]{:S(2)}) collective-permute-start(bf16[48,3584]{1,0:T(8,128)(2,1)} %get-tuple-element.122), channel_id=1, source_target_pairs={{0,28},{1,29},{2,30},{3,31},{4,24},{5,25},{6,26},{7,27},{8,4},{9,5... | collective-permute-start | bytes 1032200 | tf_op jit(solution)/shard_map/ppermute | solution.py:33
  157.5 51.8 %collective-permute-start.26 = (bf16[48,3584]{1,0:T(8,128)(2,1)}, bf16[48,3584]{1,0:T(8,128)(2,1)}, u32[]{:S(2)}, u32[]{:S(2)}) collective-permute-start(bf16[48,3584]{1,0:T(8,128)(2,1)} %get-tuple-element.123), channel_id=1, source_target_pairs={{0,8},{1,9},{2,10},{3,11},{4,12},{5,13},{6,14},{7,15},{8,16},{9,17... | collective-permute-start | bytes 1032200 | tf_op jit(solution)/shard_map/ppermute | solution.py:27
  (17 other events, 343.4 us)

commit v19 on v18

--- a/solution.py
+++ b/solution.py
@@ -277,7 +277,7 @@
     planes = n_ep // split
     count, width = rows.shape
     slots = -(-3 * count * picks.shape[1] // (2 * planes * 16)) * 16
-    chunk = width // 4
+    chunk = width // 2
     upper = lax.axis_index("ep") // YBIT % 2
     span = width // 4
 

time: 213 us -> 213 us (level)
  no operation moved by 1% of the time
where the time goes in v19:
time: 213 us; the launch traced here: 212 us
  waiting for transfers between devices  132 us (62%)
  Pallas kernels  33.5 us (16%)
  starting transfers between devices  30 us (14%)
  other arithmetic  8.61 us (4%)
  local copies, waits for them, and re-layouts  5.61 us (3%)
    ppermute x18, waiting for transfers between devices, swap(): return lax.ppermute(value, 'ep', [(i, i ^ bit) for i in range(count)])  49.1 us
    ppermute x6, waiting for transfers between devices, shift(): lax.ppermute(value, 'ep', [(i, (i + step) % count) for i in range(count)])  42.3 us
    ppermute x3, waiting for transfers between devices, cross(): return lax.ppermute(value, 'ep', pairs)  20.3 us
    all_to_all x1, waiting for transfers between devices, layer(): lax.all_to_all(outgoing, 'ep', split_axis=0, concat_axis=0, tiled=True)  20.2 us
    ppermute x18, starting transfers between devices, swap(): return lax.ppermute(value, 'ep', [(i, i ^ bit) for i in range(count)])  14 us
    pallas_call x1, Pallas kernels, hidden_units(): pl.pallas_call(partial(hidden_kernel, len(units)), grid=(width // chunk,)...  11 us
    ppermute x6, starting transfers between devices, shift(): lax.ppermute(value, 'ep', [(i, (i + step) % count) for i in range(count)])  9.44 us
    pallas_call x1, Pallas kernels, attend(): pl.pallas_call(attend_kernel, grid=(requests,), in_specs=[pl.BlockSpec(me...  9.1 us
  transfers between devices with their start and end apart: 28, of which 14 were waited for; matrix products, arithmetic and copies ran while one was open for 7% of the time, Pallas kernels for 11%

profile of v19, /device:TPU:16, one launch (start us, length us, event | category | flops | bytes accessed | tf_op | source)
XLA Modules:
  0.0 212.4 jit_solution(11320359296212566768)
XLA Ops:
  5.3 2.5 %shard_map.131 = (bf16[48,7168]{1,0:T(8,128)(2,1)S(1)}, bf16[48,7168]{1,0:T(8,128)(2,1)}, bf16[48,7168]{1,0:T(8,128)(2,1)S(1)}, bf16[48,7168]{1,0:T(8,128)(2,1)}) custom-call(bf16[192,64]{1,0:T(8,128)(2,1)S(1)} %fusion.3.chosen, bf16[64,7168]{1,0:T(8,128)(2,1)S(1)} %bitcast.28), custom_call_target="tpu_custom_call" | custom-call | flops 176160768 | bytes 3670016 | tf_op jit(solution)/shard_map/pallas_call | solution.py:60
  11.8 1.9 convolution_convert_fusion
  13.6 1.9 copy.32
  17.4 23.2 %collective-permute-done.refs_1_ = bf16[48,7168]{1,0:T(8,128)(2,1)} collective-permute-done((bf16[48,7168]{1,0:T(8,128)(2,1)}, bf16[48,7168]{1,0:T(8,128)(2,1)}, u32[]{:S(2)}, u32[]{:S(2)}) %collective-permute-start) | collective-permute-done | bytes 688160 | tf_op jit(solution)/shard_map/ppermute | solution.py:27
  42.1 1.9 collective-permute-done.4.refs_10_
  46.1 2.5 %fusion.1 = (bf16[256,1792]{1,0:T(8,128)(2,1)}, bf16[256,1792]{1,0:T(8,128)(2,1)}) fusion(bf16[128,3584]{1,0:T(8,128)(2,1)S(1)} %constant_dynamic-slice_fusion, bf16[128,3584]{1,0:T(8,128)(2,1)} %collective-permute-done.3), kind=kLoop, calls=%fused_computation.7 | loop fusion | flops 3670016 | bytes 3670016 | tf_op jit(solution)/shard_map/concatenate | solution.py:307
  48.7 2.6 %pad_maximum_fusion.own = bf16[256,3584]{1,0:T(8,128)(2,1)} fusion(bf16[128,3584]{1,0:T(8,128)(2,1)} %collective-permute-done.3, bf16[128,3584]{1,0:T(8,128)(2,1)S(1)} %constant_dynamic-slice_fusion), kind=kLoop, calls=%fused_computation.2 | loop fusion | flops 3670016 | bytes 3670016 | tf_op jit(solution)/shard_map/concatenate | solution.py:307
  51.3 30.8 %collective-permute-done.8.refs_14_ = bf16[7168,128]{1,0:T(8,128)(2,1)} collective-permute-done((bf16[7168,128]{1,0:T(8,128)(2,1)}, bf16[7168,128]{1,0:T(8,128)(2,1)}, u32[]{:S(2)}, u32[]{:S(2)}) %collective-permute-start.8) | collective-permute-done | bytes 1835040 | tf_op jit(solution)/shard_map/ppermute | solution.py:22
  85.8 4.1 %all-to-all-start = ((bf16[32,8,640]{2,1,0:T(8,128)(2,1)}), bf16[32,8,640]{2,1,0:T(8,128)(2,1)S(1)}, u32[]{:S(2)}, u32[]{:S(2)}) async-start(bf16[32,8,640]{2,1,0:T(8,128)(2,1)} %maximum_maximum_fusion), calls=%async_computation | async-start | bytes 655360 | tf_op jit(solution)/shard_map/all_to_all | solution.py:316
  90.0 20.2 %all-to-all-done = bf16[32,8,640]{2,1,0:T(8,128)(2,1)S(1)} async-done(((bf16[32,8,640]{2,1,0:T(8,128)(2,1)}), bf16[32,8,640]{2,1,0:T(8,128)(2,1)S(1)}, u32[]{:S(2)}, u32[]{:S(2)}) %all-to-all-start) | async-done | bytes 327712 | tf_op jit(solution)/shard_map/all_to_all | solution.py:316
  112.0 11.0 %shard_map.132.mine = bf16[384,512]{1,0:T(8,128)(2,1)} custom-call(bf16[48,7168]{1,0:T(8,128)(2,1)} %copy-done.3, bf16[48,7168]{1,0:T(8,128)(2,1)} %collective-permute-done.refs_1_, bf16[48,7168]{1,0:T(8,128)(2,1)} %collective-permute-done.5.refs_2_, bf16[48,7168]{1,0:T(8,128)(2,1)} %collective-permute-done.1.refs_3_, ...), custom_call_target="tpu_custom_call" | custom-call | flops 5637144576 | bytes 20185088 | tf_op jit(solution)/shard_map/pallas_call | solution.py:105
  124.4 8.9 %collective-permute-done.18.side_1 = bf16[256,1792]{1,0:T(8,128)(2,1)} collective-permute-done((bf16[256,1792]{1,0:T(8,128)(2,1)S(1)}, bf16[256,1792]{1,0:T(8,128)(2,1)}, u32[]{:S(2)}, u32[]{:S(2)}) %collective-permute-start.18) | collective-permute-done | bytes 917536 | tf_op jit(solution)/shard_map/ppermute | solution.py:22
  134.3 2.7 %collective-permute-done.19.side_1c = bf16[256,1792]{1,0:T(8,128)(2,1)S(1)} collective-permute-done((bf16[256,1792]{1,0:T(8,128)(2,1)}, bf16[256,1792]{1,0:T(8,128)(2,1)S(1)}, u32[]{:S(2)}, u32[]{:S(2)}) %collective-permute-start.19) | collective-permute-done | bytes 917536 | tf_op jit(solution)/shard_map/ppermute | solution.py:22
  137.9 7.7 %shard_map.133 = (bf16[48,3584]{1,0:T(8,128)(2,1)}, bf16[48,3584]{1,0:T(8,128)(2,1)}, bf16[48,3584]{1,0:T(8,128)(2,1)}, bf16[48,3584]{1,0:T(8,128)(2,1)}, bf16[4...) custom-call(bf16[384,512]{1,0:T(8,128)(2,1)} %shard_map.132.mine, ...), custom_call_target="tpu_custom_call" | custom-call | flops 2818572288 | bytes 10092544 | tf_op jit(solution)/shard_map/pallas_call | solution.py:160
  146.8 3.5 %collective-permute-start.22 = (bf16[48,3584]{1,0:T(8,128)(2,1)}, bf16[48,3584]{1,0:T(8,128)(2,1)S(1)}, u32[]{:S(2)}, u32[]{:S(2)}) collective-permute-start(bf16[48,3584]{1,0:T(8,128)(2,1)} %get-tuple-element.119), channel_id=1, source_target_pairs={{0,16},{1,17},{2,18},{3,19},{4,20},{5,21},{6,22},{7,23},{8,24},{9,... | collective-permute-start | bytes 1032200 | tf_op jit(solution)/shard_map/ppermute | solution.py:27
  152.2 3.8 %collective-permute-done.20.refs_0_ = bf16[48,3584]{1,0:T(8,128)(2,1)S(1)} collective-permute-done((bf16[48,3584]{1,0:T(8,128)(2,1)}, bf16[48,3584]{1,0:T(8,128)(2,1)S(1)}, u32[]{:S(2)}, u32[]{:S(2)}) %collective-permute-start.20) | collective-permute-done | bytes 344096 | tf_op jit(solution)/shard_map/ppermute | solution.py:22
  157.5 3.5 %collective-permute-start.26 = (bf16[48,3584]{1,0:T(8,128)(2,1)}, bf16[48,3584]{1,0:T(8,128)(2,1)}, u32[]{:S(2)}, u32[]{:S(2)}) collective-permute-start(bf16[48,3584]{1,0:T(8,128)(2,1)} %get-tuple-element.123), channel_id=1, source_target_pairs={{0,8},{1,9},{2,10},{3,11},{4,12},{5,13},{6,14},{7,15},{8,16},{9,17... | collective-permute-start | bytes 1032200 | tf_op jit(solution)/shard_map/ppermute | solution.py:27
  161.7 9.1 %shard_map.134 = bf16[8,128,512]{2,1,0:T(8,128)(2,1)} custom-call(s32[8]{0:T(128)} %lens.1, bf16[8,576,128]{2,1,0:T(8,128)(2,1)} %bitcast.33, bf16[8,576,256]{2,1,0:T(8,128)(2,1)} %bitcast.29, bf16[256,640]{1,0:T(8,128)(2,1)} %bitcast.31, f32[1,256]{1,0:T(1,128)} %bitcast.41), custom_call_target="tpu_custom_call" | custom-call | flops 1140850688 | bytes 4587520 | tf_op jit(solution)/shard_map/pallas_call | solution.py:375
  170.8 14.9 %collective-permute-done.22.refs_2_ = bf16[48,3584]{1,0:T(8,128)(2,1)S(1)} collective-permute-done((bf16[48,3584]{1,0:T(8,128)(2,1)}, bf16[48,3584]{1,0:T(8,128)(2,1)S(1)}, u32[]{:S(2)}, u32[]{:S(2)}) %collective-permute-start.22) | collective-permute-done | bytes 344096 | tf_op jit(solution)/shard_map/ppermute | solution.py:27
  185.7 14.1 %collective-permute-done.23.refs_3_ = bf16[48,3584]{1,0:T(8,128)(2,1)S(1)} collective-permute-done((bf16[48,3584]{1,0:T(8,128)(2,1)}, bf16[48,3584]{1,0:T(8,128)(2,1)S(1)}, u32[]{:S(2)}, u32[]{:S(2)}) %collective-permute-start.23) | collective-permute-done | bytes 344096 | tf_op jit(solution)/shard_map/ppermute | solution.py:33
  199.8 3.7 %collective-permute-done.24.refs_4_ = bf16[48,3584]{1,0:T(8,128)(2,1)S(1)} collective-permute-done((bf16[48,3584]{1,0:T(8,128)(2,1)}, bf16[48,3584]{1,0:T(8,128)(2,1)S(1)}, u32[]{:S(2)}, u32[]{:S(2)}) %collective-permute-start.24) | collective-permute-done | bytes 344096 | tf_op jit(solution)/shard_map/ppermute | solution.py:33
  203.5 2.6 %collective-permute-done.25.refs_5_ = bf16[48,3584]{1,0:T(8,128)(2,1)} collective-permute-done((bf16[48,3584]{1,0:T(8,128)(2,1)}, bf16[48,3584]{1,0:T(8,128)(2,1)}, u32[]{:S(2)}, u32[]{:S(2)}) %collective-permute-start.25) | collective-permute-done | bytes 344096 | tf_op jit(solution)/shard_map/ppermute | solution.py:33
  206.0 3.3 %collective-permute-done.26.refs_6_ = bf16[48,3584]{1,0:T(8,128)(2,1)} collective-permute-done((bf16[48,3584]{1,0:T(8,128)(2,1)}, bf16[48,3584]{1,0:T(8,128)(2,1)}, u32[]{:S(2)}, u32[]{:S(2)}) %collective-permute-start.26) | collective-permute-done | bytes 344096 | tf_op jit(solution)/shard_map/ppermute | solution.py:27
  209.3 3.1 %shard_map.135 = bf16[64,7168]{1,0:T(8,128)(2,1)} custom-call(s32[1]{0:T(128)} %bitcast.upper, bf16[64,192]{1,0:T(8,128)(2,1)S(1)} %get-tuple-element.107.high, bf16[64,192]{1,0:T(8,128)(2,1)S(1)} %get-tuple-element.108.low, bf16[48,3584]{1,0:T(8,128)(2,1)S(1)} %collective-permute-done.20.refs_0_, bf16[48,3584]{1,0:T(8,128)(2,1)S(1)} %collective-permute-done.21.refs_1_, ...), custom_call_target="tpu_custom_call" | custom-call | flops 352321536 | bytes 3670016 | tf_op jit(solution)/shard_map/pallas_call | solution.py:217
  (99 shorter events, 28.2 us)
Async XLA Ops:
  0.7 43.3 %collective-permute-start.4 = (bf16[7168,128]{1,0:T(8,128)(2,1)}, bf16[7168,128]{1,0:T(8,128)(2,1)}, u32[]{:S(2)}, u32[]{:S(2)}) collective-permute-start(bf16[7168,128]{1,0:T(8,128)(2,1)} %refs_8_), channel_id=1, source_target_pairs={{0,2},{1,3},{2,0},{3,1},{4,6},{5,7},{6,4},{7,5},{8,10},{9,11},{10,... | collective-permute-start | bytes 5505032 | tf_op jit(solution)/shard_map/ppermute | solution.py:22
  3.2 38.8 %collective-permute-start.3 = (bf16[128,3584]{1,0:T(8,128)(2,1)}, bf16[128,3584]{1,0:T(8,128)(2,1)}, u32[]{:S(2)}, u32[]{:S(2)}) collective-permute-start(bf16[128,3584]{1,0:T(8,128)(2,1)} %constant_dynamic-slice_fusion.1), channel_id=1, source_target_pairs={{0,4},{1,5},{2,6},{3,7},{4,0},{5,1},{6,2},{7,3},{8,12},{9,13},{10,... | collective-permute-start | bytes 2752520 | tf_op jit(solution)/shard_map/ppermute | solution.py:22
  8.7 31.9 %collective-permute-start = (bf16[48,7168]{1,0:T(8,128)(2,1)}, bf16[48,7168]{1,0:T(8,128)(2,1)}, u32[]{:S(2)}, u32[]{:S(2)}) collective-permute-start(bf16[48,7168]{1,0:T(8,128)(2,1)} %get-tuple-element.68), channel_id=1, source_target_pairs={{0,8},{1,9},{2,10},{3,11},{4,12},{5,13},{6,14},{7,15},{8,16},{9,17... | collective-permute-start | bytes 2064392 | tf_op jit(solution)/shard_map/ppermute | solution.py:27
  10.3 31.8 %collective-permute-start.1 = (bf16[48,7168]{1,0:T(8,128)(2,1)}, bf16[48,7168]{1,0:T(8,128)(2,1)}, u32[]{:S(2)}, u32[]{:S(2)}) collective-permute-start(bf16[48,7168]{1,0:T(8,128)(2,1)} %get-tuple-element.69), channel_id=1, source_target_pairs={{0,24},{1,25},{2,26},{3,27},{4,28},{5,29},{6,30},{7,31},{8,0},{9,1... | collective-permute-start | bytes 2064392 | tf_op jit(solution)/shard_map/ppermute | solution.py:27
  10.7 31.3 %collective-permute-start.2 = (bf16[48,7168]{1,0:T(8,128)(2,1)S(1)}, bf16[48,7168]{1,0:T(8,128)(2,1)}, u32[]{:S(2)}, u32[]{:S(2)}) collective-permute-start(bf16[48,7168]{1,0:T(8,128)(2,1)S(1)} %get-tuple-element.67.refs_0_), channel_id=1, source_target_pairs={{0,4},{1,5},{2,6},{3,7},{4,0},{5,1},{6,2},{7,3},{8,12},{9,13},{10,... | collective-permute-start | bytes 2064392 | tf_op jit(solution)/shard_map/ppermute | solution.py:22
  40.5 41.6 %collective-permute-start.8 = (bf16[7168,128]{1,0:T(8,128)(2,1)}, bf16[7168,128]{1,0:T(8,128)(2,1)}, u32[]{:S(2)}, u32[]{:S(2)}) collective-permute-start(bf16[7168,128]{1,0:T(8,128)(2,1)} %refs_12_), channel_id=1, source_target_pairs={{0,2},{1,3},{2,0},{3,1},{4,6},{5,7},{6,4},{7,5},{8,10},{9,11},{10,... | collective-permute-start | bytes 5505032 | tf_op jit(solution)/shard_map/ppermute | solution.py:22
  44.0 38.2 %collective-permute-start.9 = (bf16[7168,128]{1,0:T(8,128)(2,1)}, bf16[7168,128]{1,0:T(8,128)(2,1)}, u32[]{:S(2)}, u32[]{:S(2)}) collective-permute-start(bf16[7168,128]{1,0:T(8,128)(2,1)} %refs_8_), channel_id=1, source_target_pairs={{0,1},{1,0},{2,3},{3,2},{4,5},{5,4},{6,7},{7,6},{8,9},{9,8},{10,11... | collective-permute-start | bytes 5505032 | tf_op jit(solution)/shard_map/ppermute | solution.py:22
  44.0 38.2 %collective-permute-start.5 = (bf16[48,7168]{1,0:T(8,128)(2,1)S(1)}, bf16[48,7168]{1,0:T(8,128)(2,1)}, u32[]{:S(2)}, u32[]{:S(2)}) collective-permute-start(bf16[48,7168]{1,0:T(8,128)(2,1)S(1)} %copy-done.5), channel_id=1, source_target_pairs={{0,16},{1,17},{2,18},{3,19},{4,20},{5,21},{6,22},{7,23},{8,24},{9,... | collective-permute-start | bytes 2064392 | tf_op jit(solution)/shard_map/ppermute | solution.py:27
  44.0 38.2 %collective-permute-start.6 = (bf16[48,7168]{1,0:T(8,128)(2,1)}, bf16[48,7168]{1,0:T(8,128)(2,1)}, u32[]{:S(2)}, u32[]{:S(2)}) collective-permute-start(bf16[48,7168]{1,0:T(8,128)(2,1)} %collective-permute-done.refs_1_), channel_id=1, source_target_pairs={{0,4},{1,5},{2,6},{3,7},{4,0},{5,1},{6,2},{7,3},{8,12},{9,13},{10,... | collective-permute-start | bytes 2064392 | tf_op jit(solution)/shard_map/ppermute | solution.py:22
  45.8 36.3 %collective-permute-start.7 = (bf16[48,7168]{1,0:T(8,128)(2,1)}, bf16[48,7168]{1,0:T(8,128)(2,1)}, u32[]{:S(2)}, u32[]{:S(2)}) collective-permute-start(bf16[48,7168]{1,0:T(8,128)(2,1)} %collective-permute-done.1.refs_3_), channel_id=1, source_target_pairs={{0,4},{1,5},{2,6},{3,7},{4,0},{5,1},{6,2},{7,3},{8,12},{9,13},{10,... | collective-permute-start | bytes 2064392 | tf_op jit(solution)/shard_map/ppermute | solution.py:22
  82.2 28.0 %collective-permute-start.11 = (bf16[7168,128]{1,0:T(8,128)(2,1)}, bf16[7168,128]{1,0:T(8,128)(2,1)}, u32[]{:S(2)}, u32[]{:S(2)}) collective-permute-start(bf16[7168,128]{1,0:T(8,128)(2,1)} %refs_12_), channel_id=1, source_target_pairs={{0,1},{1,0},{2,3},{3,2},{4,5},{5,4},{6,7},{7,6},{8,9},{9,8},{10,11... | collective-permute-start | bytes 5505032 | tf_op jit(solution)/shard_map/ppermute | solution.py:22
  82.2 28.0 %collective-permute-start.12 = (bf16[7168,128]{1,0:T(8,128)(2,1)}, bf16[7168,128]{1,0:T(8,128)(2,1)}, u32[]{:S(2)}, u32[]{:S(2)}) collective-permute-start(bf16[7168,128]{1,0:T(8,128)(2,1)} %collective-permute-done.4.refs_10_), channel_id=1, source_target_pairs={{0,1},{1,0},{2,3},{3,2},{4,5},{5,4},{6,7},{7,6},{8,9},{9,8},{10,11... | collective-permute-start | bytes 5505032 | tf_op jit(solution)/shard_map/ppermute | solution.py:22
  82.7 27.5 %collective-permute-start.13 = (bf16[7168,128]{1,0:T(8,128)(2,1)}, bf16[7168,128]{1,0:T(8,128)(2,1)}, u32[]{:S(2)}, u32[]{:S(2)}) collective-permute-start(bf16[7168,128]{1,0:T(8,128)(2,1)} %collective-permute-done.8.refs_14_), channel_id=1, source_target_pairs={{0,1},{1,0},{2,3},{3,2},{4,5},{5,4},{6,7},{7,6},{8,9},{9,8},{10,11... | collective-permute-start | bytes 5505032 | tf_op jit(solution)/shard_map/ppermute | solution.py:22
  82.8 27.4 %collective-permute-start.14 = (bf16[256,1792]{1,0:T(8,128)(2,1)}, bf16[256,1792]{1,0:T(8,128)(2,1)}, u32[]{:S(2)}, u32[]{:S(2)}) collective-permute-start(bf16[256,1792]{1,0:T(8,128)(2,1)} %get-tuple-element.89), channel_id=1, source_target_pairs={{0,2},{1,3},{2,0},{3,1},{4,6},{5,7},{6,4},{7,5},{8,10},{9,11},{10,... | collective-permute-start | bytes 2752520 | tf_op jit(solution)/shard_map/ppermute | solution.py:22
  84.3 25.9 %collective-permute-start.10 = (bf16[48,7168]{1,0:T(8,128)(2,1)}, bf16[48,7168]{1,0:T(8,128)(2,1)}, u32[]{:S(2)}, u32[]{:S(2)}) collective-permute-start(bf16[48,7168]{1,0:T(8,128)(2,1)} %collective-permute-done.5.refs_2_), channel_id=1, source_target_pairs={{0,4},{1,5},{2,6},{3,7},{4,0},{5,1},{6,2},{7,3},{8,12},{9,13},{10,... | collective-permute-start | bytes 2064392 | tf_op jit(solution)/shard_map/ppermute | solution.py:22
  85.8 24.4 %all-to-all-start = ((bf16[32,8,640]{2,1,0:T(8,128)(2,1)}), bf16[32,8,640]{2,1,0:T(8,128)(2,1)S(1)}, u32[]{:S(2)}, u32[]{:S(2)}) async-start(bf16[32,8,640]{2,1,0:T(8,128)(2,1)} %maximum_maximum_fusion), calls=%async_computation | async-start | bytes 655360 | tf_op jit(solution)/shard_map/all_to_all | solution.py:316
  110.2 12.8 %collective-permute-start.15 = (bf16[256,3584]{1,0:T(8,128)(2,1)}, bf16[256,3584]{1,0:T(8,128)(2,1)}, u32[]{:S(2)}, u32[]{:S(2)}) collective-permute-start(bf16[256,3584]{1,0:T(8,128)(2,1)} %pad_maximum_fusion.own), channel_id=1, source_target_pairs={{0,1},{1,0},{2,3},{3,2},{4,5},{5,4},{6,7},{7,6},{8,9},{9,8},{10,11... | collective-permute-start | bytes 5505032 | tf_op jit(solution)/shard_map/ppermute | solution.py:22
  110.3 12.7 %collective-permute-start.16 = (bf16[256,1792]{1,0:T(8,128)(2,1)}, bf16[256,1792]{1,0:T(8,128)(2,1)}, u32[]{:S(2)}, u32[]{:S(2)}) collective-permute-start(bf16[256,1792]{1,0:T(8,128)(2,1)} %collective-permute-done.14.side_0), channel_id=1, source_target_pairs={{0,1},{1,0},{2,3},{3,2},{4,5},{5,4},{6,7},{7,6},{8,9},{9,8},{10,11... | collective-permute-start | bytes 2752520 | tf_op jit(solution)/shard_map/ppermute | solution.py:22
  110.8 22.4 %collective-permute-start.18 = (bf16[256,1792]{1,0:T(8,128)(2,1)S(1)}, bf16[256,1792]{1,0:T(8,128)(2,1)}, u32[]{:S(2)}, u32[]{:S(2)}) collective-permute-start(bf16[256,1792]{1,0:T(8,128)(2,1)S(1)} %copy-done.7), channel_id=1, source_target_pairs={{0,2},{1,3},{2,0},{3,1},{4,6},{5,7},{6,4},{7,5},{8,10},{9,11},{10,... | collective-permute-start | bytes 2752520 | tf_op jit(solution)/shard_map/ppermute | solution.py:22
  146.8 39.0 %collective-permute-start.22 = (bf16[48,3584]{1,0:T(8,128)(2,1)}, bf16[48,3584]{1,0:T(8,128)(2,1)S(1)}, u32[]{:S(2)}, u32[]{:S(2)}) collective-permute-start(bf16[48,3584]{1,0:T(8,128)(2,1)} %get-tuple-element.119), channel_id=1, source_target_pairs={{0,16},{1,17},{2,18},{3,19},{4,20},{5,21},{6,22},{7,23},{8,24},{9,... | collective-permute-start | bytes 1032200 | tf_op jit(solution)/shard_map/ppermute | solution.py:27
  150.2 49.5 %collective-permute-start.23 = (bf16[48,3584]{1,0:T(8,128)(2,1)}, bf16[48,3584]{1,0:T(8,128)(2,1)S(1)}, u32[]{:S(2)}, u32[]{:S(2)}) collective-permute-start(bf16[48,3584]{1,0:T(8,128)(2,1)} %get-tuple-element.120), channel_id=1, source_target_pairs={{0,20},{1,21},{2,22},{3,23},{4,16},{5,17},{6,18},{7,19},{8,28},{9,... | collective-permute-start | bytes 1032200 | tf_op jit(solution)/shard_map/ppermute | solution.py:33
  151.0 52.4 %collective-permute-start.24 = (bf16[48,3584]{1,0:T(8,128)(2,1)}, bf16[48,3584]{1,0:T(8,128)(2,1)S(1)}, u32[]{:S(2)}, u32[]{:S(2)}) collective-permute-start(bf16[48,3584]{1,0:T(8,128)(2,1)} %get-tuple-element.121), channel_id=1, source_target_pairs={{0,12},{1,13},{2,14},{3,15},{4,8},{5,9},{6,10},{7,11},{8,20},{9,21... | collective-permute-start | bytes 1032200 | tf_op jit(solution)/shard_map/ppermute | solution.py:33
  155.9 50.1 %collective-permute-start.25 = (bf16[48,3584]{1,0:T(8,128)(2,1)}, bf16[48,3584]{1,0:T(8,128)(2,1)}, u32[]{:S(2)}, u32[]{:S(2)}) collective-permute-start(bf16[48,3584]{1,0:T(8,128)(2,1)} %get-tuple-element.122), channel_id=1, source_target_pairs={{0,28},{1,29},{2,30},{3,31},{4,24},{5,25},{6,26},{7,27},{8,4},{9,5... | collective-permute-start | bytes 1032200 | tf_op jit(solution)/shard_map/ppermute | solution.py:33
  157.5 51.8 %collective-permute-start.26 = (bf16[48,3584]{1,0:T(8,128)(2,1)}, bf16[48,3584]{1,0:T(8,128)(2,1)}, u32[]{:S(2)}, u32[]{:S(2)}) collective-permute-start(bf16[48,3584]{1,0:T(8,128)(2,1)} %get-tuple-element.123), channel_id=1, source_target_pairs={{0,8},{1,9},{2,10},{3,11},{4,12},{5,13},{6,14},{7,15},{8,16},{9,17... | collective-permute-start | bytes 1032200 | tf_op jit(solution)/shard_map/ppermute | solution.py:27
  (17 other events, 343.4 us)
